TPU v7x, 32 devices: a whole 2x2x4 slice. The times are simulated.
32 devices in a mesh: group: 2 (over x), expert: 16 (over z, y, core).
Axes of the slice: x: 2, y: 2, z: 4, core: 2. Of those that a mesh axis runs over, the one named last changes fastest.
Arguments:
- resid: bfloat16 [4096, 2048], P(('group', 'expert')), may hold values from -6 to 6
- queries: bfloat16 [4096, 2048], P(('group', 'expert')), may hold values from -48 to 48
- span_kv: bfloat16 [2, 4096, 2048], P(None, ('group', 'expert')), may hold values from -4 to 4
- cache_kv: bfloat16 [2, 32, 2, 128, 2048], P(None, ('group', 'expert')), may hold values from -6 to 6
- seg_len: int32 [32, 2], P(('group', 'expert')), may hold values from 0 to 128, as said below
- o_rows: bfloat16 [2048, 2048], P('expert'), may hold values from -0.125 to 0.125
- norm_gain: float32 [2048], replicated, may hold values from 0.25 to 1.75
- routes: int32 [4096, 8], P(('group', 'expert')), may hold values from 0 to 15, all different within a row; in each aligned block of 128 rows (0 to 127, 128 to 255, ...) at most 96 rows name the same one
- route_wts: float32 [4096, 8], P(('group', 'expert')), may hold values from 0.05 to 0.6
- w_in: bfloat16 [16, 2048, 1024], P('expert'), may hold values from -0.125 to 0.125
- w_out: bfloat16 [16, 512, 2048], P('expert'), may hold values from -0.25 to 0.25
Outputs:
- layer_out: bfloat16 [4096, 2048], P(('group', 'expert'))
Inputs may be any that keep to these rules, and one draw needn't show every extreme that they name: seg_len[d, 0] is 1 to 128; seg_len[d, 1] is 0 (the paired request is short) or 1 to 128; seg_len[0, 0] and seg_len[0, 1] are 128 and seg_len[1, 1] is 0. `routes`: each row names 8 different experts; among the 128 rows of one device no expert is named more than 96 times.
All inputs are finite; a program needn't handle non-finite values.
Results may differ from a plain program's by a relative error of at most 0.0053.
Values may be sent and summed in bfloat16 or wider, within the bound.
No kernel may reach another device: no remote copies, remote signals or barrier semaphores. Data moves between devices by JAX's collectives and lax.ppermute only.
A program may use at most 128 MiB of HBM per device.

v0:
```python
import math

import jax
import jax.numpy as jnp
from jax import lax
from jax.sharding import PartitionSpec as P

HEADS = 16
HD = 128
FF = 512
TOPK = 8


def swapped(block, axis, distance):
    count = lax.axis_size(axis)
    route = []
    for low in range(count):
        high = low | 1 << distance
        if high != low and high < count:
            route += [(low, high), (high, low)]
    return lax.ppermute(block, axis, route)


def attend(query_rows, key_rows, value_rows, valid_keys):
    q_heads = query_rows.reshape(query_rows.shape[0], HEADS, HD)
    k_heads = key_rows.reshape(key_rows.shape[0], HEADS, HD)
    v_heads = value_rows.reshape(value_rows.shape[0], HEADS, HD)
    scores = jnp.einsum("chd,shd->hcs", q_heads, k_heads, preferred_element_type=jnp.float32) * (
        1.0 / math.sqrt(HD)
    )
    scores = jnp.where(valid_keys[None, None, :], scores, -1e30)
    peak_score = jnp.max(scores, axis=-1)
    expo = jnp.where(valid_keys[None, None, :], jnp.exp(scores - peak_score[..., None]), 0.0)
    totals = jnp.sum(expo, axis=-1)
    probs_low = expo.astype(jnp.bfloat16)
    accum_out = jnp.einsum("hcs,shd->chd", probs_low, v_heads, preferred_element_type=jnp.float32)
    return (peak_score, totals, accum_out)


def merge_parts(first, second):
    peak_a, total_a, accum_a = first
    peak_b, total_b, accum_b = second
    peak_both = jnp.maximum(peak_a, peak_b)
    scale_a = jnp.exp(peak_a - peak_both).T
    scale_b = jnp.exp(peak_b - peak_both).T
    numer = accum_a * scale_a[:, :, None] + accum_b * scale_b[:, :, None]
    denom = total_a.T * scale_a + total_b.T * scale_b
    merged = numer / denom[:, :, None]
    return merged.reshape(merged.shape[0], -1).astype(jnp.bfloat16)


def expert_mlp(token_rows, weight_in, weight_out):
    joined = jnp.dot(token_rows, weight_in, preferred_element_type=jnp.float32)
    hidden = (jax.nn.silu(joined[:, :FF]) * joined[:, FF:]).astype(jnp.bfloat16)
    return jnp.dot(hidden, weight_out, preferred_element_type=jnp.float32).astype(jnp.bfloat16)


def shards(
    resid, queries, span_kv, cache_kv, seg_len, o_rows, norm_gain, routes, route_wts, w_in, w_out
):
    span_rows = queries.shape[0]
    seg_rows = cache_kv.shape[3]
    width = queries.shape[1]
    experts_here = lax.axis_size("expert")
    positions = jnp.arange(seg_rows, dtype=jnp.int32)
    keys_a = jnp.concatenate([span_kv[0], cache_kv[0, 0, 0]], axis=0)
    vals_a = jnp.concatenate([span_kv[1], cache_kv[1, 0, 0]], axis=0)
    valid_a = jnp.concatenate([jnp.ones((span_rows,), bool), positions < seg_len[0, 0]])
    part_a = attend(queries, keys_a, vals_a, valid_a)
    length_low = seg_len[0, 1:2].astype(jnp.float32).astype(jnp.bfloat16)
    fetched, fetched_len = swapped((cache_kv[:, 0, 1], length_low), "group", 0)
    valid_b = positions.astype(jnp.float32) < fetched_len[0].astype(jnp.float32)
    part_b = attend(queries, fetched[0], fetched[1], valid_b)
    attended = merge_parts(part_a, part_b)
    projected = jnp.dot(
        attended,
        lax.all_gather(o_rows, "expert", axis=0, tiled=True),
        preferred_element_type=jnp.float32,
    )
    residual = resid.astype(jnp.float32) + projected
    normed = (
        residual
        * lax.rsqrt(jnp.mean(residual * residual, axis=-1, keepdims=True) + 1e-05)
        * norm_gain
    ).astype(jnp.bfloat16)
    capacity = min(span_rows, span_rows * TOPK * 3 // (2 * experts_here))
    onehot = (
        routes[:, :, None] == jnp.arange(experts_here, dtype=jnp.int32)[None, None, :]
    ).astype(jnp.int32)
    counts = jnp.sum(onehot, axis=1)
    before = jnp.cumsum(counts, axis=0) - counts
    slot_ids = jnp.sum(onehot * before[:, None, :], axis=-1)
    flat_slot = routes * capacity + slot_ids
    placing = jnp.any(
        flat_slot[None, :, :]
        == jnp.arange(experts_here * capacity, dtype=jnp.int32)[:, None, None],
        axis=-1,
    )
    outgoing = jnp.dot(
        placing.astype(jnp.bfloat16), normed, preferred_element_type=jnp.float32
    ).astype(jnp.bfloat16)
    outgoing = outgoing.reshape(experts_here, capacity, width)
    arrived = lax.all_to_all(outgoing, "expert", split_axis=0, concat_axis=0, tiled=True)
    flat_rows = arrived.reshape(-1, width)
    output_rows = expert_mlp(flat_rows, w_in[0], w_out[0]).reshape(arrived.shape)
    returned_rows = lax.all_to_all(output_rows, "expert", split_axis=0, concat_axis=0, tiled=True)
    returned_rows = returned_rows.reshape(experts_here * capacity, width)
    expert_sum = jnp.zeros((span_rows, width), jnp.float32)
    for route_k in range(TOPK):
        picked = returned_rows[flat_slot[:, route_k]].astype(jnp.float32)
        expert_sum = expert_sum + route_wts[:, route_k, None] * picked
    return (residual + expert_sum).astype(jnp.bfloat16)


def solution(mesh):
    placed = (
        P(("group", "expert"), None),
        P(("group", "expert"), None),
        P(None, ("group", "expert"), None),
        P(None, ("group", "expert"), None, None, None),
        P(("group", "expert"), None),
        P("expert", None),
        P(),
        P(("group", "expert"), None),
        P(("group", "expert"), None),
        P("expert", None, None),
        P("expert", None, None),
    )
    return jax.shard_map(
        shards, mesh=mesh, in_specs=placed, out_specs=P(("group", "expert"), None), check_vma=False
    )
```

profile of v0, /device:TPU:13, one launch (start us, length us, event | category | flops | bytes accessed | tf_op | source)
XLA Modules:
  0.0 446.2 jit_solution(6489206779009563548)
XLA Ops:
  6.5 0.0 copy-start
  6.5 0.0 slice-start
  6.5 0.0 all-gather.2.cloned.1.call-start
  6.5 0.7 all-gather.2.cloned.1.call-update
  7.3 1.5 fusion.66
  9.4 2.0 collective-permute-start
  11.4 0.0 slice-done
  11.4 1.3 copy.55
  12.7 0.3 collective-permute-start.1
  13.0 2.1 fusion.65
  15.0 1.3 copy.53
  16.4 1.1 copy.39
  17.4 0.0 copy-start.6
  17.4 2.4 fusion.63
  19.8 1.4 copy.54
  21.2 1.1 copy.40
  22.2 1.0 copy.35
  23.3 2.1 copy.36
  25.3 0.0 copy-done.6
  25.3 0.1 copy.47
  25.4 0.2 reduce_window_sum.11
  25.6 0.1 copy.49
  25.7 0.7 iota_compare_fusion.2
  26.5 5.6 %fusion = pred[1536,128]{1,0:T(8,128)(4,1)S(1)} fusion(s32[128,8]{0,1:T(8,128)S(1)} %multiply_add_fusion), kind=kLoop, calls=%fused_computation.11 | loop fusion | flops 2949120 | bytes 200704 | tf_op jit(solution)/shard_map/reduce_or | solution.py:94
  32.0 1.9 bitcast_reduce_fusion
  33.9 0.0 copy-start.1
  33.9 0.0 copy-start.3
  33.9 1.3 copy-done.1
  35.3 0.6 fusion.9
  35.9 0.0 copy-start.4
  36.6 0.0 copy-start.2
  36.6 0.0 copy-start.5
  36.7 0.0 collective-permute-done.1
  36.7 1.4 fusion.64
  38.1 0.0 copy-done.3
  38.1 0.5 fusion.67
  38.6 0.2 fusion.31
  38.9 0.0 copy-done.4
  38.9 0.0 copy-done.2
  38.9 0.0 copy-done.5
  38.9 0.8 fusion.14
  39.7 1.2 fusion.16
  40.9 43.6 %all-gather.2.cloned.1.call-done = bf16[2048,2048]{1,0:T(8,128)(2,1)} async-done(((bf16[128,2048]{1,0:T(8,128)(2,1)}), bf16[2048,2048]{1,0:T(8,128)(2,1)}) %all-gather.2.cloned.1.call-update) | async-done | bytes 8388624 | tf_op jit(solution)/shard_map/all_gather | solution.py:77
  84.5 4.9 %multiply_reduce_fusion = (f32[128]{0:T(128)S(1)}, f32[128,2048]{1,0:T(8,128)S(1)}) fusion(bf16[128,2048]{0,1:T(8,128)(2,1)} %bitcast.126, bf16[2048,2048]{1,0:T(8,128)(2,1)} %all-gather.2.cloned.1.call-done, bf16[128,2048]{1,0:T(8,128)(2,1)} %param.11), kind=kOutput, calls=%fused_computation.44 | convolution fusion | flops 1074790272 | bytes 10486272 | tf_op jit(solution)/shard_map/dot_general | solution.py:75
  89.4 0.0 copy-done.7
  89.4 1.9 convolution_convert_fusion.1
  91.3 0.0 copy-start.9
  91.3 142.1 %all_to_all.10 = bf16[16,96,2048]{2,1,0:T(8,128)(2,1)S(1)} all-to-all(bf16[16,96,2048]{2,1,0:T(8,128)(2,1)S(1)} %bitcast.120), channel_id=1, replica_groups=mesh['group'=2,'expert'=16] {'expert'}, dimensions={0} | all-to-all | bytes 12582912 | tf_op jit(solution)/shard_map/all_to_all | solution.py:103
  233.4 0.0 copy-done.9
  233.5 6.8 %fusion.1 = f32[1536,1024]{1,0:T(8,128)S(1)} fusion(bf16[1536,2048]{1,0:T(8,128)(2,1)S(1)} %bitcast.122, bf16[1,2048,1024]{2,1,0:T(8,128)(2,1)S(1)} %copy-done.9), kind=kOutput, calls=%fused_computation.12 | convolution fusion | flops 6442450944 | bytes 16777216 | tf_op jit(solution)/shard_map/dot_general | solution.py:53
  240.3 0.0 copy-done
  240.3 5.4 %convolution_convert_fusion = bf16[1536,2048]{1,0:T(8,128)(2,1)} fusion(bf16[1,512,2048]{2,1,0:T(8,128)(2,1)S(1)} %copy-done, f32[1536,1024]{1,0:T(8,128)S(1)} %fusion.1), kind=kOutput, calls=%fused_computation.8 | convolution fusion | flops 3229089792 | bytes 14680064 | tf_op jit(solution)/shard_map/dot_general | solution.py:55
  245.7 5.4 %all-to-all-start.1 = ((bf16[16,96,2048]{2,1,0:T(8,128)(2,1)}), bf16[16,96,2048]{2,1,0:T(8,128)(2,1)}, u32[]{:S(2)}, u32[]{:S(2)}) async-start(bf16[16,96,2048]{2,1,0:T(8,128)(2,1)} %bitcast.121), calls=%async_computation.1 | async-start | bytes 12582912 | tf_op jit(solution)/shard_map/all_to_all | solution.py:106
  251.1 0.0 copy-done.8
  251.2 137.3 %all-to-all-done.1 = bf16[16,96,2048]{2,1,0:T(8,128)(2,1)} async-done(((bf16[16,96,2048]{2,1,0:T(8,128)(2,1)}), bf16[16,96,2048]{2,1,0:T(8,128)(2,1)}, u32[]{:S(2)}, u32[]{:S(2)}) %all-to-all-start.1) | async-done | bytes 6291488 | tf_op jit(solution)/shard_map/all_to_all | solution.py:106
  388.5 5.8 %gather_fusion = bf16[128,2048]{1,0:T(8,128)(2,1)} fusion(bf16[1536,2048]{1,0:T(8,128)(2,1)} %bitcast.24, s32[1024]{0:T(1024)S(1)} %get-tuple-element.45), kind=kCustom, calls=%fused_computation | custom fusion | bytes 1049088 | tf_op jit(solution)/shard_map/gather | solution.py:110
  394.3 5.9 %gather_fusion.1 = bf16[128,2048]{1,0:T(8,128)(2,1)} fusion(bf16[1536,2048]{1,0:T(8,128)(2,1)} %bitcast.24, s32[1024]{0:T(1024)S(1)} %get-tuple-element.44), kind=kCustom, calls=%fused_computation.1 | custom fusion | bytes 1049088 | tf_op jit(solution)/shard_map/gather | solution.py:110
  400.2 5.9 %gather_fusion.2 = bf16[128,2048]{1,0:T(8,128)(2,1)} fusion(bf16[1536,2048]{1,0:T(8,128)(2,1)} %bitcast.24, s32[1024]{0:T(1024)S(1)} %get-tuple-element.43), kind=kCustom, calls=%fused_computation.2 | custom fusion | bytes 1049088 | tf_op jit(solution)/shard_map/gather | solution.py:110
  406.0 5.9 %gather_fusion.3 = bf16[128,2048]{1,0:T(8,128)(2,1)} fusion(bf16[1536,2048]{1,0:T(8,128)(2,1)} %bitcast.24, s32[1024]{0:T(1024)S(1)} %get-tuple-element.42), kind=kCustom, calls=%fused_computation.3 | custom fusion | bytes 1049088 | tf_op jit(solution)/shard_map/gather | solution.py:110
  411.9 5.8 %gather_fusion.4 = bf16[128,2048]{1,0:T(8,128)(2,1)} fusion(bf16[1536,2048]{1,0:T(8,128)(2,1)} %bitcast.24, s32[1024]{0:T(1024)S(1)} %get-tuple-element.41), kind=kCustom, calls=%fused_computation.4 | custom fusion | bytes 1049088 | tf_op jit(solution)/shard_map/gather | solution.py:110
  417.7 5.8 %gather_fusion.5 = bf16[128,2048]{1,0:T(8,128)(2,1)} fusion(bf16[1536,2048]{1,0:T(8,128)(2,1)} %bitcast.24, s32[1024]{0:T(1024)S(1)} %get-tuple-element.40), kind=kCustom, calls=%fused_computation.5 | custom fusion | bytes 1049088 | tf_op jit(solution)/shard_map/gather | solution.py:110
  423.6 6.1 %gather_fusion.6 = bf16[128,2048]{1,0:T(8,128)(2,1)} fusion(bf16[1536,2048]{1,0:T(8,128)(2,1)} %bitcast.24, s32[1024]{0:T(1024)S(1)} %get-tuple-element.39), kind=kCustom, calls=%fused_computation.6 | custom fusion | bytes 1049088 | tf_op jit(solution)/shard_map/gather | solution.py:110
  429.7 5.8 %gather_fusion.7 = bf16[128,2048]{1,0:T(8,128)(2,1)} fusion(bf16[1536,2048]{1,0:T(8,128)(2,1)} %bitcast.24, s32[1024]{0:T(1024)S(1)} %get-tuple-element.38), kind=kCustom, calls=%fused_computation.7 | custom fusion | bytes 1049088 | tf_op jit(solution)/shard_map/gather | solution.py:110
  435.5 3.9 add_convert_fusion
  (17 shorter events, 0.1 us)
Async XLA Ops:
  6.5 233.7 %copy-start = (bf16[1,512,2048]{2,1,0:T(8,128)(2,1)S(1)}, bf16[1,512,2048]{2,1,0:T(8,128)(2,1)}, u32[]{:S(2)}) copy-start(bf16[1,512,2048]{2,1,0:T(8,128)(2,1)} %param.21) | copy-start | bytes 6291460
  6.5 4.9 %slice-start = ((bf16[2,1,2,128,2048]{4,3,2,1,0:T(8,128)(2,1)}), bf16[2,1,1,128,2048]{4,3,2,1,0:T(8,128)(2,1)S(1)}, s32[]{:S(2)}) async-start(bf16[2,1,2,128,2048]{4,3,2,1,0:T(8,128)(2,1)} %param.14), calls=%async_computation.3 | async-start | bytes 2097152 | tf_op jit(solution)/shard_map/slice | solution.py:71
  6.5 77.9 %all-gather.2.cloned.1.call-start = ((), (), s32[]{:S(2)}) async-start(), calls=%async_computation.2 | async-start | bytes 8912896 | tf_op jit(solution)/shard_map/all_gather | solution.py:77
  9.4 26.5 %collective-permute-start = (bf16[1]{0:T(256)(128)(2,1)}, bf16[1]{0:T(256)(128)(2,1)}, u32[]{:S(2)}, u32[]{:S(2)}) collective-permute-start(bf16[1]{0:T(256)(128)(2,1)} %bitcast.8), channel_id=1, source_target_pairs={{0,16},{16,0},{1,17},{17,1},{2,18},{18,2},{3,19},{19,3},{4,20},{20... | collective-permute-start | bytes 14 | tf_op jit(solution)/shard_map/ppermute | solution.py:21
  12.7 24.0 %collective-permute-start.1 = (bf16[2,128,2048]{1,2,0:T(8,128)(2,1)}, bf16[2,128,2048]{1,2,0:T(8,128)(2,1)}, u32[]{:S(2)}, u32[]{:S(2)}) collective-permute-start(bf16[2,128,2048]{1,2,0:T(8,128)(2,1)} %bitcast.127), channel_id=1, source_target_pairs={{0,16},{16,0},{1,17},{17,1},{2,18},{18,2},{3,19},{19,3},{4,20},{20... | collective-permute-start | bytes 3145736 | tf_op jit(solution)/shard_map/ppermute | solution.py:21
  17.4 7.9 %copy-start.6 = (s32[128,8]{0,1:T(8,128)S(1)}, s32[128,8]{0,1:T(8,128)}, u32[]{:S(2)}) copy-start(s32[128,8]{0,1:T(8,128)} %param.18) | copy-start | bytes 12292
  33.9 1.4 copy-start.1
  33.9 4.2 copy-start.3
  35.9 3.0 copy-start.4
  36.6 2.3 copy-start.2
  36.6 2.3 copy-start.5
  84.5 5.0 %copy-start.7 = (f32[2048]{0:T(1024)S(1)}, f32[2048]{0:T(1024)}, u32[]{:S(2)}) copy-start(f32[2048]{0:T(1024)} %param.17) | copy-start | bytes 24580
  91.3 142.1 %copy-start.9 = (bf16[1,2048,1024]{2,1,0:T(8,128)(2,1)S(1)}, bf16[1,2048,1024]{2,1,0:T(8,128)(2,1)}, u32[]{:S(2)}) copy-start(bf16[1,2048,1024]{2,1,0:T(8,128)(2,1)} %param.20) | copy-start | bytes 12582916
  245.7 5.5 %copy-start.8 = (f32[128,8]{0,1:T(8,128)S(1)}, f32[128,8]{0,1:T(8,128)}, u32[]{:S(2)}) copy-start(f32[128,8]{0,1:T(8,128)} %param.19) | copy-start | bytes 12292
  245.7 142.8 %all-to-all-start.1 = ((bf16[16,96,2048]{2,1,0:T(8,128)(2,1)}), bf16[16,96,2048]{2,1,0:T(8,128)(2,1)}, u32[]{:S(2)}, u32[]{:S(2)}) async-start(bf16[16,96,2048]{2,1,0:T(8,128)(2,1)} %bitcast.121), calls=%async_computation.1 | async-start | bytes 12582912 | tf_op jit(solution)/shard_map/all_to_all | solution.py:106
Sparse Core Ops, SparseCore 0:
  9.5 74.9 all-gather.1
where the time goes:
time: 447 us; the launch traced here: 446 us
  waiting for transfers between devices  182 us (41%)
  blocking collectives  142 us (32%)
  local copies, waits for them, and re-layouts  65.1 us (15%)
  matrix products  23.4 us (5%)
  between operations  15 us (3%)
  other arithmetic  11.3 us (3%)
  starting transfers between devices  7.65 us (2%)
    all_to_all x1, blocking collectives, shards(): lax.all_to_all(outgoing, 'expert', split_axis=0, concat_axis=0, tiled=True)  142 us
    all_to_all x1, waiting for transfers between devices, shards(): lax.all_to_all(output_rows, 'expert', split_axis=0, concat_axis=0, tiled=...  137 us
    gather x8, local copies, waits for them, and re-layouts, shards(): picked = returned_rows[flat_slot[:, route_k]].astype(jnp.float32)  47 us
    all_gather x1, waiting for transfers between devices, shards(): lax.all_gather(o_rows, 'expert', axis=0, tiled=True)  43.6 us
  transfers between devices with their start and end apart: 4, of which 2 were waited for; matrix products, arithmetic and copies ran while one was open for 6% of the time, Pallas kernels for 0%

commit v1 on v0

v1 whole, which is shorter than its diff:
```python
import functools
import math

import jax
import jax.numpy as jnp
from jax import lax
from jax.experimental import pallas as pl
from jax.experimental.pallas import tpu as pltpu
from jax.sharding import PartitionSpec as P

HEADS = 16
HD = 128
FF = 512
F32 = jnp.float32
BF16 = jnp.bfloat16
SMEM = pltpu.SMEM


class Ring:
    def __init__(self, count):
        self.count = count
        self.pairs = count // 2
        chips = list(range(0, self.pairs, 2)) + list(range(1, self.pairs, 2))[::-1]
        self.device = [[2 * c, 2 * c + 1] for c in chips]
        self.place = {self.device[i][k]: (i, k) for i in range(self.pairs) for k in (0, 1)}

    def at(self, i, k):
        return self.device[i % self.pairs][k]

    def step(self):
        route = []
        for i in range(self.pairs):
            route += [(self.at(i, 0), self.at(i + 1, 0)), (self.at(i, 1), self.at(i - 1, 1))]
        return route

    def sibling(self):
        return [(e, e ^ 1) for e in range(self.count)]

    def source(self, s, flip_lane, flip_way):
        out = []
        for e in range(self.count):
            i, k = self.place[e]
            way = 1 if k == 0 else -1
            if flip_way:
                way = -way
            out.append(self.at(i - s * way, k ^ flip_lane))
        return out


def swap_pairs(axis):
    count = lax.axis_size(axis)
    route = []
    for low in range(0, count - 1, 2):
        route += [(low, low + 1), (low + 1, low)]
    return route


def attend_body(len_ref, far_len_ref, q_ref, kv_ref, near_ref, fk_ref, fv_ref, out_ref):
    rows = q_ref.shape[0]
    seg = fk_ref.shape[0]
    near_len = len_ref[0, 0]
    far_len = far_len_ref[0]
    pos = lax.broadcasted_iota(jnp.int32, (rows, seg), 1)
    near_ok = pos < near_len
    far_ok = pos < far_len
    scale = 1.0 / math.sqrt(HD)
    dims = (((1,), (1,)), ((), ()))
    for h in range(q_ref.shape[1] // HD):
        cols = slice(h * HD, (h + 1) * HD)
        q = q_ref[:, cols]
        s0 = lax.dot_general(q, kv_ref[0, :, cols], dims, preferred_element_type=F32) * scale
        s1 = lax.dot_general(q, near_ref[0, 0, 0, :, cols], dims, preferred_element_type=F32) * scale
        s2 = lax.dot_general(q, fk_ref[:, cols], dims, preferred_element_type=F32) * scale
        s1 = jnp.where(near_ok, s1, -1e30)
        s2 = jnp.where(far_ok, s2, -1e30)
        m = jnp.maximum(
            jnp.max(s0, axis=1, keepdims=True),
            jnp.max(jnp.maximum(s1, s2), axis=1, keepdims=True),
        )
        w0 = jnp.exp(s0 - m)
        w1 = jnp.where(near_ok, jnp.exp(s1 - m), 0.0)
        w2 = jnp.where(far_ok, jnp.exp(s2 - m), 0.0)
        l = jnp.sum(w0, axis=1, keepdims=True) + jnp.sum(w1 + w2, axis=1, keepdims=True)
        a = jnp.dot(w0.astype(BF16), kv_ref[1, :, cols], preferred_element_type=F32)
        a += jnp.dot(w1.astype(BF16), near_ref[1, 0, 0, :, cols], preferred_element_type=F32)
        a += jnp.dot(w2.astype(BF16), fv_ref[:, cols], preferred_element_type=F32)
        out_ref[h] = (a / l).astype(BF16)


def attend(queries, span_kv, cache_kv, far_k, far_v, seg_len, far_len):
    rows, width = queries.shape
    seg = far_k.shape[0]
    per = 4
    wide = per * HD
    return pl.pallas_call(
        attend_body,
        grid=(width // wide,),
        out_shape=jax.ShapeDtypeStruct((width // HD, rows, HD), BF16),
        in_specs=[
            pl.BlockSpec(memory_space=SMEM),
            pl.BlockSpec(memory_space=SMEM),
            pl.BlockSpec((rows, wide), lambda i: (0, i)),
            pl.BlockSpec((2, rows, wide), lambda i: (0, 0, i)),
            pl.BlockSpec((2, 1, 1, seg, wide), lambda i: (0, 0, 0, 0, i)),
            pl.BlockSpec((seg, wide), lambda i: (0, i)),
            pl.BlockSpec((seg, wide), lambda i: (0, i)),
        ],
        out_specs=pl.BlockSpec((per, rows, HD), lambda i: (i, 0, 0)),
        cost_estimate=pl.CostEstimate(
            flops=12 * rows * rows * width, bytes_accessed=16 * rows * width, transcendentals=0
        ),
        compiler_params=pltpu.CompilerParams(vmem_limit_bytes=16 * 2**20),
        name="attend",
    )(seg_len, far_len, queries, span_kv, cache_kv, far_k, far_v)


def project_body(count, idx_ref, mine_ref, theirs_ref, *refs):
    blocks, (own_ref, give_ref) = refs[:count], refs[count:]
    rows = mine_ref.shape[1]
    total = None
    for b in range(count):
        i = idx_ref[b]
        both = jnp.concatenate([mine_ref[i], theirs_ref[i]], axis=0)
        part = jnp.dot(both, blocks[b][...], preferred_element_type=F32)
        total = part if total is None else total + part
    own_ref[...] = total[:rows]
    give_ref[...] = total[rows:]


def project(index, mine, theirs, blocks):
    count = len(blocks)
    rows = mine.shape[1]
    half = blocks[0].shape[1]
    full = pl.BlockSpec(memory_space=pltpu.VMEM)
    out = jax.ShapeDtypeStruct((rows, half), F32)
    return pl.pallas_call(
        functools.partial(project_body, count),
        out_shape=(out, out),
        in_specs=[pl.BlockSpec(memory_space=SMEM)] + [full] * (2 + count),
        out_specs=(full, full),
        cost_estimate=pl.CostEstimate(
            flops=8 * rows * half * half * 2, bytes_accessed=4 * half * half, transcendentals=0
        ),
        compiler_params=pltpu.CompilerParams(vmem_limit_bytes=24 * 2**20),
        name="project",
    )(index, mine, theirs, *blocks)


def norm_body(lane_ref, resid_ref, own_ref, got_ref, gain_ref, sum_ref, out_ref):
    first = lane_ref[0] == 0
    half = own_ref.shape[1]
    own = own_ref[...]
    got = got_ref[...]
    low = resid_ref[:, :half].astype(F32) + jnp.where(first, own, got)
    high = resid_ref[:, half:].astype(F32) + jnp.where(first, got, own)
    sum_ref[:, :half] = low
    sum_ref[:, half:] = high
    square = jnp.sum(low * low + high * high, axis=1, keepdims=True)
    scale = lax.rsqrt(square * (1.0 / (2 * half)) + 1e-05)
    out_ref[:, :half] = (low * scale * gain_ref[:, :half]).astype(BF16)
    out_ref[:, half:] = (high * scale * gain_ref[:, half:]).astype(BF16)


def norm(lane, resid, own, got, gain):
    full = pl.BlockSpec(memory_space=pltpu.VMEM)
    return pl.pallas_call(
        norm_body,
        out_shape=(
            jax.ShapeDtypeStruct(resid.shape, F32),
            jax.ShapeDtypeStruct(resid.shape, BF16),
        ),
        in_specs=[pl.BlockSpec(memory_space=SMEM)] + [full] * 4,
        out_specs=(full, full),
        cost_estimate=pl.CostEstimate(
            flops=8 * resid.size, bytes_accessed=12 * resid.size, transcendentals=0
        ),
        compiler_params=pltpu.CompilerParams(vmem_limit_bytes=16 * 2**20),
        name="norm",
    )(lane, resid, own, got, gain.reshape(1, -1))


def expert_body(src_ref, x_ref, y_ref, wt_ref, gate_ref, up_ref, down_ref, cx_ref, cy_ref, acc_ref):
    j = pl.program_id(0)
    rows = x_ref.shape[0]
    both = jnp.concatenate([x_ref[...], y_ref[...]], axis=0)
    gate = jnp.dot(both, gate_ref[0], preferred_element_type=F32)
    up = jnp.dot(both, up_ref[0], preferred_element_type=F32)
    hidden = (gate * jax.nn.sigmoid(gate) * up).astype(BF16)
    part = jnp.dot(hidden, down_ref[0], preferred_element_type=F32)

    @pl.when(j == 0)
    def _():
        acc_ref[...] = part

    @pl.when(j > 0)
    def _():
        acc_ref[...] += part

    @pl.when(j == pl.num_programs(0) - 1)
    def _():
        lanes = lax.broadcasted_iota(jnp.int32, wt_ref.shape, 1)
        wts = wt_ref[...]
        wx = jnp.sum(jnp.where(lanes == src_ref[0], wts, 0.0), axis=1, keepdims=True)
        wy = jnp.sum(jnp.where(lanes == src_ref[1], wts, 0.0), axis=1, keepdims=True)
        cx_ref[...] = (acc_ref[:rows] * wx).astype(BF16)
        cy_ref[...] = (acc_ref[rows:] * wy).astype(BF16)


def expert(src, x, y, wts, w_in, w_out):
    rows, width = x.shape
    chunk = 256
    steps = FF // chunk
    whole = pl.BlockSpec((rows, width), lambda j: (0, 0))
    out = jax.ShapeDtypeStruct((rows, width), BF16)
    return pl.pallas_call(
        expert_body,
        grid=(steps,),
        out_shape=(out, out),
        in_specs=[
            pl.BlockSpec(memory_space=SMEM),
            whole,
            whole,
            pl.BlockSpec(wts.shape, lambda j: (0, 0)),
            pl.BlockSpec((1, width, chunk), lambda j: (0, 0, j)),
            pl.BlockSpec((1, width, chunk), lambda j: (0, 0, j + steps)),
            pl.BlockSpec((1, chunk, width), lambda j: (0, j, 0)),
        ],
        out_specs=(whole, whole),
        scratch_shapes=[pltpu.VMEM((2 * rows, width), F32)],
        cost_estimate=pl.CostEstimate(
            flops=12 * rows * width * FF, bytes_accessed=6 * width * FF, transcendentals=0
        ),
        compiler_params=pltpu.CompilerParams(vmem_limit_bytes=24 * 2**20),
        name="expert",
    )(src, x, y, wts, w_in, w_in, w_out)


def shards(
    ring, resid, queries, span_kv, cache_kv, seg_len, o_rows, norm_gain, routes, route_wts, w_in, w_out
):
    count, pairs = ring.count, ring.pairs
    rows, width = queries.shape
    half = width // 2
    me = lax.axis_index("expert")
    lane = me % 2
    forward, sibling = ring.step(), ring.sibling()

    def look(table):
        return jnp.asarray(table, jnp.int32)[me]

    def ahead(block):
        return lax.ppermute(block, "expert", forward)

    def across(block):
        return lax.ppermute(block, "expert", sibling)

    group_swap = swap_pairs("group")
    far_len = lax.ppermute(seg_len[0, 1:2], "group", group_swap)
    far_k = lax.ppermute(cache_kv[0, 0, 1], "group", group_swap)
    far_v = lax.ppermute(cache_kv[1, 0, 1], "group", group_swap)

    picks = routes[:, :, None] == jnp.arange(count, dtype=jnp.int32)[None, None, :]
    dense = jnp.sum(jnp.where(picks, route_wts[:, :, None], 0.0), axis=1)
    wts = lax.all_to_all(dense.T, "expert", split_axis=0, concat_axis=0, tiled=True).T

    own_half = lax.dynamic_slice_in_dim(o_rows, lane * half, half, 1)
    other_half = lax.dynamic_slice_in_dim(o_rows, (1 - lane) * half, half, 1)
    chain_a, chain_b = own_half, across(other_half)
    blocks, index = [chain_a, chain_b], [me, me ^ 1]
    for s in range(1, pairs):
        chain_a = ahead(chain_a)
        chain_b = ahead(chain_b)
        blocks += [chain_a, chain_b]
        index += [look(ring.source(s, 0, False)), look(ring.source(s, 1, False))]

    mine = attend(queries, span_kv, cache_kv, far_k, far_v, seg_len, far_len)
    slab = o_rows.shape[0]
    if slab != HD:
        mine = mine.transpose(1, 0, 2).reshape(rows, count, slab).transpose(1, 0, 2)
    theirs = across(mine)
    own, give = project(jnp.stack(index), mine, theirs, blocks)
    got = across(give)
    residual, normed = norm(lane[None], resid, own, got, norm_gain)

    x = normed
    y = across(x)
    keep, give = expert(jnp.stack([me, me ^ 1]), x, y, wts, w_in, w_out)
    total = residual + keep.astype(F32) + across(give).astype(F32)
    travelling = None
    for s in range(1, pairs):
        x = ahead(x)
        y = across(x)
        src = jnp.stack([look(ring.source(s, 0, False)), look(ring.source(s, 1, True))])
        keep, give = expert(src, x, y, wts, w_in, w_out)
        part = keep.astype(F32) + across(give).astype(F32)
        if travelling is not None:
            part = part + travelling.astype(F32)
        travelling = ahead(part.astype(BF16))
    return (total + travelling.astype(F32)).astype(BF16)


def solution(mesh):
    placed = (
        P(("group", "expert"), None),
        P(("group", "expert"), None),
        P(None, ("group", "expert"), None),
        P(None, ("group", "expert"), None, None, None),
        P(("group", "expert"), None),
        P("expert", None),
        P(),
        P(("group", "expert"), None),
        P(("group", "expert"), None),
        P("expert", None, None),
        P("expert", None, None),
    )
    ring = Ring(mesh.shape["expert"])
    return jax.shard_map(
        functools.partial(shards, ring),
        mesh=mesh,
        in_specs=placed,
        out_specs=P(("group", "expert"), None),
        check_vma=False,
    )
```

time: 447 us -> 218 us (0.49)
  the two profiles are of different devices: /device:TPU:13 before, /device:TPU:0 now
where the time goes in v1:
time: 218 us; the launch traced here: 217 us
  waiting for transfers between devices  75.3 us (35%)
  local copies, waits for them, and re-layouts  46.7 us (21%)
  starting transfers between devices  41.4 us (19%)
  Pallas kernels  40.3 us (18%)
  other arithmetic  12.6 us (6%)
    ppermute x28, waiting for transfers between devices, ahead(): return lax.ppermute(block, 'expert', forward)  60 us
    ppermute x28, starting transfers between devices, ahead(): return lax.ppermute(block, 'expert', forward)  29.1 us
    pallas_call x8, Pallas kernels, expert(): pl.pallas_call(expert_body, grid=(steps,), out_shape=(out, out), in_specs...  28.9 us
    unnamed x114, local copies, waits for them, and re-layouts  26.2 us
    another operation x7, other arithmetic, shards(): jnp.stack([look(ring.source(s, 0, False)), look(ring.source(s, 1, True))])  9.22 us
    another operation x1, local copies, waits for them, and re-layouts, shards(): own, give = project(jnp.stack(index), mine, theirs, blocks)  8.82 us
    ppermute x1, waiting for transfers between devices, shards(): far_len = lax.ppermute(seg_len[0, 1:2], 'group', group_swap)  8.69 us
    dynamic_slice x14, local copies, waits for them, and re-layouts, look(): return jnp.asarray(table, jnp.int32)[me]  8.56 us
  transfers between devices with their start and end apart: 51, of which 24 were waited for; matrix products, arithmetic and copies ran while one was open for 14% of the time, Pallas kernels for 17%

profile of v1, /device:TPU:0, one launch (start us, length us, event | category | flops | bytes accessed | tf_op | source)
XLA Modules:
  0.0 216.9 jit_solution(18291289677361291513)
XLA Ops:
  0.0 1.2 constant_dynamic-slice_fusion
  1.8 2.6 %collective-permute-start.5 = (bf16[128,1024]{1,0:T(8,128)(2,1)S(1)}, bf16[128,1024]{1,0:T(8,128)(2,1)S(1)}, u32[]{:S(2)}, u32[]{:S(2)}) collective-permute-start(bf16[128,1024]{1,0:T(8,128)(2,1)S(1)} %get-tuple-element.48.refs_0_), channel_id=1, source_target_pairs={{0,4},{1,3},{4,8},{5,1},{8,12},{9,5},{12,14},{13,9},{14,10},{15,13... | collective-permute-start | bytes 786440 | tf_op jit(solution)/shard_map/ppermute | solution.py:252
  4.4 1.6 collective-permute-start.6
  6.7 2.0 collective-permute-done.5.refs_2_
  8.7 2.1 collective-permute-start.7
  11.5 2.1 collective-permute-start.8
  15.1 2.1 collective-permute-start.9
  17.9 2.1 collective-permute-start.10
  20.0 1.3 slice_bitcast_fusion
  21.3 1.6 collective-permute-start.1
  23.4 1.6 collective-permute-start.11
  25.6 1.6 collective-permute-start.12
  27.9 1.8 collective-permute-done.11.refs_8_
  29.7 1.6 collective-permute-start.13
  31.3 1.2 collective-permute-done.12.refs_9_
  32.6 1.6 collective-permute-start.14
  34.7 1.5 collective-permute-start
  36.2 8.7 %collective-permute-done.far_len_ref = s32[1]{0:T(128)} collective-permute-done((s32[1]{0:T(128)}, s32[1]{0:T(128)}, u32[]{:S(2)}, u32[]{:S(2)}) %collective-permute-start) | collective-permute-done | bytes 36 | tf_op jit(solution)/shard_map/ppermute | solution.py:258
  45.0 1.0 copy-done.8
  46.1 7.5 %attend.1.mine_ref = bf16[16,128,128]{2,1,0:T(8,128)(2,1)} custom-call(s32[1,2]{1,0:T(1,128)S(1)} %copy-done.10, s32[1]{0:T(128)} %collective-permute-done.far_len_ref, bf16[128,2048]{1,0:T(8,128)(2,1)S(1)} %copy-done.8, bf16[2,128,2048]{2,1,0:T(8,128)(2,1)S(1)} %copy-done.4, bf16[2,1,2,128,2048]{4,3,2,1,0:T(8,128)(2,1)S(1)} %copy-done.3, ...), custom_call_target="tpu_custom_call" | custom-call | flops 402653184 | bytes 4194304 | tf_op jit(solution)/shard_map/attend/pallas_call | solution.py:95
  54.8 1.6 collective-permute-start.16
  57.2 2.9 %collective-permute-done.15.refs_12_ = bf16[128,1024]{1,0:T(8,128)(2,1)S(1)} collective-permute-done((bf16[128,1024]{1,0:T(8,128)(2,1)S(1)}, bf16[128,1024]{1,0:T(8,128)(2,1)S(1)}, u32[]{:S(2)}, u32[]{:S(2)}) %collective-permute-start.15) | collective-permute-done | bytes 262176 | tf_op jit(solution)/shard_map/ppermute | solution.py:252
  61.2 1.6 collective-permute-done.16.refs_13_
  72.6 8.8 %stack.37.idx_ref = s32[16]{0:T(128)S(1)} concatenate(s32[1]{0:T(128)} %bitcast.1, s32[1]{0:T(128)} %bitcast.2, s32[1]{0:T(128)} %dynamic_slice.90, s32[1]{0:T(128)} %dynamic_slice.91, s32[1]{0:T(128)} %dynamic_slice.92, s32[1]{0:T(128)} %dynamic_slice.93, s32[1]{0:T(128)} %dynamic_slice.94, s32[1]{0:T(128)} %dynamic_slice.95, s32[1]{0:T(128)} %dynamic_slice.96, ...), dimensions={0} | concatenate | bytes 128 | tf_op jit(solution)/shard_map/stack | solution.py:281
  83.8 0.9 copy-done.14
  84.8 0.9 copy-done.16
  86.7 0.9 copy-done.20
  87.7 0.9 copy-done.22
  97.2 3.5 %project.1 = (f32[128,1024]{1,0:T(8,128)S(1)}, f32[128,1024]{1,0:T(8,128)S(1)}) custom-call(s32[16]{0:T(128)S(1)} %stack.37.idx_ref, bf16[16,128,128]{2,1,0:T(8,128)(2,1)} %attend.1.mine_ref, bf16[16,128,128]{2,1,0:T(8,128)(2,1)S(1)} %collective-permute-done.3.theirs_ref, bf16[128,1024]{1,0:T(8,128)(2,1)S(1)} %get-tuple-element.48.refs_0_, ...), custom_call_target="tpu_custom_call" | custom-call | flops 2147483648 | bytes 4194304 | tf_op jit(solution)/shard_map/project/pallas_call | solution.py:136
  101.2 1.5 collective-permute-done.19.got_ref
  103.9 1.6 collective-permute-start.22
  105.5 7.7 %collective-permute-done.22.x_ref = bf16[128,2048]{1,0:T(8,128)(2,1)} collective-permute-done((bf16[128,2048]{1,0:T(8,128)(2,1)S(1)}, bf16[128,2048]{1,0:T(8,128)(2,1)}, u32[]{:S(2)}, u32[]{:S(2)}) %collective-permute-start.22) | collective-permute-done | bytes 524320 | tf_op jit(solution)/shard_map/ppermute | solution.py:252
  113.8 6.0 %all-to-all-start = ((f32[16,1,128]{2,1,0:T(1,128)}), f32[16,1,128]{2,1,0:T(1,128)S(1)}, u32[]{:S(2)}, u32[]{:S(2)}) async-start(f32[16,1,128]{2,1,0:T(1,128)} %bitcast.9), calls=%async_computation | async-start | bytes 16384 | tf_op jit(solution)/shard_map/all_to_all | solution.py:264
  119.9 1.3 pad_add_fusion.7.src_ref
  121.2 5.1 %all-to-all-done = f32[16,1,128]{2,1,0:T(1,128)S(1)} async-done(((f32[16,1,128]{2,1,0:T(1,128)}), f32[16,1,128]{2,1,0:T(1,128)S(1)}, u32[]{:S(2)}, u32[]{:S(2)}) %all-to-all-start) | async-done | bytes 8224 | tf_op jit(solution)/shard_map/all_to_all | solution.py:264
  126.8 2.2 %copy-done = bf16[1,2048,1024]{2,1,0:T(8,128)(2,1)S(1)} copy-done((bf16[1,2048,1024]{2,1,0:T(8,128)(2,1)S(1)}, bf16[1,2048,1024]{2,1,0:T(8,128)(2,1)}, u32[]{:S(2)}) %copy-start) | copy-done | bytes 4194328
  129.0 4.3 %expert.15 = (bf16[128,2048]{1,0:T(8,128)(2,1)S(1)}, bf16[128,2048]{1,0:T(8,128)(2,1)S(1)}) custom-call(s32[2]{0:T(128)S(1)} %pad_add_fusion.7.src_ref, bf16[128,2048]{1,0:T(8,128)(2,1)} %collective-permute-done.22.x_ref, bf16[128,2048]{1,0:T(8,128)(2,1)} %collective-permute-done.41.y_ref, f32[128,16]{1,0:T(8,128)S(1)} %bitcast.17, ...), custom_call_target="tpu_custom_call" | custom-call | flops 1610612736 | bytes 6291456 | tf_op jit(solution)/shard_map/expert/pallas_call | solution.py:215
  133.4 2.4 %collective-permute-done.23.x_ref = bf16[128,2048]{1,0:T(8,128)(2,1)S(1)} collective-permute-done((bf16[128,2048]{1,0:T(8,128)(2,1)}, bf16[128,2048]{1,0:T(8,128)(2,1)S(1)}, u32[]{:S(2)}, u32[]{:S(2)}) %collective-permute-start.23) | collective-permute-done | bytes 524320 | tf_op jit(solution)/shard_map/ppermute | solution.py:252
  135.8 1.3 pad_add_fusion.6.src_ref
  138.2 3.5 %expert.14 = (bf16[128,2048]{1,0:T(8,128)(2,1)S(1)}, bf16[128,2048]{1,0:T(8,128)(2,1)S(1)}) custom-call(s32[2]{0:T(128)S(1)} %pad_add_fusion.6.src_ref, bf16[128,2048]{1,0:T(8,128)(2,1)S(1)} %collective-permute-done.23.x_ref, bf16[128,2048]{1,0:T(8,128)(2,1)S(1)} %collective-permute-done.39.y_ref, f32[128,16]{1,0:T(8,128)S(1)} %bitcast.18, ...), custom_call_target="tpu_custom_call" | custom-call | flops 1610612736 | bytes 6291456 | tf_op jit(solution)/shard_map/expert/pallas_call | solution.py:215
  141.9 4.4 %collective-permute-done.24.x_ref = bf16[128,2048]{1,0:T(8,128)(2,1)S(1)} collective-permute-done((bf16[128,2048]{1,0:T(8,128)(2,1)S(1)}, bf16[128,2048]{1,0:T(8,128)(2,1)S(1)}, u32[]{:S(2)}, u32[]{:S(2)}) %collective-permute-start.24) | collective-permute-done | bytes 524320 | tf_op jit(solution)/shard_map/ppermute | solution.py:252
  146.2 1.4 pad_add_fusion.5.src_ref
  148.0 3.8 %collective-permute-done.43 = bf16[128,2048]{1,0:T(8,128)(2,1)S(1)} collective-permute-done((bf16[128,2048]{1,0:T(8,128)(2,1)S(1)}, bf16[128,2048]{1,0:T(8,128)(2,1)S(1)}, u32[]{:S(2)}, u32[]{:S(2)}) %collective-permute-start.43) | collective-permute-done | bytes 524320 | tf_op jit(solution)/shard_map/ppermute | solution.py:252
  152.5 3.5 %expert.13 = (bf16[128,2048]{1,0:T(8,128)(2,1)S(1)}, bf16[128,2048]{1,0:T(8,128)(2,1)S(1)}) custom-call(s32[2]{0:T(128)S(1)} %pad_add_fusion.5.src_ref, bf16[128,2048]{1,0:T(8,128)(2,1)S(1)} %collective-permute-done.24.x_ref, bf16[128,2048]{1,0:T(8,128)(2,1)S(1)} %collective-permute-done.37.y_ref, f32[128,16]{1,0:T(8,128)S(1)} %bitcast.19, ...), custom_call_target="tpu_custom_call" | custom-call | flops 1610612736 | bytes 6291456 | tf_op jit(solution)/shard_map/expert/pallas_call | solution.py:215
  156.1 1.3 collective-permute-done.25.x_ref
  157.5 1.3 pad_add_fusion.4.src_ref
  159.4 3.7 %collective-permute-done.44 = bf16[128,2048]{1,0:T(8,128)(2,1)S(1)} collective-permute-done((bf16[128,2048]{1,0:T(8,128)(2,1)S(1)}, bf16[128,2048]{1,0:T(8,128)(2,1)S(1)}, u32[]{:S(2)}, u32[]{:S(2)}) %collective-permute-start.44) | collective-permute-done | bytes 524320 | tf_op jit(solution)/shard_map/ppermute | solution.py:252
  163.8 3.5 %expert.12 = (bf16[128,2048]{1,0:T(8,128)(2,1)S(1)}, bf16[128,2048]{1,0:T(8,128)(2,1)S(1)}) custom-call(s32[2]{0:T(128)S(1)} %pad_add_fusion.4.src_ref, bf16[128,2048]{1,0:T(8,128)(2,1)S(1)} %collective-permute-done.25.x_ref, bf16[128,2048]{1,0:T(8,128)(2,1)S(1)} %collective-permute-done.35.y_ref, f32[128,16]{1,0:T(8,128)S(1)} %bitcast.20, ...), custom_call_target="tpu_custom_call" | custom-call | flops 1610612736 | bytes 6291456 | tf_op jit(solution)/shard_map/expert/pallas_call | solution.py:215
  167.4 1.3 collective-permute-done.26.x_ref
  168.7 1.3 pad_add_fusion.3.src_ref
  170.4 3.9 %collective-permute-done.45 = bf16[128,2048]{1,0:T(8,128)(2,1)S(1)} collective-permute-done((bf16[128,2048]{1,0:T(8,128)(2,1)S(1)}, bf16[128,2048]{1,0:T(8,128)(2,1)S(1)}, u32[]{:S(2)}, u32[]{:S(2)}) %collective-permute-start.45) | collective-permute-done | bytes 524320 | tf_op jit(solution)/shard_map/ppermute | solution.py:252
  175.0 3.5 %expert.11 = (bf16[128,2048]{1,0:T(8,128)(2,1)S(1)}, bf16[128,2048]{1,0:T(8,128)(2,1)S(1)}) custom-call(s32[2]{0:T(128)S(1)} %pad_add_fusion.3.src_ref, bf16[128,2048]{1,0:T(8,128)(2,1)S(1)} %collective-permute-done.26.x_ref, bf16[128,2048]{1,0:T(8,128)(2,1)S(1)} %collective-permute-done.33.y_ref, f32[128,16]{1,0:T(8,128)S(1)} %bitcast.21, ...), custom_call_target="tpu_custom_call" | custom-call | flops 1610612736 | bytes 6291456 | tf_op jit(solution)/shard_map/expert/pallas_call | solution.py:215
  178.6 1.3 collective-permute-done.27.x_ref
  180.0 1.3 pad_add_fusion.2.src_ref
  181.7 3.9 %collective-permute-done.46 = bf16[128,2048]{1,0:T(8,128)(2,1)S(1)} collective-permute-done((bf16[128,2048]{1,0:T(8,128)(2,1)S(1)}, bf16[128,2048]{1,0:T(8,128)(2,1)S(1)}, u32[]{:S(2)}, u32[]{:S(2)}) %collective-permute-start.46) | collective-permute-done | bytes 524320 | tf_op jit(solution)/shard_map/ppermute | solution.py:252
  186.3 3.5 %expert.10 = (bf16[128,2048]{1,0:T(8,128)(2,1)S(1)}, bf16[128,2048]{1,0:T(8,128)(2,1)S(1)}) custom-call(s32[2]{0:T(128)S(1)} %pad_add_fusion.2.src_ref, bf16[128,2048]{1,0:T(8,128)(2,1)S(1)} %collective-permute-done.27.x_ref, bf16[128,2048]{1,0:T(8,128)(2,1)S(1)} %collective-permute-done.31.y_ref, f32[128,16]{1,0:T(8,128)S(1)} %bitcast.22, ...), custom_call_target="tpu_custom_call" | custom-call | flops 1610612736 | bytes 6291456 | tf_op jit(solution)/shard_map/expert/pallas_call | solution.py:215
  189.9 1.3 collective-permute-done.28.x_ref
  191.2 1.3 pad_add_fusion.1.src_ref
  193.0 3.8 %collective-permute-done.47 = bf16[128,2048]{1,0:T(8,128)(2,1)S(1)} collective-permute-done((bf16[128,2048]{1,0:T(8,128)(2,1)S(1)}, bf16[128,2048]{1,0:T(8,128)(2,1)S(1)}, u32[]{:S(2)}, u32[]{:S(2)}) %collective-permute-start.47) | collective-permute-done | bytes 524320 | tf_op jit(solution)/shard_map/ppermute | solution.py:252
  197.5 3.5 %expert.9 = (bf16[128,2048]{1,0:T(8,128)(2,1)S(1)}, bf16[128,2048]{1,0:T(8,128)(2,1)S(1)}) custom-call(s32[2]{0:T(128)S(1)} %pad_add_fusion.1.src_ref, bf16[128,2048]{1,0:T(8,128)(2,1)S(1)} %collective-permute-done.28.x_ref, bf16[128,2048]{1,0:T(8,128)(2,1)S(1)} %collective-permute-done.29.y_ref, f32[128,16]{1,0:T(8,128)S(1)} %bitcast.23, ...), custom_call_target="tpu_custom_call" | custom-call | flops 1610612736 | bytes 6291456 | tf_op jit(solution)/shard_map/expert/pallas_call | solution.py:215
  201.2 3.5 %expert.8 = (bf16[128,2048]{1,0:T(8,128)(2,1)S(1)}, bf16[128,2048]{1,0:T(8,128)(2,1)S(1)}) custom-call(s32[2]{0:T(128)S(1)} %pad_add_fusion.src_ref, bf16[128,2048]{1,0:T(8,128)(2,1)S(1)} %copy-done.6, bf16[128,2048]{1,0:T(8,128)(2,1)S(1)} %collective-permute-done.20.y_ref, f32[128,16]{1,0:T(8,128)S(1)} %bitcast.24, bf16[1,2048,1024]{2,1,0:T(8,128)(2,1)S(1)} %copy-done.1, ...), custom_call_target="tpu_custom_call" | custom-call | flops 1610612736 | bytes 6291456 | tf_op jit(solution)/shard_map/expert/pallas_call | solution.py:215
  205.2 1.0 collective-permute-done.48
  207.0 8.8 %collective-permute-done.49 = bf16[128,2048]{1,0:T(8,128)(2,1)S(1)} collective-permute-done((bf16[128,2048]{1,0:T(8,128)(2,1)S(1)}, bf16[128,2048]{1,0:T(8,128)(2,1)S(1)}, u32[]{:S(2)}, u32[]{:S(2)}) %collective-permute-start.49) | collective-permute-done | bytes 524320 | tf_op jit(solution)/shard_map/ppermute | solution.py:252
  215.8 1.1 add_convert_fusion
  (199 shorter events, 42.9 us)
Async XLA Ops:
  0.0 44.9 %copy-start.3 = (bf16[2,1,2,128,2048]{4,3,2,1,0:T(8,128)(2,1)S(1)}, bf16[2,1,2,128,2048]{4,3,2,1,0:T(8,128)(2,1)}, u32[]{:S(2)}) copy-start(bf16[2,1,2,128,2048]{4,3,2,1,0:T(8,128)(2,1)} %near_ref.1) | copy-start | bytes 6291460
  0.0 34.1 %copy-start.10 = (s32[1,2]{1,0:T(1,128)S(1)}, s32[1,2]{1,0:T(1,128)}, u32[]{:S(2)}) copy-start(s32[1,2]{1,0:T(1,128)} %len_ref.1) | copy-start | bytes 28
  0.0 44.9 %copy-start.4 = (bf16[2,128,2048]{2,1,0:T(8,128)(2,1)S(1)}, bf16[2,128,2048]{2,1,0:T(8,128)(2,1)}, u32[]{:S(2)}) copy-start(bf16[2,128,2048]{2,1,0:T(8,128)(2,1)} %kv_ref.1) | copy-start | bytes 3145732
  1.2 3.2 %collective-permute-start.4 = (bf16[128,1024]{1,0:T(8,128)(2,1)S(1)}, bf16[128,1024]{1,0:T(8,128)(2,1)S(1)}, u32[]{:S(2)}, u32[]{:S(2)}) collective-permute-start(bf16[128,1024]{1,0:T(8,128)(2,1)S(1)} %get-tuple-element.47), channel_id=1, source_target_pairs={{0,1},{1,0},{2,3},{3,2},{4,5},{5,4},{6,7},{7,6},{8,9},{9,8},{10,11... | collective-permute-start | bytes 786440 | tf_op jit(solution)/shard_map/ppermute | solution.py:255
  1.8 6.9 %collective-permute-start.5 = (bf16[128,1024]{1,0:T(8,128)(2,1)S(1)}, bf16[128,1024]{1,0:T(8,128)(2,1)S(1)}, u32[]{:S(2)}, u32[]{:S(2)}) collective-permute-start(bf16[128,1024]{1,0:T(8,128)(2,1)S(1)} %get-tuple-element.48.refs_0_), channel_id=1, source_target_pairs={{0,4},{1,3},{4,8},{5,1},{8,12},{9,5},{12,14},{13,9},{14,10},{15,13... | collective-permute-start | bytes 786440 | tf_op jit(solution)/shard_map/ppermute | solution.py:252
  4.4 7.1 %collective-permute-start.6 = (bf16[128,1024]{1,0:T(8,128)(2,1)S(1)}, bf16[128,1024]{1,0:T(8,128)(2,1)S(1)}, u32[]{:S(2)}, u32[]{:S(2)}) collective-permute-start(bf16[128,1024]{1,0:T(8,128)(2,1)S(1)} %collective-permute-done.4.refs_1_), channel_id=1, source_target_pairs={{0,4},{1,3},{4,8},{5,1},{8,12},{9,5},{12,14},{13,9},{14,10},{15,13... | collective-permute-start | bytes 786440 | tf_op jit(solution)/shard_map/ppermute | solution.py:252
  8.7 6.4 %collective-permute-start.7 = (bf16[128,1024]{1,0:T(8,128)(2,1)S(1)}, bf16[128,1024]{1,0:T(8,128)(2,1)S(1)}, u32[]{:S(2)}, u32[]{:S(2)}) collective-permute-start(bf16[128,1024]{1,0:T(8,128)(2,1)S(1)} %collective-permute-done.5.refs_2_), channel_id=1, source_target_pairs={{0,4},{1,3},{4,8},{5,1},{8,12},{9,5},{12,14},{13,9},{14,10},{15,13... | collective-permute-start | bytes 786440 | tf_op jit(solution)/shard_map/ppermute | solution.py:252
  11.5 6.4 %collective-permute-start.8 = (bf16[128,1024]{1,0:T(8,128)(2,1)S(1)}, bf16[128,1024]{1,0:T(8,128)(2,1)S(1)}, u32[]{:S(2)}, u32[]{:S(2)}) collective-permute-start(bf16[128,1024]{1,0:T(8,128)(2,1)S(1)} %collective-permute-done.6.refs_3_), channel_id=1, source_target_pairs={{0,4},{1,3},{4,8},{5,1},{8,12},{9,5},{12,14},{13,9},{14,10},{15,13... | collective-permute-start | bytes 786440 | tf_op jit(solution)/shard_map/ppermute | solution.py:252
  15.1 29.8 %copy-start.17 = (bf16[128,1024]{1,0:T(8,128)(2,1)}, bf16[128,1024]{1,0:T(8,128)(2,1)S(1)}, u32[]{:S(2)}) copy-start(bf16[128,1024]{1,0:T(8,128)(2,1)S(1)} %collective-permute-done.7.refs_4_) | copy-start | bytes 786436
  15.1 8.3 %collective-permute-start.9 = (bf16[128,1024]{1,0:T(8,128)(2,1)S(1)}, bf16[128,1024]{1,0:T(8,128)(2,1)S(1)}, u32[]{:S(2)}, u32[]{:S(2)}) collective-permute-start(bf16[128,1024]{1,0:T(8,128)(2,1)S(1)} %collective-permute-done.7.refs_4_), channel_id=1, source_target_pairs={{0,4},{1,3},{4,8},{5,1},{8,12},{9,5},{12,14},{13,9},{14,10},{15,13... | collective-permute-start | bytes 786440 | tf_op jit(solution)/shard_map/ppermute | solution.py:252
  17.9 7.8 %collective-permute-start.10 = (bf16[128,1024]{1,0:T(8,128)(2,1)S(1)}, bf16[128,1024]{1,0:T(8,128)(2,1)S(1)}, u32[]{:S(2)}, u32[]{:S(2)}) collective-permute-start(bf16[128,1024]{1,0:T(8,128)(2,1)S(1)} %collective-permute-done.8.refs_5_), channel_id=1, source_target_pairs={{0,4},{1,3},{4,8},{5,1},{8,12},{9,5},{12,14},{13,9},{14,10},{15,13... | collective-permute-start | bytes 786440 | tf_op jit(solution)/shard_map/ppermute | solution.py:252
  21.3 23.7 %collective-permute-start.1 = (bf16[128,2048]{1,0:T(8,128)(2,1)S(1)}, bf16[128,2048]{1,0:T(8,128)(2,1)S(1)}, u32[]{:S(2)}, u32[]{:S(2)}) collective-permute-start(bf16[128,2048]{1,0:T(8,128)(2,1)S(1)} %get-tuple-element.46), channel_id=1, source_target_pairs={{0,16},{16,0},{1,17},{17,1},{2,18},{18,2},{3,19},{19,3},{4,20},{20... | collective-permute-start | bytes 1572872 | tf_op jit(solution)/shard_map/ppermute | solution.py:259
  22.8 22.1 %collective-permute-start.2 = (bf16[128,2048]{1,0:T(8,128)(2,1)S(1)}, bf16[128,2048]{1,0:T(8,128)(2,1)S(1)}, u32[]{:S(2)}, u32[]{:S(2)}) collective-permute-start(bf16[128,2048]{1,0:T(8,128)(2,1)S(1)} %get-tuple-element.45), channel_id=1, source_target_pairs={{0,16},{16,0},{1,17},{17,1},{2,18},{18,2},{3,19},{19,3},{4,20},{20... | collective-permute-start | bytes 1572872 | tf_op jit(solution)/shard_map/ppermute | solution.py:260
  23.4 6.4 %collective-permute-start.11 = (bf16[128,1024]{1,0:T(8,128)(2,1)S(1)}, bf16[128,1024]{1,0:T(8,128)(2,1)S(1)}, u32[]{:S(2)}, u32[]{:S(2)}) collective-permute-start(bf16[128,1024]{1,0:T(8,128)(2,1)S(1)} %collective-permute-done.9.refs_6_), channel_id=1, source_target_pairs={{0,4},{1,3},{4,8},{5,1},{8,12},{9,5},{12,14},{13,9},{14,10},{15,13... | collective-permute-start | bytes 786440 | tf_op jit(solution)/shard_map/ppermute | solution.py:252
  25.6 6.9 %collective-permute-start.12 = (bf16[128,1024]{1,0:T(8,128)(2,1)S(1)}, bf16[128,1024]{1,0:T(8,128)(2,1)S(1)}, u32[]{:S(2)}, u32[]{:S(2)}) collective-permute-start(bf16[128,1024]{1,0:T(8,128)(2,1)S(1)} %collective-permute-done.10.refs_7_), channel_id=1, source_target_pairs={{0,4},{1,3},{4,8},{5,1},{8,12},{9,5},{12,14},{13,9},{14,10},{15,13... | collective-permute-start | bytes 786440 | tf_op jit(solution)/shard_map/ppermute | solution.py:252
  29.7 23.9 %collective-permute-start.13 = (bf16[128,1024]{1,0:T(8,128)(2,1)S(1)}, bf16[128,1024]{1,0:T(8,128)(2,1)S(1)}, u32[]{:S(2)}, u32[]{:S(2)}) collective-permute-start(bf16[128,1024]{1,0:T(8,128)(2,1)S(1)} %collective-permute-done.11.refs_8_), channel_id=1, source_target_pairs={{0,4},{1,3},{4,8},{5,1},{8,12},{9,5},{12,14},{13,9},{14,10},{15,13... | collective-permute-start | bytes 786440 | tf_op jit(solution)/shard_map/ppermute | solution.py:252
  32.6 22.3 %collective-permute-start.14 = (bf16[128,1024]{1,0:T(8,128)(2,1)S(1)}, bf16[128,1024]{1,0:T(8,128)(2,1)S(1)}, u32[]{:S(2)}, u32[]{:S(2)}) collective-permute-start(bf16[128,1024]{1,0:T(8,128)(2,1)S(1)} %collective-permute-done.12.refs_9_), channel_id=1, source_target_pairs={{0,4},{1,3},{4,8},{5,1},{8,12},{9,5},{12,14},{13,9},{14,10},{15,13... | collective-permute-start | bytes 786440 | tf_op jit(solution)/shard_map/ppermute | solution.py:252
  34.1 34.2 %copy-start.49 = (s32[16]{0:T(128)S(1)}, s32[16]{0:T(128)}, u32[]{:S(2)}) copy-start(s32[16]{0:T(128)} %constant.61.clone) | copy-start | bytes 196
  34.1 34.7 %copy-start.48 = (s32[16]{0:T(128)S(1)}, s32[16]{0:T(128)}, u32[]{:S(2)}) copy-start(s32[16]{0:T(128)} %constant.62.clone) | copy-start | bytes 196
  34.1 35.4 %copy-start.47 = (s32[16]{0:T(128)S(1)}, s32[16]{0:T(128)}, u32[]{:S(2)}) copy-start(s32[16]{0:T(128)} %constant.63.clone) | copy-start | bytes 196
  34.1 36.0 %copy-start.46 = (s32[16]{0:T(128)S(1)}, s32[16]{0:T(128)}, u32[]{:S(2)}) copy-start(s32[16]{0:T(128)} %constant.64.clone) | copy-start | bytes 196
  34.7 36.1 %copy-start.45 = (s32[16]{0:T(128)S(1)}, s32[16]{0:T(128)}, u32[]{:S(2)}) copy-start(s32[16]{0:T(128)} %constant.65.clone) | copy-start | bytes 196
  34.7 36.7 %copy-start.44 = (s32[16]{0:T(128)S(1)}, s32[16]{0:T(128)}, u32[]{:S(2)}) copy-start(s32[16]{0:T(128)} %constant.66.clone) | copy-start | bytes 196
  34.7 37.2 %copy-start.43 = (s32[16]{0:T(128)S(1)}, s32[16]{0:T(128)}, u32[]{:S(2)}) copy-start(s32[16]{0:T(128)} %constant.67.clone) | copy-start | bytes 196
  34.7 10.2 %collective-permute-start = (s32[1]{0:T(128)}, s32[1]{0:T(128)}, u32[]{:S(2)}, u32[]{:S(2)}) collective-permute-start(s32[1]{0:T(128)} %bitcast.3), channel_id=1, source_target_pairs={{0,16},{16,0},{1,17},{17,1},{2,18},{18,2},{3,19},{19,3},{4,20},{20... | collective-permute-start | bytes 20 | tf_op jit(solution)/shard_map/ppermute | solution.py:258
  53.6 27.9 %collective-permute-start.3 = (bf16[16,128,128]{2,1,0:T(8,128)(2,1)}, bf16[16,128,128]{2,1,0:T(8,128)(2,1)S(1)}, u32[]{:S(2)}, u32[]{:S(2)}) collective-permute-start(bf16[16,128,128]{2,1,0:T(8,128)(2,1)} %attend.1.mine_ref), channel_id=1, source_target_pairs={{0,1},{1,0},{2,3},{3,2},{4,5},{5,4},{6,7},{7,6},{8,9},{9,8},{10,11... | collective-permute-start | bytes 1572872 | tf_op jit(solution)/shard_map/ppermute | solution.py:255
  53.6 6.4 %collective-permute-start.15 = (bf16[128,1024]{1,0:T(8,128)(2,1)S(1)}, bf16[128,1024]{1,0:T(8,128)(2,1)S(1)}, u32[]{:S(2)}, u32[]{:S(2)}) collective-permute-start(bf16[128,1024]{1,0:T(8,128)(2,1)S(1)} %collective-permute-done.13.refs_10_), channel_id=1, source_target_pairs={{0,4},{1,3},{4,8},{5,1},{8,12},{9,5},{12,14},{13,9},{14,10},{15,13... | collective-permute-start | bytes 786440 | tf_op jit(solution)/shard_map/ppermute | solution.py:252
  54.8 8.0 %collective-permute-start.16 = (bf16[128,1024]{1,0:T(8,128)(2,1)S(1)}, bf16[128,1024]{1,0:T(8,128)(2,1)S(1)}, u32[]{:S(2)}, u32[]{:S(2)}) collective-permute-start(bf16[128,1024]{1,0:T(8,128)(2,1)S(1)} %collective-permute-done.14.refs_11_), channel_id=1, source_target_pairs={{0,4},{1,3},{4,8},{5,1},{8,12},{9,5},{12,14},{13,9},{14,10},{15,13... | collective-permute-start | bytes 786440 | tf_op jit(solution)/shard_map/ppermute | solution.py:252
  60.0 21.4 %collective-permute-start.17 = (bf16[128,1024]{1,0:T(8,128)(2,1)S(1)}, bf16[128,1024]{1,0:T(8,128)(2,1)S(1)}, u32[]{:S(2)}, u32[]{:S(2)}) collective-permute-start(bf16[128,1024]{1,0:T(8,128)(2,1)S(1)} %collective-permute-done.15.refs_12_), channel_id=1, source_target_pairs={{0,4},{1,3},{4,8},{5,1},{8,12},{9,5},{12,14},{13,9},{14,10},{15,13... | collective-permute-start | bytes 786440 | tf_op jit(solution)/shard_map/ppermute | solution.py:252
  62.8 19.3 %collective-permute-start.18 = (bf16[128,1024]{1,0:T(8,128)(2,1)S(1)}, bf16[128,1024]{1,0:T(8,128)(2,1)S(1)}, u32[]{:S(2)}, u32[]{:S(2)}) collective-permute-start(bf16[128,1024]{1,0:T(8,128)(2,1)S(1)} %collective-permute-done.16.refs_13_), channel_id=1, source_target_pairs={{0,4},{1,3},{4,8},{5,1},{8,12},{9,5},{12,14},{13,9},{14,10},{15,13... | collective-permute-start | bytes 786440 | tf_op jit(solution)/shard_map/ppermute | solution.py:252
  72.6 40.6 %copy-start.41 = (f32[128,8]{0,1:T(8,128)S(1)}, f32[128,8]{0,1:T(8,128)}, u32[]{:S(2)}) copy-start(f32[128,8]{0,1:T(8,128)} %param.47) | copy-start | bytes 12292
  72.6 40.6 %copy-start.42 = (s32[128,8]{0,1:T(8,128)S(1)}, s32[128,8]{0,1:T(8,128)}, u32[]{:S(2)}) copy-start(s32[128,8]{0,1:T(8,128)} %param.46) | copy-start | bytes 12292
  100.7 2.1 collective-permute-start.19
  103.9 9.3 %collective-permute-start.22 = (bf16[128,2048]{1,0:T(8,128)(2,1)S(1)}, bf16[128,2048]{1,0:T(8,128)(2,1)}, u32[]{:S(2)}, u32[]{:S(2)}) collective-permute-start(bf16[128,2048]{1,0:T(8,128)(2,1)S(1)} %get-tuple-element.28.x_ref), channel_id=1, source_target_pairs={{0,4},{1,3},{4,8},{5,1},{8,12},{9,5},{12,14},{13,9},{14,10},{15,13... | collective-permute-start | bytes 1572872 | tf_op jit(solution)/shard_map/ppermute | solution.py:252
  113.2 13.6 %collective-permute-start.41 = (bf16[128,2048]{1,0:T(8,128)(2,1)}, bf16[128,2048]{1,0:T(8,128)(2,1)}, u32[]{:S(2)}, u32[]{:S(2)}) collective-permute-start(bf16[128,2048]{1,0:T(8,128)(2,1)} %collective-permute-done.22.x_ref), channel_id=1, source_target_pairs={{0,1},{1,0},{2,3},{3,2},{4,5},{5,4},{6,7},{7,6},{8,9},{9,8},{10,11... | collective-permute-start | bytes 1572872 | tf_op jit(solution)/shard_map/ppermute | solution.py:255
  113.8 12.4 %all-to-all-start = ((f32[16,1,128]{2,1,0:T(1,128)}), f32[16,1,128]{2,1,0:T(1,128)S(1)}, u32[]{:S(2)}, u32[]{:S(2)}) async-start(f32[16,1,128]{2,1,0:T(1,128)} %bitcast.9), calls=%async_computation | async-start | bytes 16384 | tf_op jit(solution)/shard_map/all_to_all | solution.py:264
  126.4 9.4 %collective-permute-start.23 = (bf16[128,2048]{1,0:T(8,128)(2,1)}, bf16[128,2048]{1,0:T(8,128)(2,1)S(1)}, u32[]{:S(2)}, u32[]{:S(2)}) collective-permute-start(bf16[128,2048]{1,0:T(8,128)(2,1)} %collective-permute-done.22.x_ref), channel_id=1, source_target_pairs={{0,4},{1,3},{4,8},{5,1},{8,12},{9,5},{12,14},{13,9},{14,10},{15,13... | collective-permute-start | bytes 1572872 | tf_op jit(solution)/shard_map/ppermute | solution.py:252
  133.3 4.1 %collective-permute-start.42 = (bf16[128,2048]{1,0:T(8,128)(2,1)S(1)}, bf16[128,2048]{1,0:T(8,128)(2,1)S(1)}, u32[]{:S(2)}, u32[]{:S(2)}) collective-permute-start(bf16[128,2048]{1,0:T(8,128)(2,1)S(1)} %get-tuple-element.44), channel_id=1, source_target_pairs={{0,1},{1,0},{2,3},{3,2},{4,5},{5,4},{6,7},{7,6},{8,9},{9,8},{10,11... | collective-permute-start | bytes 1572872 | tf_op jit(solution)/shard_map/ppermute | solution.py:255
  135.8 2.4 %collective-permute-start.39 = (bf16[128,2048]{1,0:T(8,128)(2,1)S(1)}, bf16[128,2048]{1,0:T(8,128)(2,1)S(1)}, u32[]{:S(2)}, u32[]{:S(2)}) collective-permute-start(bf16[128,2048]{1,0:T(8,128)(2,1)S(1)} %collective-permute-done.23.x_ref), channel_id=1, source_target_pairs={{0,1},{1,0},{2,3},{3,2},{4,5},{5,4},{6,7},{7,6},{8,9},{9,8},{10,11... | collective-permute-start | bytes 1572872 | tf_op jit(solution)/shard_map/ppermute | solution.py:255
  137.1 9.2 %collective-permute-start.24 = (bf16[128,2048]{1,0:T(8,128)(2,1)S(1)}, bf16[128,2048]{1,0:T(8,128)(2,1)S(1)}, u32[]{:S(2)}, u32[]{:S(2)}) collective-permute-start(bf16[128,2048]{1,0:T(8,128)(2,1)S(1)} %collective-permute-done.23.x_ref), channel_id=1, source_target_pairs={{0,4},{1,3},{4,8},{5,1},{8,12},{9,5},{12,14},{13,9},{14,10},{15,13... | collective-permute-start | bytes 1572872 | tf_op jit(solution)/shard_map/ppermute | solution.py:252
  137.6 14.3 %collective-permute-start.43 = (bf16[128,2048]{1,0:T(8,128)(2,1)S(1)}, bf16[128,2048]{1,0:T(8,128)(2,1)S(1)}, u32[]{:S(2)}, u32[]{:S(2)}) collective-permute-start(bf16[128,2048]{1,0:T(8,128)(2,1)S(1)} %add_convert_fusion.7), channel_id=1, source_target_pairs={{0,4},{1,3},{4,8},{5,1},{8,12},{9,5},{12,14},{13,9},{14,10},{15,13... | collective-permute-start | bytes 1572872 | tf_op jit(solution)/shard_map/ppermute | solution.py:252
  141.7 10.1 %collective-permute-start.40 = (bf16[128,2048]{1,0:T(8,128)(2,1)S(1)}, bf16[128,2048]{1,0:T(8,128)(2,1)S(1)}, u32[]{:S(2)}, u32[]{:S(2)}) collective-permute-start(bf16[128,2048]{1,0:T(8,128)(2,1)S(1)} %get-tuple-element.42), channel_id=1, source_target_pairs={{0,1},{1,0},{2,3},{3,2},{4,5},{5,4},{6,7},{7,6},{8,9},{9,8},{10,11... | collective-permute-start | bytes 1572872 | tf_op jit(solution)/shard_map/ppermute | solution.py:255
  146.2 6.3 %collective-permute-start.37 = (bf16[128,2048]{1,0:T(8,128)(2,1)S(1)}, bf16[128,2048]{1,0:T(8,128)(2,1)S(1)}, u32[]{:S(2)}, u32[]{:S(2)}) collective-permute-start(bf16[128,2048]{1,0:T(8,128)(2,1)S(1)} %collective-permute-done.24.x_ref), channel_id=1, source_target_pairs={{0,1},{1,0},{2,3},{3,2},{4,5},{5,4},{6,7},{7,6},{8,9},{9,8},{10,11... | collective-permute-start | bytes 1572872 | tf_op jit(solution)/shard_map/ppermute | solution.py:255
  147.6 9.8 %collective-permute-start.25 = (bf16[128,2048]{1,0:T(8,128)(2,1)S(1)}, bf16[128,2048]{1,0:T(8,128)(2,1)S(1)}, u32[]{:S(2)}, u32[]{:S(2)}) collective-permute-start(bf16[128,2048]{1,0:T(8,128)(2,1)S(1)} %collective-permute-done.24.x_ref), channel_id=1, source_target_pairs={{0,4},{1,3},{4,8},{5,1},{8,12},{9,5},{12,14},{13,9},{14,10},{15,13... | collective-permute-start | bytes 1572872 | tf_op jit(solution)/shard_map/ppermute | solution.py:252
  152.1 11.0 %collective-permute-start.44 = (bf16[128,2048]{1,0:T(8,128)(2,1)S(1)}, bf16[128,2048]{1,0:T(8,128)(2,1)S(1)}, u32[]{:S(2)}, u32[]{:S(2)}) collective-permute-start(bf16[128,2048]{1,0:T(8,128)(2,1)S(1)} %add_convert_fusion.6), channel_id=1, source_target_pairs={{0,4},{1,3},{4,8},{5,1},{8,12},{9,5},{12,14},{13,9},{14,10},{15,13... | collective-permute-start | bytes 1572872 | tf_op jit(solution)/shard_map/ppermute | solution.py:252
  156.1 7.0 %collective-permute-start.38 = (bf16[128,2048]{1,0:T(8,128)(2,1)S(1)}, bf16[128,2048]{1,0:T(8,128)(2,1)S(1)}, u32[]{:S(2)}, u32[]{:S(2)}) collective-permute-start(bf16[128,2048]{1,0:T(8,128)(2,1)S(1)} %get-tuple-element.40), channel_id=1, source_target_pairs={{0,1},{1,0},{2,3},{3,2},{4,5},{5,4},{6,7},{7,6},{8,9},{9,8},{10,11... | collective-permute-start | bytes 1572872 | tf_op jit(solution)/shard_map/ppermute | solution.py:255
  157.5 6.3 %collective-permute-start.35 = (bf16[128,2048]{1,0:T(8,128)(2,1)S(1)}, bf16[128,2048]{1,0:T(8,128)(2,1)S(1)}, u32[]{:S(2)}, u32[]{:S(2)}) collective-permute-start(bf16[128,2048]{1,0:T(8,128)(2,1)S(1)} %collective-permute-done.25.x_ref), channel_id=1, source_target_pairs={{0,1},{1,0},{2,3},{3,2},{4,5},{5,4},{6,7},{7,6},{8,9},{9,8},{10,11... | collective-permute-start | bytes 1572872 | tf_op jit(solution)/shard_map/ppermute | solution.py:255
  158.8 9.9 %collective-permute-start.26 = (bf16[128,2048]{1,0:T(8,128)(2,1)S(1)}, bf16[128,2048]{1,0:T(8,128)(2,1)S(1)}, u32[]{:S(2)}, u32[]{:S(2)}) collective-permute-start(bf16[128,2048]{1,0:T(8,128)(2,1)S(1)} %collective-permute-done.25.x_ref), channel_id=1, source_target_pairs={{0,4},{1,3},{4,8},{5,1},{8,12},{9,5},{12,14},{13,9},{14,10},{15,13... | collective-permute-start | bytes 1572872 | tf_op jit(solution)/shard_map/ppermute | solution.py:252
  163.3 11.0 %collective-permute-start.45 = (bf16[128,2048]{1,0:T(8,128)(2,1)S(1)}, bf16[128,2048]{1,0:T(8,128)(2,1)S(1)}, u32[]{:S(2)}, u32[]{:S(2)}) collective-permute-start(bf16[128,2048]{1,0:T(8,128)(2,1)S(1)} %add_convert_fusion.5), channel_id=1, source_target_pairs={{0,4},{1,3},{4,8},{5,1},{8,12},{9,5},{12,14},{13,9},{14,10},{15,13... | collective-permute-start | bytes 1572872 | tf_op jit(solution)/shard_map/ppermute | solution.py:252
  167.3 7.0 %collective-permute-start.36 = (bf16[128,2048]{1,0:T(8,128)(2,1)S(1)}, bf16[128,2048]{1,0:T(8,128)(2,1)S(1)}, u32[]{:S(2)}, u32[]{:S(2)}) collective-permute-start(bf16[128,2048]{1,0:T(8,128)(2,1)S(1)} %get-tuple-element.38), channel_id=1, source_target_pairs={{0,1},{1,0},{2,3},{3,2},{4,5},{5,4},{6,7},{7,6},{8,9},{9,8},{10,11... | collective-permute-start | bytes 1572872 | tf_op jit(solution)/shard_map/ppermute | solution.py:255
  168.7 6.3 %collective-permute-start.33 = (bf16[128,2048]{1,0:T(8,128)(2,1)S(1)}, bf16[128,2048]{1,0:T(8,128)(2,1)S(1)}, u32[]{:S(2)}, u32[]{:S(2)}) collective-permute-start(bf16[128,2048]{1,0:T(8,128)(2,1)S(1)} %collective-permute-done.26.x_ref), channel_id=1, source_target_pairs={{0,1},{1,0},{2,3},{3,2},{4,5},{5,4},{6,7},{7,6},{8,9},{9,8},{10,11... | collective-permute-start | bytes 1572872 | tf_op jit(solution)/shard_map/ppermute | solution.py:255
  170.1 9.9 %collective-permute-start.27 = (bf16[128,2048]{1,0:T(8,128)(2,1)S(1)}, bf16[128,2048]{1,0:T(8,128)(2,1)S(1)}, u32[]{:S(2)}, u32[]{:S(2)}) collective-permute-start(bf16[128,2048]{1,0:T(8,128)(2,1)S(1)} %collective-permute-done.26.x_ref), channel_id=1, source_target_pairs={{0,4},{1,3},{4,8},{5,1},{8,12},{9,5},{12,14},{13,9},{14,10},{15,13... | collective-permute-start | bytes 1572872 | tf_op jit(solution)/shard_map/ppermute | solution.py:252
  174.6 11.0 %collective-permute-start.46 = (bf16[128,2048]{1,0:T(8,128)(2,1)S(1)}, bf16[128,2048]{1,0:T(8,128)(2,1)S(1)}, u32[]{:S(2)}, u32[]{:S(2)}) collective-permute-start(bf16[128,2048]{1,0:T(8,128)(2,1)S(1)} %add_convert_fusion.4), channel_id=1, source_target_pairs={{0,4},{1,3},{4,8},{5,1},{8,12},{9,5},{12,14},{13,9},{14,10},{15,13... | collective-permute-start | bytes 1572872 | tf_op jit(solution)/shard_map/ppermute | solution.py:252
  178.5 7.0 %collective-permute-start.34 = (bf16[128,2048]{1,0:T(8,128)(2,1)S(1)}, bf16[128,2048]{1,0:T(8,128)(2,1)S(1)}, u32[]{:S(2)}, u32[]{:S(2)}) collective-permute-start(bf16[128,2048]{1,0:T(8,128)(2,1)S(1)} %get-tuple-element.36), channel_id=1, source_target_pairs={{0,1},{1,0},{2,3},{3,2},{4,5},{5,4},{6,7},{7,6},{8,9},{9,8},{10,11... | collective-permute-start | bytes 1572872 | tf_op jit(solution)/shard_map/ppermute | solution.py:255
  179.9 6.3 %collective-permute-start.31 = (bf16[128,2048]{1,0:T(8,128)(2,1)S(1)}, bf16[128,2048]{1,0:T(8,128)(2,1)S(1)}, u32[]{:S(2)}, u32[]{:S(2)}) collective-permute-start(bf16[128,2048]{1,0:T(8,128)(2,1)S(1)} %collective-permute-done.27.x_ref), channel_id=1, source_target_pairs={{0,1},{1,0},{2,3},{3,2},{4,5},{5,4},{6,7},{7,6},{8,9},{9,8},{10,11... | collective-permute-start | bytes 1572872 | tf_op jit(solution)/shard_map/ppermute | solution.py:255
  181.3 9.9 %collective-permute-start.28 = (bf16[128,2048]{1,0:T(8,128)(2,1)S(1)}, bf16[128,2048]{1,0:T(8,128)(2,1)S(1)}, u32[]{:S(2)}, u32[]{:S(2)}) collective-permute-start(bf16[128,2048]{1,0:T(8,128)(2,1)S(1)} %collective-permute-done.27.x_ref), channel_id=1, source_target_pairs={{0,4},{1,3},{4,8},{5,1},{8,12},{9,5},{12,14},{13,9},{14,10},{15,13... | collective-permute-start | bytes 1572872 | tf_op jit(solution)/shard_map/ppermute | solution.py:252
  185.8 11.0 %collective-permute-start.47 = (bf16[128,2048]{1,0:T(8,128)(2,1)S(1)}, bf16[128,2048]{1,0:T(8,128)(2,1)S(1)}, u32[]{:S(2)}, u32[]{:S(2)}) collective-permute-start(bf16[128,2048]{1,0:T(8,128)(2,1)S(1)} %add_convert_fusion.3), channel_id=1, source_target_pairs={{0,4},{1,3},{4,8},{5,1},{8,12},{9,5},{12,14},{13,9},{14,10},{15,13... | collective-permute-start | bytes 1572872 | tf_op jit(solution)/shard_map/ppermute | solution.py:252
  189.8 7.0 %collective-permute-start.32 = (bf16[128,2048]{1,0:T(8,128)(2,1)S(1)}, bf16[128,2048]{1,0:T(8,128)(2,1)S(1)}, u32[]{:S(2)}, u32[]{:S(2)}) collective-permute-start(bf16[128,2048]{1,0:T(8,128)(2,1)S(1)} %get-tuple-element.34), channel_id=1, source_target_pairs={{0,1},{1,0},{2,3},{3,2},{4,5},{5,4},{6,7},{7,6},{8,9},{9,8},{10,11... | collective-permute-start | bytes 1572872 | tf_op jit(solution)/shard_map/ppermute | solution.py:255
  191.2 6.3 %collective-permute-start.29 = (bf16[128,2048]{1,0:T(8,128)(2,1)S(1)}, bf16[128,2048]{1,0:T(8,128)(2,1)S(1)}, u32[]{:S(2)}, u32[]{:S(2)}) collective-permute-start(bf16[128,2048]{1,0:T(8,128)(2,1)S(1)} %collective-permute-done.28.x_ref), channel_id=1, source_target_pairs={{0,1},{1,0},{2,3},{3,2},{4,5},{5,4},{6,7},{7,6},{8,9},{9,8},{10,11... | collective-permute-start | bytes 1572872 | tf_op jit(solution)/shard_map/ppermute | solution.py:255
  192.4 8.7 %collective-permute-start.20 = (bf16[128,2048]{1,0:T(8,128)(2,1)S(1)}, bf16[128,2048]{1,0:T(8,128)(2,1)S(1)}, u32[]{:S(2)}, u32[]{:S(2)}) collective-permute-start(bf16[128,2048]{1,0:T(8,128)(2,1)S(1)} %copy-done.6), channel_id=1, source_target_pairs={{0,1},{1,0},{2,3},{3,2},{4,5},{5,4},{6,7},{7,6},{8,9},{9,8},{10,11... | collective-permute-start | bytes 1572872 | tf_op jit(solution)/shard_map/ppermute | solution.py:255
  197.1 9.2 %collective-permute-start.48 = (bf16[128,2048]{1,0:T(8,128)(2,1)S(1)}, bf16[128,2048]{1,0:T(8,128)(2,1)S(1)}, u32[]{:S(2)}, u32[]{:S(2)}) collective-permute-start(bf16[128,2048]{1,0:T(8,128)(2,1)S(1)} %add_convert_fusion.2), channel_id=1, source_target_pairs={{0,4},{1,3},{4,8},{5,1},{8,12},{9,5},{12,14},{13,9},{14,10},{15,13... | collective-permute-start | bytes 1572872 | tf_op jit(solution)/shard_map/ppermute | solution.py:252
  201.0 5.3 %collective-permute-start.30 = (bf16[128,2048]{1,0:T(8,128)(2,1)S(1)}, bf16[128,2048]{1,0:T(8,128)(2,1)S(1)}, u32[]{:S(2)}, u32[]{:S(2)}) collective-permute-start(bf16[128,2048]{1,0:T(8,128)(2,1)S(1)} %get-tuple-element.32), channel_id=1, source_target_pairs={{0,1},{1,0},{2,3},{3,2},{4,5},{5,4},{6,7},{7,6},{8,9},{9,8},{10,11... | collective-permute-start | bytes 1572872 | tf_op jit(solution)/shard_map/ppermute | solution.py:255
  204.7 2.3 %collective-permute-start.21 = (bf16[128,2048]{1,0:T(8,128)(2,1)S(1)}, bf16[128,2048]{1,0:T(8,128)(2,1)S(1)}, u32[]{:S(2)}, u32[]{:S(2)}) collective-permute-start(bf16[128,2048]{1,0:T(8,128)(2,1)S(1)} %get-tuple-element.30), channel_id=1, source_target_pairs={{0,1},{1,0},{2,3},{3,2},{4,5},{5,4},{6,7},{7,6},{8,9},{9,8},{10,11... | collective-permute-start | bytes 1572872 | tf_op jit(solution)/shard_map/ppermute | solution.py:255
  206.5 9.2 %collective-permute-start.49 = (bf16[128,2048]{1,0:T(8,128)(2,1)S(1)}, bf16[128,2048]{1,0:T(8,128)(2,1)S(1)}, u32[]{:S(2)}, u32[]{:S(2)}) collective-permute-start(bf16[128,2048]{1,0:T(8,128)(2,1)S(1)} %add_convert_fusion.1), channel_id=1, source_target_pairs={{0,4},{1,3},{4,8},{5,1},{8,12},{9,5},{12,14},{13,9},{14,10},{15,13... | collective-permute-start | bytes 1572872 | tf_op jit(solution)/shard_map/ppermute | solution.py:252
  (44 other events, 324.6 us)

commit v2 on v1

v2 whole, which is shorter than its diff:
```python
import functools
import math

import jax
import jax.numpy as jnp
from jax import lax
from jax.experimental import pallas as pl
from jax.experimental.pallas import tpu as pltpu
from jax.sharding import PartitionSpec as P

HEADS = 16
HD = 128
FF = 512
F32 = jnp.float32
BF16 = jnp.bfloat16
SMEM = pltpu.SMEM


class Ring:
    def __init__(self, count):
        self.count = count
        self.pairs = count // 2
        chips = list(range(0, self.pairs, 2)) + list(range(1, self.pairs, 2))[::-1]
        self.device = [[2 * c, 2 * c + 1] for c in chips]
        self.place = {self.device[i][k]: (i, k) for i in range(self.pairs) for k in (0, 1)}

    def at(self, i, k):
        return self.device[i % self.pairs][k]

    def step(self):
        route = []
        for i in range(self.pairs):
            route += [(self.at(i, 0), self.at(i + 1, 0)), (self.at(i, 1), self.at(i - 1, 1))]
        return route

    def sibling(self):
        return [(e, e ^ 1) for e in range(self.count)]

    def source(self, s, flip_lane, flip_way):
        out = []
        for e in range(self.count):
            i, k = self.place[e]
            way = 1 if k == 0 else -1
            if flip_way:
                way = -way
            out.append(self.at(i - s * way, k ^ flip_lane))
        return out


def swap_pairs(axis):
    count = lax.axis_size(axis)
    route = []
    for low in range(0, count - 1, 2):
        route += [(low, low + 1), (low + 1, low)]
    return route


def attend_body(first, count, len_ref, far_len_ref, q_ref, kv_ref, cache_ref, fk_ref, fv_ref, out_ref):
    rows = q_ref.shape[0]
    seg = fk_ref.shape[0]
    near_len = len_ref[0, 0]
    far_len = far_len_ref[0]
    pos = lax.broadcasted_iota(jnp.int32, (rows, seg), 1)
    near_ok = pos < near_len
    far_ok = pos < far_len
    scale = 1.0 / math.sqrt(HD)
    dims = (((1,), (1,)), ((), ()))
    for h in range(count):
        cols = slice((first + h) * HD, (first + h + 1) * HD)
        q = q_ref[:, cols]
        s0 = lax.dot_general(q, kv_ref[0, :, cols], dims, preferred_element_type=F32) * scale
        s1 = lax.dot_general(q, cache_ref[0, 0, 0, :, cols], dims, preferred_element_type=F32) * scale
        s2 = lax.dot_general(q, fk_ref[:, cols], dims, preferred_element_type=F32) * scale
        s1 = jnp.where(near_ok, s1, -1e30)
        s2 = jnp.where(far_ok, s2, -1e30)
        m = jnp.max(jnp.maximum(jnp.maximum(s0, s1), s2), axis=1, keepdims=True)
        w0 = jnp.exp(s0 - m)
        w1 = jnp.where(near_ok, jnp.exp(s1 - m), 0.0)
        w2 = jnp.where(far_ok, jnp.exp(s2 - m), 0.0)
        l = jnp.sum(w0 + w1 + w2, axis=1, keepdims=True)
        a = jnp.dot(w0.astype(BF16), kv_ref[1, :, cols], preferred_element_type=F32)
        a += jnp.dot(w1.astype(BF16), cache_ref[1, 0, 0, :, cols], preferred_element_type=F32)
        a += jnp.dot(w2.astype(BF16), fv_ref[:, cols], preferred_element_type=F32)
        out_ref[h] = (a / l).astype(BF16)


def full():
    return pl.BlockSpec(memory_space=pltpu.VMEM)


def scalars():
    return pl.BlockSpec(memory_space=SMEM)


def attend(first, count, queries, span_kv, cache_kv, far_k, far_v, seg_len, far_len):
    rows = queries.shape[0]
    return pl.pallas_call(
        functools.partial(attend_body, first, count),
        out_shape=jax.ShapeDtypeStruct((count, rows, HD), BF16),
        in_specs=[scalars(), scalars()] + [full()] * 5,
        out_specs=full(),
        cost_estimate=pl.CostEstimate(
            flops=40 * rows * rows * HD * count, bytes_accessed=16 * rows * HD * count, transcendentals=0
        ),
        compiler_params=pltpu.CompilerParams(vmem_limit_bytes=16 * 2**20),
        name="attend",
    )(seg_len, far_len, queries, span_kv, cache_kv, far_k, far_v)


def pack_body(count, lane_ref, rows_ref, routes_ref, wts_ref, own_ref, other_ref):
    slab, half = rows_ref.shape[0], own_ref.shape[1]
    lane = lane_ref[0]
    own_ref[:slab] = rows_ref[:, pl.ds(pl.multiple_of(lane * half, HD), half)]
    other_ref[:slab] = rows_ref[:, pl.ds(pl.multiple_of((1 - lane) * half, HD), half)]
    routes = routes_ref[...]
    wts = wts_ref[...]
    tokens = wts.shape[1]
    high, low = [], []
    for group in range(count // 8):
        dense = jnp.concatenate(
            [
                jnp.sum(jnp.where(routes == group * 8 + j, wts, 0.0), axis=0, keepdims=True)
                for j in range(8)
            ],
            axis=0,
        )
        top = dense.astype(BF16)
        high.append(top)
        low.append((dense - top.astype(F32)).astype(BF16))
    tail = jnp.concatenate(high + low, axis=1)
    for out in (own_ref, other_ref):
        out[slab:, : tail.shape[1]] = tail
        if tail.shape[1] < half:
            out[slab:, tail.shape[1] :] = jnp.zeros((8, half - tail.shape[1]), BF16)


def pack(count, lane, o_rows, routes, route_wts):
    slab, width = o_rows.shape
    out = jax.ShapeDtypeStruct((slab + 8, width // 2), BF16)
    return pl.pallas_call(
        functools.partial(pack_body, count),
        out_shape=(out, out),
        in_specs=[scalars()] + [full()] * 3,
        out_specs=(full(), full()),
        cost_estimate=pl.CostEstimate(flops=slab * width, bytes_accessed=4 * slab * width, transcendentals=0),
        compiler_params=pltpu.CompilerParams(vmem_limit_bytes=8 * 2**20),
        name="pack",
    )(lane, o_rows, routes.T, route_wts.T)


def project_body(first, blocks, pieces, carried, table_ref, me_ref, *refs):
    refs = list(refs)
    mine = [refs.pop(0) for _ in range(pieces)]
    theirs = [refs.pop(0) for _ in range(pieces)]
    before = [refs.pop(0) for _ in range(2 if carried else 0)]
    source = [refs.pop(0) for _ in range(blocks)]
    own_ref, give_ref, wts_ref, att, held, sems = refs
    rows = own_ref.shape[0]
    slab = att.shape[2]
    me = me_ref[0]
    copies = [pltpu.make_async_copy(source[b], held.at[b], sems.at[b]) for b in range(blocks)]
    for copy in copies:
        copy.start()
    at = 0
    for a, b in zip(mine, theirs):
        att[at : at + a.shape[0], :rows] = a[...]
        att[at : at + a.shape[0], rows:] = b[...]
        at += a.shape[0]
    sub, group = lax.rem(me, 8), me // 8
    groups = att.shape[0] // 8
    pick = lax.broadcasted_iota(jnp.int32, (8, rows), 0) == sub
    total = None
    lines = []
    for b in range(blocks):
        copies[b].wait()
        block = held[b, :slab]
        part = jnp.dot(att[table_ref[me, first + b]], block, preferred_element_type=F32)
        total = part if total is None else total + part
        high = held[b, slab:, pl.ds(pl.multiple_of(group * rows, 128), rows)].astype(F32)
        low = held[b, slab:, pl.ds(pl.multiple_of((groups + group) * rows, 128), rows)].astype(F32)
        lines.append(jnp.sum(jnp.where(pick, high + low, 0.0), axis=0, keepdims=True))
    if carried:
        own_ref[...] = before[0][...] + total[:rows]
        give_ref[...] = before[1][...] + total[rows:]
    else:
        own_ref[...] = total[:rows]
        give_ref[...] = total[rows:]
    lines.append(jnp.zeros((128 - blocks, rows), F32))
    wts_ref[...] = jnp.concatenate(lines, axis=0).T


def project(table, me, first, mine, theirs, before, blocks):
    count = sum(part.shape[0] for part in mine)
    rows, slab = mine[0].shape[1:]
    half = blocks[0].shape[1]
    out = jax.ShapeDtypeStruct((rows, half), F32)
    number = len(blocks)
    return pl.pallas_call(
        functools.partial(project_body, first, number, len(mine), bool(before)),
        out_shape=(out, out, jax.ShapeDtypeStruct((rows, 128), F32)),
        in_specs=[scalars(), scalars()]
        + [full()] * (2 * len(mine) + len(before))
        + [pl.BlockSpec(memory_space=pl.ANY)] * number,
        out_specs=(full(), full(), full()),
        scratch_shapes=[
            pltpu.VMEM((count, 2 * rows, slab), BF16),
            pltpu.VMEM((number,) + blocks[0].shape, BF16),
            pltpu.SemaphoreType.DMA((number,)),
        ],
        cost_estimate=pl.CostEstimate(
            flops=4 * rows * half * slab * number, bytes_accessed=2 * half * slab * number, transcendentals=0
        ),
        compiler_params=pltpu.CompilerParams(vmem_limit_bytes=20 * 2**20),
        name="project",
    )(table, me, *mine, *theirs, *before, *blocks)


def norm_body(lane_ref, resid_ref, own_ref, got_ref, gain_ref, sum_ref, out_ref):
    first = lane_ref[0] == 0
    half = own_ref.shape[1]
    own = own_ref[...]
    got = got_ref[...]
    low = resid_ref[:, :half].astype(F32) + jnp.where(first, own, got)
    high = resid_ref[:, half:].astype(F32) + jnp.where(first, got, own)
    sum_ref[:, :half] = low
    sum_ref[:, half:] = high
    square = jnp.sum(low * low + high * high, axis=1, keepdims=True)
    scale = lax.rsqrt(square * (1.0 / (2 * half)) + 1e-05)
    out_ref[:, :half] = (low * scale * gain_ref[:, :half]).astype(BF16)
    out_ref[:, half:] = (high * scale * gain_ref[:, half:]).astype(BF16)


def norm(lane, resid, own, got, gain):
    return pl.pallas_call(
        norm_body,
        out_shape=(
            jax.ShapeDtypeStruct(resid.shape, F32),
            jax.ShapeDtypeStruct(resid.shape, BF16),
        ),
        in_specs=[scalars()] + [full()] * 4,
        out_specs=(full(), full()),
        cost_estimate=pl.CostEstimate(
            flops=8 * resid.size, bytes_accessed=12 * resid.size, transcendentals=0
        ),
        compiler_params=pltpu.CompilerParams(vmem_limit_bytes=16 * 2**20),
        name="norm",
    )(lane, resid, own, got, gain.reshape(1, -1))


def expert_body(cols, xa_ref, xb_ref, ya_ref, yb_ref, wx_ref, wy_ref, in_ref, down_ref, cx_ref, cy_ref):
    rows, width = cx_ref.shape
    both = jnp.concatenate([xa_ref[...], xb_ref[...], ya_ref[...], yb_ref[...]], axis=0)
    gate = jnp.dot(both, in_ref[0, :, :FF], preferred_element_type=F32)
    up = jnp.dot(both, in_ref[0, :, FF:], preferred_element_type=F32)
    hidden = (gate * jax.nn.sigmoid(gate) * up).astype(BF16)
    wx = wx_ref[:, cols[0] : cols[0] + 1]
    wy = wy_ref[:, cols[1] : cols[1] + 1]
    step = 512
    for at in range(0, width, step):
        out = jnp.dot(hidden, down_ref[0, :, at : at + step], preferred_element_type=F32)
        cx_ref[:, at : at + step] = (out[:rows] * wx).astype(BF16)
        cy_ref[:, at : at + step] = (out[rows:] * wy).astype(BF16)


def expert(cols, x, y, wx, wy, w_in, w_out):
    rows, width = 2 * x[0].shape[0], x[0].shape[1]
    out = jax.ShapeDtypeStruct((rows, width), BF16)
    return pl.pallas_call(
        functools.partial(expert_body, cols),
        out_shape=(out, out),
        in_specs=[full()] * 8,
        out_specs=(full(), full()),
        cost_estimate=pl.CostEstimate(
            flops=12 * rows * width * FF, bytes_accessed=6 * width * FF, transcendentals=0
        ),
        compiler_params=pltpu.CompilerParams(vmem_limit_bytes=24 * 2**20),
        name="expert",
    )(*x, *y, wx, wy, w_in, w_out)


def shards(
    ring, resid, queries, span_kv, cache_kv, seg_len, o_rows, norm_gain, routes, route_wts, w_in, w_out
):
    count, pairs = ring.count, ring.pairs
    rows, width = queries.shape
    me = lax.axis_index("expert")
    lane = me % 2
    forward, sibling = ring.step(), ring.sibling()

    def ahead(block):
        return lax.ppermute(block, "expert", forward)

    def across(block):
        return lax.ppermute(block, "expert", sibling)

    group_swap = swap_pairs("group")
    far_len = lax.ppermute(seg_len[0, 1:2], "group", group_swap)
    far_k = lax.ppermute(cache_kv[0, 0, 1], "group", group_swap)
    far_v = lax.ppermute(cache_kv[1, 0, 1], "group", group_swap)

    chain_a, other = pack(count, lane[None], o_rows, routes, route_wts)
    chain_b = across(other)
    blocks = [chain_a, chain_b]
    for s in range(1, pairs):
        chain_a = ahead(chain_a)
        chain_b = ahead(chain_b)
        blocks += [chain_a, chain_b]
    sources = []
    for s in range(pairs):
        sources += [ring.source(s, 0, False), ring.source(s, 1, False)]
    table = jnp.asarray([[line[e] for line in sources] for e in range(count)], jnp.int32)

    mine, theirs = [], []
    for first in range(0, HEADS, HEADS // 2):
        part = attend(first, HEADS // 2, queries, span_kv, cache_kv, far_k, far_v, seg_len, far_len)
        mine.append(part)
        theirs.append(across(part))
    slab = o_rows.shape[0]
    if slab != HD:
        mine, theirs = (
            [jnp.concatenate(p).transpose(1, 0, 2).reshape(rows, count, slab).transpose(1, 0, 2)]
            for p in (mine, theirs)
        )
    early = 2 * (pairs * 5 // 8)
    first_own, first_give, wts_early = project(table, me[None], 0, mine, theirs, [], blocks[:early])
    own, give, wts_late = project(
        table, me[None], early, mine, theirs, [first_own, first_give], blocks[early:]
    )
    got = across(give)
    residual, normed = norm(lane[None], resid, own, got, norm_gain)

    def gate_at(column):
        return (wts_early, column) if column < early else (wts_late, column - early)

    part_rows = rows // 2
    x = [normed[:part_rows], normed[part_rows:]]
    y = [across(p) for p in x]
    travelling = None
    for s in range(pairs):
        wx, column_x = gate_at(2 * s)
        wy, column_y = gate_at(2 * ((pairs - s) % pairs) + 1)
        keep, give = expert((column_x, column_y), x, y, wx, wy, w_in, w_out)
        back = across(give)
        if s == 0:
            total = residual + keep.astype(F32) + back.astype(F32)
        else:
            part = [
                keep[at : at + part_rows].astype(F32) + back[at : at + part_rows].astype(F32)
                for at in (0, part_rows)
            ]
            if travelling is not None:
                part = [p + t.astype(F32) for p, t in zip(part, travelling)]
            travelling = [ahead(p.astype(BF16)) for p in part]
        if s + 1 < pairs:
            x = [ahead(p) for p in x]
            y = [across(p) for p in x]
    out = [
        total[i * part_rows : (i + 1) * part_rows] + t.astype(F32) for i, t in enumerate(travelling)
    ]
    return jnp.concatenate(out, axis=0).astype(BF16)


def solution(mesh):
    placed = (
        P(("group", "expert"), None),
        P(("group", "expert"), None),
        P(None, ("group", "expert"), None),
        P(None, ("group", "expert"), None, None, None),
        P(("group", "expert"), None),
        P("expert", None),
        P(),
        P(("group", "expert"), None),
        P(("group", "expert"), None),
        P("expert", None, None),
        P("expert", None, None),
    )
    ring = Ring(mesh.shape["expert"])
    return jax.shard_map(
        functools.partial(shards, ring),
        mesh=mesh,
        in_specs=placed,
        out_specs=P(("group", "expert"), None),
        check_vma=False,
    )
```

time: 218 us -> 181 us (0.83)
  local copies, waits for them, and re-layouts: 46.7 us -> 5.74 us
  starting transfers between devices: 41.4 us -> 63.5 us
  Pallas kernels: 40.3 us -> 27.8 us
  other arithmetic: 12.6 us -> 2.65 us
  waiting for transfers between devices: 75.3 us -> 81 us
    ppermute x28 -> x42, starting transfers between devices: 29.1 us -> 54 us  [ahead(): return lax.ppermute(block, 'expert', forward)]
    unnamed x114 -> x24, local copies, waits for them, and re-layouts: 26.2 us -> 3.82 us
    pallas_call x10 -> x13, Pallas kernels: 40 us -> 27.4 us  [the longest x8 15 us: expert(): pl.pallas_call(functools.partial(expert_body, cols), out_shape=(out, out)...]
    ppermute x28 -> x42, waiting for transfers between devices: 60 us -> 71.1 us  [ahead(): return lax.ppermute(block, 'expert', forward)]
    dynamic_slice x15 -> x0, local copies, waits for them, and re-layouts: 9.78 us -> none  [the longest x14 8.56 us: look(): return jnp.asarray(table, jnp.int32)[me]]
    another operation x8 -> x1, other arithmetic: 9.3 us -> 0.1 us  [the longest x7 9.22 us: shards(): jnp.stack([look(ring.source(s, 0, False)), look(ring.source(s, 1, True))])]
    another operation x1 -> x0, local copies, waits for them, and re-layouts: 8.82 us -> none  [shards(): own, give = project(jnp.stack(index), mine, theirs, blocks)]
    all_to_all x1 -> x0, starting transfers between devices: 6.04 us -> none  [shards(): lax.all_to_all(dense.T, 'expert', split_axis=0, concat_axis=0, tiled=True)]
  transfers between devices with their start and end apart: 51 -> 73, of which waited for: 24 -> 35; matrix products, arithmetic and copies ran while one was open for 14% -> 2% of each run, Pallas kernels for 17% -> 14%
where the time goes in v2:
time: 181 us
  waiting for transfers between devices  81 us (45%)
  starting transfers between devices  63.5 us (35%)
  Pallas kernels  27.8 us (15%)
  local copies, waits for them, and re-layouts  5.74 us (3%)
  other arithmetic  2.65 us (1%)
    ppermute x42, waiting for transfers between devices, ahead(): return lax.ppermute(block, 'expert', forward)  71.1 us
    ppermute x42, starting transfers between devices, ahead(): return lax.ppermute(block, 'expert', forward)  54 us
    pallas_call x8, Pallas kernels, expert(): pl.pallas_call(functools.partial(expert_body, cols), out_shape=(out, out)...  15 us
    ppermute x1, waiting for transfers between devices, shards(): far_len = lax.ppermute(seg_len[0, 1:2], 'group', group_swap)  7.93 us
    pallas_call x2, Pallas kernels, attend(): pl.pallas_call(functools.partial(attend_body, first, count), out_shape=ja...  7.18 us
    ppermute x28, starting transfers between devices, across(): return lax.ppermute(block, 'expert', sibling)  5.92 us
    pallas_call x2, Pallas kernels, project(): pl.pallas_call(functools.partial(project_body, first, number, len(mine),...  5.17 us
    unnamed x24, local copies, waits for them, and re-layouts  3.82 us
  transfers between devices with their start and end apart: 73, of which 35 were waited for; matrix products, arithmetic and copies ran while one was open for 2% of the time, Pallas kernels for 14%

profile of v2, /device:TPU:0, one launch (start us, length us, event | category | flops | bytes accessed | tf_op | source)
XLA Modules:
  0.0 181.1 jit_solution(14056687179412025199)
XLA Ops:
  3.1 2.6 %collective-permute-start.6 = (bf16[136,1024]{1,0:T(8,128)(2,1)S(1)}, bf16[136,1024]{1,0:T(8,128)(2,1)S(1)}, u32[]{:S(2)}, u32[]{:S(2)}) collective-permute-start(bf16[136,1024]{1,0:T(8,128)(2,1)S(1)} %get-tuple-element.31.refs_4_), channel_id=1, source_target_pairs={{0,4},{1,3},{4,8},{5,1},{8,12},{9,5},{12,14},{13,9},{14,10},{15,13... | collective-permute-start | bytes 835592 | tf_op jit(solution)/shard_map/ppermute | solution.py:291
  5.8 1.6 collective-permute-start.7
  7.4 2.9 %collective-permute-done.6.refs_6_ = bf16[136,1024]{1,0:T(8,128)(2,1)S(1)} collective-permute-done((bf16[136,1024]{1,0:T(8,128)(2,1)S(1)}, bf16[136,1024]{1,0:T(8,128)(2,1)S(1)}, u32[]{:S(2)}, u32[]{:S(2)}) %collective-permute-start.6) | collective-permute-done | bytes 278560 | tf_op jit(solution)/shard_map/ppermute | solution.py:291
  10.2 2.1 %collective-permute-start.8 = (bf16[136,1024]{1,0:T(8,128)(2,1)S(1)}, bf16[136,1024]{1,0:T(8,128)(2,1)S(1)}, u32[]{:S(2)}, u32[]{:S(2)}) collective-permute-start(bf16[136,1024]{1,0:T(8,128)(2,1)S(1)} %collective-permute-done.6.refs_6_), channel_id=1, source_target_pairs={{0,4},{1,3},{4,8},{5,1},{8,12},{9,5},{12,14},{13,9},{14,10},{15,13... | collective-permute-start | bytes 835592 | tf_op jit(solution)/shard_map/ppermute | solution.py:291
  13.2 2.1 %collective-permute-start.9 = (bf16[136,1024]{1,0:T(8,128)(2,1)S(1)}, bf16[136,1024]{1,0:T(8,128)(2,1)S(1)}, u32[]{:S(2)}, u32[]{:S(2)}) collective-permute-start(bf16[136,1024]{1,0:T(8,128)(2,1)S(1)} %collective-permute-done.7.refs_7_), channel_id=1, source_target_pairs={{0,4},{1,3},{4,8},{5,1},{8,12},{9,5},{12,14},{13,9},{14,10},{15,13... | collective-permute-start | bytes 835592 | tf_op jit(solution)/shard_map/ppermute | solution.py:291
  16.8 2.1 %collective-permute-start.10 = (bf16[136,1024]{1,0:T(8,128)(2,1)S(1)}, bf16[136,1024]{1,0:T(8,128)(2,1)S(1)}, u32[]{:S(2)}, u32[]{:S(2)}) collective-permute-start(bf16[136,1024]{1,0:T(8,128)(2,1)S(1)} %collective-permute-done.8.refs_8_), channel_id=1, source_target_pairs={{0,4},{1,3},{4,8},{5,1},{8,12},{9,5},{12,14},{13,9},{14,10},{15,13... | collective-permute-start | bytes 835592 | tf_op jit(solution)/shard_map/ppermute | solution.py:291
  19.8 2.1 %collective-permute-start.11 = (bf16[136,1024]{1,0:T(8,128)(2,1)S(1)}, bf16[136,1024]{1,0:T(8,128)(2,1)S(1)}, u32[]{:S(2)}, u32[]{:S(2)}) collective-permute-start(bf16[136,1024]{1,0:T(8,128)(2,1)S(1)} %collective-permute-done.9.refs_9_), channel_id=1, source_target_pairs={{0,4},{1,3},{4,8},{5,1},{8,12},{9,5},{12,14},{13,9},{14,10},{15,13... | collective-permute-start | bytes 835592 | tf_op jit(solution)/shard_map/ppermute | solution.py:291
  23.3 2.1 %collective-permute-start.12 = (bf16[136,1024]{1,0:T(8,128)(2,1)S(1)}, bf16[136,1024]{1,0:T(8,128)(2,1)S(1)}, u32[]{:S(2)}, u32[]{:S(2)}) collective-permute-start(bf16[136,1024]{1,0:T(8,128)(2,1)S(1)} %collective-permute-done.10.refs_10_), channel_id=1, source_target_pairs={{0,4},{1,3},{4,8},{5,1},{8,12},{9,5},{12,14},{13,9},{14,10},{15,13... | collective-permute-start | bytes 835592 | tf_op jit(solution)/shard_map/ppermute | solution.py:291
  26.3 2.1 %collective-permute-start.13 = (bf16[136,1024]{1,0:T(8,128)(2,1)S(1)}, bf16[136,1024]{1,0:T(8,128)(2,1)S(1)}, u32[]{:S(2)}, u32[]{:S(2)}) collective-permute-start(bf16[136,1024]{1,0:T(8,128)(2,1)S(1)} %collective-permute-done.11.refs_11_), channel_id=1, source_target_pairs={{0,4},{1,3},{4,8},{5,1},{8,12},{9,5},{12,14},{13,9},{14,10},{15,13... | collective-permute-start | bytes 835592 | tf_op jit(solution)/shard_map/ppermute | solution.py:291
  29.7 1.6 collective-permute-start.1
  31.8 1.6 collective-permute-start.14
  33.4 1.6 collective-permute-start.15
  34.9 3.4 %collective-permute-done.14.refs_6_ = bf16[136,1024]{1,0:T(8,128)(2,1)S(1)} collective-permute-done((bf16[136,1024]{1,0:T(8,128)(2,1)S(1)}, bf16[136,1024]{1,0:T(8,128)(2,1)S(1)}, u32[]{:S(2)}, u32[]{:S(2)}) %collective-permute-start.14) | collective-permute-done | bytes 278560 | tf_op jit(solution)/shard_map/ppermute | solution.py:291
  38.3 1.6 collective-permute-start.16
  41.3 1.6 collective-permute-start.17
  43.5 1.5 collective-permute-start
  45.0 7.9 %collective-permute-done.far_len_ref = s32[1]{0:T(128)} collective-permute-done((s32[1]{0:T(128)}, s32[1]{0:T(128)}, u32[]{:S(2)}, u32[]{:S(2)}) %collective-permute-start) | collective-permute-done | bytes 36 | tf_op jit(solution)/shard_map/ppermute | solution.py:297
  54.2 3.6 %attend.2.refs_0_ = bf16[8,128,128]{2,1,0:T(8,128)(2,1)S(1)} custom-call(s32[1,2]{1,0:T(1,128)S(1)} %copy-done.11, s32[1]{0:T(128)} %collective-permute-done.far_len_ref, bf16[128,2048]{1,0:T(8,128)(2,1)S(1)} %copy-done.4, bf16[2,128,2048]{2,1,0:T(8,128)(2,1)S(1)} %copy-done.3, bf16[2,1,2,128,2048]{4,3,2,1,0:T(8,128)(2,1)S(1)} %copy-done.2, ...), custom_call_target="tpu_custom_call" | custom-call | flops 671088640 | bytes 2097152 | tf_op jit(solution)/shard_map/attend/pallas_call | solution.py:97
  57.9 3.6 %attend.3.refs_1_ = bf16[8,128,128]{2,1,0:T(8,128)(2,1)S(1)} custom-call(s32[1,2]{1,0:T(1,128)S(1)} %copy-done.11, s32[1]{0:T(128)} %collective-permute-done.far_len_ref, bf16[128,2048]{1,0:T(8,128)(2,1)S(1)} %copy-done.4, bf16[2,128,2048]{2,1,0:T(8,128)(2,1)S(1)} %copy-done.3, bf16[2,1,2,128,2048]{4,3,2,1,0:T(8,128)(2,1)S(1)} %copy-done.2, ...), custom_call_target="tpu_custom_call" | custom-call | flops 671088640 | bytes 2097152 | tf_op jit(solution)/shard_map/attend/pallas_call | solution.py:97
  62.4 1.7 collective-permute-start.19
  64.1 3.0 %project.2 = (f32[128,1024]{1,0:T(8,128)S(1)}, f32[128,1024]{1,0:T(8,128)S(1)}, f32[128,128]{1,0:T(8,128)S(1)}) custom-call(s32[16,16]{1,0:T(8,128)S(1)} %copy-done.7, s32[1]{0:T(128)} %bitcast.1.me_ref, bf16[8,128,128]{2,1,0:T(8,128)(2,1)S(1)} %attend.2.refs_0_, bf16[8,128,128]{2,1,0:T(8,128)(2,1)S(1)} %attend.3.refs_1_, ...), custom_call_target="tpu_custom_call" | custom-call | flops 671088640 | bytes 2621440 | tf_op jit(solution)/shard_map/project/pallas_call | solution.py:198
  68.6 3.0 %collective-permute-done.19.refs_11_ = bf16[136,1024]{1,0:T(8,128)(2,1)S(1)} collective-permute-done((bf16[136,1024]{1,0:T(8,128)(2,1)S(1)}, bf16[136,1024]{1,0:T(8,128)(2,1)S(1)}, u32[]{:S(2)}, u32[]{:S(2)}) %collective-permute-start.19) | collective-permute-done | bytes 278560 | tf_op jit(solution)/shard_map/ppermute | solution.py:291
  71.6 2.1 %project.3 = (f32[128,1024]{1,0:T(8,128)S(1)}, f32[128,1024]{1,0:T(8,128)S(1)}, f32[128,128]{1,0:T(8,128)S(1)}) custom-call(s32[16,16]{1,0:T(8,128)S(1)} %copy-done.7, s32[1]{0:T(128)} %bitcast.1.me_ref, bf16[8,128,128]{2,1,0:T(8,128)(2,1)S(1)} %attend.2.refs_0_, bf16[8,128,128]{2,1,0:T(8,128)(2,1)S(1)} %attend.3.refs_1_, ...), custom_call_target="tpu_custom_call" | custom-call | flops 402653184 | bytes 1572864 | tf_op jit(solution)/shard_map/project/pallas_call | solution.py:198
  73.8 1.9 %collective-permute-done.20.got_ref = f32[128,1024]{1,0:T(8,128)S(1)} collective-permute-done((f32[128,1024]{1,0:T(8,128)S(1)}, f32[128,1024]{1,0:T(8,128)S(1)}, u32[]{:S(2)}, u32[]{:S(2)}) %collective-permute-start.20) | collective-permute-done | bytes 524320 | tf_op jit(solution)/shard_map/ppermute | solution.py:294
  76.5 1.7 collective-permute-start.31
  78.3 4.3 %collective-permute-done.24.xa_ref = bf16[64,2048]{1,0:T(8,128)(2,1)S(1)} collective-permute-done((bf16[64,2048]{1,0:T(8,128)(2,1)S(1)}, bf16[64,2048]{1,0:T(8,128)(2,1)S(1)}, u32[]{:S(2)}, u32[]{:S(2)}) %collective-permute-start.24) | collective-permute-done | bytes 262176 | tf_op jit(solution)/shard_map/ppermute | solution.py:291
  82.6 2.8 %collective-permute-done.31.xb_ref = bf16[64,2048]{1,0:T(8,128)(2,1)S(1)} collective-permute-done((bf16[64,2048]{1,0:T(8,128)(2,1)S(1)}, bf16[64,2048]{1,0:T(8,128)(2,1)S(1)}, u32[]{:S(2)}, u32[]{:S(2)}) %collective-permute-start.31) | collective-permute-done | bytes 262176 | tf_op jit(solution)/shard_map/ppermute | solution.py:291
  85.7 1.7 collective-permute-start.32
  87.5 1.9 %expert.15 = (bf16[128,2048]{1,0:T(8,128)(2,1)S(1)}, bf16[128,2048]{1,0:T(8,128)(2,1)S(1)}) custom-call(bf16[64,2048]{1,0:T(8,128)(2,1)S(1)} %collective-permute-done.24.xa_ref, bf16[64,2048]{1,0:T(8,128)(2,1)S(1)} %collective-permute-done.31.xb_ref, bf16[64,2048]{1,0:T(8,128)(2,1)S(1)} %collective-permute-done.56.ya_ref, ...), custom_call_target="tpu_custom_call" | custom-call | flops 1610612736 | bytes 6291456 | tf_op jit(solution)/shard_map/expert/pallas_call | solution.py:268
  91.8 2.8 %collective-permute-done.32.xb_ref = bf16[64,2048]{1,0:T(8,128)(2,1)S(1)} collective-permute-done((bf16[64,2048]{1,0:T(8,128)(2,1)S(1)}, bf16[64,2048]{1,0:T(8,128)(2,1)S(1)}, u32[]{:S(2)}, u32[]{:S(2)}) %collective-permute-start.32) | collective-permute-done | bytes 262176 | tf_op jit(solution)/shard_map/ppermute | solution.py:291
  94.9 1.7 collective-permute-start.33
  96.7 1.9 %expert.14 = (bf16[128,2048]{1,0:T(8,128)(2,1)S(1)}, bf16[128,2048]{1,0:T(8,128)(2,1)S(1)}) custom-call(bf16[64,2048]{1,0:T(8,128)(2,1)S(1)} %collective-permute-done.25.xa_ref, bf16[64,2048]{1,0:T(8,128)(2,1)S(1)} %collective-permute-done.32.xb_ref, bf16[64,2048]{1,0:T(8,128)(2,1)S(1)} %collective-permute-done.53.ya_ref, ...), custom_call_target="tpu_custom_call" | custom-call | flops 1610612736 | bytes 6291456 | tf_op jit(solution)/shard_map/expert/pallas_call | solution.py:268
  101.3 2.5 %collective-permute-done.33.xb_ref = bf16[64,2048]{1,0:T(8,128)(2,1)S(1)} collective-permute-done((bf16[64,2048]{1,0:T(8,128)(2,1)S(1)}, bf16[64,2048]{1,0:T(8,128)(2,1)S(1)}, u32[]{:S(2)}, u32[]{:S(2)}) %collective-permute-start.33) | collective-permute-done | bytes 262176 | tf_op jit(solution)/shard_map/ppermute | solution.py:291
  104.2 1.8 collective-permute-start.59
  106.0 1.6 collective-permute-start.66
  107.6 1.9 %expert.13 = (bf16[128,2048]{1,0:T(8,128)(2,1)S(1)}, bf16[128,2048]{1,0:T(8,128)(2,1)S(1)}) custom-call(bf16[64,2048]{1,0:T(8,128)(2,1)S(1)} %collective-permute-done.26.xa_ref, bf16[64,2048]{1,0:T(8,128)(2,1)S(1)} %collective-permute-done.33.xb_ref, bf16[64,2048]{1,0:T(8,128)(2,1)S(1)} %collective-permute-done.50.ya_ref, ...), custom_call_target="tpu_custom_call" | custom-call | flops 1610612736 | bytes 6291456 | tf_op jit(solution)/shard_map/expert/pallas_call | solution.py:268
  110.4 2.5 %collective-permute-done.59 = bf16[64,2048]{1,0:T(8,128)(2,1)S(1)} collective-permute-done((bf16[64,2048]{1,0:T(8,128)(2,1)S(1)}, bf16[64,2048]{1,0:T(8,128)(2,1)S(1)}, u32[]{:S(2)}, u32[]{:S(2)}) %collective-permute-start.59) | collective-permute-done | bytes 262176 | tf_op jit(solution)/shard_map/ppermute | solution.py:291
  113.9 1.9 %collective-permute-done.66 = bf16[64,2048]{1,0:T(8,128)(2,1)S(1)} collective-permute-done((bf16[64,2048]{1,0:T(8,128)(2,1)S(1)}, bf16[64,2048]{1,0:T(8,128)(2,1)S(1)}, u32[]{:S(2)}, u32[]{:S(2)}) %collective-permute-start.66) | collective-permute-done | bytes 262176 | tf_op jit(solution)/shard_map/ppermute | solution.py:291
  116.3 1.8 collective-permute-start.60
  118.1 1.6 collective-permute-start.67
  119.7 1.9 %expert.12 = (bf16[128,2048]{1,0:T(8,128)(2,1)S(1)}, bf16[128,2048]{1,0:T(8,128)(2,1)S(1)}) custom-call(bf16[64,2048]{1,0:T(8,128)(2,1)S(1)} %collective-permute-done.27.xa_ref, bf16[64,2048]{1,0:T(8,128)(2,1)S(1)} %collective-permute-done.34.xb_ref, bf16[64,2048]{1,0:T(8,128)(2,1)S(1)} %collective-permute-done.47.ya_ref, ...), custom_call_target="tpu_custom_call" | custom-call | flops 1610612736 | bytes 6291456 | tf_op jit(solution)/shard_map/expert/pallas_call | solution.py:268
  122.2 2.7 %collective-permute-done.60 = bf16[64,2048]{1,0:T(8,128)(2,1)S(1)} collective-permute-done((bf16[64,2048]{1,0:T(8,128)(2,1)S(1)}, bf16[64,2048]{1,0:T(8,128)(2,1)S(1)}, u32[]{:S(2)}, u32[]{:S(2)}) %collective-permute-start.60) | collective-permute-done | bytes 262176 | tf_op jit(solution)/shard_map/ppermute | solution.py:291
  125.3 2.5 %collective-permute-done.67 = bf16[64,2048]{1,0:T(8,128)(2,1)S(1)} collective-permute-done((bf16[64,2048]{1,0:T(8,128)(2,1)S(1)}, bf16[64,2048]{1,0:T(8,128)(2,1)S(1)}, u32[]{:S(2)}, u32[]{:S(2)}) %collective-permute-start.67) | collective-permute-done | bytes 262176 | tf_op jit(solution)/shard_map/ppermute | solution.py:291
  128.3 1.8 collective-permute-start.61
  130.1 1.6 collective-permute-start.68
  131.7 1.9 %expert.11 = (bf16[128,2048]{1,0:T(8,128)(2,1)S(1)}, bf16[128,2048]{1,0:T(8,128)(2,1)S(1)}) custom-call(bf16[64,2048]{1,0:T(8,128)(2,1)S(1)} %collective-permute-done.28.xa_ref, bf16[64,2048]{1,0:T(8,128)(2,1)S(1)} %collective-permute-done.35.xb_ref, bf16[64,2048]{1,0:T(8,128)(2,1)S(1)} %collective-permute-done.44.ya_ref, ...), custom_call_target="tpu_custom_call" | custom-call | flops 1610612736 | bytes 6291456 | tf_op jit(solution)/shard_map/expert/pallas_call | solution.py:268
  134.2 2.7 %collective-permute-done.61 = bf16[64,2048]{1,0:T(8,128)(2,1)S(1)} collective-permute-done((bf16[64,2048]{1,0:T(8,128)(2,1)S(1)}, bf16[64,2048]{1,0:T(8,128)(2,1)S(1)}, u32[]{:S(2)}, u32[]{:S(2)}) %collective-permute-start.61) | collective-permute-done | bytes 262176 | tf_op jit(solution)/shard_map/ppermute | solution.py:291
  137.3 2.5 %collective-permute-done.68 = bf16[64,2048]{1,0:T(8,128)(2,1)S(1)} collective-permute-done((bf16[64,2048]{1,0:T(8,128)(2,1)S(1)}, bf16[64,2048]{1,0:T(8,128)(2,1)S(1)}, u32[]{:S(2)}, u32[]{:S(2)}) %collective-permute-start.68) | collective-permute-done | bytes 262176 | tf_op jit(solution)/shard_map/ppermute | solution.py:291
  140.3 1.8 collective-permute-start.62
  142.1 1.6 collective-permute-start.69
  143.7 1.9 %expert.10 = (bf16[128,2048]{1,0:T(8,128)(2,1)S(1)}, bf16[128,2048]{1,0:T(8,128)(2,1)S(1)}) custom-call(bf16[64,2048]{1,0:T(8,128)(2,1)S(1)} %collective-permute-done.29.xa_ref, bf16[64,2048]{1,0:T(8,128)(2,1)S(1)} %collective-permute-done.36.xb_ref, bf16[64,2048]{1,0:T(8,128)(2,1)S(1)} %collective-permute-done.41.ya_ref, ...), custom_call_target="tpu_custom_call" | custom-call | flops 1610612736 | bytes 6291456 | tf_op jit(solution)/shard_map/expert/pallas_call | solution.py:268
  146.2 2.7 %collective-permute-done.62 = bf16[64,2048]{1,0:T(8,128)(2,1)S(1)} collective-permute-done((bf16[64,2048]{1,0:T(8,128)(2,1)S(1)}, bf16[64,2048]{1,0:T(8,128)(2,1)S(1)}, u32[]{:S(2)}, u32[]{:S(2)}) %collective-permute-start.62) | collective-permute-done | bytes 262176 | tf_op jit(solution)/shard_map/ppermute | solution.py:291
  148.9 2.8 %collective-permute-done.69 = bf16[64,2048]{1,0:T(8,128)(2,1)S(1)} collective-permute-done((bf16[64,2048]{1,0:T(8,128)(2,1)S(1)}, bf16[64,2048]{1,0:T(8,128)(2,1)S(1)}, u32[]{:S(2)}, u32[]{:S(2)}) %collective-permute-start.69) | collective-permute-done | bytes 262176 | tf_op jit(solution)/shard_map/ppermute | solution.py:291
  152.4 1.7 collective-permute-start.70
  154.6 1.9 %expert.9 = (bf16[128,2048]{1,0:T(8,128)(2,1)S(1)}, bf16[128,2048]{1,0:T(8,128)(2,1)S(1)}) custom-call(bf16[64,2048]{1,0:T(8,128)(2,1)S(1)} %collective-permute-done.30.xa_ref, bf16[64,2048]{1,0:T(8,128)(2,1)S(1)} %collective-permute-done.37.xb_ref, bf16[64,2048]{1,0:T(8,128)(2,1)S(1)} %collective-permute-done.38.ya_ref, ...), custom_call_target="tpu_custom_call" | custom-call | flops 1610612736 | bytes 6291456 | tf_op jit(solution)/shard_map/expert/pallas_call | solution.py:268
  156.5 1.9 %collective-permute-done.63 = bf16[64,2048]{1,0:T(8,128)(2,1)S(1)} collective-permute-done((bf16[64,2048]{1,0:T(8,128)(2,1)S(1)}, bf16[64,2048]{1,0:T(8,128)(2,1)S(1)}, u32[]{:S(2)}, u32[]{:S(2)}) %collective-permute-start.63) | collective-permute-done | bytes 262176 | tf_op jit(solution)/shard_map/ppermute | solution.py:291
  158.4 2.8 %collective-permute-done.70 = bf16[64,2048]{1,0:T(8,128)(2,1)S(1)} collective-permute-done((bf16[64,2048]{1,0:T(8,128)(2,1)S(1)}, bf16[64,2048]{1,0:T(8,128)(2,1)S(1)}, u32[]{:S(2)}, u32[]{:S(2)}) %collective-permute-start.70) | collective-permute-done | bytes 262176 | tf_op jit(solution)/shard_map/ppermute | solution.py:291
  161.8 1.7 collective-permute-start.71
  163.6 1.9 %expert.8 = (bf16[128,2048]{1,0:T(8,128)(2,1)S(1)}, bf16[128,2048]{1,0:T(8,128)(2,1)S(1)}) custom-call(bf16[64,2048]{1,0:T(8,128)(2,1)S(1)} %get-tuple-element.76.xa_ref, bf16[64,2048]{1,0:T(8,128)(2,1)S(1)} %get-tuple-element.75.xb_ref, bf16[64,2048]{1,0:T(8,128)(2,1)S(1)} %collective-permute-done.21.ya_ref, ...), custom_call_target="tpu_custom_call" | custom-call | flops 1610612736 | bytes 6291456 | tf_op jit(solution)/shard_map/expert/pallas_call | solution.py:268
  165.6 2.3 %collective-permute-done.64 = bf16[64,2048]{1,0:T(8,128)(2,1)S(1)} collective-permute-done((bf16[64,2048]{1,0:T(8,128)(2,1)S(1)}, bf16[64,2048]{1,0:T(8,128)(2,1)S(1)}, u32[]{:S(2)}, u32[]{:S(2)}) %collective-permute-start.64) | collective-permute-done | bytes 262176 | tf_op jit(solution)/shard_map/ppermute | solution.py:291
  167.9 2.8 %collective-permute-done.71 = bf16[64,2048]{1,0:T(8,128)(2,1)S(1)} collective-permute-done((bf16[64,2048]{1,0:T(8,128)(2,1)S(1)}, bf16[64,2048]{1,0:T(8,128)(2,1)S(1)}, u32[]{:S(2)}, u32[]{:S(2)}) %collective-permute-start.71) | collective-permute-done | bytes 262176 | tf_op jit(solution)/shard_map/ppermute | solution.py:291
  171.3 1.7 collective-permute-start.72
  173.2 4.1 %collective-permute-done.65 = bf16[64,2048]{1,0:T(8,128)(2,1)S(1)} collective-permute-done((bf16[64,2048]{1,0:T(8,128)(2,1)S(1)}, bf16[64,2048]{1,0:T(8,128)(2,1)S(1)}, u32[]{:S(2)}, u32[]{:S(2)}) %collective-permute-start.65) | collective-permute-done | bytes 262176 | tf_op jit(solution)/shard_map/ppermute | solution.py:291
  177.3 2.8 %collective-permute-done.72 = bf16[64,2048]{1,0:T(8,128)(2,1)S(1)} collective-permute-done((bf16[64,2048]{1,0:T(8,128)(2,1)S(1)}, bf16[64,2048]{1,0:T(8,128)(2,1)S(1)}, u32[]{:S(2)}, u32[]{:S(2)}) %collective-permute-start.72) | collective-permute-done | bytes 262176 | tf_op jit(solution)/shard_map/ppermute | solution.py:291
  (133 shorter events, 33.0 us)
Async XLA Ops:
  3.1 7.1 %collective-permute-start.6 = (bf16[136,1024]{1,0:T(8,128)(2,1)S(1)}, bf16[136,1024]{1,0:T(8,128)(2,1)S(1)}, u32[]{:S(2)}, u32[]{:S(2)}) collective-permute-start(bf16[136,1024]{1,0:T(8,128)(2,1)S(1)} %get-tuple-element.31.refs_4_), channel_id=1, source_target_pairs={{0,4},{1,3},{4,8},{5,1},{8,12},{9,5},{12,14},{13,9},{14,10},{15,13... | collective-permute-start | bytes 835592 | tf_op jit(solution)/shard_map/ppermute | solution.py:291
  5.8 7.5 %collective-permute-start.7 = (bf16[136,1024]{1,0:T(8,128)(2,1)S(1)}, bf16[136,1024]{1,0:T(8,128)(2,1)S(1)}, u32[]{:S(2)}, u32[]{:S(2)}) collective-permute-start(bf16[136,1024]{1,0:T(8,128)(2,1)S(1)} %collective-permute-done.5.refs_5_), channel_id=1, source_target_pairs={{0,4},{1,3},{4,8},{5,1},{8,12},{9,5},{12,14},{13,9},{14,10},{15,13... | collective-permute-start | bytes 835592 | tf_op jit(solution)/shard_map/ppermute | solution.py:291
  10.2 6.5 %collective-permute-start.8 = (bf16[136,1024]{1,0:T(8,128)(2,1)S(1)}, bf16[136,1024]{1,0:T(8,128)(2,1)S(1)}, u32[]{:S(2)}, u32[]{:S(2)}) collective-permute-start(bf16[136,1024]{1,0:T(8,128)(2,1)S(1)} %collective-permute-done.6.refs_6_), channel_id=1, source_target_pairs={{0,4},{1,3},{4,8},{5,1},{8,12},{9,5},{12,14},{13,9},{14,10},{15,13... | collective-permute-start | bytes 835592 | tf_op jit(solution)/shard_map/ppermute | solution.py:291
  13.2 6.5 %collective-permute-start.9 = (bf16[136,1024]{1,0:T(8,128)(2,1)S(1)}, bf16[136,1024]{1,0:T(8,128)(2,1)S(1)}, u32[]{:S(2)}, u32[]{:S(2)}) collective-permute-start(bf16[136,1024]{1,0:T(8,128)(2,1)S(1)} %collective-permute-done.7.refs_7_), channel_id=1, source_target_pairs={{0,4},{1,3},{4,8},{5,1},{8,12},{9,5},{12,14},{13,9},{14,10},{15,13... | collective-permute-start | bytes 835592 | tf_op jit(solution)/shard_map/ppermute | solution.py:291
  16.8 6.5 %collective-permute-start.10 = (bf16[136,1024]{1,0:T(8,128)(2,1)S(1)}, bf16[136,1024]{1,0:T(8,128)(2,1)S(1)}, u32[]{:S(2)}, u32[]{:S(2)}) collective-permute-start(bf16[136,1024]{1,0:T(8,128)(2,1)S(1)} %collective-permute-done.8.refs_8_), channel_id=1, source_target_pairs={{0,4},{1,3},{4,8},{5,1},{8,12},{9,5},{12,14},{13,9},{14,10},{15,13... | collective-permute-start | bytes 835592 | tf_op jit(solution)/shard_map/ppermute | solution.py:291
  19.8 6.5 %collective-permute-start.11 = (bf16[136,1024]{1,0:T(8,128)(2,1)S(1)}, bf16[136,1024]{1,0:T(8,128)(2,1)S(1)}, u32[]{:S(2)}, u32[]{:S(2)}) collective-permute-start(bf16[136,1024]{1,0:T(8,128)(2,1)S(1)} %collective-permute-done.9.refs_9_), channel_id=1, source_target_pairs={{0,4},{1,3},{4,8},{5,1},{8,12},{9,5},{12,14},{13,9},{14,10},{15,13... | collective-permute-start | bytes 835592 | tf_op jit(solution)/shard_map/ppermute | solution.py:291
  23.3 8.4 %collective-permute-start.12 = (bf16[136,1024]{1,0:T(8,128)(2,1)S(1)}, bf16[136,1024]{1,0:T(8,128)(2,1)S(1)}, u32[]{:S(2)}, u32[]{:S(2)}) collective-permute-start(bf16[136,1024]{1,0:T(8,128)(2,1)S(1)} %collective-permute-done.10.refs_10_), channel_id=1, source_target_pairs={{0,4},{1,3},{4,8},{5,1},{8,12},{9,5},{12,14},{13,9},{14,10},{15,13... | collective-permute-start | bytes 835592 | tf_op jit(solution)/shard_map/ppermute | solution.py:291
  26.3 7.0 %collective-permute-start.13 = (bf16[136,1024]{1,0:T(8,128)(2,1)S(1)}, bf16[136,1024]{1,0:T(8,128)(2,1)S(1)}, u32[]{:S(2)}, u32[]{:S(2)}) collective-permute-start(bf16[136,1024]{1,0:T(8,128)(2,1)S(1)} %collective-permute-done.11.refs_11_), channel_id=1, source_target_pairs={{0,4},{1,3},{4,8},{5,1},{8,12},{9,5},{12,14},{13,9},{14,10},{15,13... | collective-permute-start | bytes 835592 | tf_op jit(solution)/shard_map/ppermute | solution.py:291
  29.7 23.2 %collective-permute-start.1 = (bf16[128,2048]{1,0:T(8,128)(2,1)S(1)}, bf16[128,2048]{1,0:T(8,128)(2,1)S(1)}, u32[]{:S(2)}, u32[]{:S(2)}) collective-permute-start(bf16[128,2048]{1,0:T(8,128)(2,1)S(1)} %get-tuple-element.58), channel_id=1, source_target_pairs={{0,16},{16,0},{1,17},{17,1},{2,18},{18,2},{3,19},{19,3},{4,20},{20... | collective-permute-start | bytes 1572872 | tf_op jit(solution)/shard_map/ppermute | solution.py:298
  31.2 21.7 %collective-permute-start.2 = (bf16[128,2048]{1,0:T(8,128)(2,1)S(1)}, bf16[128,2048]{1,0:T(8,128)(2,1)S(1)}, u32[]{:S(2)}, u32[]{:S(2)}) collective-permute-start(bf16[128,2048]{1,0:T(8,128)(2,1)S(1)} %get-tuple-element.57), channel_id=1, source_target_pairs={{0,16},{16,0},{1,17},{17,1},{2,18},{18,2},{3,19},{19,3},{4,20},{20... | collective-permute-start | bytes 1572872 | tf_op jit(solution)/shard_map/ppermute | solution.py:299
  31.8 6.5 %collective-permute-start.14 = (bf16[136,1024]{1,0:T(8,128)(2,1)S(1)}, bf16[136,1024]{1,0:T(8,128)(2,1)S(1)}, u32[]{:S(2)}, u32[]{:S(2)}) collective-permute-start(bf16[136,1024]{1,0:T(8,128)(2,1)S(1)} %collective-permute-done.12.refs_12_), channel_id=1, source_target_pairs={{0,4},{1,3},{4,8},{5,1},{8,12},{9,5},{12,14},{13,9},{14,10},{15,13... | collective-permute-start | bytes 835592 | tf_op jit(solution)/shard_map/ppermute | solution.py:291
  33.4 8.0 %collective-permute-start.15 = (bf16[136,1024]{1,0:T(8,128)(2,1)S(1)}, bf16[136,1024]{1,0:T(8,128)(2,1)S(1)}, u32[]{:S(2)}, u32[]{:S(2)}) collective-permute-start(bf16[136,1024]{1,0:T(8,128)(2,1)S(1)} %collective-permute-done.13.refs_13_), channel_id=1, source_target_pairs={{0,4},{1,3},{4,8},{5,1},{8,12},{9,5},{12,14},{13,9},{14,10},{15,13... | collective-permute-start | bytes 835592 | tf_op jit(solution)/shard_map/ppermute | solution.py:291
  38.3 23.7 %collective-permute-start.16 = (bf16[136,1024]{1,0:T(8,128)(2,1)S(1)}, bf16[136,1024]{1,0:T(8,128)(2,1)S(1)}, u32[]{:S(2)}, u32[]{:S(2)}) collective-permute-start(bf16[136,1024]{1,0:T(8,128)(2,1)S(1)} %collective-permute-done.14.refs_6_), channel_id=1, source_target_pairs={{0,4},{1,3},{4,8},{5,1},{8,12},{9,5},{12,14},{13,9},{14,10},{15,13... | collective-permute-start | bytes 835592 | tf_op jit(solution)/shard_map/ppermute | solution.py:291
  41.3 21.1 %collective-permute-start.17 = (bf16[136,1024]{1,0:T(8,128)(2,1)S(1)}, bf16[136,1024]{1,0:T(8,128)(2,1)S(1)}, u32[]{:S(2)}, u32[]{:S(2)}) collective-permute-start(bf16[136,1024]{1,0:T(8,128)(2,1)S(1)} %collective-permute-done.15.refs_7_), channel_id=1, source_target_pairs={{0,4},{1,3},{4,8},{5,1},{8,12},{9,5},{12,14},{13,9},{14,10},{15,13... | collective-permute-start | bytes 835592 | tf_op jit(solution)/shard_map/ppermute | solution.py:291
  43.5 9.4 %collective-permute-start = (s32[1]{0:T(128)}, s32[1]{0:T(128)}, u32[]{:S(2)}, u32[]{:S(2)}) collective-permute-start(s32[1]{0:T(128)} %bitcast.2), channel_id=1, source_target_pairs={{0,16},{16,0},{1,17},{17,1},{2,18},{18,2},{3,19},{19,3},{4,20},{20... | collective-permute-start | bytes 20 | tf_op jit(solution)/shard_map/ppermute | solution.py:297
  57.8 6.3 %collective-permute-start.3 = (bf16[8,128,128]{2,1,0:T(8,128)(2,1)S(1)}, bf16[8,128,128]{2,1,0:T(8,128)(2,1)S(1)}, u32[]{:S(2)}, u32[]{:S(2)}) collective-permute-start(bf16[8,128,128]{2,1,0:T(8,128)(2,1)S(1)} %attend.2.refs_0_), channel_id=1, source_target_pairs={{0,1},{1,0},{2,3},{3,2},{4,5},{5,4},{6,7},{7,6},{8,9},{9,8},{10,11... | collective-permute-start | bytes 786440 | tf_op jit(solution)/shard_map/ppermute | solution.py:294
  62.0 6.5 %collective-permute-start.18 = (bf16[136,1024]{1,0:T(8,128)(2,1)S(1)}, bf16[136,1024]{1,0:T(8,128)(2,1)S(1)}, u32[]{:S(2)}, u32[]{:S(2)}) collective-permute-start(bf16[136,1024]{1,0:T(8,128)(2,1)S(1)} %collective-permute-done.16.refs_8_), channel_id=1, source_target_pairs={{0,4},{1,3},{4,8},{5,1},{8,12},{9,5},{12,14},{13,9},{14,10},{15,13... | collective-permute-start | bytes 835592 | tf_op jit(solution)/shard_map/ppermute | solution.py:291
  62.4 9.2 %collective-permute-start.19 = (bf16[136,1024]{1,0:T(8,128)(2,1)S(1)}, bf16[136,1024]{1,0:T(8,128)(2,1)S(1)}, u32[]{:S(2)}, u32[]{:S(2)}) collective-permute-start(bf16[136,1024]{1,0:T(8,128)(2,1)S(1)} %collective-permute-done.17.refs_9_), channel_id=1, source_target_pairs={{0,4},{1,3},{4,8},{5,1},{8,12},{9,5},{12,14},{13,9},{14,10},{15,13... | collective-permute-start | bytes 835592 | tf_op jit(solution)/shard_map/ppermute | solution.py:291
  76.1 6.4 %collective-permute-start.24 = (bf16[64,2048]{1,0:T(8,128)(2,1)S(1)}, bf16[64,2048]{1,0:T(8,128)(2,1)S(1)}, u32[]{:S(2)}, u32[]{:S(2)}) collective-permute-start(bf16[64,2048]{1,0:T(8,128)(2,1)S(1)} %get-tuple-element.76.xa_ref), channel_id=1, source_target_pairs={{0,4},{1,3},{4,8},{5,1},{8,12},{9,5},{12,14},{13,9},{14,10},{15,13... | collective-permute-start | bytes 786440 | tf_op jit(solution)/shard_map/ppermute | solution.py:291
  76.5 8.8 %collective-permute-start.31 = (bf16[64,2048]{1,0:T(8,128)(2,1)S(1)}, bf16[64,2048]{1,0:T(8,128)(2,1)S(1)}, u32[]{:S(2)}, u32[]{:S(2)}) collective-permute-start(bf16[64,2048]{1,0:T(8,128)(2,1)S(1)} %get-tuple-element.75.xb_ref), channel_id=1, source_target_pairs={{0,4},{1,3},{4,8},{5,1},{8,12},{9,5},{12,14},{13,9},{14,10},{15,13... | collective-permute-start | bytes 786440 | tf_op jit(solution)/shard_map/ppermute | solution.py:291
  82.6 4.9 %collective-permute-start.56 = (bf16[64,2048]{1,0:T(8,128)(2,1)S(1)}, bf16[64,2048]{1,0:T(8,128)(2,1)S(1)}, u32[]{:S(2)}, u32[]{:S(2)}) collective-permute-start(bf16[64,2048]{1,0:T(8,128)(2,1)S(1)} %collective-permute-done.24.xa_ref), channel_id=1, source_target_pairs={{0,1},{1,0},{2,3},{3,2},{4,5},{5,4},{6,7},{7,6},{8,9},{9,8},{10,11... | collective-permute-start | bytes 786440 | tf_op jit(solution)/shard_map/ppermute | solution.py:294
  85.4 6.4 %collective-permute-start.25 = (bf16[64,2048]{1,0:T(8,128)(2,1)S(1)}, bf16[64,2048]{1,0:T(8,128)(2,1)S(1)}, u32[]{:S(2)}, u32[]{:S(2)}) collective-permute-start(bf16[64,2048]{1,0:T(8,128)(2,1)S(1)} %collective-permute-done.24.xa_ref), channel_id=1, source_target_pairs={{0,4},{1,3},{4,8},{5,1},{8,12},{9,5},{12,14},{13,9},{14,10},{15,13... | collective-permute-start | bytes 786440 | tf_op jit(solution)/shard_map/ppermute | solution.py:291
  85.7 8.8 %collective-permute-start.32 = (bf16[64,2048]{1,0:T(8,128)(2,1)S(1)}, bf16[64,2048]{1,0:T(8,128)(2,1)S(1)}, u32[]{:S(2)}, u32[]{:S(2)}) collective-permute-start(bf16[64,2048]{1,0:T(8,128)(2,1)S(1)} %collective-permute-done.31.xb_ref), channel_id=1, source_target_pairs={{0,4},{1,3},{4,8},{5,1},{8,12},{9,5},{12,14},{13,9},{14,10},{15,13... | collective-permute-start | bytes 786440 | tf_op jit(solution)/shard_map/ppermute | solution.py:291
  89.4 14.4 %collective-permute-start.58 = (bf16[128,2048]{1,0:T(8,128)(2,1)S(1)}, bf16[128,2048]{1,0:T(8,128)(2,1)S(1)}, u32[]{:S(2)}, u32[]{:S(2)}) collective-permute-start(bf16[128,2048]{1,0:T(8,128)(2,1)S(1)} %get-tuple-element.56), channel_id=1, source_target_pairs={{0,1},{1,0},{2,3},{3,2},{4,5},{5,4},{6,7},{7,6},{8,9},{9,8},{10,11... | collective-permute-start | bytes 1572872 | tf_op jit(solution)/shard_map/ppermute | solution.py:294
  91.8 4.9 %collective-permute-start.53 = (bf16[64,2048]{1,0:T(8,128)(2,1)S(1)}, bf16[64,2048]{1,0:T(8,128)(2,1)S(1)}, u32[]{:S(2)}, u32[]{:S(2)}) collective-permute-start(bf16[64,2048]{1,0:T(8,128)(2,1)S(1)} %collective-permute-done.25.xa_ref), channel_id=1, source_target_pairs={{0,1},{1,0},{2,3},{3,2},{4,5},{5,4},{6,7},{7,6},{8,9},{9,8},{10,11... | collective-permute-start | bytes 786440 | tf_op jit(solution)/shard_map/ppermute | solution.py:294
  94.6 6.4 %collective-permute-start.26 = (bf16[64,2048]{1,0:T(8,128)(2,1)S(1)}, bf16[64,2048]{1,0:T(8,128)(2,1)S(1)}, u32[]{:S(2)}, u32[]{:S(2)}) collective-permute-start(bf16[64,2048]{1,0:T(8,128)(2,1)S(1)} %collective-permute-done.25.xa_ref), channel_id=1, source_target_pairs={{0,4},{1,3},{4,8},{5,1},{8,12},{9,5},{12,14},{13,9},{14,10},{15,13... | collective-permute-start | bytes 786440 | tf_op jit(solution)/shard_map/ppermute | solution.py:291
  94.9 8.8 %collective-permute-start.33 = (bf16[64,2048]{1,0:T(8,128)(2,1)S(1)}, bf16[64,2048]{1,0:T(8,128)(2,1)S(1)}, u32[]{:S(2)}, u32[]{:S(2)}) collective-permute-start(bf16[64,2048]{1,0:T(8,128)(2,1)S(1)} %collective-permute-done.32.xb_ref), channel_id=1, source_target_pairs={{0,4},{1,3},{4,8},{5,1},{8,12},{9,5},{12,14},{13,9},{14,10},{15,13... | collective-permute-start | bytes 786440 | tf_op jit(solution)/shard_map/ppermute | solution.py:291
  98.5 14.7 %collective-permute-start.55 = (bf16[128,2048]{1,0:T(8,128)(2,1)S(1)}, bf16[128,2048]{1,0:T(8,128)(2,1)S(1)}, u32[]{:S(2)}, u32[]{:S(2)}) collective-permute-start(bf16[128,2048]{1,0:T(8,128)(2,1)S(1)} %get-tuple-element.54), channel_id=1, source_target_pairs={{0,1},{1,0},{2,3},{3,2},{4,5},{5,4},{6,7},{7,6},{8,9},{9,8},{10,11... | collective-permute-start | bytes 1572872 | tf_op jit(solution)/shard_map/ppermute | solution.py:294
  100.9 8.6 %collective-permute-start.27 = (bf16[64,2048]{1,0:T(8,128)(2,1)S(1)}, bf16[64,2048]{1,0:T(8,128)(2,1)S(1)}, u32[]{:S(2)}, u32[]{:S(2)}) collective-permute-start(bf16[64,2048]{1,0:T(8,128)(2,1)S(1)} %collective-permute-done.26.xa_ref), channel_id=1, source_target_pairs={{0,4},{1,3},{4,8},{5,1},{8,12},{9,5},{12,14},{13,9},{14,10},{15,13... | collective-permute-start | bytes 786440 | tf_op jit(solution)/shard_map/ppermute | solution.py:291
  103.8 6.6 %collective-permute-start.34 = (bf16[64,2048]{1,0:T(8,128)(2,1)S(1)}, bf16[64,2048]{1,0:T(8,128)(2,1)S(1)}, u32[]{:S(2)}, u32[]{:S(2)}) collective-permute-start(bf16[64,2048]{1,0:T(8,128)(2,1)S(1)} %collective-permute-done.33.xb_ref), channel_id=1, source_target_pairs={{0,4},{1,3},{4,8},{5,1},{8,12},{9,5},{12,14},{13,9},{14,10},{15,13... | collective-permute-start | bytes 786440 | tf_op jit(solution)/shard_map/ppermute | solution.py:291
  104.2 8.7 %collective-permute-start.59 = (bf16[64,2048]{1,0:T(8,128)(2,1)S(1)}, bf16[64,2048]{1,0:T(8,128)(2,1)S(1)}, u32[]{:S(2)}, u32[]{:S(2)}) collective-permute-start(bf16[64,2048]{1,0:T(8,128)(2,1)S(1)} %get-tuple-element.73), channel_id=1, source_target_pairs={{0,4},{1,3},{4,8},{5,1},{8,12},{9,5},{12,14},{13,9},{14,10},{15,13... | collective-permute-start | bytes 786440 | tf_op jit(solution)/shard_map/ppermute | solution.py:291
  106.0 9.7 %collective-permute-start.66 = (bf16[64,2048]{1,0:T(8,128)(2,1)S(1)}, bf16[64,2048]{1,0:T(8,128)(2,1)S(1)}, u32[]{:S(2)}, u32[]{:S(2)}) collective-permute-start(bf16[64,2048]{1,0:T(8,128)(2,1)S(1)} %get-tuple-element.74), channel_id=1, source_target_pairs={{0,4},{1,3},{4,8},{5,1},{8,12},{9,5},{12,14},{13,9},{14,10},{15,13... | collective-permute-start | bytes 786440 | tf_op jit(solution)/shard_map/ppermute | solution.py:291
  109.5 15.8 %collective-permute-start.52 = (bf16[128,2048]{1,0:T(8,128)(2,1)S(1)}, bf16[128,2048]{1,0:T(8,128)(2,1)S(1)}, u32[]{:S(2)}, u32[]{:S(2)}) collective-permute-start(bf16[128,2048]{1,0:T(8,128)(2,1)S(1)} %get-tuple-element.52), channel_id=1, source_target_pairs={{0,1},{1,0},{2,3},{3,2},{4,5},{5,4},{6,7},{7,6},{8,9},{9,8},{10,11... | collective-permute-start | bytes 1572872 | tf_op jit(solution)/shard_map/ppermute | solution.py:294
  110.3 6.0 %collective-permute-start.47 = (bf16[64,2048]{1,0:T(8,128)(2,1)S(1)}, bf16[64,2048]{1,0:T(8,128)(2,1)S(1)}, u32[]{:S(2)}, u32[]{:S(2)}) collective-permute-start(bf16[64,2048]{1,0:T(8,128)(2,1)S(1)} %collective-permute-done.27.xa_ref), channel_id=1, source_target_pairs={{0,1},{1,0},{2,3},{3,2},{4,5},{5,4},{6,7},{7,6},{8,9},{9,8},{10,11... | collective-permute-start | bytes 786440 | tf_op jit(solution)/shard_map/ppermute | solution.py:294
  112.9 8.7 %collective-permute-start.28 = (bf16[64,2048]{1,0:T(8,128)(2,1)S(1)}, bf16[64,2048]{1,0:T(8,128)(2,1)S(1)}, u32[]{:S(2)}, u32[]{:S(2)}) collective-permute-start(bf16[64,2048]{1,0:T(8,128)(2,1)S(1)} %collective-permute-done.27.xa_ref), channel_id=1, source_target_pairs={{0,4},{1,3},{4,8},{5,1},{8,12},{9,5},{12,14},{13,9},{14,10},{15,13... | collective-permute-start | bytes 786440 | tf_op jit(solution)/shard_map/ppermute | solution.py:291
  115.7 6.4 %collective-permute-start.35 = (bf16[64,2048]{1,0:T(8,128)(2,1)S(1)}, bf16[64,2048]{1,0:T(8,128)(2,1)S(1)}, u32[]{:S(2)}, u32[]{:S(2)}) collective-permute-start(bf16[64,2048]{1,0:T(8,128)(2,1)S(1)} %collective-permute-done.34.xb_ref), channel_id=1, source_target_pairs={{0,4},{1,3},{4,8},{5,1},{8,12},{9,5},{12,14},{13,9},{14,10},{15,13... | collective-permute-start | bytes 786440 | tf_op jit(solution)/shard_map/ppermute | solution.py:291
  116.3 8.6 %collective-permute-start.60 = (bf16[64,2048]{1,0:T(8,128)(2,1)S(1)}, bf16[64,2048]{1,0:T(8,128)(2,1)S(1)}, u32[]{:S(2)}, u32[]{:S(2)}) collective-permute-start(bf16[64,2048]{1,0:T(8,128)(2,1)S(1)} %get-tuple-element.71), channel_id=1, source_target_pairs={{0,4},{1,3},{4,8},{5,1},{8,12},{9,5},{12,14},{13,9},{14,10},{15,13... | collective-permute-start | bytes 786440 | tf_op jit(solution)/shard_map/ppermute | solution.py:291
  118.1 9.6 %collective-permute-start.67 = (bf16[64,2048]{1,0:T(8,128)(2,1)S(1)}, bf16[64,2048]{1,0:T(8,128)(2,1)S(1)}, u32[]{:S(2)}, u32[]{:S(2)}) collective-permute-start(bf16[64,2048]{1,0:T(8,128)(2,1)S(1)} %get-tuple-element.72), channel_id=1, source_target_pairs={{0,4},{1,3},{4,8},{5,1},{8,12},{9,5},{12,14},{13,9},{14,10},{15,13... | collective-permute-start | bytes 786440 | tf_op jit(solution)/shard_map/ppermute | solution.py:291
  121.6 15.7 %collective-permute-start.49 = (bf16[128,2048]{1,0:T(8,128)(2,1)S(1)}, bf16[128,2048]{1,0:T(8,128)(2,1)S(1)}, u32[]{:S(2)}, u32[]{:S(2)}) collective-permute-start(bf16[128,2048]{1,0:T(8,128)(2,1)S(1)} %get-tuple-element.50), channel_id=1, source_target_pairs={{0,1},{1,0},{2,3},{3,2},{4,5},{5,4},{6,7},{7,6},{8,9},{9,8},{10,11... | collective-permute-start | bytes 1572872 | tf_op jit(solution)/shard_map/ppermute | solution.py:294
  122.1 6.2 %collective-permute-start.44 = (bf16[64,2048]{1,0:T(8,128)(2,1)S(1)}, bf16[64,2048]{1,0:T(8,128)(2,1)S(1)}, u32[]{:S(2)}, u32[]{:S(2)}) collective-permute-start(bf16[64,2048]{1,0:T(8,128)(2,1)S(1)} %collective-permute-done.28.xa_ref), channel_id=1, source_target_pairs={{0,1},{1,0},{2,3},{3,2},{4,5},{5,4},{6,7},{7,6},{8,9},{9,8},{10,11... | collective-permute-start | bytes 786440 | tf_op jit(solution)/shard_map/ppermute | solution.py:294
  124.9 8.7 %collective-permute-start.29 = (bf16[64,2048]{1,0:T(8,128)(2,1)S(1)}, bf16[64,2048]{1,0:T(8,128)(2,1)S(1)}, u32[]{:S(2)}, u32[]{:S(2)}) collective-permute-start(bf16[64,2048]{1,0:T(8,128)(2,1)S(1)} %collective-permute-done.28.xa_ref), channel_id=1, source_target_pairs={{0,4},{1,3},{4,8},{5,1},{8,12},{9,5},{12,14},{13,9},{14,10},{15,13... | collective-permute-start | bytes 786440 | tf_op jit(solution)/shard_map/ppermute | solution.py:291
  125.3 4.9 %collective-permute-start.45 = (bf16[64,2048]{1,0:T(8,128)(2,1)S(1)}, bf16[64,2048]{1,0:T(8,128)(2,1)S(1)}, u32[]{:S(2)}, u32[]{:S(2)}) collective-permute-start(bf16[64,2048]{1,0:T(8,128)(2,1)S(1)} %collective-permute-done.35.xb_ref), channel_id=1, source_target_pairs={{0,1},{1,0},{2,3},{3,2},{4,5},{5,4},{6,7},{7,6},{8,9},{9,8},{10,11... | collective-permute-start | bytes 786440 | tf_op jit(solution)/shard_map/ppermute | solution.py:294
  127.7 6.4 %collective-permute-start.36 = (bf16[64,2048]{1,0:T(8,128)(2,1)S(1)}, bf16[64,2048]{1,0:T(8,128)(2,1)S(1)}, u32[]{:S(2)}, u32[]{:S(2)}) collective-permute-start(bf16[64,2048]{1,0:T(8,128)(2,1)S(1)} %collective-permute-done.35.xb_ref), channel_id=1, source_target_pairs={{0,4},{1,3},{4,8},{5,1},{8,12},{9,5},{12,14},{13,9},{14,10},{15,13... | collective-permute-start | bytes 786440 | tf_op jit(solution)/shard_map/ppermute | solution.py:291
  128.3 8.6 %collective-permute-start.61 = (bf16[64,2048]{1,0:T(8,128)(2,1)S(1)}, bf16[64,2048]{1,0:T(8,128)(2,1)S(1)}, u32[]{:S(2)}, u32[]{:S(2)}) collective-permute-start(bf16[64,2048]{1,0:T(8,128)(2,1)S(1)} %get-tuple-element.69), channel_id=1, source_target_pairs={{0,4},{1,3},{4,8},{5,1},{8,12},{9,5},{12,14},{13,9},{14,10},{15,13... | collective-permute-start | bytes 786440 | tf_op jit(solution)/shard_map/ppermute | solution.py:291
  130.1 9.6 %collective-permute-start.68 = (bf16[64,2048]{1,0:T(8,128)(2,1)S(1)}, bf16[64,2048]{1,0:T(8,128)(2,1)S(1)}, u32[]{:S(2)}, u32[]{:S(2)}) collective-permute-start(bf16[64,2048]{1,0:T(8,128)(2,1)S(1)} %get-tuple-element.70), channel_id=1, source_target_pairs={{0,4},{1,3},{4,8},{5,1},{8,12},{9,5},{12,14},{13,9},{14,10},{15,13... | collective-permute-start | bytes 786440 | tf_op jit(solution)/shard_map/ppermute | solution.py:291
  133.6 15.3 %collective-permute-start.46 = (bf16[128,2048]{1,0:T(8,128)(2,1)S(1)}, bf16[128,2048]{1,0:T(8,128)(2,1)S(1)}, u32[]{:S(2)}, u32[]{:S(2)}) collective-permute-start(bf16[128,2048]{1,0:T(8,128)(2,1)S(1)} %get-tuple-element.48), channel_id=1, source_target_pairs={{0,1},{1,0},{2,3},{3,2},{4,5},{5,4},{6,7},{7,6},{8,9},{9,8},{10,11... | collective-permute-start | bytes 1572872 | tf_op jit(solution)/shard_map/ppermute | solution.py:294
  134.1 6.2 %collective-permute-start.41 = (bf16[64,2048]{1,0:T(8,128)(2,1)S(1)}, bf16[64,2048]{1,0:T(8,128)(2,1)S(1)}, u32[]{:S(2)}, u32[]{:S(2)}) collective-permute-start(bf16[64,2048]{1,0:T(8,128)(2,1)S(1)} %collective-permute-done.29.xa_ref), channel_id=1, source_target_pairs={{0,1},{1,0},{2,3},{3,2},{4,5},{5,4},{6,7},{7,6},{8,9},{9,8},{10,11... | collective-permute-start | bytes 786440 | tf_op jit(solution)/shard_map/ppermute | solution.py:294
  136.9 8.7 %collective-permute-start.30 = (bf16[64,2048]{1,0:T(8,128)(2,1)S(1)}, bf16[64,2048]{1,0:T(8,128)(2,1)S(1)}, u32[]{:S(2)}, u32[]{:S(2)}) collective-permute-start(bf16[64,2048]{1,0:T(8,128)(2,1)S(1)} %collective-permute-done.29.xa_ref), channel_id=1, source_target_pairs={{0,4},{1,3},{4,8},{5,1},{8,12},{9,5},{12,14},{13,9},{14,10},{15,13... | collective-permute-start | bytes 786440 | tf_op jit(solution)/shard_map/ppermute | solution.py:291
  139.7 6.4 %collective-permute-start.37 = (bf16[64,2048]{1,0:T(8,128)(2,1)S(1)}, bf16[64,2048]{1,0:T(8,128)(2,1)S(1)}, u32[]{:S(2)}, u32[]{:S(2)}) collective-permute-start(bf16[64,2048]{1,0:T(8,128)(2,1)S(1)} %collective-permute-done.36.xb_ref), channel_id=1, source_target_pairs={{0,4},{1,3},{4,8},{5,1},{8,12},{9,5},{12,14},{13,9},{14,10},{15,13... | collective-permute-start | bytes 786440 | tf_op jit(solution)/shard_map/ppermute | solution.py:291
  140.3 8.6 %collective-permute-start.62 = (bf16[64,2048]{1,0:T(8,128)(2,1)S(1)}, bf16[64,2048]{1,0:T(8,128)(2,1)S(1)}, u32[]{:S(2)}, u32[]{:S(2)}) collective-permute-start(bf16[64,2048]{1,0:T(8,128)(2,1)S(1)} %get-tuple-element.67), channel_id=1, source_target_pairs={{0,4},{1,3},{4,8},{5,1},{8,12},{9,5},{12,14},{13,9},{14,10},{15,13... | collective-permute-start | bytes 786440 | tf_op jit(solution)/shard_map/ppermute | solution.py:291
  142.1 9.6 %collective-permute-start.69 = (bf16[64,2048]{1,0:T(8,128)(2,1)S(1)}, bf16[64,2048]{1,0:T(8,128)(2,1)S(1)}, u32[]{:S(2)}, u32[]{:S(2)}) collective-permute-start(bf16[64,2048]{1,0:T(8,128)(2,1)S(1)} %get-tuple-element.68), channel_id=1, source_target_pairs={{0,4},{1,3},{4,8},{5,1},{8,12},{9,5},{12,14},{13,9},{14,10},{15,13... | collective-permute-start | bytes 786440 | tf_op jit(solution)/shard_map/ppermute | solution.py:291
  145.6 12.8 %collective-permute-start.43 = (bf16[128,2048]{1,0:T(8,128)(2,1)S(1)}, bf16[128,2048]{1,0:T(8,128)(2,1)S(1)}, u32[]{:S(2)}, u32[]{:S(2)}) collective-permute-start(bf16[128,2048]{1,0:T(8,128)(2,1)S(1)} %get-tuple-element.46), channel_id=1, source_target_pairs={{0,1},{1,0},{2,3},{3,2},{4,5},{5,4},{6,7},{7,6},{8,9},{9,8},{10,11... | collective-permute-start | bytes 1572872 | tf_op jit(solution)/shard_map/ppermute | solution.py:294
  146.1 8.0 %collective-permute-start.38 = (bf16[64,2048]{1,0:T(8,128)(2,1)S(1)}, bf16[64,2048]{1,0:T(8,128)(2,1)S(1)}, u32[]{:S(2)}, u32[]{:S(2)}) collective-permute-start(bf16[64,2048]{1,0:T(8,128)(2,1)S(1)} %collective-permute-done.30.xa_ref), channel_id=1, source_target_pairs={{0,1},{1,0},{2,3},{3,2},{4,5},{5,4},{6,7},{7,6},{8,9},{9,8},{10,11... | collective-permute-start | bytes 786440 | tf_op jit(solution)/shard_map/ppermute | solution.py:294
  148.9 5.2 %collective-permute-start.39 = (bf16[64,2048]{1,0:T(8,128)(2,1)S(1)}, bf16[64,2048]{1,0:T(8,128)(2,1)S(1)}, u32[]{:S(2)}, u32[]{:S(2)}) collective-permute-start(bf16[64,2048]{1,0:T(8,128)(2,1)S(1)} %collective-permute-done.37.xb_ref), channel_id=1, source_target_pairs={{0,1},{1,0},{2,3},{3,2},{4,5},{5,4},{6,7},{7,6},{8,9},{9,8},{10,11... | collective-permute-start | bytes 786440 | tf_op jit(solution)/shard_map/ppermute | solution.py:294
  152.0 6.4 %collective-permute-start.63 = (bf16[64,2048]{1,0:T(8,128)(2,1)S(1)}, bf16[64,2048]{1,0:T(8,128)(2,1)S(1)}, u32[]{:S(2)}, u32[]{:S(2)}) collective-permute-start(bf16[64,2048]{1,0:T(8,128)(2,1)S(1)} %get-tuple-element.65), channel_id=1, source_target_pairs={{0,4},{1,3},{4,8},{5,1},{8,12},{9,5},{12,14},{13,9},{14,10},{15,13... | collective-permute-start | bytes 786440 | tf_op jit(solution)/shard_map/ppermute | solution.py:291
  152.4 8.8 %collective-permute-start.70 = (bf16[64,2048]{1,0:T(8,128)(2,1)S(1)}, bf16[64,2048]{1,0:T(8,128)(2,1)S(1)}, u32[]{:S(2)}, u32[]{:S(2)}) collective-permute-start(bf16[64,2048]{1,0:T(8,128)(2,1)S(1)} %get-tuple-element.66), channel_id=1, source_target_pairs={{0,4},{1,3},{4,8},{5,1},{8,12},{9,5},{12,14},{13,9},{14,10},{15,13... | collective-permute-start | bytes 786440 | tf_op jit(solution)/shard_map/ppermute | solution.py:291
  154.1 9.5 %collective-permute-start.21 = (bf16[64,2048]{1,0:T(8,128)(2,1)S(1)}, bf16[64,2048]{1,0:T(8,128)(2,1)S(1)}, u32[]{:S(2)}, u32[]{:S(2)}) collective-permute-start(bf16[64,2048]{1,0:T(8,128)(2,1)S(1)} %get-tuple-element.76.xa_ref), channel_id=1, source_target_pairs={{0,1},{1,0},{2,3},{3,2},{4,5},{5,4},{6,7},{7,6},{8,9},{9,8},{10,11... | collective-permute-start | bytes 786440 | tf_op jit(solution)/shard_map/ppermute | solution.py:294
  154.1 9.5 %collective-permute-start.22 = (bf16[64,2048]{1,0:T(8,128)(2,1)S(1)}, bf16[64,2048]{1,0:T(8,128)(2,1)S(1)}, u32[]{:S(2)}, u32[]{:S(2)}) collective-permute-start(bf16[64,2048]{1,0:T(8,128)(2,1)S(1)} %get-tuple-element.75.xb_ref), channel_id=1, source_target_pairs={{0,1},{1,0},{2,3},{3,2},{4,5},{5,4},{6,7},{7,6},{8,9},{9,8},{10,11... | collective-permute-start | bytes 786440 | tf_op jit(solution)/shard_map/ppermute | solution.py:294
  158.4 9.5 %collective-permute-start.40 = (bf16[128,2048]{1,0:T(8,128)(2,1)S(1)}, bf16[128,2048]{1,0:T(8,128)(2,1)S(1)}, u32[]{:S(2)}, u32[]{:S(2)}) collective-permute-start(bf16[128,2048]{1,0:T(8,128)(2,1)S(1)} %get-tuple-element.44), channel_id=1, source_target_pairs={{0,1},{1,0},{2,3},{3,2},{4,5},{5,4},{6,7},{7,6},{8,9},{9,8},{10,11... | collective-permute-start | bytes 1572872 | tf_op jit(solution)/shard_map/ppermute | solution.py:294
  161.4 6.4 %collective-permute-start.64 = (bf16[64,2048]{1,0:T(8,128)(2,1)S(1)}, bf16[64,2048]{1,0:T(8,128)(2,1)S(1)}, u32[]{:S(2)}, u32[]{:S(2)}) collective-permute-start(bf16[64,2048]{1,0:T(8,128)(2,1)S(1)} %get-tuple-element.63), channel_id=1, source_target_pairs={{0,4},{1,3},{4,8},{5,1},{8,12},{9,5},{12,14},{13,9},{14,10},{15,13... | collective-permute-start | bytes 786440 | tf_op jit(solution)/shard_map/ppermute | solution.py:291
  161.8 8.8 %collective-permute-start.71 = (bf16[64,2048]{1,0:T(8,128)(2,1)S(1)}, bf16[64,2048]{1,0:T(8,128)(2,1)S(1)}, u32[]{:S(2)}, u32[]{:S(2)}) collective-permute-start(bf16[64,2048]{1,0:T(8,128)(2,1)S(1)} %get-tuple-element.64), channel_id=1, source_target_pairs={{0,4},{1,3},{4,8},{5,1},{8,12},{9,5},{12,14},{13,9},{14,10},{15,13... | collective-permute-start | bytes 786440 | tf_op jit(solution)/shard_map/ppermute | solution.py:291
  165.5 7.6 %collective-permute-start.23 = (bf16[128,2048]{1,0:T(8,128)(2,1)S(1)}, bf16[128,2048]{1,0:T(8,128)(2,1)S(1)}, u32[]{:S(2)}, u32[]{:S(2)}) collective-permute-start(bf16[128,2048]{1,0:T(8,128)(2,1)S(1)} %get-tuple-element.41), channel_id=1, source_target_pairs={{0,1},{1,0},{2,3},{3,2},{4,5},{5,4},{6,7},{7,6},{8,9},{9,8},{10,11... | collective-permute-start | bytes 1572872 | tf_op jit(solution)/shard_map/ppermute | solution.py:294
  170.9 6.4 %collective-permute-start.65 = (bf16[64,2048]{1,0:T(8,128)(2,1)S(1)}, bf16[64,2048]{1,0:T(8,128)(2,1)S(1)}, u32[]{:S(2)}, u32[]{:S(2)}) collective-permute-start(bf16[64,2048]{1,0:T(8,128)(2,1)S(1)} %get-tuple-element.61), channel_id=1, source_target_pairs={{0,4},{1,3},{4,8},{5,1},{8,12},{9,5},{12,14},{13,9},{14,10},{15,13... | collective-permute-start | bytes 786440 | tf_op jit(solution)/shard_map/ppermute | solution.py:291
  171.3 8.8 %collective-permute-start.72 = (bf16[64,2048]{1,0:T(8,128)(2,1)S(1)}, bf16[64,2048]{1,0:T(8,128)(2,1)S(1)}, u32[]{:S(2)}, u32[]{:S(2)}) collective-permute-start(bf16[64,2048]{1,0:T(8,128)(2,1)S(1)} %get-tuple-element.62), channel_id=1, source_target_pairs={{0,4},{1,3},{4,8},{5,1},{8,12},{9,5},{12,14},{13,9},{14,10},{15,13... | collective-permute-start | bytes 786440 | tf_op jit(solution)/shard_map/ppermute | solution.py:291
  (21 other events, 233.4 us)

commit v3 on v2

--- a/solution.py
+++ b/solution.py
@@ -55,9 +55,10 @@
     return route
 
 
-def attend_body(first, count, len_ref, far_len_ref, q_ref, kv_ref, cache_ref, fk_ref, fv_ref, out_ref):
+def attend_body(first, count, len_ref, far_len_ref, q_ref, kv_ref, cache_ref, far_ref, held_ref, out_ref, pass_ref):
+    del held_ref, pass_ref
     rows = q_ref.shape[0]
-    seg = fk_ref.shape[0]
+    seg = far_ref.shape[1]
     near_len = len_ref[0, 0]
     far_len = far_len_ref[0]
     pos = lax.broadcasted_iota(jnp.int32, (rows, seg), 1)
@@ -67,10 +68,11 @@
     dims = (((1,), (1,)), ((), ()))
     for h in range(count):
         cols = slice((first + h) * HD, (first + h + 1) * HD)
+        far_cols = slice(h * HD, (h + 1) * HD)
         q = q_ref[:, cols]
         s0 = lax.dot_general(q, kv_ref[0, :, cols], dims, preferred_element_type=F32) * scale
         s1 = lax.dot_general(q, cache_ref[0, 0, 0, :, cols], dims, preferred_element_type=F32) * scale
-        s2 = lax.dot_general(q, fk_ref[:, cols], dims, preferred_element_type=F32) * scale
+        s2 = lax.dot_general(q, far_ref[0, :, far_cols], dims, preferred_element_type=F32) * scale
         s1 = jnp.where(near_ok, s1, -1e30)
         s2 = jnp.where(far_ok, s2, -1e30)
         m = jnp.max(jnp.maximum(jnp.maximum(s0, s1), s2), axis=1, keepdims=True)
@@ -80,7 +82,7 @@
         l = jnp.sum(w0 + w1 + w2, axis=1, keepdims=True)
         a = jnp.dot(w0.astype(BF16), kv_ref[1, :, cols], preferred_element_type=F32)
         a += jnp.dot(w1.astype(BF16), cache_ref[1, 0, 0, :, cols], preferred_element_type=F32)
-        a += jnp.dot(w2.astype(BF16), fv_ref[:, cols], preferred_element_type=F32)
+        a += jnp.dot(w2.astype(BF16), far_ref[1, :, far_cols], preferred_element_type=F32)
         out_ref[h] = (a / l).astype(BF16)
 
 
@@ -92,19 +94,27 @@
     return pl.BlockSpec(memory_space=SMEM)
 
 
-def attend(first, count, queries, span_kv, cache_kv, far_k, far_v, seg_len, far_len):
+def anywhere():
+    return pl.BlockSpec(memory_space=pl.ANY)
+
+
+def attend(first, count, queries, span_kv, cache_kv, far, seg_len, far_len, held):
     rows = queries.shape[0]
     return pl.pallas_call(
         functools.partial(attend_body, first, count),
-        out_shape=jax.ShapeDtypeStruct((count, rows, HD), BF16),
-        in_specs=[scalars(), scalars()] + [full()] * 5,
-        out_specs=full(),
+        out_shape=(
+            jax.ShapeDtypeStruct((count, rows, HD), BF16),
+            jax.ShapeDtypeStruct(held.shape, held.dtype),
+        ),
+        in_specs=[scalars(), scalars()] + [full()] * 4 + [anywhere()],
+        out_specs=(full(), anywhere()),
+        input_output_aliases={6: 1},
         cost_estimate=pl.CostEstimate(
             flops=40 * rows * rows * HD * count, bytes_accessed=16 * rows * HD * count, transcendentals=0
         ),
         compiler_params=pltpu.CompilerParams(vmem_limit_bytes=16 * 2**20),
         name="attend",
-    )(seg_len, far_len, queries, span_kv, cache_kv, far_k, far_v)
+    )(seg_len, far_len, queries, span_kv, cache_kv, far, held)
 
 
 def pack_body(count, lane_ref, rows_ref, routes_ref, wts_ref, own_ref, other_ref):
@@ -247,9 +257,12 @@
     )(lane, resid, own, got, gain.reshape(1, -1))
 
 
-def expert_body(cols, xa_ref, xb_ref, ya_ref, yb_ref, wx_ref, wy_ref, in_ref, down_ref, cx_ref, cy_ref):
+def expert_body(cols, after, *refs):
+    refs = list(refs)
+    x_ref, y_ref, wx_ref, wy_ref, in_ref, down_ref = refs[:6]
+    cx_ref, cy_ref = refs[6 + after :]
     rows, width = cx_ref.shape
-    both = jnp.concatenate([xa_ref[...], xb_ref[...], ya_ref[...], yb_ref[...]], axis=0)
+    both = jnp.concatenate([x_ref[...], y_ref[...]], axis=0)
     gate = jnp.dot(both, in_ref[0, :, :FF], preferred_element_type=F32)
     up = jnp.dot(both, in_ref[0, :, FF:], preferred_element_type=F32)
     hidden = (gate * jax.nn.sigmoid(gate) * up).astype(BF16)
@@ -262,20 +275,42 @@
         cy_ref[:, at : at + step] = (out[rows:] * wy).astype(BF16)
 
 
-def expert(cols, x, y, wx, wy, w_in, w_out):
-    rows, width = 2 * x[0].shape[0], x[0].shape[1]
+def expert(cols, x, y, wx, wy, w_in, w_out, after=()):
+    rows, width = x.shape
     out = jax.ShapeDtypeStruct((rows, width), BF16)
     return pl.pallas_call(
-        functools.partial(expert_body, cols),
+        functools.partial(expert_body, cols, len(after)),
         out_shape=(out, out),
-        in_specs=[full()] * 8,
+        in_specs=[full()] * 6 + [anywhere()] * len(after),
         out_specs=(full(), full()),
         cost_estimate=pl.CostEstimate(
             flops=12 * rows * width * FF, bytes_accessed=6 * width * FF, transcendentals=0
         ),
         compiler_params=pltpu.CompilerParams(vmem_limit_bytes=24 * 2**20),
         name="expert",
-    )(*x, *y, wx, wy, w_in, w_out)
+    )(x, y, wx, wy, w_in, w_out, *after)
+
+
+def add_body(*refs):
+    total = refs[0][...].astype(F32)
+    for ref in refs[1:-1]:
+        total = total + ref[...].astype(F32)
+    refs[-1][...] = total.astype(BF16)
+
+
+def add(*terms):
+    size = terms[0].size
+    return pl.pallas_call(
+        add_body,
+        out_shape=jax.ShapeDtypeStruct(terms[0].shape, BF16),
+        in_specs=[full()] * len(terms),
+        out_specs=full(),
+        cost_estimate=pl.CostEstimate(
+            flops=len(terms) * size, bytes_accessed=4 * len(terms) * size, transcendentals=0
+        ),
+        compiler_params=pltpu.CompilerParams(vmem_limit_bytes=8 * 2**20),
+        name="add",
+    )(*terms)
 
 
 def shards(
@@ -294,27 +329,35 @@
         return lax.ppermute(block, "expert", sibling)
 
     group_swap = swap_pairs("group")
+    groups = 4
+    heads = HEADS // groups
+    wide = heads * HD
     far_len = lax.ppermute(seg_len[0, 1:2], "group", group_swap)
-    far_k = lax.ppermute(cache_kv[0, 0, 1], "group", group_swap)
-    far_v = lax.ppermute(cache_kv[1, 0, 1], "group", group_swap)
+    far = [
+        lax.ppermute(cache_kv[:, 0, 1, :, j * wide : (j + 1) * wide], "group", group_swap)
+        for j in range(groups)
+    ]
 
     chain_a, other = pack(count, lane[None], o_rows, routes, route_wts)
     chain_b = across(other)
     blocks = [chain_a, chain_b]
+    mine, theirs = [], []
     for s in range(1, pairs):
         chain_a = ahead(chain_a)
         chain_b = ahead(chain_b)
+        if len(mine) < groups:
+            j = len(mine)
+            part, chain_a = attend(
+                j * heads, heads, queries, span_kv, cache_kv, far[j], seg_len, far_len, chain_a
+            )
+            mine.append(part)
+            theirs.append(across(part))
         blocks += [chain_a, chain_b]
     sources = []
     for s in range(pairs):
         sources += [ring.source(s, 0, False), ring.source(s, 1, False)]
     table = jnp.asarray([[line[e] for line in sources] for e in range(count)], jnp.int32)
 
-    mine, theirs = [], []
-    for first in range(0, HEADS, HEADS // 2):
-        part = attend(first, HEADS // 2, queries, span_kv, cache_kv, far_k, far_v, seg_len, far_len)
-        mine.append(part)
-        theirs.append(across(part))
     slab = o_rows.shape[0]
     if slab != HD:
         mine, theirs = (
@@ -332,32 +375,22 @@
     def gate_at(column):
         return (wts_early, column) if column < early else (wts_late, column - early)
 
-    part_rows = rows // 2
-    x = [normed[:part_rows], normed[part_rows:]]
-    y = [across(p) for p in x]
-    travelling = None
-    for s in range(pairs):
+    x = [normed]
+    y = [across(normed)]
+    for s in range(1, pairs):
+        x.append(ahead(x[-1]))
+        y.append(across(x[-1]))
+
+    def sums(s, after=()):
         wx, column_x = gate_at(2 * s)
         wy, column_y = gate_at(2 * ((pairs - s) % pairs) + 1)
-        keep, give = expert((column_x, column_y), x, y, wx, wy, w_in, w_out)
-        back = across(give)
-        if s == 0:
-            total = residual + keep.astype(F32) + back.astype(F32)
-        else:
-            part = [
-                keep[at : at + part_rows].astype(F32) + back[at : at + part_rows].astype(F32)
-                for at in (0, part_rows)
-            ]
-            if travelling is not None:
-                part = [p + t.astype(F32) for p, t in zip(part, travelling)]
-            travelling = [ahead(p.astype(BF16)) for p in part]
-        if s + 1 < pairs:
-            x = [ahead(p) for p in x]
-            y = [across(p) for p in x]
-    out = [
-        total[i * part_rows : (i + 1) * part_rows] + t.astype(F32) for i, t in enumerate(travelling)
-    ]
-    return jnp.concatenate(out, axis=0).astype(BF16)
+        keep, give = expert((column_x, column_y), x[s], y[s], wx, wy, w_in, w_out, after)
+        return keep, across(give)
+
+    travelling = ()
+    for s in range(1, pairs):
+        travelling = (ahead(add(*sums(s), *travelling)),)
+    return add(residual, *sums(0, (x[min(3, pairs - 1)],)), *travelling)
 
 
 def solution(mesh):

time: 181 us -> 178 us (0.983)
  starting transfers between devices: 63.5 us -> 42.3 us
  waiting for transfers between devices: 81 us -> 96.8 us
  Pallas kernels: 27.8 us -> 32.4 us
  other arithmetic: 2.65 us -> 0 us
    ppermute x42 -> x28, starting transfers between devices: 54 us -> 25.1 us  [ahead(): return lax.ppermute(block, 'expert', forward)]
    ppermute x2 -> x4, waiting for transfers between devices: 0.01 us -> 9.93 us  [shards(): lax.ppermute(cache_kv[:, 0, 1, :, j * wide:(j + 1) * wide], 'group', grou...]
    ppermute x42 -> x28, waiting for transfers between devices: 71.1 us -> 77.4 us  [ahead(): return lax.ppermute(block, 'expert', forward)]
    ppermute x28 -> x22, starting transfers between devices: 5.92 us -> 10.7 us  [across(): return lax.ppermute(block, 'expert', sibling)]
    pallas_call x10 -> x20, Pallas kernels: 22.2 us -> 26.8 us  [the longest x8 15 us: expert(): pl.pallas_call(functools.partial(expert_body, cols, len(after)), out_shap...]
    ppermute x2 -> x4, starting transfers between devices: 2.09 us -> 6.03 us  [shards(): lax.ppermute(cache_kv[:, 0, 1, :, j * wide:(j + 1) * wide], 'group', grou...]
    ppermute x1, waiting for transfers between devices: 7.93 us -> 4.63 us  [shards(): far_len = lax.ppermute(seg_len[0, 1:2], 'group', group_swap)]
    ppermute x28 -> x22, waiting for transfers between devices: 1.97 us -> 4.86 us  [across(): return lax.ppermute(block, 'expert', sibling)]
  transfers between devices with their start and end apart: 73 -> 55, of which waited for: 35 -> 28; matrix products, arithmetic and copies ran while one was open for 2% -> 1% of each run, Pallas kernels for 14% -> 16%
where the time goes in v3:
time: 178 us
  waiting for transfers between devices  96.8 us (54%)
  starting transfers between devices  42.3 us (24%)
  Pallas kernels  32.4 us (18%)
  local copies, waits for them, and re-layouts  5.77 us (3%)
    ppermute x28, waiting for transfers between devices, ahead(): return lax.ppermute(block, 'expert', forward)  77.4 us
    ppermute x28, starting transfers between devices, ahead(): return lax.ppermute(block, 'expert', forward)  25.1 us
    pallas_call x8, Pallas kernels, expert(): pl.pallas_call(functools.partial(expert_body, cols, len(after)), out_shap...  15 us
    ppermute x22, starting transfers between devices, across(): return lax.ppermute(block, 'expert', sibling)  10.7 us
    ppermute x4, waiting for transfers between devices, shards(): lax.ppermute(cache_kv[:, 0, 1, :, j * wide:(j + 1) * wide], 'group', grou...  9.93 us
    pallas_call x4, Pallas kernels, attend(): pl.pallas_call(functools.partial(attend_body, first, count), out_shape=(j...  9.57 us
    ppermute x4, starting transfers between devices, shards(): lax.ppermute(cache_kv[:, 0, 1, :, j * wide:(j + 1) * wide], 'group', grou...  6.03 us
    pallas_call x2, Pallas kernels, project(): pl.pallas_call(functools.partial(project_body, first, number, len(mine),...  5.16 us
  transfers between devices with their start and end apart: 55, of which 28 were waited for; matrix products, arithmetic and copies ran while one was open for 1% of the time, Pallas kernels for 16%

profile of v3, /device:TPU:0, one launch (start us, length us, event | category | flops | bytes accessed | tf_op | source)
XLA Modules:
  0.0 177.6 jit_solution(4930511228525577517)
XLA Ops:
  0.0 1.2 copy-done.5
  2.6 3.1 %collective-permute-start.2 = (bf16[136,1024]{1,0:T(8,128)(2,1)S(1)}, bf16[136,1024]{1,0:T(8,128)(2,1)S(1)}, u32[]{:S(2)}, u32[]{:S(2)}) collective-permute-start(bf16[136,1024]{1,0:T(8,128)(2,1)S(1)} %get-tuple-element.39.refs_8_), channel_id=1, source_target_pairs={{0,4},{1,3},{4,8},{5,1},{8,12},{9,5},{12,14},{13,9},{14,10},{15,13... | collective-permute-start | bytes 835592 | tf_op jit(solution)/shard_map/ppermute | solution.py:326
  5.7 1.3 slice_bitcast_fusion
  7.0 1.6 collective-permute-start.1
  8.6 1.6 collective-permute-start.14
  11.3 4.6 %collective-permute-done.far_len_ref = s32[1]{0:T(128)} collective-permute-done((s32[1]{0:T(128)}, s32[1]{0:T(128)}, u32[]{:S(2)}, u32[]{:S(2)}) %collective-permute-start) | collective-permute-done | bytes 36 | tf_op jit(solution)/shard_map/ppermute | solution.py:335
  16.0 1.2 copy-done.3
  17.2 2.4 %attend.4 = (bf16[4,128,128]{2,1,0:T(8,128)(2,1)S(1)}, bf16[136,1024]{1,0:T(8,128)(2,1)S(1)}) custom-call(s32[1,2]{1,0:T(1,128)S(1)} %copy-done.9, s32[1]{0:T(128)} %collective-permute-done.far_len_ref, bf16[128,2048]{1,0:T(8,128)(2,1)S(1)} %copy-done.4, bf16[2,128,2048]{2,1,0:T(8,128)(2,1)S(1)} %copy-done.3, ...), custom_call_target="tpu_custom_call", output_to_operand_aliasing={{1}: (6, {})} | custom-call | flops 335544320 | bytes 1048576 | tf_op jit(solution)/shard_map/attend/pallas_call | solution.py:103
  19.6 1.6 collective-permute-start.4
  21.2 1.5 collective-permute-start.3
  22.7 1.6 collective-permute-start.15
  24.3 3.3 %collective-permute-done.3.far_ref = bf16[2,128,512]{2,1,0:T(8,128)(2,1)S(1)} collective-permute-done((bf16[2,128,512]{2,1,0:T(8,128)(2,1)S(1)}, bf16[2,128,512]{2,1,0:T(8,128)(2,1)S(1)}, u32[]{:S(2)}, u32[]{:S(2)}) %collective-permute-start.3) | collective-permute-done | bytes 262176 | tf_op jit(solution)/shard_map/ppermute | solution.py:337
  27.6 2.4 %attend.5 = (bf16[4,128,128]{2,1,0:T(8,128)(2,1)S(1)}, bf16[136,1024]{1,0:T(8,128)(2,1)S(1)}) custom-call(s32[1,2]{1,0:T(1,128)S(1)} %copy-done.9, s32[1]{0:T(128)} %collective-permute-done.far_len_ref, bf16[128,2048]{1,0:T(8,128)(2,1)S(1)} %copy-done.4, bf16[2,128,2048]{2,1,0:T(8,128)(2,1)S(1)} %copy-done.3, ...), custom_call_target="tpu_custom_call", output_to_operand_aliasing={{1}: (6, {})} | custom-call | flops 335544320 | bytes 1048576 | tf_op jit(solution)/shard_map/attend/pallas_call | solution.py:103
  30.0 1.6 collective-permute-start.6
  31.6 1.5 collective-permute-start.5
  33.1 1.6 collective-permute-start.16
  34.7 3.3 %collective-permute-done.5.far_ref = bf16[2,128,512]{2,1,0:T(8,128)(2,1)S(1)} collective-permute-done((bf16[2,128,512]{2,1,0:T(8,128)(2,1)S(1)}, bf16[2,128,512]{2,1,0:T(8,128)(2,1)S(1)}, u32[]{:S(2)}, u32[]{:S(2)}) %collective-permute-start.5) | collective-permute-done | bytes 262176 | tf_op jit(solution)/shard_map/ppermute | solution.py:337
  38.0 2.4 %attend.6 = (bf16[4,128,128]{2,1,0:T(8,128)(2,1)S(1)}, bf16[136,1024]{1,0:T(8,128)(2,1)S(1)}) custom-call(s32[1,2]{1,0:T(1,128)S(1)} %copy-done.9, s32[1]{0:T(128)} %collective-permute-done.far_len_ref, bf16[128,2048]{1,0:T(8,128)(2,1)S(1)} %copy-done.4, bf16[2,128,2048]{2,1,0:T(8,128)(2,1)S(1)} %copy-done.3, ...), custom_call_target="tpu_custom_call", output_to_operand_aliasing={{1}: (6, {})} | custom-call | flops 335544320 | bytes 1048576 | tf_op jit(solution)/shard_map/attend/pallas_call | solution.py:103
  40.4 1.6 collective-permute-start.8
  42.0 1.5 collective-permute-start.7
  43.5 1.6 collective-permute-start.17
  45.1 3.3 %collective-permute-done.7.far_ref = bf16[2,128,512]{2,1,0:T(8,128)(2,1)S(1)} collective-permute-done((bf16[2,128,512]{2,1,0:T(8,128)(2,1)S(1)}, bf16[2,128,512]{2,1,0:T(8,128)(2,1)S(1)}, u32[]{:S(2)}, u32[]{:S(2)}) %collective-permute-start.7) | collective-permute-done | bytes 262176 | tf_op jit(solution)/shard_map/ppermute | solution.py:337
  48.4 2.4 %attend.7 = (bf16[4,128,128]{2,1,0:T(8,128)(2,1)S(1)}, bf16[136,1024]{1,0:T(8,128)(2,1)S(1)}) custom-call(s32[1,2]{1,0:T(1,128)S(1)} %copy-done.9, s32[1]{0:T(128)} %collective-permute-done.far_len_ref, bf16[128,2048]{1,0:T(8,128)(2,1)S(1)} %copy-done.4, bf16[2,128,2048]{2,1,0:T(8,128)(2,1)S(1)} %copy-done.3, ...), custom_call_target="tpu_custom_call", output_to_operand_aliasing={{1}: (6, {})} | custom-call | flops 335544320 | bytes 1048576 | tf_op jit(solution)/shard_map/attend/pallas_call | solution.py:103
  50.8 1.6 collective-permute-start.18
  52.4 1.5 collective-permute-start.19
  54.0 4.2 %collective-permute-done.18.refs_10_ = bf16[136,1024]{1,0:T(8,128)(2,1)S(1)} collective-permute-done((bf16[136,1024]{1,0:T(8,128)(2,1)S(1)}, bf16[136,1024]{1,0:T(8,128)(2,1)S(1)}, u32[]{:S(2)}, u32[]{:S(2)}) %collective-permute-start.18) | collective-permute-done | bytes 278560 | tf_op jit(solution)/shard_map/ppermute | solution.py:326
  59.0 2.1 %collective-permute-done.19.refs_11_ = bf16[136,1024]{1,0:T(8,128)(2,1)S(1)} collective-permute-done((bf16[136,1024]{1,0:T(8,128)(2,1)S(1)}, bf16[136,1024]{1,0:T(8,128)(2,1)S(1)}, u32[]{:S(2)}, u32[]{:S(2)}) %collective-permute-start.19) | collective-permute-done | bytes 278560 | tf_op jit(solution)/shard_map/ppermute | solution.py:326
  62.6 2.6 %collective-permute-done.20.refs_12_ = bf16[136,1024]{1,0:T(8,128)(2,1)S(1)} collective-permute-done((bf16[136,1024]{1,0:T(8,128)(2,1)S(1)}, bf16[136,1024]{1,0:T(8,128)(2,1)S(1)}, u32[]{:S(2)}, u32[]{:S(2)}) %collective-permute-start.20) | collective-permute-done | bytes 278560 | tf_op jit(solution)/shard_map/ppermute | solution.py:326
  65.5 2.7 %collective-permute-done.21.refs_13_ = bf16[136,1024]{1,0:T(8,128)(2,1)S(1)} collective-permute-done((bf16[136,1024]{1,0:T(8,128)(2,1)S(1)}, bf16[136,1024]{1,0:T(8,128)(2,1)S(1)}, u32[]{:S(2)}, u32[]{:S(2)}) %collective-permute-start.21) | collective-permute-done | bytes 278560 | tf_op jit(solution)/shard_map/ppermute | solution.py:326
  70.4 3.0 %project.2 = (f32[128,1024]{1,0:T(8,128)S(1)}, f32[128,1024]{1,0:T(8,128)S(1)}, f32[128,128]{1,0:T(8,128)S(1)}) custom-call(s32[16,16]{1,0:T(8,128)S(1)} %copy-done.7, s32[1]{0:T(128)} %bitcast.1.me_ref, bf16[4,128,128]{2,1,0:T(8,128)(2,1)S(1)} %get-tuple-element.40.refs_0_, bf16[4,128,128]{2,1,0:T(8,128)(2,1)S(1)} %get-tuple-element.42.refs_1_, ...), custom_call_target="tpu_custom_call" | custom-call | flops 671088640 | bytes 2621440 | tf_op jit(solution)/shard_map/project/pallas_call | solution.py:208
  73.4 1.4 collective-permute-done.23.refs_15_
  74.8 2.1 %project.3 = (f32[128,1024]{1,0:T(8,128)S(1)}, f32[128,1024]{1,0:T(8,128)S(1)}, f32[128,128]{1,0:T(8,128)S(1)}) custom-call(s32[16,16]{1,0:T(8,128)S(1)} %copy-done.7, s32[1]{0:T(128)} %bitcast.1.me_ref, bf16[4,128,128]{2,1,0:T(8,128)(2,1)S(1)} %get-tuple-element.40.refs_0_, bf16[4,128,128]{2,1,0:T(8,128)(2,1)S(1)} %get-tuple-element.42.refs_1_, ...), custom_call_target="tpu_custom_call" | custom-call | flops 402653184 | bytes 1572864 | tf_op jit(solution)/shard_map/project/pallas_call | solution.py:208
  77.1 1.9 %collective-permute-done.24.got_ref = f32[128,1024]{1,0:T(8,128)S(1)} collective-permute-done((f32[128,1024]{1,0:T(8,128)S(1)}, f32[128,1024]{1,0:T(8,128)S(1)}, u32[]{:S(2)}, u32[]{:S(2)}) %collective-permute-start.24) | collective-permute-done | bytes 524320 | tf_op jit(solution)/shard_map/ppermute | solution.py:329
  79.6 8.9 %collective-permute-done.26.refs_0_ = bf16[128,2048]{1,0:T(8,128)(2,1)S(1)} collective-permute-done((bf16[128,2048]{1,0:T(8,128)(2,1)S(1)}, bf16[128,2048]{1,0:T(8,128)(2,1)S(1)}, u32[]{:S(2)}, u32[]{:S(2)}) %collective-permute-start.26) | collective-permute-done | bytes 524320 | tf_op jit(solution)/shard_map/ppermute | solution.py:326
  88.8 1.7 collective-permute-done.46.refs_1_
  90.5 1.9 %expert.15 = (bf16[128,2048]{1,0:T(8,128)(2,1)S(1)}, bf16[128,2048]{1,0:T(8,128)(2,1)S(1)}) custom-call(bf16[128,2048]{1,0:T(8,128)(2,1)S(1)} %collective-permute-done.26.refs_0_, bf16[128,2048]{1,0:T(8,128)(2,1)S(1)} %collective-permute-done.46.refs_1_, f32[128,128]{1,0:T(8,128)S(1)} %get-tuple-element.55.refs_2_.refs_3_, ...), custom_call_target="tpu_custom_call" | custom-call | flops 1610612736 | bytes 6291456 | tf_op jit(solution)/shard_map/expert/pallas_call | solution.py:281
  92.8 5.0 %collective-permute-done.27.refs_0_ = bf16[128,2048]{1,0:T(8,128)(2,1)S(1)} collective-permute-done((bf16[128,2048]{1,0:T(8,128)(2,1)S(1)}, bf16[128,2048]{1,0:T(8,128)(2,1)S(1)}, u32[]{:S(2)}, u32[]{:S(2)}) %collective-permute-start.27) | collective-permute-done | bytes 524320 | tf_op jit(solution)/shard_map/ppermute | solution.py:326
  98.1 1.8 collective-permute-start.48
  99.9 1.9 %expert.14 = (bf16[128,2048]{1,0:T(8,128)(2,1)S(1)}, bf16[128,2048]{1,0:T(8,128)(2,1)S(1)}) custom-call(bf16[128,2048]{1,0:T(8,128)(2,1)S(1)} %collective-permute-done.27.refs_0_, bf16[128,2048]{1,0:T(8,128)(2,1)S(1)} %collective-permute-done.44.refs_1_, f32[128,128]{1,0:T(8,128)S(1)} %get-tuple-element.55.refs_2_.refs_3_, ...), custom_call_target="tpu_custom_call" | custom-call | flops 1610612736 | bytes 6291456 | tf_op jit(solution)/shard_map/expert/pallas_call | solution.py:281
  101.8 2.3 %collective-permute-start.45 = (bf16[128,2048]{1,0:T(8,128)(2,1)S(1)}, bf16[128,2048]{1,0:T(8,128)(2,1)S(1)}, u32[]{:S(2)}, u32[]{:S(2)}) collective-permute-start(bf16[128,2048]{1,0:T(8,128)(2,1)S(1)} %get-tuple-element.70), channel_id=1, source_target_pairs={{0,1},{1,0},{2,3},{3,2},{4,5},{5,4},{6,7},{7,6},{8,9},{9,8},{10,11... | collective-permute-start | bytes 1572872 | tf_op jit(solution)/shard_map/ppermute | solution.py:329
  104.1 2.9 %collective-permute-done.28.refs_6_.refs_0_ = bf16[128,2048]{1,0:T(8,128)(2,1)S(1)} collective-permute-done((bf16[128,2048]{1,0:T(8,128)(2,1)S(1)}, bf16[128,2048]{1,0:T(8,128)(2,1)S(1)}, u32[]{:S(2)}, u32[]{:S(2)}) %collective-permute-start.28) | collective-permute-done | bytes 524320 | tf_op jit(solution)/shard_map/ppermute | solution.py:326
  107.2 5.4 %collective-permute-done.48.refs_2_ = bf16[128,2048]{1,0:T(8,128)(2,1)S(1)} collective-permute-done((bf16[128,2048]{1,0:T(8,128)(2,1)S(1)}, bf16[128,2048]{1,0:T(8,128)(2,1)S(1)}, u32[]{:S(2)}, u32[]{:S(2)}) %collective-permute-start.48) | collective-permute-done | bytes 524320 | tf_op jit(solution)/shard_map/ppermute | solution.py:326
  113.1 1.9 %expert.13 = (bf16[128,2048]{1,0:T(8,128)(2,1)S(1)}, bf16[128,2048]{1,0:T(8,128)(2,1)S(1)}) custom-call(bf16[128,2048]{1,0:T(8,128)(2,1)S(1)} %collective-permute-done.28.refs_6_.refs_0_, bf16[128,2048]{1,0:T(8,128)(2,1)S(1)} %collective-permute-done.42.refs_1_, f32[128,128]{1,0:T(8,128)S(1)} %get-tuple-element.55.refs_2_.refs_3_, ...), custom_call_target="tpu_custom_call" | custom-call | flops 1610612736 | bytes 6291456 | tf_op jit(solution)/shard_map/expert/pallas_call | solution.py:281
  114.9 1.2 collective-permute-start.43
  116.2 2.0 %collective-permute-done.30.refs_0_ = bf16[128,2048]{1,0:T(8,128)(2,1)S(1)} collective-permute-done((bf16[128,2048]{1,0:T(8,128)(2,1)S(1)}, bf16[128,2048]{1,0:T(8,128)(2,1)S(1)}, u32[]{:S(2)}, u32[]{:S(2)}) %collective-permute-start.30) | collective-permute-done | bytes 524320 | tf_op jit(solution)/shard_map/ppermute | solution.py:326
  118.4 5.4 %collective-permute-done.49.refs_2_ = bf16[128,2048]{1,0:T(8,128)(2,1)S(1)} collective-permute-done((bf16[128,2048]{1,0:T(8,128)(2,1)S(1)}, bf16[128,2048]{1,0:T(8,128)(2,1)S(1)}, u32[]{:S(2)}, u32[]{:S(2)}) %collective-permute-start.49) | collective-permute-done | bytes 524320 | tf_op jit(solution)/shard_map/ppermute | solution.py:326
  124.3 1.9 %expert.12 = (bf16[128,2048]{1,0:T(8,128)(2,1)S(1)}, bf16[128,2048]{1,0:T(8,128)(2,1)S(1)}) custom-call(bf16[128,2048]{1,0:T(8,128)(2,1)S(1)} %collective-permute-done.30.refs_0_, bf16[128,2048]{1,0:T(8,128)(2,1)S(1)} %collective-permute-done.40.refs_1_, f32[128,128]{1,0:T(8,128)S(1)} %get-tuple-element.55.refs_2_.refs_3_, ...), custom_call_target="tpu_custom_call" | custom-call | flops 1610612736 | bytes 6291456 | tf_op jit(solution)/shard_map/expert/pallas_call | solution.py:281
  126.2 1.2 collective-permute-start.41
  127.4 2.0 %collective-permute-done.31.refs_0_ = bf16[128,2048]{1,0:T(8,128)(2,1)S(1)} collective-permute-done((bf16[128,2048]{1,0:T(8,128)(2,1)S(1)}, bf16[128,2048]{1,0:T(8,128)(2,1)S(1)}, u32[]{:S(2)}, u32[]{:S(2)}) %collective-permute-start.31) | collective-permute-done | bytes 524320 | tf_op jit(solution)/shard_map/ppermute | solution.py:326
  129.7 5.4 %collective-permute-done.50.refs_2_ = bf16[128,2048]{1,0:T(8,128)(2,1)S(1)} collective-permute-done((bf16[128,2048]{1,0:T(8,128)(2,1)S(1)}, bf16[128,2048]{1,0:T(8,128)(2,1)S(1)}, u32[]{:S(2)}, u32[]{:S(2)}) %collective-permute-start.50) | collective-permute-done | bytes 524320 | tf_op jit(solution)/shard_map/ppermute | solution.py:326
  135.5 1.9 %expert.11 = (bf16[128,2048]{1,0:T(8,128)(2,1)S(1)}, bf16[128,2048]{1,0:T(8,128)(2,1)S(1)}) custom-call(bf16[128,2048]{1,0:T(8,128)(2,1)S(1)} %collective-permute-done.31.refs_0_, bf16[128,2048]{1,0:T(8,128)(2,1)S(1)} %collective-permute-done.38.refs_1_, f32[128,128]{1,0:T(8,128)S(1)} %get-tuple-element.58.refs_2_.refs_3_, ...), custom_call_target="tpu_custom_call" | custom-call | flops 1610612736 | bytes 6291456 | tf_op jit(solution)/shard_map/expert/pallas_call | solution.py:281
  137.4 1.2 collective-permute-start.39
  138.6 2.0 %collective-permute-done.32.refs_0_ = bf16[128,2048]{1,0:T(8,128)(2,1)S(1)} collective-permute-done((bf16[128,2048]{1,0:T(8,128)(2,1)S(1)}, bf16[128,2048]{1,0:T(8,128)(2,1)S(1)}, u32[]{:S(2)}, u32[]{:S(2)}) %collective-permute-start.32) | collective-permute-done | bytes 524320 | tf_op jit(solution)/shard_map/ppermute | solution.py:326
  140.9 5.4 %collective-permute-done.51.refs_2_ = bf16[128,2048]{1,0:T(8,128)(2,1)S(1)} collective-permute-done((bf16[128,2048]{1,0:T(8,128)(2,1)S(1)}, bf16[128,2048]{1,0:T(8,128)(2,1)S(1)}, u32[]{:S(2)}, u32[]{:S(2)}) %collective-permute-start.51) | collective-permute-done | bytes 524320 | tf_op jit(solution)/shard_map/ppermute | solution.py:326
  146.8 1.9 %expert.10 = (bf16[128,2048]{1,0:T(8,128)(2,1)S(1)}, bf16[128,2048]{1,0:T(8,128)(2,1)S(1)}) custom-call(bf16[128,2048]{1,0:T(8,128)(2,1)S(1)} %collective-permute-done.32.refs_0_, bf16[128,2048]{1,0:T(8,128)(2,1)S(1)} %collective-permute-done.36.refs_1_, f32[128,128]{1,0:T(8,128)S(1)} %get-tuple-element.58.refs_2_.refs_3_, ...), custom_call_target="tpu_custom_call" | custom-call | flops 1610612736 | bytes 6291456 | tf_op jit(solution)/shard_map/expert/pallas_call | solution.py:281
  148.7 1.2 collective-permute-start.37
  149.9 2.0 %collective-permute-done.33.refs_0_ = bf16[128,2048]{1,0:T(8,128)(2,1)S(1)} collective-permute-done((bf16[128,2048]{1,0:T(8,128)(2,1)S(1)}, bf16[128,2048]{1,0:T(8,128)(2,1)S(1)}, u32[]{:S(2)}, u32[]{:S(2)}) %collective-permute-start.33) | collective-permute-done | bytes 524320 | tf_op jit(solution)/shard_map/ppermute | solution.py:326
  152.4 5.1 %collective-permute-done.52.refs_2_ = bf16[128,2048]{1,0:T(8,128)(2,1)S(1)} collective-permute-done((bf16[128,2048]{1,0:T(8,128)(2,1)S(1)}, bf16[128,2048]{1,0:T(8,128)(2,1)S(1)}, u32[]{:S(2)}, u32[]{:S(2)}) %collective-permute-start.52) | collective-permute-done | bytes 524320 | tf_op jit(solution)/shard_map/ppermute | solution.py:326
  158.2 1.9 %expert.9 = (bf16[128,2048]{1,0:T(8,128)(2,1)S(1)}, bf16[128,2048]{1,0:T(8,128)(2,1)S(1)}) custom-call(bf16[128,2048]{1,0:T(8,128)(2,1)S(1)} %collective-permute-done.33.refs_0_, bf16[128,2048]{1,0:T(8,128)(2,1)S(1)} %collective-permute-done.34.refs_1_, f32[128,128]{1,0:T(8,128)S(1)} %get-tuple-element.58.refs_2_.refs_3_, ...), custom_call_target="tpu_custom_call" | custom-call | flops 1610612736 | bytes 6291456 | tf_op jit(solution)/shard_map/expert/pallas_call | solution.py:281
  160.1 1.2 collective-permute-start.35
  161.3 1.9 %expert.8 = (bf16[128,2048]{1,0:T(8,128)(2,1)S(1)}, bf16[128,2048]{1,0:T(8,128)(2,1)S(1)}) custom-call(bf16[128,2048]{1,0:T(8,128)(2,1)S(1)} %get-tuple-element.54.refs_0_, bf16[128,2048]{1,0:T(8,128)(2,1)S(1)} %collective-permute-done.25.refs_1_, f32[128,128]{1,0:T(8,128)S(1)} %get-tuple-element.55.refs_2_.refs_3_, ...), custom_call_target="tpu_custom_call" | custom-call | flops 1610612736 | bytes 6291456 | tf_op jit(solution)/shard_map/expert/pallas_call | solution.py:281
  163.3 3.9 %collective-permute-done.53.refs_2_ = bf16[128,2048]{1,0:T(8,128)(2,1)S(1)} collective-permute-done((bf16[128,2048]{1,0:T(8,128)(2,1)S(1)}, bf16[128,2048]{1,0:T(8,128)(2,1)S(1)}, u32[]{:S(2)}, u32[]{:S(2)}) %collective-permute-start.53) | collective-permute-done | bytes 524320 | tf_op jit(solution)/shard_map/ppermute | solution.py:326
  167.7 8.9 %collective-permute-done.54.refs_3_ = bf16[128,2048]{1,0:T(8,128)(2,1)S(1)} collective-permute-done((bf16[128,2048]{1,0:T(8,128)(2,1)S(1)}, bf16[128,2048]{1,0:T(8,128)(2,1)S(1)}, u32[]{:S(2)}, u32[]{:S(2)}) %collective-permute-start.54) | collective-permute-done | bytes 524320 | tf_op jit(solution)/shard_map/ppermute | solution.py:326
  176.6 1.0 add.20
  (96 shorter events, 13.9 us)
Async XLA Ops:
  0.0 16.0 %copy-start.2 = (bf16[2,1,2,128,2048]{4,3,2,1,0:T(8,128)(2,1)S(1)}, bf16[2,1,2,128,2048]{4,3,2,1,0:T(8,128)(2,1)}, u32[]{:S(2)}) copy-start(bf16[2,1,2,128,2048]{4,3,2,1,0:T(8,128)(2,1)} %cache_ref.7) | copy-start | bytes 6291460
  0.0 16.0 %copy-start.4 = (bf16[128,2048]{1,0:T(8,128)(2,1)S(1)}, bf16[128,2048]{1,0:T(8,128)(2,1)}, u32[]{:S(2)}) copy-start(bf16[128,2048]{1,0:T(8,128)(2,1)} %q_ref.7) | copy-start | bytes 1572868
  2.6 7.6 %copy-start.9 = (s32[1,2]{1,0:T(1,128)S(1)}, s32[1,2]{1,0:T(1,128)}, u32[]{:S(2)}) copy-start(s32[1,2]{1,0:T(1,128)} %len_ref.7) | copy-start | bytes 28
  2.6 13.3 %collective-permute-start.2 = (bf16[136,1024]{1,0:T(8,128)(2,1)S(1)}, bf16[136,1024]{1,0:T(8,128)(2,1)S(1)}, u32[]{:S(2)}, u32[]{:S(2)}) collective-permute-start(bf16[136,1024]{1,0:T(8,128)(2,1)S(1)} %get-tuple-element.39.refs_8_), channel_id=1, source_target_pairs={{0,4},{1,3},{4,8},{5,1},{8,12},{9,5},{12,14},{13,9},{14,10},{15,13... | collective-permute-start | bytes 835592 | tf_op jit(solution)/shard_map/ppermute | solution.py:326
  5.7 2.9 %collective-permute-start.13 = (bf16[136,1024]{1,0:T(8,128)(2,1)S(1)}, bf16[136,1024]{1,0:T(8,128)(2,1)S(1)}, u32[]{:S(2)}, u32[]{:S(2)}) collective-permute-start(bf16[136,1024]{1,0:T(8,128)(2,1)S(1)} %get-tuple-element.47), channel_id=1, source_target_pairs={{0,1},{1,0},{2,3},{3,2},{4,5},{5,4},{6,7},{7,6},{8,9},{9,8},{10,11... | collective-permute-start | bytes 835592 | tf_op jit(solution)/shard_map/ppermute | solution.py:329
  7.0 9.0 %collective-permute-start.1 = (bf16[2,128,512]{2,1,0:T(8,128)(2,1)S(1)}, bf16[2,128,512]{2,1,0:T(8,128)(2,1)S(1)}, u32[]{:S(2)}, u32[]{:S(2)}) collective-permute-start(bf16[2,128,512]{2,1,0:T(8,128)(2,1)S(1)} %get-tuple-element.76), channel_id=1, source_target_pairs={{0,16},{16,0},{1,17},{17,1},{2,18},{18,2},{3,19},{19,3},{4,20},{20... | collective-permute-start | bytes 786440 | tf_op jit(solution)/shard_map/ppermute | solution.py:337
  8.6 14.2 %collective-permute-start.14 = (bf16[136,1024]{1,0:T(8,128)(2,1)S(1)}, bf16[136,1024]{1,0:T(8,128)(2,1)S(1)}, u32[]{:S(2)}, u32[]{:S(2)}) collective-permute-start(bf16[136,1024]{1,0:T(8,128)(2,1)S(1)} %collective-permute-done.13.refs_9_), channel_id=1, source_target_pairs={{0,4},{1,3},{4,8},{5,1},{8,12},{9,5},{12,14},{13,9},{14,10},{15,13... | collective-permute-start | bytes 835592 | tf_op jit(solution)/shard_map/ppermute | solution.py:326
  10.8 5.2 %collective-permute-start = (s32[1]{0:T(128)}, s32[1]{0:T(128)}, u32[]{:S(2)}, u32[]{:S(2)}) collective-permute-start(s32[1]{0:T(128)} %bitcast.2), channel_id=1, source_target_pairs={{0,16},{16,0},{1,17},{17,1},{2,18},{18,2},{3,19},{19,3},{4,20},{20... | collective-permute-start | bytes 20 | tf_op jit(solution)/shard_map/ppermute | solution.py:335
  16.0 1.2 copy-start.3
  19.6 8.0 %collective-permute-start.4 = (bf16[136,1024]{1,0:T(8,128)(2,1)S(1)}, bf16[136,1024]{1,0:T(8,128)(2,1)S(1)}, u32[]{:S(2)}, u32[]{:S(2)}) collective-permute-start(bf16[136,1024]{1,0:T(8,128)(2,1)S(1)} %get-tuple-element.41.refs_10_), channel_id=1, source_target_pairs={{0,4},{1,3},{4,8},{5,1},{8,12},{9,5},{12,14},{13,9},{14,10},{15,13... | collective-permute-start | bytes 835592 | tf_op jit(solution)/shard_map/ppermute | solution.py:326
  21.2 6.4 %collective-permute-start.3 = (bf16[2,128,512]{2,1,0:T(8,128)(2,1)S(1)}, bf16[2,128,512]{2,1,0:T(8,128)(2,1)S(1)}, u32[]{:S(2)}, u32[]{:S(2)}) collective-permute-start(bf16[2,128,512]{2,1,0:T(8,128)(2,1)S(1)} %get-tuple-element.75), channel_id=1, source_target_pairs={{0,16},{16,0},{1,17},{17,1},{2,18},{18,2},{3,19},{19,3},{4,20},{20... | collective-permute-start | bytes 786440 | tf_op jit(solution)/shard_map/ppermute | solution.py:337
  22.7 10.4 %collective-permute-start.15 = (bf16[136,1024]{1,0:T(8,128)(2,1)S(1)}, bf16[136,1024]{1,0:T(8,128)(2,1)S(1)}, u32[]{:S(2)}, u32[]{:S(2)}) collective-permute-start(bf16[136,1024]{1,0:T(8,128)(2,1)S(1)} %collective-permute-done.14.refs_11_), channel_id=1, source_target_pairs={{0,4},{1,3},{4,8},{5,1},{8,12},{9,5},{12,14},{13,9},{14,10},{15,13... | collective-permute-start | bytes 835592 | tf_op jit(solution)/shard_map/ppermute | solution.py:326
  30.0 8.0 %collective-permute-start.6 = (bf16[136,1024]{1,0:T(8,128)(2,1)S(1)}, bf16[136,1024]{1,0:T(8,128)(2,1)S(1)}, u32[]{:S(2)}, u32[]{:S(2)}) collective-permute-start(bf16[136,1024]{1,0:T(8,128)(2,1)S(1)} %get-tuple-element.43.refs_12_), channel_id=1, source_target_pairs={{0,4},{1,3},{4,8},{5,1},{8,12},{9,5},{12,14},{13,9},{14,10},{15,13... | collective-permute-start | bytes 835592 | tf_op jit(solution)/shard_map/ppermute | solution.py:326
  31.6 6.4 %collective-permute-start.5 = (bf16[2,128,512]{2,1,0:T(8,128)(2,1)S(1)}, bf16[2,128,512]{2,1,0:T(8,128)(2,1)S(1)}, u32[]{:S(2)}, u32[]{:S(2)}) collective-permute-start(bf16[2,128,512]{2,1,0:T(8,128)(2,1)S(1)} %get-tuple-element.74), channel_id=1, source_target_pairs={{0,16},{16,0},{1,17},{17,1},{2,18},{18,2},{3,19},{19,3},{4,20},{20... | collective-permute-start | bytes 786440 | tf_op jit(solution)/shard_map/ppermute | solution.py:337
  33.1 10.4 %collective-permute-start.16 = (bf16[136,1024]{1,0:T(8,128)(2,1)S(1)}, bf16[136,1024]{1,0:T(8,128)(2,1)S(1)}, u32[]{:S(2)}, u32[]{:S(2)}) collective-permute-start(bf16[136,1024]{1,0:T(8,128)(2,1)S(1)} %collective-permute-done.15.refs_13_), channel_id=1, source_target_pairs={{0,4},{1,3},{4,8},{5,1},{8,12},{9,5},{12,14},{13,9},{14,10},{15,13... | collective-permute-start | bytes 835592 | tf_op jit(solution)/shard_map/ppermute | solution.py:326
  40.4 8.0 %collective-permute-start.8 = (bf16[136,1024]{1,0:T(8,128)(2,1)S(1)}, bf16[136,1024]{1,0:T(8,128)(2,1)S(1)}, u32[]{:S(2)}, u32[]{:S(2)}) collective-permute-start(bf16[136,1024]{1,0:T(8,128)(2,1)S(1)} %get-tuple-element.45.refs_14_), channel_id=1, source_target_pairs={{0,4},{1,3},{4,8},{5,1},{8,12},{9,5},{12,14},{13,9},{14,10},{15,13... | collective-permute-start | bytes 835592 | tf_op jit(solution)/shard_map/ppermute | solution.py:326
  42.0 28.4 %copy-start.7 = (s32[16,16]{1,0:T(8,128)S(1)}, s32[16,16]{1,0:T(8,128)}, u32[]{:S(2)}) copy-start(s32[16,16]{1,0:T(8,128)} %constant.19.clone.table_ref) | copy-start | bytes 3076
  42.0 6.4 %collective-permute-start.7 = (bf16[2,128,512]{2,1,0:T(8,128)(2,1)S(1)}, bf16[2,128,512]{2,1,0:T(8,128)(2,1)S(1)}, u32[]{:S(2)}, u32[]{:S(2)}) collective-permute-start(bf16[2,128,512]{2,1,0:T(8,128)(2,1)S(1)} %get-tuple-element.73), channel_id=1, source_target_pairs={{0,16},{16,0},{1,17},{17,1},{2,18},{18,2},{3,19},{19,3},{4,20},{20... | collective-permute-start | bytes 786440 | tf_op jit(solution)/shard_map/ppermute | solution.py:337
  43.5 8.9 %collective-permute-start.17 = (bf16[136,1024]{1,0:T(8,128)(2,1)S(1)}, bf16[136,1024]{1,0:T(8,128)(2,1)S(1)}, u32[]{:S(2)}, u32[]{:S(2)}) collective-permute-start(bf16[136,1024]{1,0:T(8,128)(2,1)S(1)} %collective-permute-done.16.refs_15_), channel_id=1, source_target_pairs={{0,4},{1,3},{4,8},{5,1},{8,12},{9,5},{12,14},{13,9},{14,10},{15,13... | collective-permute-start | bytes 835592 | tf_op jit(solution)/shard_map/ppermute | solution.py:326
  50.8 7.3 %collective-permute-start.18 = (bf16[136,1024]{1,0:T(8,128)(2,1)S(1)}, bf16[136,1024]{1,0:T(8,128)(2,1)S(1)}, u32[]{:S(2)}, u32[]{:S(2)}) collective-permute-start(bf16[136,1024]{1,0:T(8,128)(2,1)S(1)} %get-tuple-element.48.refs_16_), channel_id=1, source_target_pairs={{0,4},{1,3},{4,8},{5,1},{8,12},{9,5},{12,14},{13,9},{14,10},{15,13... | collective-permute-start | bytes 835592 | tf_op jit(solution)/shard_map/ppermute | solution.py:326
  52.4 8.7 %collective-permute-start.19 = (bf16[136,1024]{1,0:T(8,128)(2,1)S(1)}, bf16[136,1024]{1,0:T(8,128)(2,1)S(1)}, u32[]{:S(2)}, u32[]{:S(2)}) collective-permute-start(bf16[136,1024]{1,0:T(8,128)(2,1)S(1)} %collective-permute-done.17.refs_17_), channel_id=1, source_target_pairs={{0,4},{1,3},{4,8},{5,1},{8,12},{9,5},{12,14},{13,9},{14,10},{15,13... | collective-permute-start | bytes 835592 | tf_op jit(solution)/shard_map/ppermute | solution.py:326
  58.2 7.1 %collective-permute-start.20 = (bf16[136,1024]{1,0:T(8,128)(2,1)S(1)}, bf16[136,1024]{1,0:T(8,128)(2,1)S(1)}, u32[]{:S(2)}, u32[]{:S(2)}) collective-permute-start(bf16[136,1024]{1,0:T(8,128)(2,1)S(1)} %collective-permute-done.18.refs_10_), channel_id=1, source_target_pairs={{0,4},{1,3},{4,8},{5,1},{8,12},{9,5},{12,14},{13,9},{14,10},{15,13... | collective-permute-start | bytes 835592 | tf_op jit(solution)/shard_map/ppermute | solution.py:326
  61.1 7.1 %collective-permute-start.21 = (bf16[136,1024]{1,0:T(8,128)(2,1)S(1)}, bf16[136,1024]{1,0:T(8,128)(2,1)S(1)}, u32[]{:S(2)}, u32[]{:S(2)}) collective-permute-start(bf16[136,1024]{1,0:T(8,128)(2,1)S(1)} %collective-permute-done.19.refs_11_), channel_id=1, source_target_pairs={{0,4},{1,3},{4,8},{5,1},{8,12},{9,5},{12,14},{13,9},{14,10},{15,13... | collective-permute-start | bytes 835592 | tf_op jit(solution)/shard_map/ppermute | solution.py:326
  62.0 7.1 %collective-permute-start.9 = (bf16[4,128,128]{2,1,0:T(8,128)(2,1)S(1)}, bf16[4,128,128]{2,1,0:T(8,128)(2,1)S(1)}, u32[]{:S(2)}, u32[]{:S(2)}) collective-permute-start(bf16[4,128,128]{2,1,0:T(8,128)(2,1)S(1)} %get-tuple-element.40.refs_0_), channel_id=1, source_target_pairs={{0,1},{1,0},{2,3},{3,2},{4,5},{5,4},{6,7},{7,6},{8,9},{9,8},{10,11... | collective-permute-start | bytes 393224 | tf_op jit(solution)/shard_map/ppermute | solution.py:329
  65.3 8.1 %collective-permute-start.22 = (bf16[136,1024]{1,0:T(8,128)(2,1)S(1)}, bf16[136,1024]{1,0:T(8,128)(2,1)S(1)}, u32[]{:S(2)}, u32[]{:S(2)}) collective-permute-start(bf16[136,1024]{1,0:T(8,128)(2,1)S(1)} %collective-permute-done.20.refs_12_), channel_id=1, source_target_pairs={{0,4},{1,3},{4,8},{5,1},{8,12},{9,5},{12,14},{13,9},{14,10},{15,13... | collective-permute-start | bytes 835592 | tf_op jit(solution)/shard_map/ppermute | solution.py:326
  68.3 6.5 %collective-permute-start.23 = (bf16[136,1024]{1,0:T(8,128)(2,1)S(1)}, bf16[136,1024]{1,0:T(8,128)(2,1)S(1)}, u32[]{:S(2)}, u32[]{:S(2)}) collective-permute-start(bf16[136,1024]{1,0:T(8,128)(2,1)S(1)} %collective-permute-done.21.refs_13_), channel_id=1, source_target_pairs={{0,4},{1,3},{4,8},{5,1},{8,12},{9,5},{12,14},{13,9},{14,10},{15,13... | collective-permute-start | bytes 835592 | tf_op jit(solution)/shard_map/ppermute | solution.py:326
  68.5 1.3 collective-permute-start.10
  68.6 1.4 collective-permute-start.11
  69.0 1.3 collective-permute-start.12
  70.4 20.1 %copy-start.1 = (bf16[1,512,2048]{2,1,0:T(8,128)(2,1)S(1)}, bf16[1,512,2048]{2,1,0:T(8,128)(2,1)}, u32[]{:S(2)}) copy-start(bf16[1,512,2048]{2,1,0:T(8,128)(2,1)} %refs_5_.15) | copy-start | bytes 6291460
  73.4 5.5 %copy-start.6 = (bf16[128,2048]{1,0:T(8,128)(2,1)S(1)}, bf16[128,2048]{1,0:T(8,128)(2,1)}, u32[]{:S(2)}) copy-start(bf16[128,2048]{1,0:T(8,128)(2,1)} %resid_ref.1) | copy-start | bytes 1572868
  73.4 5.5 %copy-start.8 = (f32[2048]{0:T(1024)S(1)}, f32[2048]{0:T(1024)}, u32[]{:S(2)}) copy-start(f32[2048]{0:T(1024)} %param.18) | copy-start | bytes 24580
  74.8 15.7 %copy-start = (bf16[1,2048,1024]{2,1,0:T(8,128)(2,1)S(1)}, bf16[1,2048,1024]{2,1,0:T(8,128)(2,1)}, u32[]{:S(2)}) copy-start(bf16[1,2048,1024]{2,1,0:T(8,128)(2,1)} %refs_4_.15) | copy-start | bytes 12582916
  77.0 2.0 %collective-permute-start.24 = (f32[128,1024]{1,0:T(8,128)S(1)}, f32[128,1024]{1,0:T(8,128)S(1)}, u32[]{:S(2)}, u32[]{:S(2)}) collective-permute-start(f32[128,1024]{1,0:T(8,128)S(1)} %get-tuple-element.52), channel_id=1, source_target_pairs={{0,1},{1,0},{2,3},{3,2},{4,5},{5,4},{6,7},{7,6},{8,9},{9,8},{10,11... | collective-permute-start | bytes 1572872 | tf_op jit(solution)/shard_map/ppermute | solution.py:329
  79.3 9.2 %collective-permute-start.26 = (bf16[128,2048]{1,0:T(8,128)(2,1)S(1)}, bf16[128,2048]{1,0:T(8,128)(2,1)S(1)}, u32[]{:S(2)}, u32[]{:S(2)}) collective-permute-start(bf16[128,2048]{1,0:T(8,128)(2,1)S(1)} %get-tuple-element.54.refs_0_), channel_id=1, source_target_pairs={{0,4},{1,3},{4,8},{5,1},{8,12},{9,5},{12,14},{13,9},{14,10},{15,13... | collective-permute-start | bytes 1572872 | tf_op jit(solution)/shard_map/ppermute | solution.py:326
  88.6 1.9 %collective-permute-start.46 = (bf16[128,2048]{1,0:T(8,128)(2,1)S(1)}, bf16[128,2048]{1,0:T(8,128)(2,1)S(1)}, u32[]{:S(2)}, u32[]{:S(2)}) collective-permute-start(bf16[128,2048]{1,0:T(8,128)(2,1)S(1)} %collective-permute-done.26.refs_0_), channel_id=1, source_target_pairs={{0,1},{1,0},{2,3},{3,2},{4,5},{5,4},{6,7},{7,6},{8,9},{9,8},{10,11... | collective-permute-start | bytes 1572872 | tf_op jit(solution)/shard_map/ppermute | solution.py:329
  88.6 9.2 %collective-permute-start.27 = (bf16[128,2048]{1,0:T(8,128)(2,1)S(1)}, bf16[128,2048]{1,0:T(8,128)(2,1)S(1)}, u32[]{:S(2)}, u32[]{:S(2)}) collective-permute-start(bf16[128,2048]{1,0:T(8,128)(2,1)S(1)} %collective-permute-done.26.refs_0_), channel_id=1, source_target_pairs={{0,4},{1,3},{4,8},{5,1},{8,12},{9,5},{12,14},{13,9},{14,10},{15,13... | collective-permute-start | bytes 1572872 | tf_op jit(solution)/shard_map/ppermute | solution.py:326
  92.4 5.6 %collective-permute-start.47 = (bf16[128,2048]{1,0:T(8,128)(2,1)S(1)}, bf16[128,2048]{1,0:T(8,128)(2,1)S(1)}, u32[]{:S(2)}, u32[]{:S(2)}) collective-permute-start(bf16[128,2048]{1,0:T(8,128)(2,1)S(1)} %get-tuple-element.72), channel_id=1, source_target_pairs={{0,1},{1,0},{2,3},{3,2},{4,5},{5,4},{6,7},{7,6},{8,9},{9,8},{10,11... | collective-permute-start | bytes 1572872 | tf_op jit(solution)/shard_map/ppermute | solution.py:329
  97.8 2.1 %collective-permute-start.44 = (bf16[128,2048]{1,0:T(8,128)(2,1)S(1)}, bf16[128,2048]{1,0:T(8,128)(2,1)S(1)}, u32[]{:S(2)}, u32[]{:S(2)}) collective-permute-start(bf16[128,2048]{1,0:T(8,128)(2,1)S(1)} %collective-permute-done.27.refs_0_), channel_id=1, source_target_pairs={{0,1},{1,0},{2,3},{3,2},{4,5},{5,4},{6,7},{7,6},{8,9},{9,8},{10,11... | collective-permute-start | bytes 1572872 | tf_op jit(solution)/shard_map/ppermute | solution.py:329
  97.8 9.2 %collective-permute-start.28 = (bf16[128,2048]{1,0:T(8,128)(2,1)S(1)}, bf16[128,2048]{1,0:T(8,128)(2,1)S(1)}, u32[]{:S(2)}, u32[]{:S(2)}) collective-permute-start(bf16[128,2048]{1,0:T(8,128)(2,1)S(1)} %collective-permute-done.27.refs_0_), channel_id=1, source_target_pairs={{0,4},{1,3},{4,8},{5,1},{8,12},{9,5},{12,14},{13,9},{14,10},{15,13... | collective-permute-start | bytes 1572872 | tf_op jit(solution)/shard_map/ppermute | solution.py:326
  98.1 14.4 %collective-permute-start.48 = (bf16[128,2048]{1,0:T(8,128)(2,1)S(1)}, bf16[128,2048]{1,0:T(8,128)(2,1)S(1)}, u32[]{:S(2)}, u32[]{:S(2)}) collective-permute-start(bf16[128,2048]{1,0:T(8,128)(2,1)S(1)} %add.13), channel_id=1, source_target_pairs={{0,4},{1,3},{4,8},{5,1},{8,12},{9,5},{12,14},{13,9},{14,10},{15,13... | collective-permute-start | bytes 1572872 | tf_op jit(solution)/shard_map/ppermute | solution.py:326
  101.8 10.8 %collective-permute-start.45 = (bf16[128,2048]{1,0:T(8,128)(2,1)S(1)}, bf16[128,2048]{1,0:T(8,128)(2,1)S(1)}, u32[]{:S(2)}, u32[]{:S(2)}) collective-permute-start(bf16[128,2048]{1,0:T(8,128)(2,1)S(1)} %get-tuple-element.70), channel_id=1, source_target_pairs={{0,1},{1,0},{2,3},{3,2},{4,5},{5,4},{6,7},{7,6},{8,9},{9,8},{10,11... | collective-permute-start | bytes 1572872 | tf_op jit(solution)/shard_map/ppermute | solution.py:329
  107.0 6.1 %collective-permute-start.42 = (bf16[128,2048]{1,0:T(8,128)(2,1)S(1)}, bf16[128,2048]{1,0:T(8,128)(2,1)S(1)}, u32[]{:S(2)}, u32[]{:S(2)}) collective-permute-start(bf16[128,2048]{1,0:T(8,128)(2,1)S(1)} %collective-permute-done.28.refs_6_.refs_0_), channel_id=1, source_target_pairs={{0,1},{1,0},{2,3},{3,2},{4,5},{5,4},{6,7},{7,6},{8,9},{9,8},{10,11... | collective-permute-start | bytes 1572872 | tf_op jit(solution)/shard_map/ppermute | solution.py:329
  107.0 11.2 %collective-permute-start.30 = (bf16[128,2048]{1,0:T(8,128)(2,1)S(1)}, bf16[128,2048]{1,0:T(8,128)(2,1)S(1)}, u32[]{:S(2)}, u32[]{:S(2)}) collective-permute-start(bf16[128,2048]{1,0:T(8,128)(2,1)S(1)} %collective-permute-done.28.refs_6_.refs_0_), channel_id=1, source_target_pairs={{0,4},{1,3},{4,8},{5,1},{8,12},{9,5},{12,14},{13,9},{14,10},{15,13... | collective-permute-start | bytes 1572872 | tf_op jit(solution)/shard_map/ppermute | solution.py:326
  112.8 11.0 %collective-permute-start.49 = (bf16[128,2048]{1,0:T(8,128)(2,1)S(1)}, bf16[128,2048]{1,0:T(8,128)(2,1)S(1)}, u32[]{:S(2)}, u32[]{:S(2)}) collective-permute-start(bf16[128,2048]{1,0:T(8,128)(2,1)S(1)} %add.14), channel_id=1, source_target_pairs={{0,4},{1,3},{4,8},{5,1},{8,12},{9,5},{12,14},{13,9},{14,10},{15,13... | collective-permute-start | bytes 1572872 | tf_op jit(solution)/shard_map/ppermute | solution.py:326
  114.9 8.9 %collective-permute-start.43 = (bf16[128,2048]{1,0:T(8,128)(2,1)S(1)}, bf16[128,2048]{1,0:T(8,128)(2,1)S(1)}, u32[]{:S(2)}, u32[]{:S(2)}) collective-permute-start(bf16[128,2048]{1,0:T(8,128)(2,1)S(1)} %get-tuple-element.68), channel_id=1, source_target_pairs={{0,1},{1,0},{2,3},{3,2},{4,5},{5,4},{6,7},{7,6},{8,9},{9,8},{10,11... | collective-permute-start | bytes 1572872 | tf_op jit(solution)/shard_map/ppermute | solution.py:329
  118.2 6.1 %collective-permute-start.40 = (bf16[128,2048]{1,0:T(8,128)(2,1)S(1)}, bf16[128,2048]{1,0:T(8,128)(2,1)S(1)}, u32[]{:S(2)}, u32[]{:S(2)}) collective-permute-start(bf16[128,2048]{1,0:T(8,128)(2,1)S(1)} %collective-permute-done.30.refs_0_), channel_id=1, source_target_pairs={{0,1},{1,0},{2,3},{3,2},{4,5},{5,4},{6,7},{7,6},{8,9},{9,8},{10,11... | collective-permute-start | bytes 1572872 | tf_op jit(solution)/shard_map/ppermute | solution.py:329
  118.2 11.2 %collective-permute-start.31 = (bf16[128,2048]{1,0:T(8,128)(2,1)S(1)}, bf16[128,2048]{1,0:T(8,128)(2,1)S(1)}, u32[]{:S(2)}, u32[]{:S(2)}) collective-permute-start(bf16[128,2048]{1,0:T(8,128)(2,1)S(1)} %collective-permute-done.30.refs_0_), channel_id=1, source_target_pairs={{0,4},{1,3},{4,8},{5,1},{8,12},{9,5},{12,14},{13,9},{14,10},{15,13... | collective-permute-start | bytes 1572872 | tf_op jit(solution)/shard_map/ppermute | solution.py:326
  124.0 11.0 %collective-permute-start.50 = (bf16[128,2048]{1,0:T(8,128)(2,1)S(1)}, bf16[128,2048]{1,0:T(8,128)(2,1)S(1)}, u32[]{:S(2)}, u32[]{:S(2)}) collective-permute-start(bf16[128,2048]{1,0:T(8,128)(2,1)S(1)} %add.15), channel_id=1, source_target_pairs={{0,4},{1,3},{4,8},{5,1},{8,12},{9,5},{12,14},{13,9},{14,10},{15,13... | collective-permute-start | bytes 1572872 | tf_op jit(solution)/shard_map/ppermute | solution.py:326
  126.2 8.9 %collective-permute-start.41 = (bf16[128,2048]{1,0:T(8,128)(2,1)S(1)}, bf16[128,2048]{1,0:T(8,128)(2,1)S(1)}, u32[]{:S(2)}, u32[]{:S(2)}) collective-permute-start(bf16[128,2048]{1,0:T(8,128)(2,1)S(1)} %get-tuple-element.66), channel_id=1, source_target_pairs={{0,1},{1,0},{2,3},{3,2},{4,5},{5,4},{6,7},{7,6},{8,9},{9,8},{10,11... | collective-permute-start | bytes 1572872 | tf_op jit(solution)/shard_map/ppermute | solution.py:329
  129.4 6.1 %collective-permute-start.38 = (bf16[128,2048]{1,0:T(8,128)(2,1)S(1)}, bf16[128,2048]{1,0:T(8,128)(2,1)S(1)}, u32[]{:S(2)}, u32[]{:S(2)}) collective-permute-start(bf16[128,2048]{1,0:T(8,128)(2,1)S(1)} %collective-permute-done.31.refs_0_), channel_id=1, source_target_pairs={{0,1},{1,0},{2,3},{3,2},{4,5},{5,4},{6,7},{7,6},{8,9},{9,8},{10,11... | collective-permute-start | bytes 1572872 | tf_op jit(solution)/shard_map/ppermute | solution.py:329
  129.4 11.2 %collective-permute-start.32 = (bf16[128,2048]{1,0:T(8,128)(2,1)S(1)}, bf16[128,2048]{1,0:T(8,128)(2,1)S(1)}, u32[]{:S(2)}, u32[]{:S(2)}) collective-permute-start(bf16[128,2048]{1,0:T(8,128)(2,1)S(1)} %collective-permute-done.31.refs_0_), channel_id=1, source_target_pairs={{0,4},{1,3},{4,8},{5,1},{8,12},{9,5},{12,14},{13,9},{14,10},{15,13... | collective-permute-start | bytes 1572872 | tf_op jit(solution)/shard_map/ppermute | solution.py:326
  135.2 11.0 %collective-permute-start.51 = (bf16[128,2048]{1,0:T(8,128)(2,1)S(1)}, bf16[128,2048]{1,0:T(8,128)(2,1)S(1)}, u32[]{:S(2)}, u32[]{:S(2)}) collective-permute-start(bf16[128,2048]{1,0:T(8,128)(2,1)S(1)} %add.16), channel_id=1, source_target_pairs={{0,4},{1,3},{4,8},{5,1},{8,12},{9,5},{12,14},{13,9},{14,10},{15,13... | collective-permute-start | bytes 1572872 | tf_op jit(solution)/shard_map/ppermute | solution.py:326
  137.4 8.9 %collective-permute-start.39 = (bf16[128,2048]{1,0:T(8,128)(2,1)S(1)}, bf16[128,2048]{1,0:T(8,128)(2,1)S(1)}, u32[]{:S(2)}, u32[]{:S(2)}) collective-permute-start(bf16[128,2048]{1,0:T(8,128)(2,1)S(1)} %get-tuple-element.64), channel_id=1, source_target_pairs={{0,1},{1,0},{2,3},{3,2},{4,5},{5,4},{6,7},{7,6},{8,9},{9,8},{10,11... | collective-permute-start | bytes 1572872 | tf_op jit(solution)/shard_map/ppermute | solution.py:329
  140.7 6.1 %collective-permute-start.36 = (bf16[128,2048]{1,0:T(8,128)(2,1)S(1)}, bf16[128,2048]{1,0:T(8,128)(2,1)S(1)}, u32[]{:S(2)}, u32[]{:S(2)}) collective-permute-start(bf16[128,2048]{1,0:T(8,128)(2,1)S(1)} %collective-permute-done.32.refs_0_), channel_id=1, source_target_pairs={{0,1},{1,0},{2,3},{3,2},{4,5},{5,4},{6,7},{7,6},{8,9},{9,8},{10,11... | collective-permute-start | bytes 1572872 | tf_op jit(solution)/shard_map/ppermute | solution.py:329
  140.7 11.2 %collective-permute-start.33 = (bf16[128,2048]{1,0:T(8,128)(2,1)S(1)}, bf16[128,2048]{1,0:T(8,128)(2,1)S(1)}, u32[]{:S(2)}, u32[]{:S(2)}) collective-permute-start(bf16[128,2048]{1,0:T(8,128)(2,1)S(1)} %collective-permute-done.32.refs_0_), channel_id=1, source_target_pairs={{0,4},{1,3},{4,8},{5,1},{8,12},{9,5},{12,14},{13,9},{14,10},{15,13... | collective-permute-start | bytes 1572872 | tf_op jit(solution)/shard_map/ppermute | solution.py:326
  146.5 11.0 %collective-permute-start.52 = (bf16[128,2048]{1,0:T(8,128)(2,1)S(1)}, bf16[128,2048]{1,0:T(8,128)(2,1)S(1)}, u32[]{:S(2)}, u32[]{:S(2)}) collective-permute-start(bf16[128,2048]{1,0:T(8,128)(2,1)S(1)} %add.17), channel_id=1, source_target_pairs={{0,4},{1,3},{4,8},{5,1},{8,12},{9,5},{12,14},{13,9},{14,10},{15,13... | collective-permute-start | bytes 1572872 | tf_op jit(solution)/shard_map/ppermute | solution.py:326
  148.7 8.9 %collective-permute-start.37 = (bf16[128,2048]{1,0:T(8,128)(2,1)S(1)}, bf16[128,2048]{1,0:T(8,128)(2,1)S(1)}, u32[]{:S(2)}, u32[]{:S(2)}) collective-permute-start(bf16[128,2048]{1,0:T(8,128)(2,1)S(1)} %get-tuple-element.62), channel_id=1, source_target_pairs={{0,1},{1,0},{2,3},{3,2},{4,5},{5,4},{6,7},{7,6},{8,9},{9,8},{10,11... | collective-permute-start | bytes 1572872 | tf_op jit(solution)/shard_map/ppermute | solution.py:329
  151.9 6.3 %collective-permute-start.34 = (bf16[128,2048]{1,0:T(8,128)(2,1)S(1)}, bf16[128,2048]{1,0:T(8,128)(2,1)S(1)}, u32[]{:S(2)}, u32[]{:S(2)}) collective-permute-start(bf16[128,2048]{1,0:T(8,128)(2,1)S(1)} %collective-permute-done.33.refs_0_), channel_id=1, source_target_pairs={{0,1},{1,0},{2,3},{3,2},{4,5},{5,4},{6,7},{7,6},{8,9},{9,8},{10,11... | collective-permute-start | bytes 1572872 | tf_op jit(solution)/shard_map/ppermute | solution.py:329
  151.9 9.4 %collective-permute-start.25 = (bf16[128,2048]{1,0:T(8,128)(2,1)S(1)}, bf16[128,2048]{1,0:T(8,128)(2,1)S(1)}, u32[]{:S(2)}, u32[]{:S(2)}) collective-permute-start(bf16[128,2048]{1,0:T(8,128)(2,1)S(1)} %get-tuple-element.54.refs_0_), channel_id=1, source_target_pairs={{0,1},{1,0},{2,3},{3,2},{4,5},{5,4},{6,7},{7,6},{8,9},{9,8},{10,11... | collective-permute-start | bytes 1572872 | tf_op jit(solution)/shard_map/ppermute | solution.py:329
  157.7 9.5 %collective-permute-start.53 = (bf16[128,2048]{1,0:T(8,128)(2,1)S(1)}, bf16[128,2048]{1,0:T(8,128)(2,1)S(1)}, u32[]{:S(2)}, u32[]{:S(2)}) collective-permute-start(bf16[128,2048]{1,0:T(8,128)(2,1)S(1)} %add.18), channel_id=1, source_target_pairs={{0,4},{1,3},{4,8},{5,1},{8,12},{9,5},{12,14},{13,9},{14,10},{15,13... | collective-permute-start | bytes 1572872 | tf_op jit(solution)/shard_map/ppermute | solution.py:326
  160.1 7.1 %collective-permute-start.35 = (bf16[128,2048]{1,0:T(8,128)(2,1)S(1)}, bf16[128,2048]{1,0:T(8,128)(2,1)S(1)}, u32[]{:S(2)}, u32[]{:S(2)}) collective-permute-start(bf16[128,2048]{1,0:T(8,128)(2,1)S(1)} %get-tuple-element.60), channel_id=1, source_target_pairs={{0,1},{1,0},{2,3},{3,2},{4,5},{5,4},{6,7},{7,6},{8,9},{9,8},{10,11... | collective-permute-start | bytes 1572872 | tf_op jit(solution)/shard_map/ppermute | solution.py:329
  163.2 4.5 %collective-permute-start.29 = (bf16[128,2048]{1,0:T(8,128)(2,1)S(1)}, bf16[128,2048]{1,0:T(8,128)(2,1)S(1)}, u32[]{:S(2)}, u32[]{:S(2)}) collective-permute-start(bf16[128,2048]{1,0:T(8,128)(2,1)S(1)} %get-tuple-element.57), channel_id=1, source_target_pairs={{0,1},{1,0},{2,3},{3,2},{4,5},{5,4},{6,7},{7,6},{8,9},{9,8},{10,11... | collective-permute-start | bytes 1572872 | tf_op jit(solution)/shard_map/ppermute | solution.py:329
  167.4 9.2 %collective-permute-start.54 = (bf16[128,2048]{1,0:T(8,128)(2,1)S(1)}, bf16[128,2048]{1,0:T(8,128)(2,1)S(1)}, u32[]{:S(2)}, u32[]{:S(2)}) collective-permute-start(bf16[128,2048]{1,0:T(8,128)(2,1)S(1)} %add.19), channel_id=1, source_target_pairs={{0,4},{1,3},{4,8},{5,1},{8,12},{9,5},{12,14},{13,9},{14,10},{15,13... | collective-permute-start | bytes 1572872 | tf_op jit(solution)/shard_map/ppermute | solution.py:326
  (3 other events, 2.6 us)

commit v4 on v3

v4 whole, which is shorter than its diff:
```python
import functools
import math

import jax
import jax.numpy as jnp
from jax import lax
from jax.experimental import pallas as pl
from jax.experimental.pallas import tpu as pltpu
from jax.sharding import PartitionSpec as P

HEADS = 16
HD = 128
FF = 512
HOPS_X = 1
HELD = 4
AFTER = {3:0}
TAIL = 5
DEAD = 128.0
FAR_MIB = 60
ATT_MIB = 8
PRO_MIB = 14
EXP_MIB = 16
SPEED = 6.0
F32 = jnp.float32
BF16 = jnp.bfloat16
SMEM = pltpu.SMEM


class Ring:
    def __init__(self, groups, count):
        self.groups, self.count = groups, count
        self.pairs = count // 2
        chips = list(range(0, self.pairs, 2)) + list(range(1, self.pairs, 2))[::-1]
        self.device = [[2 * c, 2 * c + 1] for c in chips]
        self.place = {self.device[i][k]: (i, k) for i in range(self.pairs) for k in (0, 1)}

    def at(self, i, k):
        return self.device[i % self.pairs][k]

    def way(self, g, k):
        return 1 if (g + k) % 2 == 0 else -1

    def step(self, sign):
        route = []
        for g in range(self.groups):
            for e, (i, k) in self.place.items():
                target = self.at(i + sign * self.way(g, k), k)
                route.append((g * self.count + e, g * self.count + target))
        return route

    def sibling(self):
        return [(e, e ^ 1) for e in range(self.count)]

    def source(self, s, flip_lane):
        out = []
        for g in (0, 1):
            for e in range(self.count):
                i, k = self.place[e]
                out.append(self.at(i - s * self.way(g, k), k ^ flip_lane))
        return out


def swap_pairs(axis):
    count = lax.axis_size(axis)
    route = []
    for low in range(0, count - 1, 2):
        route += [(low, low + 1), (low + 1, low)]
    return route


def attend_body(first, count, after, len_ref, q_ref, kv_ref, cache_ref, far_ref, *refs):
    out_ref = refs[after]
    rows = q_ref.shape[0]
    seg = far_ref.shape[1]
    dims = (((1,), (1,)), ((), ()))
    unit = (lax.broadcasted_iota(jnp.int32, (rows, HD), 1) == 0).astype(BF16)
    mark = lax.dot_general(unit, far_ref[0, :, :HD], dims, preferred_element_type=F32)
    near_ok = lax.broadcasted_iota(jnp.int32, (rows, seg), 1) < len_ref[0, 0]
    far_ok = mark < DEAD / 2
    scale = 1.0 / math.sqrt(HD)
    for h in range(count):
        cols = slice((first + h) * HD, (first + h + 1) * HD)
        q = q_ref[:, cols]
        s0 = lax.dot_general(q, kv_ref[0, :, cols], dims, preferred_element_type=F32) * scale
        s1 = lax.dot_general(q, cache_ref[0, 0, 0, :, cols], dims, preferred_element_type=F32) * scale
        s2 = lax.dot_general(q, far_ref[0, :, cols], dims, preferred_element_type=F32) * scale
        s1 = jnp.where(near_ok, s1, -1e30)
        s2 = jnp.where(far_ok, s2, -1e30)
        m = jnp.max(jnp.maximum(jnp.maximum(s0, s1), s2), axis=1, keepdims=True)
        w0 = jnp.exp(s0 - m)
        w1 = jnp.where(near_ok, jnp.exp(s1 - m), 0.0)
        w2 = jnp.where(far_ok, jnp.exp(s2 - m), 0.0)
        l = jnp.sum(w0 + w1 + w2, axis=1, keepdims=True)
        a = jnp.dot(w0.astype(BF16), kv_ref[1, :, cols], preferred_element_type=F32)
        a += jnp.dot(w1.astype(BF16), cache_ref[1, 0, 0, :, cols], preferred_element_type=F32)
        a += jnp.dot(w2.astype(BF16), far_ref[1, :, cols], preferred_element_type=F32)
        out_ref[h] = (a / l).astype(BF16)


def far_body(len_ref, cache_ref, out_ref, sems):
    copies = [pltpu.make_async_copy(cache_ref.at[i, 0, 1], out_ref.at[i], sems.at[i]) for i in (0, 1)]
    for copy in copies:
        copy.start()
    for copy in copies:
        copy.wait()
    row = lax.broadcasted_iota(jnp.int32, out_ref.shape[1:], 0)
    out_ref[0] = jnp.where(row < len_ref[0, 1], out_ref[0].astype(F32), DEAD).astype(BF16)


def far_segment(seg_len, cache_kv):
    return pl.pallas_call(
        far_body,
        out_shape=jax.ShapeDtypeStruct((2,) + cache_kv.shape[3:], BF16),
        in_specs=[scalars(), in_hbm()],
        out_specs=full(),
        scratch_shapes=[pltpu.SemaphoreType.DMA((2,))],
        cost_estimate=cost(1.7),
        compiler_params=pltpu.CompilerParams(vmem_limit_bytes=FAR_MIB * 2**20),
        name="far_segment",
    )(seg_len, cache_kv)


def cost(micros):
    return pl.CostEstimate(flops=int(micros * 1e9 * SPEED), bytes_accessed=1000, transcendentals=0)


def full():
    return pl.BlockSpec(memory_space=pltpu.VMEM)


def scalars():
    return pl.BlockSpec(memory_space=SMEM)


def in_hbm():
    return pl.BlockSpec(memory_space=pltpu.HBM)


def anywhere():
    return pl.BlockSpec(memory_space=pl.ANY)


def attend(first, count, queries, span_kv, cache_kv, far, seg_len, held=None, after=()):
    rows = queries.shape[0]
    out = [jax.ShapeDtypeStruct((count, rows, HD), BF16)]
    passed = [] if held is None else [held]
    out += [jax.ShapeDtypeStruct(p.shape, p.dtype) for p in passed]
    return pl.pallas_call(
        functools.partial(attend_body, first, count, len(passed) + len(after)),
        out_shape=out,
        in_specs=[scalars()] + [full()] * 4 + [anywhere()] * (len(passed) + len(after)),
        out_specs=[full()] + [anywhere()] * len(passed),
        input_output_aliases={5: 1} if passed else {},
        cost_estimate=cost(2.4),
        compiler_params=pltpu.CompilerParams(vmem_limit_bytes=ATT_MIB * 2**20),
        name="attend",
    )(seg_len, queries, span_kv, cache_kv, far, *passed, *after)


def pack_body(count, lane_ref, rows_ref, routes_ref, wts_ref, own_ref, other_ref):
    slab, half = rows_ref.shape[0], own_ref.shape[1]
    lane = lane_ref[0]
    own_ref[:slab] = rows_ref[:, pl.ds(pl.multiple_of(lane * half, HD), half)]
    other_ref[:slab] = rows_ref[:, pl.ds(pl.multiple_of((1 - lane) * half, HD), half)]
    routes = routes_ref[...]
    wts = wts_ref[...]
    tokens = wts.shape[1]
    high, low = [], []
    for group in range(count // 8):
        dense = jnp.concatenate(
            [
                jnp.sum(jnp.where(routes == group * 8 + j, wts, 0.0), axis=0, keepdims=True)
                for j in range(8)
            ],
            axis=0,
        )
        top = dense.astype(BF16)
        high.append(top)
        low.append((dense - top.astype(F32)).astype(BF16))
    tail = jnp.concatenate(high + low, axis=1)
    for out in (own_ref, other_ref):
        out[slab:, : tail.shape[1]] = tail
        if tail.shape[1] < half:
            out[slab:, tail.shape[1] :] = jnp.zeros((8, half - tail.shape[1]), BF16)


def pack(count, lane, o_rows, routes, route_wts):
    slab, width = o_rows.shape
    out = jax.ShapeDtypeStruct((slab + 8, width // 2), BF16)
    return pl.pallas_call(
        functools.partial(pack_body, count),
        out_shape=(out, out),
        in_specs=[scalars()] + [full()] * 3,
        out_specs=(full(), full()),
        cost_estimate=cost(0.7),
        compiler_params=pltpu.CompilerParams(vmem_limit_bytes=8 * 2**20),
        name="pack",
    )(lane, o_rows, routes.T, route_wts.T)


def project_body(first, blocks, pieces, carried, here, tail, table_ref, me_ref, *refs):
    refs = list(refs)
    mine = [refs.pop(0) for _ in range(pieces)]
    theirs = [refs.pop(0) for _ in range(pieces)]
    before = [refs.pop(0) for _ in range(2 if carried else 0)]
    source = [refs.pop(0) for _ in range(blocks)]
    tail_refs = [refs.pop(0) for _ in range(tail // 2)]
    own_ref, give_ref, wts_ref, att = refs[:4]
    rows = own_ref.shape[0]
    slab = att.shape[2]
    count = att.shape[0]
    copies = []
    if here < blocks:
        held, sems = refs[4:]
        away = range(blocks - here)
        copies = [pltpu.make_async_copy(source[b], held.at[b], sems.at[b]) for b in away]
        for copy in copies:
            copy.start()
        source = [held.at[b] for b in away] + source[blocks - here :]
    at = 0
    for a, b in zip(mine, theirs):
        att[at : at + a.shape[0], :rows] = a[...]
        att[at : at + a.shape[0], rows:] = b[...]
        at += a.shape[0]
    place = me_ref[0]
    me = lax.rem(place, count)
    sub, group = lax.rem(me, 8), me // 8
    groups = count // 8
    pick = lax.broadcasted_iota(jnp.int32, (8, rows), 0) == sub

    def line(ref, at):
        high = ref[at : at + 8, pl.ds(pl.multiple_of(group * rows, 128), rows)].astype(F32)
        low = ref[at : at + 8, pl.ds(pl.multiple_of((groups + group) * rows, 128), rows)].astype(F32)
        return jnp.sum(jnp.where(pick, high + low, 0.0), axis=0, keepdims=True)

    total = None
    lines = [None] * blocks
    for b in [*range(blocks - here, blocks), *range(blocks - here)]:
        if b < len(copies):
            copies[b].wait()
        head = att[table_ref[place, first + b]]
        part = jnp.dot(head, source[b][:slab], preferred_element_type=F32)
        total = part if total is None else total + part
        if b >= tail:
            lines[b] = line(source[b], slab)
    for i, ref in enumerate(tail_refs):
        lines[2 * i : 2 * i + 2] = [line(ref, 0), line(ref, 8)]
    if carried:
        own_ref[...] = before[0][...] + total[:rows]
        give_ref[...] = before[1][...] + total[rows:]
    else:
        own_ref[...] = total[:rows]
        give_ref[...] = total[rows:]
    lines.append(jnp.zeros((128 - blocks, rows), F32))
    wts_ref[...] = jnp.concatenate(lines, axis=0).T


def project(table, place, first, mine, theirs, before, blocks, here, tails=()):
    count = sum(part.shape[0] for part in mine)
    rows, slab = mine[0].shape[1:]
    half = blocks[0].shape[1]
    out = jax.ShapeDtypeStruct((rows, half), F32)
    number = len(blocks)
    scratch = [pltpu.VMEM((count, 2 * rows, slab), BF16)]
    away = number - here
    if away:
        scratch += [pltpu.VMEM((away,) + blocks[0].shape, BF16), pltpu.SemaphoreType.DMA((away,))]
    return pl.pallas_call(
        functools.partial(
            project_body, first, number, len(mine), bool(before), here, 2 * len(tails)
        ),
        out_shape=(out, out, jax.ShapeDtypeStruct((rows, 128), F32)),
        in_specs=[scalars(), scalars()]
        + [full()] * (2 * len(mine) + len(before))
        + [in_hbm()] * away
        + [full()] * here
        + [full()] * len(tails),
        out_specs=(full(), full(), full()),
        scratch_shapes=scratch,
        cost_estimate=pl.CostEstimate(
            flops=4 * rows * half * slab * number, bytes_accessed=2 * half * slab * number, transcendentals=0
        ),
        compiler_params=pltpu.CompilerParams(vmem_limit_bytes=PRO_MIB * 2**20),
        name="project",
    )(table, place, *mine, *theirs, *before, *blocks, *tails)


def norm_body(lane_ref, resid_ref, own_ref, got_ref, gain_ref, sum_ref, out_ref):
    first = lane_ref[0] == 0
    half = own_ref.shape[1]
    own = own_ref[...]
    got = got_ref[...]
    low = resid_ref[:, :half].astype(F32) + jnp.where(first, own, got)
    high = resid_ref[:, half:].astype(F32) + jnp.where(first, got, own)
    sum_ref[:, :half] = low
    sum_ref[:, half:] = high
    square = jnp.sum(low * low + high * high, axis=1, keepdims=True)
    scale = lax.rsqrt(square * (1.0 / (2 * half)) + 1e-05)
    out_ref[:, :half] = (low * scale * gain_ref[:, :half]).astype(BF16)
    out_ref[:, half:] = (high * scale * gain_ref[:, half:]).astype(BF16)


def norm(lane, resid, own, got, gain):
    return pl.pallas_call(
        norm_body,
        out_shape=(
            jax.ShapeDtypeStruct(resid.shape, F32),
            jax.ShapeDtypeStruct(resid.shape, BF16),
        ),
        in_specs=[scalars()] + [full()] * 4,
        out_specs=(full(), full()),
        cost_estimate=cost(0.4),
        compiler_params=pltpu.CompilerParams(vmem_limit_bytes=16 * 2**20),
        name="norm",
    )(lane, resid, own, got, gain.reshape(1, -1))


def expert_body(cols, parts, after, *refs):
    refs = list(refs)
    xy, (wx_ref, wy_ref, in_ref, down_ref) = refs[: 2 * parts], refs[2 * parts : 2 * parts + 4]
    cx_ref, *cy_refs = refs[2 * parts + 4 + after :]
    rows, width = cx_ref.shape
    size = rows // parts
    both = jnp.concatenate([ref[...] for ref in xy], axis=0)
    gate = jnp.dot(both, in_ref[0, :, :FF], preferred_element_type=F32)
    up = jnp.dot(both, in_ref[0, :, FF:], preferred_element_type=F32)
    hidden = (gate * jax.nn.sigmoid(gate) * up).astype(BF16)
    wx = wx_ref[:, cols[0] : cols[0] + 1]
    wy = wy_ref[:, cols[1] : cols[1] + 1]
    step = 512
    for at in range(0, width, step):
        out = jnp.dot(hidden, down_ref[0, :, at : at + step], preferred_element_type=F32)
        cx_ref[:, at : at + step] = (out[:rows] * wx).astype(BF16)
        cy = (out[rows:] * wy).astype(BF16)
        for i, cy_ref in enumerate(cy_refs):
            cy_ref[:, at : at + step] = cy[i * size : (i + 1) * size]


def expert(cols, x, y, wx, wy, w_in, w_out, after=()):
    rows, width = wx.shape[0], w_out.shape[2]
    parts = len(x)
    out = jax.ShapeDtypeStruct((rows, width), BF16)
    part = jax.ShapeDtypeStruct((rows // parts, width), BF16)
    return pl.pallas_call(
        functools.partial(expert_body, cols, parts, len(after)),
        out_shape=(out,) + (part,) * parts,
        in_specs=[full()] * (2 * parts + 4) + [anywhere()] * len(after),
        out_specs=(full(),) * (1 + parts),
        cost_estimate=cost(1.9),
        compiler_params=pltpu.CompilerParams(vmem_limit_bytes=EXP_MIB * 2**20),
        name="expert",
    )(*x, *y, wx, wy, w_in, w_out, *after)


def add_body(cuts, *refs):
    total = None
    at = 0
    for cut in cuts:
        term = jnp.concatenate([ref[c].astype(F32) for ref, c in zip(refs[at:], cut)], axis=0)
        at += len(cut)
        total = term if total is None else total + term
    refs[-1][...] = total.astype(BF16)


def add(cut, rows, terms):
    used, cuts = [], []
    for term in terms:
        size = rows // len(term)
        mine = []
        for i, part in enumerate(term):
            low, high = max(cut.start - i * size, 0), min(cut.stop - i * size, size)
            if low < high:
                used.append(part)
                mine.append(slice(low, high))
        cuts.append(mine)
    return pl.pallas_call(
        functools.partial(add_body, cuts),
        out_shape=jax.ShapeDtypeStruct((cut.stop - cut.start, used[0].shape[1]), BF16),
        in_specs=[full()] * len(used),
        out_specs=full(),
        cost_estimate=cost(0.3),
        compiler_params=pltpu.CompilerParams(vmem_limit_bytes=8 * 2**20),
        name="add",
    )(*used)


def shards(
    ring, resid, queries, span_kv, cache_kv, seg_len, o_rows, norm_gain, routes, route_wts, w_in, w_out
):
    count, pairs = ring.count, ring.pairs
    rows, width = queries.shape
    me = lax.axis_index("expert")
    lane = me % 2
    forward, backward, sibling = ring.step(1), ring.step(-1), ring.sibling()
    place = lax.axis_index("group") % 2 * count + me

    def ahead(block, name="rows out"):
        with jax.named_scope(name):
            return lax.ppermute(block, ("group", "expert"), forward)

    def across(block, name="to sibling"):
        with jax.named_scope(name):
            return lax.ppermute(block, "expert", sibling)

    group_swap = swap_pairs("group")
    groups = 4
    heads = HEADS // groups
    wide = heads * HD
    groups = 4
    heads = HEADS // groups
    slab = o_rows.shape[0]
    with jax.named_scope("far segment"):
        far = lax.ppermute(far_segment(seg_len, cache_kv), "group", group_swap)

    chain_a, other = pack(count, lane[None], o_rows, routes, route_wts)
    chain_b = across(other)
    blocks = [chain_a, chain_b]
    mine, theirs = [], []
    chains = [chain_a, chain_b]
    last = []

    def heads_of(j, held=None, after=()):
        part, *held = attend(j * heads, heads, queries, span_kv, cache_kv, far, seg_len, held, after)
        mine.append(part)
        theirs.append(across(part, f"attended {j}"))
        return held

    for s in range(1, pairs - HOPS_X):
        chains = [ahead(part, f"o rows {s}{'ab'[i]}") for i, part in enumerate(chains)]
        if s <= HOPS_X:
            with jax.named_scope("o rows of partner"):
                last.append([lax.ppermute(part, "group", group_swap) for part in chains])
        if s == HELD:
            (chains[0],) = heads_of(0, chains[0])
        blocks += chains
    if HELD == 0:
        heads_of(0)
    for j in range(1, groups):
        heads_of(j, after=last[AFTER[j]] if j in AFTER and AFTER[j] < len(last) else ())
    order = list(range(pairs - 1 - HOPS_X)) + list(range(pairs - HOPS_X, pairs)) + [pairs - 1 - HOPS_X]
    blocks, ends = blocks[:-2], blocks[-2:]
    for pair in reversed(last):
        blocks += pair
    blocks += ends
    tails = []
    with jax.named_scope("gate weights back"):
        tail = jnp.concatenate([blocks[0][slab:], blocks[1][slab:]], axis=0)
        for _ in range(HOPS_X):
            tail = lax.ppermute(tail, ("group", "expert"), backward)
            tails.insert(0, tail)
    sources = []
    for s in order:
        sources += [ring.source(s, 0), ring.source(s, 1)]
    table = jnp.asarray([[line[e] for line in sources] for e in range(2 * count)], jnp.int32)

    if slab != HD:
        mine, theirs = (
            [jnp.concatenate(p).transpose(1, 0, 2).reshape(rows, count, slab).transpose(1, 0, 2)]
            for p in (mine, theirs)
        )
    early = 2 * (pairs - 1 - HOPS_X)
    place = place[None]
    first_own, first_give, wts_early = project(table, place, 0, mine, theirs, [], blocks[:early], 0)
    own, give, wts_late = project(
        table, place, early, mine, theirs, [first_own, first_give], blocks[early:], 2, tails
    )
    got = across(give, "projected")
    residual, normed = norm(lane[None], resid, own, got, norm_gain)

    def gate_at(step, flip):
        column = 2 * order.index(step) + flip
        return (wts_early, column) if column < early else (wts_late, column - early)

    x, y = [normed], [across(normed, "normed")]

    def sums(s, after=()):
        wx, column_x = gate_at(s, 0)
        wy, column_y = gate_at((pairs - s) % pairs, 1)
        keep, give = expert((column_x, column_y), [x[s]], [y[s]], wx, wy, w_in, w_out, after)
        return keep, across(give, f"sums across {s}")

    def combine(terms, parts):
        terms = [term if isinstance(term, list) else [term] for term in terms if len(term)]
        return [
            add(slice(p * rows // parts, (p + 1) * rows // parts), rows, terms) for p in range(parts)
        ]

    travelling = []
    for s in range(1, pairs):
        x.append(ahead(x[-1], f"rows out {s}"))
        y.append(across(x[-1], f"rows across {s}"))
        keep, back = sums(s)
        total = combine([keep, back, travelling], 2 if s >= TAIL else 1)
        travelling = [ahead(part, f"sums out {s}{'ab'[i]}") for i, part in enumerate(total)]
    keep, back = sums(0, (x[min(3, pairs - 1)],))
    return combine([residual, keep, back, travelling], 1)[0]


def solution(mesh):
    placed = (
        P(("group", "expert"), None),
        P(("group", "expert"), None),
        P(None, ("group", "expert"), None),
        P(None, ("group", "expert"), None, None, None),
        P(("group", "expert"), None),
        P("expert", None),
        P(),
        P(("group", "expert"), None),
        P(("group", "expert"), None),
        P("expert", None, None),
        P("expert", None, None),
    )
    ring = Ring(mesh.shape["group"], mesh.shape["expert"])
    return jax.shard_map(
        functools.partial(shards, ring),
        mesh=mesh,
        in_specs=placed,
        out_specs=P(("group", "expert"), None),
        check_vma=False,
    )
```

time: 178 us -> 161 us (0.904)
  waiting for transfers between devices: 96.8 us -> 65.8 us
  starting transfers between devices: 42.3 us -> 54.4 us
  Pallas kernels: 32.4 us -> 36.5 us
  local copies, waits for them, and re-layouts: 5.77 us -> 2.35 us
    ppermute x33, waiting for transfers between devices: 92 us -> 63.9 us  [the longest x29 61 us: ahead(): return lax.ppermute(block, ('group', 'expert'), forward)]
    ppermute x33, starting transfers between devices: 31.6 us -> 50.9 us  [the longest x29 45.4 us: ahead(): return lax.ppermute(block, ('group', 'expert'), forward)]
    ppermute x22, starting transfers between devices: 10.7 us -> 3.47 us  [across(): return lax.ppermute(block, 'expert', sibling)]
    pallas_call x20 -> x24, Pallas kernels: 26.8 us -> 30.6 us  [the longest x8 15 us: expert(): pl.pallas_call(functools.partial(expert_body, cols, parts, len(after)), o...]
    ppermute x22, waiting for transfers between devices: 4.86 us -> 1.97 us  [across(): return lax.ppermute(block, 'expert', sibling)]
    unnamed x24 -> x36, local copies, waits for them, and re-layouts: 3.82 us -> 1.75 us
  transfers between devices with their start and end apart: 55 -> 55, of which waited for: 28 -> 24; matrix products, arithmetic and copies ran while one was open for 1% -> 1% of each run, Pallas kernels for 16% -> 19%
where the time goes in v4:
time: 161 us; the launch traced here: 160 us
  waiting for transfers between devices  65.8 us (41%)
  starting transfers between devices  54.4 us (34%)
  Pallas kernels  36.5 us (23%)
  local copies, waits for them, and re-layouts  2.35 us (1%)
    ppermute x29, waiting for transfers between devices, ahead(): return lax.ppermute(block, ('group', 'expert'), forward)  61 us
    ppermute x29, starting transfers between devices, ahead(): return lax.ppermute(block, ('group', 'expert'), forward)  45.4 us
    pallas_call x8, Pallas kernels, expert(): pl.pallas_call(functools.partial(expert_body, cols, parts, len(after)), o...  15 us
    pallas_call x4, Pallas kernels, attend(): pl.pallas_call(functools.partial(attend_body, first, count, len(passed) +...  10.3 us
    pallas_call x2, Pallas kernels, project(): pl.pallas_call(functools.partial(project_body, first, number, len(mine),...  5.5 us
    ppermute x22, starting transfers between devices, across(): return lax.ppermute(block, 'expert', sibling)  3.47 us
  transfers between devices with their start and end apart: 55, of which 24 were waited for; matrix products, arithmetic and copies ran while one was open for 1% of the time, Pallas kernels for 19%

profile of v4, /device:TPU:0, one launch (start us, length us, event | category | flops | bytes accessed | tf_op | source)
XLA Modules:
  0.0 160.3 jit_solution(17747256599878994786)
XLA Ops:
  0.0 3.1 %far_segment.1 = bf16[2,128,2048]{2,1,0:T(8,128)(2,1)} custom-call(s32[1,2]{1,0:T(1,128)} %len_ref.9, bf16[2,1,2,128,2048]{4,3,2,1,0:T(8,128)(2,1)} %cache_ref.9), custom_call_target="tpu_custom_call" | custom-call | flops 10200000512 | bytes 1000 | tf_op jit(solution)/shard_map/far segment/far_segment/pallas_call | solution.py:111
  3.1 3.0 %collective-permute-start = (bf16[2,128,2048]{2,1,0:T(8,128)(2,1)}, bf16[2,128,2048]{2,1,0:T(8,128)(2,1)}, u32[]{:S(2)}, u32[]{:S(2)}) collective-permute-start(bf16[2,128,2048]{2,1,0:T(8,128)(2,1)} %far_segment.1), channel_id=1, source_target_pairs={{0,16},{16,0},{1,17},{17,1},{2,18},{18,2},{3,19},{19,3},{4,20},{20... | collective-permute-start | bytes 3145736 | tf_op jit(solution)/shard_map/far segment/ppermute | solution.py:413
  6.3 1.6 %collective-permute-start.1 = (bf16[136,1024]{1,0:T(8,128)(2,1)S(1)}, bf16[136,1024]{1,0:T(8,128)(2,1)S(1)}, u32[]{:S(2)}, u32[]{:S(2)}) collective-permute-start(bf16[136,1024]{1,0:T(8,128)(2,1)S(1)} %get-tuple-element.33.refs_8_), channel_id=1, source_target_pairs={{0,4},{1,3},{4,8},{5,1},{8,12},{9,5},{12,14},{13,9},{14,10},{15,13... | collective-permute-start | bytes 835592 | tf_op jit(solution)/shard_map/o rows 1a/ppermute | solution.py:399
  7.9 1.6 collective-permute-start.7
  9.5 3.4 %collective-permute-done.1.refs_10_ = bf16[136,1024]{1,0:T(8,128)(2,1)S(1)} collective-permute-done((bf16[136,1024]{1,0:T(8,128)(2,1)S(1)}, bf16[136,1024]{1,0:T(8,128)(2,1)S(1)}, u32[]{:S(2)}, u32[]{:S(2)}) %collective-permute-start.1) | collective-permute-done | bytes 278560 | tf_op jit(solution)/shard_map/o rows 1a/ppermute | solution.py:399
  12.9 1.6 collective-permute-start.2
  14.5 1.4 collective-permute-done.7.refs_11_
  15.9 1.6 collective-permute-start.13
  17.4 2.0 %collective-permute-done.2.refs_12_ = bf16[136,1024]{1,0:T(8,128)(2,1)S(1)} collective-permute-done((bf16[136,1024]{1,0:T(8,128)(2,1)S(1)}, bf16[136,1024]{1,0:T(8,128)(2,1)S(1)}, u32[]{:S(2)}, u32[]{:S(2)}) %collective-permute-start.2) | collective-permute-done | bytes 278560 | tf_op jit(solution)/shard_map/o rows 2a/ppermute | solution.py:399
  19.4 1.6 collective-permute-start.3
  21.5 1.5 collective-permute-start.8
  23.0 1.6 collective-permute-start.14
  24.6 1.4 collective-permute-done.3.refs_14_
  26.0 1.6 collective-permute-start.4
  27.6 2.8 %collective-permute-done.far_ref = bf16[2,128,2048]{2,1,0:T(8,128)(2,1)} collective-permute-done((bf16[2,128,2048]{2,1,0:T(8,128)(2,1)}, bf16[2,128,2048]{2,1,0:T(8,128)(2,1)}, u32[]{:S(2)}, u32[]{:S(2)}) %collective-permute-start) | collective-permute-done | bytes 1048608 | tf_op jit(solution)/shard_map/far segment/ppermute | solution.py:413
  30.4 2.5 %attend.5.refs_1_ = bf16[4,128,128]{2,1,0:T(8,128)(2,1)S(1)} custom-call(s32[1,2]{1,0:T(1,128)S(1)} %copy-done.17, bf16[128,2048]{1,0:T(8,128)(2,1)S(1)} %copy-done.12, bf16[2,128,2048]{2,1,0:T(8,128)(2,1)S(1)} %copy-done.10, bf16[2,1,2,128,2048]{4,3,2,1,0:T(8,128)(2,1)S(1)} %copy-done.8, bf16[2,128,2048]{2,1,0:T(8,128)(2,1)} %collective-permute-done.far_ref), custom_call_target="tpu_custom_call" | custom-call | flops 14400000000 | bytes 1000 | tf_op jit(solution)/shard_map/attend/pallas_call | solution.py:148
  33.1 2.2 %collective-permute-start.15 = (bf16[136,1024]{1,0:T(8,128)(2,1)S(1)}, bf16[136,1024]{1,0:T(8,128)(2,1)S(1)}, u32[]{:S(2)}, u32[]{:S(2)}) collective-permute-start(bf16[136,1024]{1,0:T(8,128)(2,1)S(1)} %collective-permute-done.14.refs_15_), channel_id=1, source_target_pairs={{0,4},{1,3},{4,8},{5,1},{8,12},{9,5},{12,14},{13,9},{14,10},{15,13... | collective-permute-start | bytes 835592 | tf_op jit(solution)/shard_map/o rows 4b/ppermute | solution.py:399
  35.3 2.5 %attend.4 = (bf16[4,128,128]{2,1,0:T(8,128)(2,1)S(1)}, bf16[136,1024]{1,0:T(8,128)(2,1)S(1)}) custom-call(s32[1,2]{1,0:T(1,128)S(1)} %copy-done.17, bf16[128,2048]{1,0:T(8,128)(2,1)S(1)} %copy-done.12, bf16[2,128,2048]{2,1,0:T(8,128)(2,1)S(1)} %copy-done.10, bf16[2,1,2,128,2048]{4,3,2,1,0:T(8,128)(2,1)S(1)} %copy-done.8, ...), custom_call_target="tpu_custom_call", output_to_operand_aliasing={{1}: (5, {})} | custom-call | flops 14400000000 | bytes 1000 | tf_op jit(solution)/shard_map/attend/pallas_call | solution.py:148
  37.8 1.6 %collective-permute-start.16 = (bf16[136,1024]{1,0:T(8,128)(2,1)S(1)}, bf16[136,1024]{1,0:T(8,128)(2,1)}, u32[]{:S(2)}, u32[]{:S(2)}) collective-permute-start(bf16[136,1024]{1,0:T(8,128)(2,1)S(1)} %get-tuple-element.36.refs_16_), channel_id=1, source_target_pairs={{0,4},{1,3},{4,8},{5,1},{8,12},{9,5},{12,14},{13,9},{14,10},{15,13... | collective-permute-start | bytes 835592 | tf_op jit(solution)/shard_map/o rows 5a/ppermute | solution.py:399
  39.7 2.1 %collective-permute-start.17 = (bf16[136,1024]{1,0:T(8,128)(2,1)S(1)}, bf16[136,1024]{1,0:T(8,128)(2,1)}, u32[]{:S(2)}, u32[]{:S(2)}) collective-permute-start(bf16[136,1024]{1,0:T(8,128)(2,1)S(1)} %collective-permute-done.15.refs_17_), channel_id=1, source_target_pairs={{0,4},{1,3},{4,8},{5,1},{8,12},{9,5},{12,14},{13,9},{14,10},{15,13... | collective-permute-start | bytes 835592 | tf_op jit(solution)/shard_map/o rows 5b/ppermute | solution.py:399
  41.8 2.5 %attend.6.refs_2_ = bf16[4,128,128]{2,1,0:T(8,128)(2,1)S(1)} custom-call(s32[1,2]{1,0:T(1,128)S(1)} %copy-done.17, bf16[128,2048]{1,0:T(8,128)(2,1)S(1)} %copy-done.12, bf16[2,128,2048]{2,1,0:T(8,128)(2,1)S(1)} %copy-done.10, bf16[2,1,2,128,2048]{4,3,2,1,0:T(8,128)(2,1)S(1)} %copy-done.8, bf16[2,128,2048]{2,1,0:T(8,128)(2,1)} %collective-permute-done.far_ref), custom_call_target="tpu_custom_call" | custom-call | flops 14400000000 | bytes 1000 | tf_op jit(solution)/shard_map/attend/pallas_call | solution.py:148
  44.5 1.6 collective-permute-start.18
  46.1 1.4 collective-permute-done.17.refs_19_
  47.5 1.6 collective-permute-start.19
  49.1 2.6 %attend.7.refs_3_ = bf16[4,128,128]{2,1,0:T(8,128)(2,1)S(1)} custom-call(s32[1,2]{1,0:T(1,128)S(1)} %copy-done.17, bf16[128,2048]{1,0:T(8,128)(2,1)S(1)} %copy-done.12, bf16[2,128,2048]{2,1,0:T(8,128)(2,1)S(1)} %copy-done.10, bf16[2,1,2,128,2048]{4,3,2,1,0:T(8,128)(2,1)S(1)} %copy-done.8, bf16[2,128,2048]{2,1,0:T(8,128)(2,1)} %collective-permute-done.far_ref, ...), custom_call_target="tpu_custom_call" | custom-call | flops 14400000000 | bytes 1000 | tf_op jit(solution)/shard_map/attend/pallas_call | solution.py:148
  55.8 3.5 %project.2 = (f32[128,1024]{1,0:T(8,128)S(1)}, f32[128,1024]{1,0:T(8,128)S(1)}, f32[128,128]{1,0:T(8,128)S(1)}) custom-call(s32[32,16]{1,0:T(8,128)S(1)} %copy-done.6, s32[1]{0:T(128)} %bitcast.1.me_ref, bf16[4,128,128]{2,1,0:T(8,128)(2,1)S(1)} %get-tuple-element.34.refs_0_, bf16[4,128,128]{2,1,0:T(8,128)(2,1)S(1)} %attend.5.refs_1_, ...), custom_call_target="tpu_custom_call" | custom-call | flops 805306368 | bytes 3145728 | tf_op jit(solution)/shard_map/project/pallas_call | solution.py:268
  59.4 2.0 %project.3 = (f32[128,1024]{1,0:T(8,128)S(1)}, f32[128,1024]{1,0:T(8,128)S(1)}, f32[128,128]{1,0:T(8,128)S(1)}) custom-call(s32[32,16]{1,0:T(8,128)S(1)} %copy-done.6, s32[1]{0:T(128)} %bitcast.1.me_ref, bf16[4,128,128]{2,1,0:T(8,128)(2,1)S(1)} %get-tuple-element.34.refs_0_, bf16[4,128,128]{2,1,0:T(8,128)(2,1)S(1)} %attend.5.refs_1_, ...), custom_call_target="tpu_custom_call" | custom-call | flops 268435456 | bytes 1048576 | tf_op jit(solution)/shard_map/project/pallas_call | solution.py:268
  62.4 1.5 collective-permute-done.21.got_ref
  64.4 1.6 collective-permute-start.23
  65.9 7.7 %collective-permute-done.23.refs_0_ = bf16[128,2048]{1,0:T(8,128)(2,1)S(1)} collective-permute-done((bf16[128,2048]{1,0:T(8,128)(2,1)S(1)}, bf16[128,2048]{1,0:T(8,128)(2,1)S(1)}, u32[]{:S(2)}, u32[]{:S(2)}) %collective-permute-start.23) | collective-permute-done | bytes 524320 | tf_op jit(solution)/shard_map/rows out 1/ppermute | solution.py:399
  73.6 1.5 collective-permute-start.24
  75.5 1.9 %expert.15 = (bf16[128,2048]{1,0:T(8,128)(2,1)S(1)}, bf16[128,2048]{1,0:T(8,128)(2,1)S(1)}) custom-call(bf16[128,2048]{1,0:T(8,128)(2,1)S(1)} %collective-permute-done.23.refs_0_, bf16[128,2048]{1,0:T(8,128)(2,1)S(1)} %collective-permute-done.43.refs_1_, f32[128,128]{1,0:T(8,128)S(1)} %get-tuple-element.43.refs_2_.refs_3_, ...), custom_call_target="tpu_custom_call" | custom-call | flops 11399999488 | bytes 1000 | tf_op jit(solution)/shard_map/expert/pallas_call | solution.py:344
  77.6 5.2 %collective-permute-done.24.refs_0_ = bf16[128,2048]{1,0:T(8,128)(2,1)S(1)} collective-permute-done((bf16[128,2048]{1,0:T(8,128)(2,1)S(1)}, bf16[128,2048]{1,0:T(8,128)(2,1)S(1)}, u32[]{:S(2)}, u32[]{:S(2)}) %collective-permute-start.24) | collective-permute-done | bytes 524320 | tf_op jit(solution)/shard_map/rows out 2/ppermute | solution.py:399
  82.8 1.5 collective-permute-start.25
  85.6 1.9 %expert.14 = (bf16[128,2048]{1,0:T(8,128)(2,1)S(1)}, bf16[128,2048]{1,0:T(8,128)(2,1)S(1)}) custom-call(bf16[128,2048]{1,0:T(8,128)(2,1)S(1)} %collective-permute-done.24.refs_0_, bf16[128,2048]{1,0:T(8,128)(2,1)S(1)} %collective-permute-done.41.refs_1_, f32[128,128]{1,0:T(8,128)S(1)} %get-tuple-element.43.refs_2_.refs_3_, ...), custom_call_target="tpu_custom_call" | custom-call | flops 11399999488 | bytes 1000 | tf_op jit(solution)/shard_map/expert/pallas_call | solution.py:344
  87.5 4.4 %collective-permute-done.25.refs_6_.refs_0_ = bf16[128,2048]{1,0:T(8,128)(2,1)S(1)} collective-permute-done((bf16[128,2048]{1,0:T(8,128)(2,1)S(1)}, bf16[128,2048]{1,0:T(8,128)(2,1)S(1)}, u32[]{:S(2)}, u32[]{:S(2)}) %collective-permute-start.25) | collective-permute-done | bytes 524320 | tf_op jit(solution)/shard_map/rows out 3/ppermute | solution.py:399
  92.0 1.5 collective-permute-start.27
  93.5 4.1 %collective-permute-done.45.refs_2_ = bf16[128,2048]{1,0:T(8,128)(2,1)S(1)} collective-permute-done((bf16[128,2048]{1,0:T(8,128)(2,1)S(1)}, bf16[128,2048]{1,0:T(8,128)(2,1)S(1)}, u32[]{:S(2)}, u32[]{:S(2)}) %collective-permute-start.45) | collective-permute-done | bytes 524320 | tf_op jit(solution)/shard_map/sums out 1a/ppermute | solution.py:399
  97.8 1.6 collective-permute-start.46
  99.4 1.9 %expert.13 = (bf16[128,2048]{1,0:T(8,128)(2,1)S(1)}, bf16[128,2048]{1,0:T(8,128)(2,1)S(1)}) custom-call(bf16[128,2048]{1,0:T(8,128)(2,1)S(1)} %collective-permute-done.25.refs_6_.refs_0_, bf16[128,2048]{1,0:T(8,128)(2,1)S(1)} %collective-permute-done.39.refs_1_, f32[128,128]{1,0:T(8,128)S(1)} %get-tuple-element.43.refs_2_.refs_3_, ...), custom_call_target="tpu_custom_call" | custom-call | flops 11399999488 | bytes 1000 | tf_op jit(solution)/shard_map/expert/pallas_call | solution.py:344
  101.3 1.9 %collective-permute-done.27.refs_0_ = bf16[128,2048]{1,0:T(8,128)(2,1)S(1)} collective-permute-done((bf16[128,2048]{1,0:T(8,128)(2,1)S(1)}, bf16[128,2048]{1,0:T(8,128)(2,1)S(1)}, u32[]{:S(2)}, u32[]{:S(2)}) %collective-permute-start.27) | collective-permute-done | bytes 524320 | tf_op jit(solution)/shard_map/rows out 4/ppermute | solution.py:399
  103.2 1.5 collective-permute-start.28
  104.7 4.1 %collective-permute-done.46.refs_2_ = bf16[128,2048]{1,0:T(8,128)(2,1)S(1)} collective-permute-done((bf16[128,2048]{1,0:T(8,128)(2,1)S(1)}, bf16[128,2048]{1,0:T(8,128)(2,1)S(1)}, u32[]{:S(2)}, u32[]{:S(2)}) %collective-permute-start.46) | collective-permute-done | bytes 524320 | tf_op jit(solution)/shard_map/sums out 2a/ppermute | solution.py:399
  109.0 1.6 collective-permute-start.47
  110.6 1.9 %expert.12 = (bf16[128,2048]{1,0:T(8,128)(2,1)S(1)}, bf16[128,2048]{1,0:T(8,128)(2,1)S(1)}) custom-call(bf16[128,2048]{1,0:T(8,128)(2,1)S(1)} %collective-permute-done.27.refs_0_, bf16[128,2048]{1,0:T(8,128)(2,1)S(1)} %collective-permute-done.37.refs_1_, f32[128,128]{1,0:T(8,128)S(1)} %get-tuple-element.43.refs_2_.refs_3_, ...), custom_call_target="tpu_custom_call" | custom-call | flops 11399999488 | bytes 1000 | tf_op jit(solution)/shard_map/expert/pallas_call | solution.py:344
  112.5 1.9 %collective-permute-done.28.refs_0_ = bf16[128,2048]{1,0:T(8,128)(2,1)S(1)} collective-permute-done((bf16[128,2048]{1,0:T(8,128)(2,1)S(1)}, bf16[128,2048]{1,0:T(8,128)(2,1)S(1)}, u32[]{:S(2)}, u32[]{:S(2)}) %collective-permute-start.28) | collective-permute-done | bytes 524320 | tf_op jit(solution)/shard_map/rows out 5/ppermute | solution.py:399
  114.4 1.5 collective-permute-start.29
  116.0 4.1 %collective-permute-done.47.refs_2_ = bf16[128,2048]{1,0:T(8,128)(2,1)S(1)} collective-permute-done((bf16[128,2048]{1,0:T(8,128)(2,1)S(1)}, bf16[128,2048]{1,0:T(8,128)(2,1)S(1)}, u32[]{:S(2)}, u32[]{:S(2)}) %collective-permute-start.47) | collective-permute-done | bytes 524320 | tf_op jit(solution)/shard_map/sums out 3a/ppermute | solution.py:399
  120.2 1.6 collective-permute-start.48
  121.8 3.8 %collective-permute-done.29.refs_0_ = bf16[128,2048]{1,0:T(8,128)(2,1)S(1)} collective-permute-done((bf16[128,2048]{1,0:T(8,128)(2,1)S(1)}, bf16[128,2048]{1,0:T(8,128)(2,1)S(1)}, u32[]{:S(2)}, u32[]{:S(2)}) %collective-permute-start.29) | collective-permute-done | bytes 524320 | tf_op jit(solution)/shard_map/rows out 6/ppermute | solution.py:399
  125.7 1.9 %expert.11 = (bf16[128,2048]{1,0:T(8,128)(2,1)S(1)}, bf16[128,2048]{1,0:T(8,128)(2,1)S(1)}) custom-call(bf16[128,2048]{1,0:T(8,128)(2,1)S(1)} %collective-permute-done.28.refs_0_, bf16[128,2048]{1,0:T(8,128)(2,1)S(1)} %collective-permute-done.35.refs_1_, f32[128,128]{1,0:T(8,128)S(1)} %get-tuple-element.43.refs_2_.refs_3_, ...), custom_call_target="tpu_custom_call" | custom-call | flops 11399999488 | bytes 1000 | tf_op jit(solution)/shard_map/expert/pallas_call | solution.py:344
  128.1 1.5 collective-permute-start.30
  129.7 1.9 %expert.10 = (bf16[128,2048]{1,0:T(8,128)(2,1)S(1)}, bf16[128,2048]{1,0:T(8,128)(2,1)S(1)}) custom-call(bf16[128,2048]{1,0:T(8,128)(2,1)S(1)} %collective-permute-done.29.refs_0_, bf16[128,2048]{1,0:T(8,128)(2,1)S(1)} %collective-permute-done.33.refs_1_, f32[128,128]{1,0:T(8,128)S(1)} %get-tuple-element.46.refs_2_.refs_3_, ...), custom_call_target="tpu_custom_call" | custom-call | flops 11399999488 | bytes 1000 | tf_op jit(solution)/shard_map/expert/pallas_call | solution.py:344
  131.7 1.2 collective-permute-start.49
  133.0 4.3 %collective-permute-done.30.refs_0_ = bf16[128,2048]{1,0:T(8,128)(2,1)S(1)} collective-permute-done((bf16[128,2048]{1,0:T(8,128)(2,1)S(1)}, bf16[128,2048]{1,0:T(8,128)(2,1)S(1)}, u32[]{:S(2)}, u32[]{:S(2)}) %collective-permute-start.30) | collective-permute-done | bytes 524320 | tf_op jit(solution)/shard_map/rows out 7/ppermute | solution.py:399
  137.4 1.6 collective-permute-start.52
  140.2 1.6 collective-permute-start.50
  141.8 2.0 %collective-permute-done.52.refs_2_ = bf16[64,2048]{1,0:T(8,128)(2,1)S(1)} collective-permute-done((bf16[64,2048]{1,0:T(8,128)(2,1)S(1)}, bf16[64,2048]{1,0:T(8,128)(2,1)S(1)}, u32[]{:S(2)}, u32[]{:S(2)}) %collective-permute-start.52) | collective-permute-done | bytes 262176 | tf_op jit(solution)/shard_map/sums out 5b/ppermute | solution.py:399
  143.9 1.6 collective-permute-start.53
  145.5 1.9 %expert.9 = (bf16[128,2048]{1,0:T(8,128)(2,1)S(1)}, bf16[128,2048]{1,0:T(8,128)(2,1)S(1)}) custom-call(bf16[128,2048]{1,0:T(8,128)(2,1)S(1)} %collective-permute-done.30.refs_0_, bf16[128,2048]{1,0:T(8,128)(2,1)S(1)} %collective-permute-done.31.refs_1_, f32[128,128]{1,0:T(8,128)S(1)} %get-tuple-element.46.refs_2_.refs_3_, ...), custom_call_target="tpu_custom_call" | custom-call | flops 11399999488 | bytes 1000 | tf_op jit(solution)/shard_map/expert/pallas_call | solution.py:344
  147.5 1.9 %expert.8 = (bf16[128,2048]{1,0:T(8,128)(2,1)S(1)}, bf16[128,2048]{1,0:T(8,128)(2,1)S(1)}) custom-call(bf16[128,2048]{1,0:T(8,128)(2,1)S(1)} %get-tuple-element.42.refs_0_, bf16[128,2048]{1,0:T(8,128)(2,1)S(1)} %collective-permute-done.22.refs_1_, f32[128,128]{1,0:T(8,128)S(1)} %get-tuple-element.43.refs_2_.refs_3_, ...), custom_call_target="tpu_custom_call" | custom-call | flops 11399999488 | bytes 1000 | tf_op jit(solution)/shard_map/expert/pallas_call | solution.py:344
  151.2 1.6 collective-permute-start.54
  152.8 3.6 %collective-permute-done.51.refs_3_ = bf16[64,2048]{1,0:T(8,128)(2,1)S(1)} collective-permute-done((bf16[64,2048]{1,0:T(8,128)(2,1)S(1)}, bf16[64,2048]{1,0:T(8,128)(2,1)S(1)}, u32[]{:S(2)}, u32[]{:S(2)}) %collective-permute-start.51) | collective-permute-done | bytes 262176 | tf_op jit(solution)/shard_map/sums out 7a/ppermute | solution.py:399
  156.4 2.8 %collective-permute-done.54.refs_4_ = bf16[64,2048]{1,0:T(8,128)(2,1)S(1)} collective-permute-done((bf16[64,2048]{1,0:T(8,128)(2,1)S(1)}, bf16[64,2048]{1,0:T(8,128)(2,1)S(1)}, u32[]{:S(2)}, u32[]{:S(2)}) %collective-permute-start.54) | collective-permute-done | bytes 262176 | tf_op jit(solution)/shard_map/sums out 7b/ppermute | solution.py:399
  (113 shorter events, 14.3 us)
Async XLA Ops:
  0.0 6.1 %copy-start.11 = (bf16[128,2048]{1,0:T(8,128)(2,1)S(1)}, bf16[128,2048]{1,0:T(8,128)(2,1)}, u32[]{:S(2)}) copy-start(bf16[128,2048]{1,0:T(8,128)(2,1)} %rows_ref.1) | copy-start | bytes 1572868
  3.1 27.3 %collective-permute-start = (bf16[2,128,2048]{2,1,0:T(8,128)(2,1)}, bf16[2,128,2048]{2,1,0:T(8,128)(2,1)}, u32[]{:S(2)}, u32[]{:S(2)}) collective-permute-start(bf16[2,128,2048]{2,1,0:T(8,128)(2,1)} %far_segment.1), channel_id=1, source_target_pairs={{0,16},{16,0},{1,17},{17,1},{2,18},{18,2},{3,19},{19,3},{4,20},{20... | collective-permute-start | bytes 3145736 | tf_op jit(solution)/shard_map/far segment/ppermute | solution.py:413
  6.1 24.3 %copy-start.8 = (bf16[2,1,2,128,2048]{4,3,2,1,0:T(8,128)(2,1)S(1)}, bf16[2,1,2,128,2048]{4,3,2,1,0:T(8,128)(2,1)}, u32[]{:S(2)}) copy-start(bf16[2,1,2,128,2048]{4,3,2,1,0:T(8,128)(2,1)} %cache_ref.9) | copy-start | bytes 6291460
  6.1 24.3 %copy-start.10 = (bf16[2,128,2048]{2,1,0:T(8,128)(2,1)S(1)}, bf16[2,128,2048]{2,1,0:T(8,128)(2,1)}, u32[]{:S(2)}) copy-start(bf16[2,128,2048]{2,1,0:T(8,128)(2,1)} %kv_ref.7) | copy-start | bytes 3145732
  6.1 24.3 %copy-start.12 = (bf16[128,2048]{1,0:T(8,128)(2,1)S(1)}, bf16[128,2048]{1,0:T(8,128)(2,1)}, u32[]{:S(2)}) copy-start(bf16[128,2048]{1,0:T(8,128)(2,1)} %q_ref.7) | copy-start | bytes 1572868
  6.1 24.3 %copy-start.17 = (s32[1,2]{1,0:T(1,128)S(1)}, s32[1,2]{1,0:T(1,128)}, u32[]{:S(2)}) copy-start(s32[1,2]{1,0:T(1,128)} %len_ref.9) | copy-start | bytes 28
  6.2 1.7 %collective-permute-start.6 = (bf16[136,1024]{1,0:T(8,128)(2,1)S(1)}, bf16[136,1024]{1,0:T(8,128)(2,1)S(1)}, u32[]{:S(2)}, u32[]{:S(2)}) collective-permute-start(bf16[136,1024]{1,0:T(8,128)(2,1)S(1)} %get-tuple-element.35), channel_id=1, source_target_pairs={{0,1},{1,0},{2,3},{3,2},{4,5},{5,4},{6,7},{7,6},{8,9},{9,8},{10,11... | collective-permute-start | bytes 835592 | tf_op jit(solution)/shard_map/to sibling/ppermute | solution.py:403
  6.3 6.6 %collective-permute-start.1 = (bf16[136,1024]{1,0:T(8,128)(2,1)S(1)}, bf16[136,1024]{1,0:T(8,128)(2,1)S(1)}, u32[]{:S(2)}, u32[]{:S(2)}) collective-permute-start(bf16[136,1024]{1,0:T(8,128)(2,1)S(1)} %get-tuple-element.33.refs_8_), channel_id=1, source_target_pairs={{0,4},{1,3},{4,8},{5,1},{8,12},{9,5},{12,14},{13,9},{14,10},{15,13... | collective-permute-start | bytes 835592 | tf_op jit(solution)/shard_map/o rows 1a/ppermute | solution.py:399
  7.9 8.0 %collective-permute-start.7 = (bf16[136,1024]{1,0:T(8,128)(2,1)S(1)}, bf16[136,1024]{1,0:T(8,128)(2,1)S(1)}, u32[]{:S(2)}, u32[]{:S(2)}) collective-permute-start(bf16[136,1024]{1,0:T(8,128)(2,1)S(1)} %collective-permute-done.6.refs_9_), channel_id=1, source_target_pairs={{0,4},{1,3},{4,8},{5,1},{8,12},{9,5},{12,14},{13,9},{14,10},{15,13... | collective-permute-start | bytes 835592 | tf_op jit(solution)/shard_map/o rows 1b/ppermute | solution.py:399
  12.9 6.5 %collective-permute-start.2 = (bf16[136,1024]{1,0:T(8,128)(2,1)S(1)}, bf16[136,1024]{1,0:T(8,128)(2,1)S(1)}, u32[]{:S(2)}, u32[]{:S(2)}) collective-permute-start(bf16[136,1024]{1,0:T(8,128)(2,1)S(1)} %collective-permute-done.1.refs_10_), channel_id=1, source_target_pairs={{0,4},{1,3},{4,8},{5,1},{8,12},{9,5},{12,14},{13,9},{14,10},{15,13... | collective-permute-start | bytes 835592 | tf_op jit(solution)/shard_map/o rows 2a/ppermute | solution.py:399
  15.9 7.2 %collective-permute-start.13 = (bf16[136,1024]{1,0:T(8,128)(2,1)S(1)}, bf16[136,1024]{1,0:T(8,128)(2,1)S(1)}, u32[]{:S(2)}, u32[]{:S(2)}) collective-permute-start(bf16[136,1024]{1,0:T(8,128)(2,1)S(1)} %collective-permute-done.7.refs_11_), channel_id=1, source_target_pairs={{0,4},{1,3},{4,8},{5,1},{8,12},{9,5},{12,14},{13,9},{14,10},{15,13... | collective-permute-start | bytes 835592 | tf_op jit(solution)/shard_map/o rows 2b/ppermute | solution.py:399
  19.4 6.5 %collective-permute-start.3 = (bf16[136,1024]{1,0:T(8,128)(2,1)S(1)}, bf16[136,1024]{1,0:T(8,128)(2,1)S(1)}, u32[]{:S(2)}, u32[]{:S(2)}) collective-permute-start(bf16[136,1024]{1,0:T(8,128)(2,1)S(1)} %collective-permute-done.2.refs_12_), channel_id=1, source_target_pairs={{0,4},{1,3},{4,8},{5,1},{8,12},{9,5},{12,14},{13,9},{14,10},{15,13... | collective-permute-start | bytes 835592 | tf_op jit(solution)/shard_map/o rows 3a/ppermute | solution.py:399
  21.0 23.4 %collective-permute-start.5 = (bf16[136,1024]{1,0:T(8,128)(2,1)S(1)}, bf16[136,1024]{1,0:T(8,128)(2,1)S(1)}, u32[]{:S(2)}, u32[]{:S(2)}) collective-permute-start(bf16[136,1024]{1,0:T(8,128)(2,1)S(1)} %collective-permute-done.1.refs_10_), channel_id=1, source_target_pairs={{0,16},{16,0},{1,17},{17,1},{2,18},{18,2},{3,19},{19,3},{4,20},{20... | collective-permute-start | bytes 835592 | tf_op jit(solution)/shard_map/o rows of partner/ppermute | solution.py:432
  21.5 27.6 %collective-permute-start.8 = (bf16[136,1024]{1,0:T(8,128)(2,1)S(1)}, bf16[136,1024]{1,0:T(8,128)(2,1)S(1)}, u32[]{:S(2)}, u32[]{:S(2)}) collective-permute-start(bf16[136,1024]{1,0:T(8,128)(2,1)S(1)} %collective-permute-done.7.refs_11_), channel_id=1, source_target_pairs={{0,16},{16,0},{1,17},{17,1},{2,18},{18,2},{3,19},{19,3},{4,20},{20... | collective-permute-start | bytes 835592 | tf_op jit(solution)/shard_map/o rows of partner/ppermute | solution.py:432
  23.0 10.0 %collective-permute-start.14 = (bf16[136,1024]{1,0:T(8,128)(2,1)S(1)}, bf16[136,1024]{1,0:T(8,128)(2,1)S(1)}, u32[]{:S(2)}, u32[]{:S(2)}) collective-permute-start(bf16[136,1024]{1,0:T(8,128)(2,1)S(1)} %collective-permute-done.13.refs_13_), channel_id=1, source_target_pairs={{0,4},{1,3},{4,8},{5,1},{8,12},{9,5},{12,14},{13,9},{14,10},{15,13... | collective-permute-start | bytes 835592 | tf_op jit(solution)/shard_map/o rows 3b/ppermute | solution.py:399
  26.0 9.3 %collective-permute-start.4 = (bf16[136,1024]{1,0:T(8,128)(2,1)S(1)}, bf16[136,1024]{1,0:T(8,128)(2,1)S(1)}, u32[]{:S(2)}, u32[]{:S(2)}) collective-permute-start(bf16[136,1024]{1,0:T(8,128)(2,1)S(1)} %collective-permute-done.3.refs_14_), channel_id=1, source_target_pairs={{0,4},{1,3},{4,8},{5,1},{8,12},{9,5},{12,14},{13,9},{14,10},{15,13... | collective-permute-start | bytes 835592 | tf_op jit(solution)/shard_map/o rows 4a/ppermute | solution.py:399
  33.0 18.9 %collective-permute-start.10 = (bf16[4,128,128]{2,1,0:T(8,128)(2,1)S(1)}, bf16[4,128,128]{2,1,0:T(8,128)(2,1)S(1)}, u32[]{:S(2)}, u32[]{:S(2)}) collective-permute-start(bf16[4,128,128]{2,1,0:T(8,128)(2,1)S(1)} %attend.5.refs_1_), channel_id=1, source_target_pairs={{0,1},{1,0},{2,3},{3,2},{4,5},{5,4},{6,7},{7,6},{8,9},{9,8},{10,11... | collective-permute-start | bytes 393224 | tf_op jit(solution)/shard_map/attended 1/ppermute | solution.py:403
  33.1 6.7 %collective-permute-start.15 = (bf16[136,1024]{1,0:T(8,128)(2,1)S(1)}, bf16[136,1024]{1,0:T(8,128)(2,1)S(1)}, u32[]{:S(2)}, u32[]{:S(2)}) collective-permute-start(bf16[136,1024]{1,0:T(8,128)(2,1)S(1)} %collective-permute-done.14.refs_15_), channel_id=1, source_target_pairs={{0,4},{1,3},{4,8},{5,1},{8,12},{9,5},{12,14},{13,9},{14,10},{15,13... | collective-permute-start | bytes 835592 | tf_op jit(solution)/shard_map/o rows 4b/ppermute | solution.py:399
  37.8 6.5 %copy-start = (bf16[136,1024]{1,0:T(8,128)(2,1)}, bf16[136,1024]{1,0:T(8,128)(2,1)S(1)}, u32[]{:S(2)}) copy-start(bf16[136,1024]{1,0:T(8,128)(2,1)S(1)} %get-tuple-element.36.refs_16_) | copy-start | bytes 835588
  37.8 6.7 %collective-permute-start.16 = (bf16[136,1024]{1,0:T(8,128)(2,1)S(1)}, bf16[136,1024]{1,0:T(8,128)(2,1)}, u32[]{:S(2)}, u32[]{:S(2)}) collective-permute-start(bf16[136,1024]{1,0:T(8,128)(2,1)S(1)} %get-tuple-element.36.refs_16_), channel_id=1, source_target_pairs={{0,4},{1,3},{4,8},{5,1},{8,12},{9,5},{12,14},{13,9},{14,10},{15,13... | collective-permute-start | bytes 835592 | tf_op jit(solution)/shard_map/o rows 5a/ppermute | solution.py:399
  39.7 7.8 %collective-permute-start.17 = (bf16[136,1024]{1,0:T(8,128)(2,1)S(1)}, bf16[136,1024]{1,0:T(8,128)(2,1)}, u32[]{:S(2)}, u32[]{:S(2)}) collective-permute-start(bf16[136,1024]{1,0:T(8,128)(2,1)S(1)} %collective-permute-done.15.refs_17_), channel_id=1, source_target_pairs={{0,4},{1,3},{4,8},{5,1},{8,12},{9,5},{12,14},{13,9},{14,10},{15,13... | collective-permute-start | bytes 835592 | tf_op jit(solution)/shard_map/o rows 5b/ppermute | solution.py:399
  44.4 7.4 %copy-start.2 = (bf16[136,1024]{1,0:T(8,128)(2,1)}, bf16[136,1024]{1,0:T(8,128)(2,1)S(1)}, u32[]{:S(2)}) copy-start(bf16[136,1024]{1,0:T(8,128)(2,1)S(1)} %collective-permute-done.5.refs_0_.refs_10_) | copy-start | bytes 835588
  44.4 9.3 %collective-permute-start.11 = (bf16[4,128,128]{2,1,0:T(8,128)(2,1)S(1)}, bf16[4,128,128]{2,1,0:T(8,128)(2,1)S(1)}, u32[]{:S(2)}, u32[]{:S(2)}) collective-permute-start(bf16[4,128,128]{2,1,0:T(8,128)(2,1)S(1)} %attend.6.refs_2_), channel_id=1, source_target_pairs={{0,1},{1,0},{2,3},{3,2},{4,5},{5,4},{6,7},{7,6},{8,9},{9,8},{10,11... | collective-permute-start | bytes 393224 | tf_op jit(solution)/shard_map/attended 2/ppermute | solution.py:403
  44.5 14.8 %collective-permute-start.18 = (bf16[136,1024]{1,0:T(8,128)(2,1)}, bf16[136,1024]{1,0:T(8,128)(2,1)}, u32[]{:S(2)}, u32[]{:S(2)}) collective-permute-start(bf16[136,1024]{1,0:T(8,128)(2,1)} %collective-permute-done.16.refs_18_), channel_id=1, source_target_pairs={{0,4},{1,3},{4,8},{5,1},{8,12},{9,5},{12,14},{13,9},{14,10},{15,13... | collective-permute-start | bytes 835592 | tf_op jit(solution)/shard_map/o rows 6a/ppermute | solution.py:399
  47.5 11.9 %collective-permute-start.19 = (bf16[136,1024]{1,0:T(8,128)(2,1)}, bf16[136,1024]{1,0:T(8,128)(2,1)}, u32[]{:S(2)}, u32[]{:S(2)}) collective-permute-start(bf16[136,1024]{1,0:T(8,128)(2,1)} %collective-permute-done.17.refs_19_), channel_id=1, source_target_pairs={{0,4},{1,3},{4,8},{5,1},{8,12},{9,5},{12,14},{13,9},{14,10},{15,13... | collective-permute-start | bytes 835592 | tf_op jit(solution)/shard_map/o rows 6b/ppermute | solution.py:399
  51.8 2.4 %collective-permute-start.12 = (bf16[4,128,128]{2,1,0:T(8,128)(2,1)S(1)}, bf16[4,128,128]{2,1,0:T(8,128)(2,1)S(1)}, u32[]{:S(2)}, u32[]{:S(2)}) collective-permute-start(bf16[4,128,128]{2,1,0:T(8,128)(2,1)S(1)} %attend.7.refs_3_), channel_id=1, source_target_pairs={{0,1},{1,0},{2,3},{3,2},{4,5},{5,4},{6,7},{7,6},{8,9},{9,8},{10,11... | collective-permute-start | bytes 393224 | tf_op jit(solution)/shard_map/attended 3/ppermute | solution.py:403
  51.9 2.3 %collective-permute-start.9 = (bf16[4,128,128]{2,1,0:T(8,128)(2,1)S(1)}, bf16[4,128,128]{2,1,0:T(8,128)(2,1)S(1)}, u32[]{:S(2)}, u32[]{:S(2)}) collective-permute-start(bf16[4,128,128]{2,1,0:T(8,128)(2,1)S(1)} %get-tuple-element.34.refs_0_), channel_id=1, source_target_pairs={{0,1},{1,0},{2,3},{3,2},{4,5},{5,4},{6,7},{7,6},{8,9},{9,8},{10,11... | collective-permute-start | bytes 393224 | tf_op jit(solution)/shard_map/attended 0/ppermute | solution.py:403
  53.7 5.7 %collective-permute-start.20 = (bf16[16,1024]{1,0:T(8,128)(2,1)S(1)}, bf16[16,1024]{1,0:T(8,128)(2,1)S(1)}, u32[]{:S(2)}, u32[]{:S(2)}) collective-permute-start(bf16[16,1024]{1,0:T(8,128)(2,1)S(1)} %pad_maximum_fusion), channel_id=1, source_target_pairs={{0,2},{1,5},{4,0},{5,9},{8,4},{9,13},{12,8},{13,15},{14,12},{15,11... | collective-permute-start | bytes 98312 | tf_op jit(solution)/shard_map/gate weights back/ppermute | solution.py:449
  61.4 2.5 %collective-permute-start.21 = (f32[128,1024]{1,0:T(8,128)S(1)}, f32[128,1024]{1,0:T(8,128)S(1)}, u32[]{:S(2)}, u32[]{:S(2)}) collective-permute-start(f32[128,1024]{1,0:T(8,128)S(1)} %get-tuple-element.40), channel_id=1, source_target_pairs={{0,1},{1,0},{2,3},{3,2},{4,5},{5,4},{6,7},{7,6},{8,9},{9,8},{10,11... | collective-permute-start | bytes 1572872 | tf_op jit(solution)/shard_map/projected/ppermute | solution.py:403
  64.0 11.5 %copy-start.7 = (bf16[1,2048,1024]{2,1,0:T(8,128)(2,1)S(1)}, bf16[1,2048,1024]{2,1,0:T(8,128)(2,1)}, u32[]{:S(2)}) copy-start(bf16[1,2048,1024]{2,1,0:T(8,128)(2,1)} %refs_4_.15) | copy-start | bytes 12582916
  64.0 11.5 %copy-start.9 = (bf16[1,512,2048]{2,1,0:T(8,128)(2,1)S(1)}, bf16[1,512,2048]{2,1,0:T(8,128)(2,1)}, u32[]{:S(2)}) copy-start(bf16[1,512,2048]{2,1,0:T(8,128)(2,1)} %refs_5_.15) | copy-start | bytes 6291460
  64.4 9.2 %collective-permute-start.23 = (bf16[128,2048]{1,0:T(8,128)(2,1)S(1)}, bf16[128,2048]{1,0:T(8,128)(2,1)S(1)}, u32[]{:S(2)}, u32[]{:S(2)}) collective-permute-start(bf16[128,2048]{1,0:T(8,128)(2,1)S(1)} %get-tuple-element.42.refs_0_), channel_id=1, source_target_pairs={{0,4},{1,3},{4,8},{5,1},{8,12},{9,5},{12,14},{13,9},{14,10},{15,13... | collective-permute-start | bytes 1572872 | tf_op jit(solution)/shard_map/rows out 1/ppermute | solution.py:399
  73.6 1.9 %collective-permute-start.43 = (bf16[128,2048]{1,0:T(8,128)(2,1)S(1)}, bf16[128,2048]{1,0:T(8,128)(2,1)S(1)}, u32[]{:S(2)}, u32[]{:S(2)}) collective-permute-start(bf16[128,2048]{1,0:T(8,128)(2,1)S(1)} %collective-permute-done.23.refs_0_), channel_id=1, source_target_pairs={{0,1},{1,0},{2,3},{3,2},{4,5},{5,4},{6,7},{7,6},{8,9},{9,8},{10,11... | collective-permute-start | bytes 1572872 | tf_op jit(solution)/shard_map/rows across 1/ppermute | solution.py:403
  73.6 9.2 %collective-permute-start.24 = (bf16[128,2048]{1,0:T(8,128)(2,1)S(1)}, bf16[128,2048]{1,0:T(8,128)(2,1)S(1)}, u32[]{:S(2)}, u32[]{:S(2)}) collective-permute-start(bf16[128,2048]{1,0:T(8,128)(2,1)S(1)} %collective-permute-done.23.refs_0_), channel_id=1, source_target_pairs={{0,4},{1,3},{4,8},{5,1},{8,12},{9,5},{12,14},{13,9},{14,10},{15,13... | collective-permute-start | bytes 1572872 | tf_op jit(solution)/shard_map/rows out 2/ppermute | solution.py:399
  77.4 6.9 %collective-permute-start.44 = (bf16[128,2048]{1,0:T(8,128)(2,1)S(1)}, bf16[128,2048]{1,0:T(8,128)(2,1)S(1)}, u32[]{:S(2)}, u32[]{:S(2)}) collective-permute-start(bf16[128,2048]{1,0:T(8,128)(2,1)S(1)} %get-tuple-element.60), channel_id=1, source_target_pairs={{0,1},{1,0},{2,3},{3,2},{4,5},{5,4},{6,7},{7,6},{8,9},{9,8},{10,11... | collective-permute-start | bytes 1572872 | tf_op jit(solution)/shard_map/sums across 1/ppermute | solution.py:403
  82.8 2.8 %collective-permute-start.41 = (bf16[128,2048]{1,0:T(8,128)(2,1)S(1)}, bf16[128,2048]{1,0:T(8,128)(2,1)S(1)}, u32[]{:S(2)}, u32[]{:S(2)}) collective-permute-start(bf16[128,2048]{1,0:T(8,128)(2,1)S(1)} %collective-permute-done.24.refs_0_), channel_id=1, source_target_pairs={{0,1},{1,0},{2,3},{3,2},{4,5},{5,4},{6,7},{7,6},{8,9},{9,8},{10,11... | collective-permute-start | bytes 1572872 | tf_op jit(solution)/shard_map/rows across 2/ppermute | solution.py:403
  82.8 9.2 %collective-permute-start.25 = (bf16[128,2048]{1,0:T(8,128)(2,1)S(1)}, bf16[128,2048]{1,0:T(8,128)(2,1)S(1)}, u32[]{:S(2)}, u32[]{:S(2)}) collective-permute-start(bf16[128,2048]{1,0:T(8,128)(2,1)S(1)} %collective-permute-done.24.refs_0_), channel_id=1, source_target_pairs={{0,4},{1,3},{4,8},{5,1},{8,12},{9,5},{12,14},{13,9},{14,10},{15,13... | collective-permute-start | bytes 1572872 | tf_op jit(solution)/shard_map/rows out 3/ppermute | solution.py:399
  84.4 13.1 %collective-permute-start.45 = (bf16[128,2048]{1,0:T(8,128)(2,1)S(1)}, bf16[128,2048]{1,0:T(8,128)(2,1)S(1)}, u32[]{:S(2)}, u32[]{:S(2)}) collective-permute-start(bf16[128,2048]{1,0:T(8,128)(2,1)S(1)} %add.24), channel_id=1, source_target_pairs={{0,4},{1,3},{4,8},{5,1},{8,12},{9,5},{12,14},{13,9},{14,10},{15,13... | collective-permute-start | bytes 1572872 | tf_op jit(solution)/shard_map/sums out 1a/ppermute | solution.py:399
  87.4 10.1 %collective-permute-start.42 = (bf16[128,2048]{1,0:T(8,128)(2,1)S(1)}, bf16[128,2048]{1,0:T(8,128)(2,1)S(1)}, u32[]{:S(2)}, u32[]{:S(2)}) collective-permute-start(bf16[128,2048]{1,0:T(8,128)(2,1)S(1)} %get-tuple-element.58), channel_id=1, source_target_pairs={{0,1},{1,0},{2,3},{3,2},{4,5},{5,4},{6,7},{7,6},{8,9},{9,8},{10,11... | collective-permute-start | bytes 1572872 | tf_op jit(solution)/shard_map/sums across 2/ppermute | solution.py:403
  92.0 7.4 %collective-permute-start.39 = (bf16[128,2048]{1,0:T(8,128)(2,1)S(1)}, bf16[128,2048]{1,0:T(8,128)(2,1)S(1)}, u32[]{:S(2)}, u32[]{:S(2)}) collective-permute-start(bf16[128,2048]{1,0:T(8,128)(2,1)S(1)} %collective-permute-done.25.refs_6_.refs_0_), channel_id=1, source_target_pairs={{0,1},{1,0},{2,3},{3,2},{4,5},{5,4},{6,7},{7,6},{8,9},{9,8},{10,11... | collective-permute-start | bytes 1572872 | tf_op jit(solution)/shard_map/rows across 3/ppermute | solution.py:403
  92.0 11.2 %collective-permute-start.27 = (bf16[128,2048]{1,0:T(8,128)(2,1)S(1)}, bf16[128,2048]{1,0:T(8,128)(2,1)S(1)}, u32[]{:S(2)}, u32[]{:S(2)}) collective-permute-start(bf16[128,2048]{1,0:T(8,128)(2,1)S(1)} %collective-permute-done.25.refs_6_.refs_0_), channel_id=1, source_target_pairs={{0,4},{1,3},{4,8},{5,1},{8,12},{9,5},{12,14},{13,9},{14,10},{15,13... | collective-permute-start | bytes 1572872 | tf_op jit(solution)/shard_map/rows out 4/ppermute | solution.py:399
  97.8 11.0 %collective-permute-start.46 = (bf16[128,2048]{1,0:T(8,128)(2,1)S(1)}, bf16[128,2048]{1,0:T(8,128)(2,1)S(1)}, u32[]{:S(2)}, u32[]{:S(2)}) collective-permute-start(bf16[128,2048]{1,0:T(8,128)(2,1)S(1)} %add.25), channel_id=1, source_target_pairs={{0,4},{1,3},{4,8},{5,1},{8,12},{9,5},{12,14},{13,9},{14,10},{15,13... | collective-permute-start | bytes 1572872 | tf_op jit(solution)/shard_map/sums out 2a/ppermute | solution.py:399
  101.2 7.6 %collective-permute-start.40 = (bf16[128,2048]{1,0:T(8,128)(2,1)S(1)}, bf16[128,2048]{1,0:T(8,128)(2,1)S(1)}, u32[]{:S(2)}, u32[]{:S(2)}) collective-permute-start(bf16[128,2048]{1,0:T(8,128)(2,1)S(1)} %get-tuple-element.56), channel_id=1, source_target_pairs={{0,1},{1,0},{2,3},{3,2},{4,5},{5,4},{6,7},{7,6},{8,9},{9,8},{10,11... | collective-permute-start | bytes 1572872 | tf_op jit(solution)/shard_map/sums across 3/ppermute | solution.py:403
  103.2 7.4 %collective-permute-start.37 = (bf16[128,2048]{1,0:T(8,128)(2,1)S(1)}, bf16[128,2048]{1,0:T(8,128)(2,1)S(1)}, u32[]{:S(2)}, u32[]{:S(2)}) collective-permute-start(bf16[128,2048]{1,0:T(8,128)(2,1)S(1)} %collective-permute-done.27.refs_0_), channel_id=1, source_target_pairs={{0,1},{1,0},{2,3},{3,2},{4,5},{5,4},{6,7},{7,6},{8,9},{9,8},{10,11... | collective-permute-start | bytes 1572872 | tf_op jit(solution)/shard_map/rows across 4/ppermute | solution.py:403
  103.2 11.2 %collective-permute-start.28 = (bf16[128,2048]{1,0:T(8,128)(2,1)S(1)}, bf16[128,2048]{1,0:T(8,128)(2,1)S(1)}, u32[]{:S(2)}, u32[]{:S(2)}) collective-permute-start(bf16[128,2048]{1,0:T(8,128)(2,1)S(1)} %collective-permute-done.27.refs_0_), channel_id=1, source_target_pairs={{0,4},{1,3},{4,8},{5,1},{8,12},{9,5},{12,14},{13,9},{14,10},{15,13... | collective-permute-start | bytes 1572872 | tf_op jit(solution)/shard_map/rows out 5/ppermute | solution.py:399
  109.0 11.0 %collective-permute-start.47 = (bf16[128,2048]{1,0:T(8,128)(2,1)S(1)}, bf16[128,2048]{1,0:T(8,128)(2,1)S(1)}, u32[]{:S(2)}, u32[]{:S(2)}) collective-permute-start(bf16[128,2048]{1,0:T(8,128)(2,1)S(1)} %add.26), channel_id=1, source_target_pairs={{0,4},{1,3},{4,8},{5,1},{8,12},{9,5},{12,14},{13,9},{14,10},{15,13... | collective-permute-start | bytes 1572872 | tf_op jit(solution)/shard_map/sums out 3a/ppermute | solution.py:399
  112.5 7.6 %collective-permute-start.38 = (bf16[128,2048]{1,0:T(8,128)(2,1)S(1)}, bf16[128,2048]{1,0:T(8,128)(2,1)S(1)}, u32[]{:S(2)}, u32[]{:S(2)}) collective-permute-start(bf16[128,2048]{1,0:T(8,128)(2,1)S(1)} %get-tuple-element.54), channel_id=1, source_target_pairs={{0,1},{1,0},{2,3},{3,2},{4,5},{5,4},{6,7},{7,6},{8,9},{9,8},{10,11... | collective-permute-start | bytes 1572872 | tf_op jit(solution)/shard_map/sums across 4/ppermute | solution.py:403
  114.4 11.2 %collective-permute-start.29 = (bf16[128,2048]{1,0:T(8,128)(2,1)S(1)}, bf16[128,2048]{1,0:T(8,128)(2,1)S(1)}, u32[]{:S(2)}, u32[]{:S(2)}) collective-permute-start(bf16[128,2048]{1,0:T(8,128)(2,1)S(1)} %collective-permute-done.28.refs_0_), channel_id=1, source_target_pairs={{0,4},{1,3},{4,8},{5,1},{8,12},{9,5},{12,14},{13,9},{14,10},{15,13... | collective-permute-start | bytes 1572872 | tf_op jit(solution)/shard_map/rows out 6/ppermute | solution.py:399
  116.0 9.7 %collective-permute-start.35 = (bf16[128,2048]{1,0:T(8,128)(2,1)S(1)}, bf16[128,2048]{1,0:T(8,128)(2,1)S(1)}, u32[]{:S(2)}, u32[]{:S(2)}) collective-permute-start(bf16[128,2048]{1,0:T(8,128)(2,1)S(1)} %collective-permute-done.28.refs_0_), channel_id=1, source_target_pairs={{0,1},{1,0},{2,3},{3,2},{4,5},{5,4},{6,7},{7,6},{8,9},{9,8},{10,11... | collective-permute-start | bytes 1572872 | tf_op jit(solution)/shard_map/rows across 5/ppermute | solution.py:403
  120.2 11.4 %collective-permute-start.48 = (bf16[128,2048]{1,0:T(8,128)(2,1)S(1)}, bf16[128,2048]{1,0:T(8,128)(2,1)S(1)}, u32[]{:S(2)}, u32[]{:S(2)}) collective-permute-start(bf16[128,2048]{1,0:T(8,128)(2,1)S(1)} %add.27), channel_id=1, source_target_pairs={{0,4},{1,3},{4,8},{5,1},{8,12},{9,5},{12,14},{13,9},{14,10},{15,13... | collective-permute-start | bytes 1572872 | tf_op jit(solution)/shard_map/sums out 4a/ppermute | solution.py:399
  125.7 4.0 %collective-permute-start.33 = (bf16[128,2048]{1,0:T(8,128)(2,1)S(1)}, bf16[128,2048]{1,0:T(8,128)(2,1)S(1)}, u32[]{:S(2)}, u32[]{:S(2)}) collective-permute-start(bf16[128,2048]{1,0:T(8,128)(2,1)S(1)} %collective-permute-done.29.refs_0_), channel_id=1, source_target_pairs={{0,1},{1,0},{2,3},{3,2},{4,5},{5,4},{6,7},{7,6},{8,9},{9,8},{10,11... | collective-permute-start | bytes 1572872 | tf_op jit(solution)/shard_map/rows across 6/ppermute | solution.py:403
  127.5 4.1 %collective-permute-start.36 = (bf16[128,2048]{1,0:T(8,128)(2,1)S(1)}, bf16[128,2048]{1,0:T(8,128)(2,1)S(1)}, u32[]{:S(2)}, u32[]{:S(2)}) collective-permute-start(bf16[128,2048]{1,0:T(8,128)(2,1)S(1)} %get-tuple-element.52), channel_id=1, source_target_pairs={{0,1},{1,0},{2,3},{3,2},{4,5},{5,4},{6,7},{7,6},{8,9},{9,8},{10,11... | collective-permute-start | bytes 1572872 | tf_op jit(solution)/shard_map/sums across 5/ppermute | solution.py:403
  128.1 9.2 %collective-permute-start.30 = (bf16[128,2048]{1,0:T(8,128)(2,1)S(1)}, bf16[128,2048]{1,0:T(8,128)(2,1)S(1)}, u32[]{:S(2)}, u32[]{:S(2)}) collective-permute-start(bf16[128,2048]{1,0:T(8,128)(2,1)S(1)} %collective-permute-done.29.refs_0_), channel_id=1, source_target_pairs={{0,4},{1,3},{4,8},{5,1},{8,12},{9,5},{12,14},{13,9},{14,10},{15,13... | collective-permute-start | bytes 1572872 | tf_op jit(solution)/shard_map/rows out 7/ppermute | solution.py:399
  131.5 8.6 %collective-permute-start.34 = (bf16[128,2048]{1,0:T(8,128)(2,1)S(1)}, bf16[128,2048]{1,0:T(8,128)(2,1)S(1)}, u32[]{:S(2)}, u32[]{:S(2)}) collective-permute-start(bf16[128,2048]{1,0:T(8,128)(2,1)S(1)} %get-tuple-element.50), channel_id=1, source_target_pairs={{0,1},{1,0},{2,3},{3,2},{4,5},{5,4},{6,7},{7,6},{8,9},{9,8},{10,11... | collective-permute-start | bytes 1572872 | tf_op jit(solution)/shard_map/sums across 6/ppermute | solution.py:403
  131.7 8.4 %collective-permute-start.49 = (bf16[64,2048]{1,0:T(8,128)(2,1)S(1)}, bf16[64,2048]{1,0:T(8,128)(2,1)S(1)}, u32[]{:S(2)}, u32[]{:S(2)}) collective-permute-start(bf16[64,2048]{1,0:T(8,128)(2,1)S(1)} %add.28), channel_id=1, source_target_pairs={{0,4},{1,3},{4,8},{5,1},{8,12},{9,5},{12,14},{13,9},{14,10},{15,13... | collective-permute-start | bytes 786440 | tf_op jit(solution)/shard_map/sums out 5a/ppermute | solution.py:399
  137.3 8.2 %collective-permute-start.31 = (bf16[128,2048]{1,0:T(8,128)(2,1)S(1)}, bf16[128,2048]{1,0:T(8,128)(2,1)S(1)}, u32[]{:S(2)}, u32[]{:S(2)}) collective-permute-start(bf16[128,2048]{1,0:T(8,128)(2,1)S(1)} %collective-permute-done.30.refs_0_), channel_id=1, source_target_pairs={{0,1},{1,0},{2,3},{3,2},{4,5},{5,4},{6,7},{7,6},{8,9},{9,8},{10,11... | collective-permute-start | bytes 1572872 | tf_op jit(solution)/shard_map/rows across 7/ppermute | solution.py:403
  137.4 6.4 %collective-permute-start.52 = (bf16[64,2048]{1,0:T(8,128)(2,1)S(1)}, bf16[64,2048]{1,0:T(8,128)(2,1)S(1)}, u32[]{:S(2)}, u32[]{:S(2)}) collective-permute-start(bf16[64,2048]{1,0:T(8,128)(2,1)S(1)} %add.31), channel_id=1, source_target_pairs={{0,4},{1,3},{4,8},{5,1},{8,12},{9,5},{12,14},{13,9},{14,10},{15,13... | collective-permute-start | bytes 786440 | tf_op jit(solution)/shard_map/sums out 5b/ppermute | solution.py:399
  139.0 8.5 %collective-permute-start.22 = (bf16[128,2048]{1,0:T(8,128)(2,1)S(1)}, bf16[128,2048]{1,0:T(8,128)(2,1)S(1)}, u32[]{:S(2)}, u32[]{:S(2)}) collective-permute-start(bf16[128,2048]{1,0:T(8,128)(2,1)S(1)} %get-tuple-element.42.refs_0_), channel_id=1, source_target_pairs={{0,1},{1,0},{2,3},{3,2},{4,5},{5,4},{6,7},{7,6},{8,9},{9,8},{10,11... | collective-permute-start | bytes 1572872 | tf_op jit(solution)/shard_map/normed/ppermute | solution.py:403
  140.2 9.7 %collective-permute-start.50 = (bf16[64,2048]{1,0:T(8,128)(2,1)S(1)}, bf16[64,2048]{1,0:T(8,128)(2,1)S(1)}, u32[]{:S(2)}, u32[]{:S(2)}) collective-permute-start(bf16[64,2048]{1,0:T(8,128)(2,1)S(1)} %add.29), channel_id=1, source_target_pairs={{0,4},{1,3},{4,8},{5,1},{8,12},{9,5},{12,14},{13,9},{14,10},{15,13... | collective-permute-start | bytes 786440 | tf_op jit(solution)/shard_map/sums out 6a/ppermute | solution.py:399
  143.9 7.2 %collective-permute-start.53 = (bf16[64,2048]{1,0:T(8,128)(2,1)S(1)}, bf16[64,2048]{1,0:T(8,128)(2,1)S(1)}, u32[]{:S(2)}, u32[]{:S(2)}) collective-permute-start(bf16[64,2048]{1,0:T(8,128)(2,1)S(1)} %add.32), channel_id=1, source_target_pairs={{0,4},{1,3},{4,8},{5,1},{8,12},{9,5},{12,14},{13,9},{14,10},{15,13... | collective-permute-start | bytes 786440 | tf_op jit(solution)/shard_map/sums out 6b/ppermute | solution.py:399
  147.4 2.5 %collective-permute-start.32 = (bf16[128,2048]{1,0:T(8,128)(2,1)S(1)}, bf16[128,2048]{1,0:T(8,128)(2,1)S(1)}, u32[]{:S(2)}, u32[]{:S(2)}) collective-permute-start(bf16[128,2048]{1,0:T(8,128)(2,1)S(1)} %get-tuple-element.48), channel_id=1, source_target_pairs={{0,1},{1,0},{2,3},{3,2},{4,5},{5,4},{6,7},{7,6},{8,9},{9,8},{10,11... | collective-permute-start | bytes 1572872 | tf_op jit(solution)/shard_map/sums across 7/ppermute | solution.py:403
  149.4 3.5 %collective-permute-start.26 = (bf16[128,2048]{1,0:T(8,128)(2,1)S(1)}, bf16[128,2048]{1,0:T(8,128)(2,1)S(1)}, u32[]{:S(2)}, u32[]{:S(2)}) collective-permute-start(bf16[128,2048]{1,0:T(8,128)(2,1)S(1)} %get-tuple-element.45), channel_id=1, source_target_pairs={{0,1},{1,0},{2,3},{3,2},{4,5},{5,4},{6,7},{7,6},{8,9},{9,8},{10,11... | collective-permute-start | bytes 1572872 | tf_op jit(solution)/shard_map/sums across 0/ppermute | solution.py:403
  150.0 6.4 %collective-permute-start.51 = (bf16[64,2048]{1,0:T(8,128)(2,1)S(1)}, bf16[64,2048]{1,0:T(8,128)(2,1)S(1)}, u32[]{:S(2)}, u32[]{:S(2)}) collective-permute-start(bf16[64,2048]{1,0:T(8,128)(2,1)S(1)} %add.30), channel_id=1, source_target_pairs={{0,4},{1,3},{4,8},{5,1},{8,12},{9,5},{12,14},{13,9},{14,10},{15,13... | collective-permute-start | bytes 786440 | tf_op jit(solution)/shard_map/sums out 7a/ppermute | solution.py:399
  151.2 8.0 %collective-permute-start.54 = (bf16[64,2048]{1,0:T(8,128)(2,1)S(1)}, bf16[64,2048]{1,0:T(8,128)(2,1)S(1)}, u32[]{:S(2)}, u32[]{:S(2)}) collective-permute-start(bf16[64,2048]{1,0:T(8,128)(2,1)S(1)} %add.33), channel_id=1, source_target_pairs={{0,4},{1,3},{4,8},{5,1},{8,12},{9,5},{12,14},{13,9},{14,10},{15,13... | collective-permute-start | bytes 786440 | tf_op jit(solution)/shard_map/sums out 7b/ppermute | solution.py:399
  (9 other events, 32.9 us)

commit v5 on v4

--- a/solution.py
+++ b/solution.py
@@ -13,9 +13,14 @@
 FF = 512
 HOPS_X = 1
 HELD = 4
-AFTER = {3:0}
+AFTER = {3: 0}
 TAIL = 5
 DEAD = 128.0
+ADD_COST = 2.0
+EXPERT_COST = 4.0
+AGP = 1
+GIVE = 1
+LATE = 3
 FAR_MIB = 60
 ATT_MIB = 8
 PRO_MIB = 14
@@ -315,12 +320,12 @@
     )(lane, resid, own, got, gain.reshape(1, -1))
 
 
-def expert_body(cols, parts, after, *refs):
+def expert_body(cols, parts, after, gives, *refs):
     refs = list(refs)
     xy, (wx_ref, wy_ref, in_ref, down_ref) = refs[: 2 * parts], refs[2 * parts : 2 * parts + 4]
     cx_ref, *cy_refs = refs[2 * parts + 4 + after :]
     rows, width = cx_ref.shape
-    size = rows // parts
+    size = rows // gives
     both = jnp.concatenate([ref[...] for ref in xy], axis=0)
     gate = jnp.dot(both, in_ref[0, :, :FF], preferred_element_type=F32)
     up = jnp.dot(both, in_ref[0, :, FF:], preferred_element_type=F32)
@@ -336,17 +341,17 @@
             cy_ref[:, at : at + step] = cy[i * size : (i + 1) * size]
 
 
-def expert(cols, x, y, wx, wy, w_in, w_out, after=()):
+def expert(cols, x, y, wx, wy, w_in, w_out, after=(), gives=1):
     rows, width = wx.shape[0], w_out.shape[2]
     parts = len(x)
     out = jax.ShapeDtypeStruct((rows, width), BF16)
-    part = jax.ShapeDtypeStruct((rows // parts, width), BF16)
-    return pl.pallas_call(
-        functools.partial(expert_body, cols, parts, len(after)),
-        out_shape=(out,) + (part,) * parts,
+    part = jax.ShapeDtypeStruct((rows // gives, width), BF16)
+    return pl.pallas_call(
+        functools.partial(expert_body, cols, parts, len(after), gives),
+        out_shape=(out,) + (part,) * gives,
         in_specs=[full()] * (2 * parts + 4) + [anywhere()] * len(after),
-        out_specs=(full(),) * (1 + parts),
-        cost_estimate=cost(1.9),
+        out_specs=(full(),) * (1 + gives),
+        cost_estimate=cost(EXPERT_COST),
         compiler_params=pltpu.CompilerParams(vmem_limit_bytes=EXP_MIB * 2**20),
         name="expert",
     )(*x, *y, wx, wy, w_in, w_out, *after)
@@ -378,7 +383,7 @@
         out_shape=jax.ShapeDtypeStruct((cut.stop - cut.start, used[0].shape[1]), BF16),
         in_specs=[full()] * len(used),
         out_specs=full(),
-        cost_estimate=cost(0.3),
+        cost_estimate=cost(ADD_COST),
         compiler_params=pltpu.CompilerParams(vmem_limit_bytes=8 * 2**20),
         name="add",
     )(*used)
@@ -471,13 +476,15 @@
         column = 2 * order.index(step) + flip
         return (wts_early, column) if column < early else (wts_late, column - early)
 
-    x, y = [normed], [across(normed, "normed")]
+    size = rows // AGP
+    x = [[normed[p * size : (p + 1) * size] for p in range(AGP)]]
+    y = [[across(part, "normed") for part in x[0]]]
 
     def sums(s, after=()):
         wx, column_x = gate_at(s, 0)
         wy, column_y = gate_at((pairs - s) % pairs, 1)
-        keep, give = expert((column_x, column_y), [x[s]], [y[s]], wx, wy, w_in, w_out, after)
-        return keep, across(give, f"sums across {s}")
+        keep, *give = expert((column_x, column_y), x[s], y[s], wx, wy, w_in, w_out, after, GIVE)
+        return keep, [across(part, f"sums across {s}{'ab'[i]}") for i, part in enumerate(give)]
 
     def combine(terms, parts):
         terms = [term if isinstance(term, list) else [term] for term in terms if len(term)]
@@ -487,12 +494,12 @@
 
     travelling = []
     for s in range(1, pairs):
-        x.append(ahead(x[-1], f"rows out {s}"))
-        y.append(across(x[-1], f"rows across {s}"))
+        x.append([ahead(part, f"rows out {s}{'ab'[i]}") for i, part in enumerate(x[-1])])
+        y.append([across(part, f"rows across {s}{'ab'[i]}") for i, part in enumerate(x[-1])])
         keep, back = sums(s)
         total = combine([keep, back, travelling], 2 if s >= TAIL else 1)
         travelling = [ahead(part, f"sums out {s}{'ab'[i]}") for i, part in enumerate(total)]
-    keep, back = sums(0, (x[min(3, pairs - 1)],))
+    keep, back = sums(0, (x[min(LATE, pairs - 1)][0],))
     return combine([residual, keep, back, travelling], 1)[0]
 
 

time: 161 us -> 158 us (0.981)
  waiting for transfers between devices: 65.8 us -> 63.9 us
    ppermute x29, waiting for transfers between devices: 61 us -> 59.1 us  [ahead(): return lax.ppermute(block, ('group', 'expert'), forward)]
  transfers between devices with their start and end apart: 55 -> 55, of which waited for: 24 -> 25; matrix products, arithmetic and copies ran while one was open for 1% -> 1% of each run, Pallas kernels for 19% -> 19%
where the time goes in v5:
time: 158 us; the launch traced here: 157 us
  waiting for transfers between devices  63.9 us (40%)
  starting transfers between devices  53.4 us (34%)
  Pallas kernels  36.5 us (23%)
  local copies, waits for them, and re-layouts  2.35 us (1%)
    ppermute x29, waiting for transfers between devices, ahead(): return lax.ppermute(block, ('group', 'expert'), forward)  59.1 us
    ppermute x29, starting transfers between devices, ahead(): return lax.ppermute(block, ('group', 'expert'), forward)  44.4 us
    pallas_call x8, Pallas kernels, expert(): pl.pallas_call(functools.partial(expert_body, cols, parts, len(after), gi...  15 us
    pallas_call x4, Pallas kernels, attend(): pl.pallas_call(functools.partial(attend_body, first, count, len(passed) +...  10.3 us
    pallas_call x2, Pallas kernels, project(): pl.pallas_call(functools.partial(project_body, first, number, len(mine),...  5.5 us
    ppermute x22, starting transfers between devices, across(): return lax.ppermute(block, 'expert', sibling)  3.55 us
  transfers between devices with their start and end apart: 55, of which 25 were waited for; matrix products, arithmetic and copies ran while one was open for 1% of the time, Pallas kernels for 19%

profile of v5, /device:TPU:0, one launch (start us, length us, event | category | flops | bytes accessed | tf_op | source)
XLA Modules:
  0.0 157.4 jit_solution(18433030321765096727)
XLA Ops:
  0.0 3.1 %far_segment.1 = bf16[2,128,2048]{2,1,0:T(8,128)(2,1)} custom-call(s32[1,2]{1,0:T(1,128)} %len_ref.9, bf16[2,1,2,128,2048]{4,3,2,1,0:T(8,128)(2,1)} %cache_ref.9), custom_call_target="tpu_custom_call" | custom-call | flops 10200000512 | bytes 1000 | tf_op jit(solution)/shard_map/far segment/far_segment/pallas_call | solution.py:116
  3.1 3.0 %collective-permute-start = (bf16[2,128,2048]{2,1,0:T(8,128)(2,1)}, bf16[2,128,2048]{2,1,0:T(8,128)(2,1)}, u32[]{:S(2)}, u32[]{:S(2)}) collective-permute-start(bf16[2,128,2048]{2,1,0:T(8,128)(2,1)} %far_segment.1), channel_id=1, source_target_pairs={{0,16},{16,0},{1,17},{17,1},{2,18},{18,2},{3,19},{19,3},{4,20},{20... | collective-permute-start | bytes 3145736 | tf_op jit(solution)/shard_map/far segment/ppermute | solution.py:418
  6.3 1.6 %collective-permute-start.1 = (bf16[136,1024]{1,0:T(8,128)(2,1)S(1)}, bf16[136,1024]{1,0:T(8,128)(2,1)S(1)}, u32[]{:S(2)}, u32[]{:S(2)}) collective-permute-start(bf16[136,1024]{1,0:T(8,128)(2,1)S(1)} %get-tuple-element.33.refs_8_), channel_id=1, source_target_pairs={{0,4},{1,3},{4,8},{5,1},{8,12},{9,5},{12,14},{13,9},{14,10},{15,13... | collective-permute-start | bytes 835592 | tf_op jit(solution)/shard_map/o rows 1a/ppermute | solution.py:404
  7.9 1.6 %collective-permute-start.7 = (bf16[136,1024]{1,0:T(8,128)(2,1)S(1)}, bf16[136,1024]{1,0:T(8,128)(2,1)S(1)}, u32[]{:S(2)}, u32[]{:S(2)}) collective-permute-start(bf16[136,1024]{1,0:T(8,128)(2,1)S(1)} %collective-permute-done.6.refs_9_), channel_id=1, source_target_pairs={{0,4},{1,3},{4,8},{5,1},{8,12},{9,5},{12,14},{13,9},{14,10},{15,13... | collective-permute-start | bytes 835592 | tf_op jit(solution)/shard_map/o rows 1b/ppermute | solution.py:404
  9.5 3.4 %collective-permute-done.1.refs_10_ = bf16[136,1024]{1,0:T(8,128)(2,1)S(1)} collective-permute-done((bf16[136,1024]{1,0:T(8,128)(2,1)S(1)}, bf16[136,1024]{1,0:T(8,128)(2,1)S(1)}, u32[]{:S(2)}, u32[]{:S(2)}) %collective-permute-start.1) | collective-permute-done | bytes 278560 | tf_op jit(solution)/shard_map/o rows 1a/ppermute | solution.py:404
  12.9 1.6 %collective-permute-start.2 = (bf16[136,1024]{1,0:T(8,128)(2,1)S(1)}, bf16[136,1024]{1,0:T(8,128)(2,1)S(1)}, u32[]{:S(2)}, u32[]{:S(2)}) collective-permute-start(bf16[136,1024]{1,0:T(8,128)(2,1)S(1)} %collective-permute-done.1.refs_10_), channel_id=1, source_target_pairs={{0,4},{1,3},{4,8},{5,1},{8,12},{9,5},{12,14},{13,9},{14,10},{15,13... | collective-permute-start | bytes 835592 | tf_op jit(solution)/shard_map/o rows 2a/ppermute | solution.py:404
  14.5 1.4 collective-permute-done.7.refs_11_
  15.9 1.6 %collective-permute-start.13 = (bf16[136,1024]{1,0:T(8,128)(2,1)S(1)}, bf16[136,1024]{1,0:T(8,128)(2,1)S(1)}, u32[]{:S(2)}, u32[]{:S(2)}) collective-permute-start(bf16[136,1024]{1,0:T(8,128)(2,1)S(1)} %collective-permute-done.7.refs_11_), channel_id=1, source_target_pairs={{0,4},{1,3},{4,8},{5,1},{8,12},{9,5},{12,14},{13,9},{14,10},{15,13... | collective-permute-start | bytes 835592 | tf_op jit(solution)/shard_map/o rows 2b/ppermute | solution.py:404
  17.4 2.0 %collective-permute-done.2.refs_12_ = bf16[136,1024]{1,0:T(8,128)(2,1)S(1)} collective-permute-done((bf16[136,1024]{1,0:T(8,128)(2,1)S(1)}, bf16[136,1024]{1,0:T(8,128)(2,1)S(1)}, u32[]{:S(2)}, u32[]{:S(2)}) %collective-permute-start.2) | collective-permute-done | bytes 278560 | tf_op jit(solution)/shard_map/o rows 2a/ppermute | solution.py:404
  19.4 1.6 %collective-permute-start.3 = (bf16[136,1024]{1,0:T(8,128)(2,1)S(1)}, bf16[136,1024]{1,0:T(8,128)(2,1)S(1)}, u32[]{:S(2)}, u32[]{:S(2)}) collective-permute-start(bf16[136,1024]{1,0:T(8,128)(2,1)S(1)} %collective-permute-done.2.refs_12_), channel_id=1, source_target_pairs={{0,4},{1,3},{4,8},{5,1},{8,12},{9,5},{12,14},{13,9},{14,10},{15,13... | collective-permute-start | bytes 835592 | tf_op jit(solution)/shard_map/o rows 3a/ppermute | solution.py:404
  21.5 1.5 collective-permute-start.8
  23.0 1.6 %collective-permute-start.14 = (bf16[136,1024]{1,0:T(8,128)(2,1)S(1)}, bf16[136,1024]{1,0:T(8,128)(2,1)S(1)}, u32[]{:S(2)}, u32[]{:S(2)}) collective-permute-start(bf16[136,1024]{1,0:T(8,128)(2,1)S(1)} %collective-permute-done.13.refs_13_), channel_id=1, source_target_pairs={{0,4},{1,3},{4,8},{5,1},{8,12},{9,5},{12,14},{13,9},{14,10},{15,13... | collective-permute-start | bytes 835592 | tf_op jit(solution)/shard_map/o rows 3b/ppermute | solution.py:404
  24.6 1.4 collective-permute-done.3.refs_14_
  26.0 1.6 %collective-permute-start.4 = (bf16[136,1024]{1,0:T(8,128)(2,1)S(1)}, bf16[136,1024]{1,0:T(8,128)(2,1)S(1)}, u32[]{:S(2)}, u32[]{:S(2)}) collective-permute-start(bf16[136,1024]{1,0:T(8,128)(2,1)S(1)} %collective-permute-done.3.refs_14_), channel_id=1, source_target_pairs={{0,4},{1,3},{4,8},{5,1},{8,12},{9,5},{12,14},{13,9},{14,10},{15,13... | collective-permute-start | bytes 835592 | tf_op jit(solution)/shard_map/o rows 4a/ppermute | solution.py:404
  27.6 2.8 %collective-permute-done.far_ref = bf16[2,128,2048]{2,1,0:T(8,128)(2,1)} collective-permute-done((bf16[2,128,2048]{2,1,0:T(8,128)(2,1)}, bf16[2,128,2048]{2,1,0:T(8,128)(2,1)}, u32[]{:S(2)}, u32[]{:S(2)}) %collective-permute-start) | collective-permute-done | bytes 1048608 | tf_op jit(solution)/shard_map/far segment/ppermute | solution.py:418
  30.4 2.5 %attend.5.refs_1_ = bf16[4,128,128]{2,1,0:T(8,128)(2,1)S(1)} custom-call(s32[1,2]{1,0:T(1,128)S(1)} %copy-done.17, bf16[128,2048]{1,0:T(8,128)(2,1)S(1)} %copy-done.12, bf16[2,128,2048]{2,1,0:T(8,128)(2,1)S(1)} %copy-done.10, bf16[2,1,2,128,2048]{4,3,2,1,0:T(8,128)(2,1)S(1)} %copy-done.8, bf16[2,128,2048]{2,1,0:T(8,128)(2,1)} %collective-permute-done.far_ref), custom_call_target="tpu_custom_call" | custom-call | flops 14400000000 | bytes 1000 | tf_op jit(solution)/shard_map/attend/pallas_call | solution.py:153
  33.1 2.2 %collective-permute-start.15 = (bf16[136,1024]{1,0:T(8,128)(2,1)S(1)}, bf16[136,1024]{1,0:T(8,128)(2,1)S(1)}, u32[]{:S(2)}, u32[]{:S(2)}) collective-permute-start(bf16[136,1024]{1,0:T(8,128)(2,1)S(1)} %collective-permute-done.14.refs_15_), channel_id=1, source_target_pairs={{0,4},{1,3},{4,8},{5,1},{8,12},{9,5},{12,14},{13,9},{14,10},{15,13... | collective-permute-start | bytes 835592 | tf_op jit(solution)/shard_map/o rows 4b/ppermute | solution.py:404
  35.3 2.5 %attend.4 = (bf16[4,128,128]{2,1,0:T(8,128)(2,1)S(1)}, bf16[136,1024]{1,0:T(8,128)(2,1)S(1)}) custom-call(s32[1,2]{1,0:T(1,128)S(1)} %copy-done.17, bf16[128,2048]{1,0:T(8,128)(2,1)S(1)} %copy-done.12, bf16[2,128,2048]{2,1,0:T(8,128)(2,1)S(1)} %copy-done.10, bf16[2,1,2,128,2048]{4,3,2,1,0:T(8,128)(2,1)S(1)} %copy-done.8, ...), custom_call_target="tpu_custom_call", output_to_operand_aliasing={{1}: (5, {})} | custom-call | flops 14400000000 | bytes 1000 | tf_op jit(solution)/shard_map/attend/pallas_call | solution.py:153
  37.8 1.6 %collective-permute-start.16 = (bf16[136,1024]{1,0:T(8,128)(2,1)S(1)}, bf16[136,1024]{1,0:T(8,128)(2,1)}, u32[]{:S(2)}, u32[]{:S(2)}) collective-permute-start(bf16[136,1024]{1,0:T(8,128)(2,1)S(1)} %get-tuple-element.36.refs_16_), channel_id=1, source_target_pairs={{0,4},{1,3},{4,8},{5,1},{8,12},{9,5},{12,14},{13,9},{14,10},{15,13... | collective-permute-start | bytes 835592 | tf_op jit(solution)/shard_map/o rows 5a/ppermute | solution.py:404
  39.7 2.1 %collective-permute-start.17 = (bf16[136,1024]{1,0:T(8,128)(2,1)S(1)}, bf16[136,1024]{1,0:T(8,128)(2,1)}, u32[]{:S(2)}, u32[]{:S(2)}) collective-permute-start(bf16[136,1024]{1,0:T(8,128)(2,1)S(1)} %collective-permute-done.15.refs_17_), channel_id=1, source_target_pairs={{0,4},{1,3},{4,8},{5,1},{8,12},{9,5},{12,14},{13,9},{14,10},{15,13... | collective-permute-start | bytes 835592 | tf_op jit(solution)/shard_map/o rows 5b/ppermute | solution.py:404
  41.8 2.5 %attend.6.refs_2_ = bf16[4,128,128]{2,1,0:T(8,128)(2,1)S(1)} custom-call(s32[1,2]{1,0:T(1,128)S(1)} %copy-done.17, bf16[128,2048]{1,0:T(8,128)(2,1)S(1)} %copy-done.12, bf16[2,128,2048]{2,1,0:T(8,128)(2,1)S(1)} %copy-done.10, bf16[2,1,2,128,2048]{4,3,2,1,0:T(8,128)(2,1)S(1)} %copy-done.8, bf16[2,128,2048]{2,1,0:T(8,128)(2,1)} %collective-permute-done.far_ref), custom_call_target="tpu_custom_call" | custom-call | flops 14400000000 | bytes 1000 | tf_op jit(solution)/shard_map/attend/pallas_call | solution.py:153
  44.5 1.6 collective-permute-start.18
  46.1 1.4 collective-permute-done.17.refs_19_
  47.5 1.6 collective-permute-start.19
  49.1 2.6 %attend.7.refs_3_ = bf16[4,128,128]{2,1,0:T(8,128)(2,1)S(1)} custom-call(s32[1,2]{1,0:T(1,128)S(1)} %copy-done.17, bf16[128,2048]{1,0:T(8,128)(2,1)S(1)} %copy-done.12, bf16[2,128,2048]{2,1,0:T(8,128)(2,1)S(1)} %copy-done.10, bf16[2,1,2,128,2048]{4,3,2,1,0:T(8,128)(2,1)S(1)} %copy-done.8, bf16[2,128,2048]{2,1,0:T(8,128)(2,1)} %collective-permute-done.far_ref, ...), custom_call_target="tpu_custom_call" | custom-call | flops 14400000000 | bytes 1000 | tf_op jit(solution)/shard_map/attend/pallas_call | solution.py:153
  55.8 3.5 %project.2 = (f32[128,1024]{1,0:T(8,128)S(1)}, f32[128,1024]{1,0:T(8,128)S(1)}, f32[128,128]{1,0:T(8,128)S(1)}) custom-call(s32[32,16]{1,0:T(8,128)S(1)} %copy-done.6, s32[1]{0:T(128)} %bitcast.1.me_ref, bf16[4,128,128]{2,1,0:T(8,128)(2,1)S(1)} %get-tuple-element.34.refs_0_, bf16[4,128,128]{2,1,0:T(8,128)(2,1)S(1)} %attend.5.refs_1_, ...), custom_call_target="tpu_custom_call" | custom-call | flops 805306368 | bytes 3145728 | tf_op jit(solution)/shard_map/project/pallas_call | solution.py:273
  59.4 2.0 %project.3 = (f32[128,1024]{1,0:T(8,128)S(1)}, f32[128,1024]{1,0:T(8,128)S(1)}, f32[128,128]{1,0:T(8,128)S(1)}) custom-call(s32[32,16]{1,0:T(8,128)S(1)} %copy-done.6, s32[1]{0:T(128)} %bitcast.1.me_ref, bf16[4,128,128]{2,1,0:T(8,128)(2,1)S(1)} %get-tuple-element.34.refs_0_, bf16[4,128,128]{2,1,0:T(8,128)(2,1)S(1)} %attend.5.refs_1_, ...), custom_call_target="tpu_custom_call" | custom-call | flops 268435456 | bytes 1048576 | tf_op jit(solution)/shard_map/project/pallas_call | solution.py:273
  62.4 1.5 collective-permute-done.21.got_ref
  64.4 1.6 %collective-permute-start.23 = (bf16[128,2048]{1,0:T(8,128)(2,1)S(1)}, bf16[128,2048]{1,0:T(8,128)(2,1)S(1)}, u32[]{:S(2)}, u32[]{:S(2)}) collective-permute-start(bf16[128,2048]{1,0:T(8,128)(2,1)S(1)} %get-tuple-element.42.refs_0_), channel_id=1, source_target_pairs={{0,4},{1,3},{4,8},{5,1},{8,12},{9,5},{12,14},{13,9},{14,10},{15,13... | collective-permute-start | bytes 1572872 | tf_op jit(solution)/shard_map/rows out 1a/ppermute | solution.py:404
  65.9 7.7 %collective-permute-done.23.refs_0_ = bf16[128,2048]{1,0:T(8,128)(2,1)S(1)} collective-permute-done((bf16[128,2048]{1,0:T(8,128)(2,1)S(1)}, bf16[128,2048]{1,0:T(8,128)(2,1)S(1)}, u32[]{:S(2)}, u32[]{:S(2)}) %collective-permute-start.23) | collective-permute-done | bytes 524320 | tf_op jit(solution)/shard_map/rows out 1a/ppermute | solution.py:404
  73.6 1.5 collective-permute-start.24
  75.5 1.9 %expert.15 = (bf16[128,2048]{1,0:T(8,128)(2,1)S(1)}, bf16[128,2048]{1,0:T(8,128)(2,1)S(1)}) custom-call(bf16[128,2048]{1,0:T(8,128)(2,1)S(1)} %collective-permute-done.23.refs_0_, bf16[128,2048]{1,0:T(8,128)(2,1)S(1)} %collective-permute-done.43.refs_1_, f32[128,128]{1,0:T(8,128)S(1)} %get-tuple-element.43.refs_2_.refs_3_, ...), custom_call_target="tpu_custom_call" | custom-call | flops 24000000000 | bytes 1000 | tf_op jit(solution)/shard_map/expert/pallas_call | solution.py:349
  77.6 5.2 %collective-permute-done.24.refs_0_ = bf16[128,2048]{1,0:T(8,128)(2,1)S(1)} collective-permute-done((bf16[128,2048]{1,0:T(8,128)(2,1)S(1)}, bf16[128,2048]{1,0:T(8,128)(2,1)S(1)}, u32[]{:S(2)}, u32[]{:S(2)}) %collective-permute-start.24) | collective-permute-done | bytes 524320 | tf_op jit(solution)/shard_map/rows out 2a/ppermute | solution.py:404
  82.8 1.5 collective-permute-start.25
  85.6 1.9 %expert.14 = (bf16[128,2048]{1,0:T(8,128)(2,1)S(1)}, bf16[128,2048]{1,0:T(8,128)(2,1)S(1)}) custom-call(bf16[128,2048]{1,0:T(8,128)(2,1)S(1)} %collective-permute-done.24.refs_0_, bf16[128,2048]{1,0:T(8,128)(2,1)S(1)} %collective-permute-done.41.refs_1_, f32[128,128]{1,0:T(8,128)S(1)} %get-tuple-element.43.refs_2_.refs_3_, ...), custom_call_target="tpu_custom_call" | custom-call | flops 24000000000 | bytes 1000 | tf_op jit(solution)/shard_map/expert/pallas_call | solution.py:349
  87.5 4.4 %collective-permute-done.25.refs_6_.refs_0_ = bf16[128,2048]{1,0:T(8,128)(2,1)S(1)} collective-permute-done((bf16[128,2048]{1,0:T(8,128)(2,1)S(1)}, bf16[128,2048]{1,0:T(8,128)(2,1)S(1)}, u32[]{:S(2)}, u32[]{:S(2)}) %collective-permute-start.25) | collective-permute-done | bytes 524320 | tf_op jit(solution)/shard_map/rows out 3a/ppermute | solution.py:404
  92.0 1.5 collective-permute-start.27
  93.5 4.1 %collective-permute-done.45.refs_2_ = bf16[128,2048]{1,0:T(8,128)(2,1)S(1)} collective-permute-done((bf16[128,2048]{1,0:T(8,128)(2,1)S(1)}, bf16[128,2048]{1,0:T(8,128)(2,1)S(1)}, u32[]{:S(2)}, u32[]{:S(2)}) %collective-permute-start.45) | collective-permute-done | bytes 524320 | tf_op jit(solution)/shard_map/sums out 1a/ppermute | solution.py:404
  97.8 1.6 %collective-permute-start.46 = (bf16[128,2048]{1,0:T(8,128)(2,1)S(1)}, bf16[128,2048]{1,0:T(8,128)(2,1)S(1)}, u32[]{:S(2)}, u32[]{:S(2)}) collective-permute-start(bf16[128,2048]{1,0:T(8,128)(2,1)S(1)} %add.25), channel_id=1, source_target_pairs={{0,4},{1,3},{4,8},{5,1},{8,12},{9,5},{12,14},{13,9},{14,10},{15,13... | collective-permute-start | bytes 1572872 | tf_op jit(solution)/shard_map/sums out 2a/ppermute | solution.py:404
  99.4 1.9 %expert.13 = (bf16[128,2048]{1,0:T(8,128)(2,1)S(1)}, bf16[128,2048]{1,0:T(8,128)(2,1)S(1)}) custom-call(bf16[128,2048]{1,0:T(8,128)(2,1)S(1)} %collective-permute-done.25.refs_6_.refs_0_, bf16[128,2048]{1,0:T(8,128)(2,1)S(1)} %collective-permute-done.39.refs_1_, f32[128,128]{1,0:T(8,128)S(1)} %get-tuple-element.43.refs_2_.refs_3_, ...), custom_call_target="tpu_custom_call" | custom-call | flops 24000000000 | bytes 1000 | tf_op jit(solution)/shard_map/expert/pallas_call | solution.py:349
  101.3 1.9 %collective-permute-done.27.refs_0_ = bf16[128,2048]{1,0:T(8,128)(2,1)S(1)} collective-permute-done((bf16[128,2048]{1,0:T(8,128)(2,1)S(1)}, bf16[128,2048]{1,0:T(8,128)(2,1)S(1)}, u32[]{:S(2)}, u32[]{:S(2)}) %collective-permute-start.27) | collective-permute-done | bytes 524320 | tf_op jit(solution)/shard_map/rows out 4a/ppermute | solution.py:404
  103.2 1.5 collective-permute-start.28
  104.7 4.1 %collective-permute-done.46.refs_2_ = bf16[128,2048]{1,0:T(8,128)(2,1)S(1)} collective-permute-done((bf16[128,2048]{1,0:T(8,128)(2,1)S(1)}, bf16[128,2048]{1,0:T(8,128)(2,1)S(1)}, u32[]{:S(2)}, u32[]{:S(2)}) %collective-permute-start.46) | collective-permute-done | bytes 524320 | tf_op jit(solution)/shard_map/sums out 2a/ppermute | solution.py:404
  109.0 1.6 %collective-permute-start.47 = (bf16[128,2048]{1,0:T(8,128)(2,1)S(1)}, bf16[128,2048]{1,0:T(8,128)(2,1)S(1)}, u32[]{:S(2)}, u32[]{:S(2)}) collective-permute-start(bf16[128,2048]{1,0:T(8,128)(2,1)S(1)} %add.26), channel_id=1, source_target_pairs={{0,4},{1,3},{4,8},{5,1},{8,12},{9,5},{12,14},{13,9},{14,10},{15,13... | collective-permute-start | bytes 1572872 | tf_op jit(solution)/shard_map/sums out 3a/ppermute | solution.py:404
  110.6 1.9 %expert.12 = (bf16[128,2048]{1,0:T(8,128)(2,1)S(1)}, bf16[128,2048]{1,0:T(8,128)(2,1)S(1)}) custom-call(bf16[128,2048]{1,0:T(8,128)(2,1)S(1)} %collective-permute-done.27.refs_0_, bf16[128,2048]{1,0:T(8,128)(2,1)S(1)} %collective-permute-done.37.refs_1_, f32[128,128]{1,0:T(8,128)S(1)} %get-tuple-element.43.refs_2_.refs_3_, ...), custom_call_target="tpu_custom_call" | custom-call | flops 24000000000 | bytes 1000 | tf_op jit(solution)/shard_map/expert/pallas_call | solution.py:349
  113.0 1.4 collective-permute-done.28.refs_0_
  114.4 1.5 collective-permute-start.29
  116.0 4.1 %collective-permute-done.47.refs_2_ = bf16[128,2048]{1,0:T(8,128)(2,1)S(1)} collective-permute-done((bf16[128,2048]{1,0:T(8,128)(2,1)S(1)}, bf16[128,2048]{1,0:T(8,128)(2,1)S(1)}, u32[]{:S(2)}, u32[]{:S(2)}) %collective-permute-start.47) | collective-permute-done | bytes 524320 | tf_op jit(solution)/shard_map/sums out 3a/ppermute | solution.py:404
  120.2 1.6 %collective-permute-start.48 = (bf16[128,2048]{1,0:T(8,128)(2,1)S(1)}, bf16[128,2048]{1,0:T(8,128)(2,1)S(1)}, u32[]{:S(2)}, u32[]{:S(2)}) collective-permute-start(bf16[128,2048]{1,0:T(8,128)(2,1)S(1)} %add.27), channel_id=1, source_target_pairs={{0,4},{1,3},{4,8},{5,1},{8,12},{9,5},{12,14},{13,9},{14,10},{15,13... | collective-permute-start | bytes 1572872 | tf_op jit(solution)/shard_map/sums out 4a/ppermute | solution.py:404
  121.8 1.9 %expert.11 = (bf16[128,2048]{1,0:T(8,128)(2,1)S(1)}, bf16[128,2048]{1,0:T(8,128)(2,1)S(1)}) custom-call(bf16[128,2048]{1,0:T(8,128)(2,1)S(1)} %collective-permute-done.28.refs_0_, bf16[128,2048]{1,0:T(8,128)(2,1)S(1)} %collective-permute-done.35.refs_1_, f32[128,128]{1,0:T(8,128)S(1)} %get-tuple-element.43.refs_2_.refs_3_, ...), custom_call_target="tpu_custom_call" | custom-call | flops 24000000000 | bytes 1000 | tf_op jit(solution)/shard_map/expert/pallas_call | solution.py:349
  123.8 1.9 %expert.8 = (bf16[128,2048]{1,0:T(8,128)(2,1)S(1)}, bf16[128,2048]{1,0:T(8,128)(2,1)S(1)}) custom-call(bf16[128,2048]{1,0:T(8,128)(2,1)S(1)} %get-tuple-element.42.refs_0_, bf16[128,2048]{1,0:T(8,128)(2,1)S(1)} %collective-permute-done.22.refs_1_, f32[128,128]{1,0:T(8,128)S(1)} %get-tuple-element.43.refs_2_.refs_3_, ...), custom_call_target="tpu_custom_call" | custom-call | flops 24000000000 | bytes 1000 | tf_op jit(solution)/shard_map/expert/pallas_call | solution.py:349
  127.4 3.9 %collective-permute-done.48.refs_2_ = bf16[128,2048]{1,0:T(8,128)(2,1)S(1)} collective-permute-done((bf16[128,2048]{1,0:T(8,128)(2,1)S(1)}, bf16[128,2048]{1,0:T(8,128)(2,1)S(1)}, u32[]{:S(2)}, u32[]{:S(2)}) %collective-permute-start.48) | collective-permute-done | bytes 524320 | tf_op jit(solution)/shard_map/sums out 4a/ppermute | solution.py:404
  131.4 1.6 %collective-permute-start.49 = (bf16[64,2048]{1,0:T(8,128)(2,1)S(1)}, bf16[64,2048]{1,0:T(8,128)(2,1)S(1)}, u32[]{:S(2)}, u32[]{:S(2)}) collective-permute-start(bf16[64,2048]{1,0:T(8,128)(2,1)S(1)} %add.28), channel_id=1, source_target_pairs={{0,4},{1,3},{4,8},{5,1},{8,12},{9,5},{12,14},{13,9},{14,10},{15,13... | collective-permute-start | bytes 786440 | tf_op jit(solution)/shard_map/sums out 5a/ppermute | solution.py:404
  133.0 1.9 %expert.10 = (bf16[128,2048]{1,0:T(8,128)(2,1)S(1)}, bf16[128,2048]{1,0:T(8,128)(2,1)S(1)}) custom-call(bf16[128,2048]{1,0:T(8,128)(2,1)S(1)} %collective-permute-done.29.refs_0_, bf16[128,2048]{1,0:T(8,128)(2,1)S(1)} %collective-permute-done.33.refs_1_, f32[128,128]{1,0:T(8,128)S(1)} %get-tuple-element.46.refs_2_.refs_3_, ...), custom_call_target="tpu_custom_call" | custom-call | flops 24000000000 | bytes 1000 | tf_op jit(solution)/shard_map/expert/pallas_call | solution.py:349
  135.0 1.1 collective-permute-start.52
  136.9 2.8 %collective-permute-done.49.refs_2_ = bf16[64,2048]{1,0:T(8,128)(2,1)S(1)} collective-permute-done((bf16[64,2048]{1,0:T(8,128)(2,1)S(1)}, bf16[64,2048]{1,0:T(8,128)(2,1)S(1)}, u32[]{:S(2)}, u32[]{:S(2)}) %collective-permute-start.49) | collective-permute-done | bytes 262176 | tf_op jit(solution)/shard_map/sums out 5a/ppermute | solution.py:404
  139.8 1.6 %collective-permute-start.50 = (bf16[64,2048]{1,0:T(8,128)(2,1)S(1)}, bf16[64,2048]{1,0:T(8,128)(2,1)S(1)}, u32[]{:S(2)}, u32[]{:S(2)}) collective-permute-start(bf16[64,2048]{1,0:T(8,128)(2,1)S(1)} %add.29), channel_id=1, source_target_pairs={{0,4},{1,3},{4,8},{5,1},{8,12},{9,5},{12,14},{13,9},{14,10},{15,13... | collective-permute-start | bytes 786440 | tf_op jit(solution)/shard_map/sums out 6a/ppermute | solution.py:404
  141.4 1.9 %expert.9 = (bf16[128,2048]{1,0:T(8,128)(2,1)S(1)}, bf16[128,2048]{1,0:T(8,128)(2,1)S(1)}) custom-call(bf16[128,2048]{1,0:T(8,128)(2,1)S(1)} %collective-permute-done.30.refs_0_, bf16[128,2048]{1,0:T(8,128)(2,1)S(1)} %collective-permute-done.31.refs_1_, f32[128,128]{1,0:T(8,128)S(1)} %get-tuple-element.46.refs_2_.refs_3_, ...), custom_call_target="tpu_custom_call" | custom-call | flops 24000000000 | bytes 1000 | tf_op jit(solution)/shard_map/expert/pallas_call | solution.py:349
  143.5 1.1 collective-permute-start.53
  144.6 1.7 %collective-permute-done.50.refs_2_ = bf16[64,2048]{1,0:T(8,128)(2,1)S(1)} collective-permute-done((bf16[64,2048]{1,0:T(8,128)(2,1)S(1)}, bf16[64,2048]{1,0:T(8,128)(2,1)S(1)}, u32[]{:S(2)}, u32[]{:S(2)}) %collective-permute-start.50) | collective-permute-done | bytes 262176 | tf_op jit(solution)/shard_map/sums out 6a/ppermute | solution.py:404
  146.3 1.6 %collective-permute-start.51 = (bf16[64,2048]{1,0:T(8,128)(2,1)S(1)}, bf16[64,2048]{1,0:T(8,128)(2,1)S(1)}, u32[]{:S(2)}, u32[]{:S(2)}) collective-permute-start(bf16[64,2048]{1,0:T(8,128)(2,1)S(1)} %add.30), channel_id=1, source_target_pairs={{0,4},{1,3},{4,8},{5,1},{8,12},{9,5},{12,14},{13,9},{14,10},{15,13... | collective-permute-start | bytes 786440 | tf_op jit(solution)/shard_map/sums out 7a/ppermute | solution.py:404
  147.9 2.0 %collective-permute-done.53.refs_2_ = bf16[64,2048]{1,0:T(8,128)(2,1)S(1)} collective-permute-done((bf16[64,2048]{1,0:T(8,128)(2,1)S(1)}, bf16[64,2048]{1,0:T(8,128)(2,1)S(1)}, u32[]{:S(2)}, u32[]{:S(2)}) %collective-permute-start.53) | collective-permute-done | bytes 262176 | tf_op jit(solution)/shard_map/sums out 6b/ppermute | solution.py:404
  151.1 1.7 %collective-permute-done.51.refs_3_ = bf16[64,2048]{1,0:T(8,128)(2,1)S(1)} collective-permute-done((bf16[64,2048]{1,0:T(8,128)(2,1)S(1)}, bf16[64,2048]{1,0:T(8,128)(2,1)S(1)}, u32[]{:S(2)}, u32[]{:S(2)}) %collective-permute-start.51) | collective-permute-done | bytes 262176 | tf_op jit(solution)/shard_map/sums out 7a/ppermute | solution.py:404
  152.8 3.7 %collective-permute-done.54.refs_4_ = bf16[64,2048]{1,0:T(8,128)(2,1)S(1)} collective-permute-done((bf16[64,2048]{1,0:T(8,128)(2,1)S(1)}, bf16[64,2048]{1,0:T(8,128)(2,1)S(1)}, u32[]{:S(2)}, u32[]{:S(2)}) %collective-permute-start.54) | collective-permute-done | bytes 262176 | tf_op jit(solution)/shard_map/sums out 7b/ppermute | solution.py:404
  (113 shorter events, 15.1 us)
Async XLA Ops:
  0.0 6.1 %copy-start.11 = (bf16[128,2048]{1,0:T(8,128)(2,1)S(1)}, bf16[128,2048]{1,0:T(8,128)(2,1)}, u32[]{:S(2)}) copy-start(bf16[128,2048]{1,0:T(8,128)(2,1)} %rows_ref.1) | copy-start | bytes 1572868
  3.1 27.3 %collective-permute-start = (bf16[2,128,2048]{2,1,0:T(8,128)(2,1)}, bf16[2,128,2048]{2,1,0:T(8,128)(2,1)}, u32[]{:S(2)}, u32[]{:S(2)}) collective-permute-start(bf16[2,128,2048]{2,1,0:T(8,128)(2,1)} %far_segment.1), channel_id=1, source_target_pairs={{0,16},{16,0},{1,17},{17,1},{2,18},{18,2},{3,19},{19,3},{4,20},{20... | collective-permute-start | bytes 3145736 | tf_op jit(solution)/shard_map/far segment/ppermute | solution.py:418
  6.1 24.3 %copy-start.8 = (bf16[2,1,2,128,2048]{4,3,2,1,0:T(8,128)(2,1)S(1)}, bf16[2,1,2,128,2048]{4,3,2,1,0:T(8,128)(2,1)}, u32[]{:S(2)}) copy-start(bf16[2,1,2,128,2048]{4,3,2,1,0:T(8,128)(2,1)} %cache_ref.9) | copy-start | bytes 6291460
  6.1 24.3 %copy-start.10 = (bf16[2,128,2048]{2,1,0:T(8,128)(2,1)S(1)}, bf16[2,128,2048]{2,1,0:T(8,128)(2,1)}, u32[]{:S(2)}) copy-start(bf16[2,128,2048]{2,1,0:T(8,128)(2,1)} %kv_ref.7) | copy-start | bytes 3145732
  6.1 24.3 %copy-start.12 = (bf16[128,2048]{1,0:T(8,128)(2,1)S(1)}, bf16[128,2048]{1,0:T(8,128)(2,1)}, u32[]{:S(2)}) copy-start(bf16[128,2048]{1,0:T(8,128)(2,1)} %q_ref.7) | copy-start | bytes 1572868
  6.1 24.3 %copy-start.17 = (s32[1,2]{1,0:T(1,128)S(1)}, s32[1,2]{1,0:T(1,128)}, u32[]{:S(2)}) copy-start(s32[1,2]{1,0:T(1,128)} %len_ref.9) | copy-start | bytes 28
  6.2 1.7 %collective-permute-start.6 = (bf16[136,1024]{1,0:T(8,128)(2,1)S(1)}, bf16[136,1024]{1,0:T(8,128)(2,1)S(1)}, u32[]{:S(2)}, u32[]{:S(2)}) collective-permute-start(bf16[136,1024]{1,0:T(8,128)(2,1)S(1)} %get-tuple-element.35), channel_id=1, source_target_pairs={{0,1},{1,0},{2,3},{3,2},{4,5},{5,4},{6,7},{7,6},{8,9},{9,8},{10,11... | collective-permute-start | bytes 835592 | tf_op jit(solution)/shard_map/to sibling/ppermute | solution.py:408
  6.3 6.6 %collective-permute-start.1 = (bf16[136,1024]{1,0:T(8,128)(2,1)S(1)}, bf16[136,1024]{1,0:T(8,128)(2,1)S(1)}, u32[]{:S(2)}, u32[]{:S(2)}) collective-permute-start(bf16[136,1024]{1,0:T(8,128)(2,1)S(1)} %get-tuple-element.33.refs_8_), channel_id=1, source_target_pairs={{0,4},{1,3},{4,8},{5,1},{8,12},{9,5},{12,14},{13,9},{14,10},{15,13... | collective-permute-start | bytes 835592 | tf_op jit(solution)/shard_map/o rows 1a/ppermute | solution.py:404
  7.9 8.0 %collective-permute-start.7 = (bf16[136,1024]{1,0:T(8,128)(2,1)S(1)}, bf16[136,1024]{1,0:T(8,128)(2,1)S(1)}, u32[]{:S(2)}, u32[]{:S(2)}) collective-permute-start(bf16[136,1024]{1,0:T(8,128)(2,1)S(1)} %collective-permute-done.6.refs_9_), channel_id=1, source_target_pairs={{0,4},{1,3},{4,8},{5,1},{8,12},{9,5},{12,14},{13,9},{14,10},{15,13... | collective-permute-start | bytes 835592 | tf_op jit(solution)/shard_map/o rows 1b/ppermute | solution.py:404
  12.9 6.5 %collective-permute-start.2 = (bf16[136,1024]{1,0:T(8,128)(2,1)S(1)}, bf16[136,1024]{1,0:T(8,128)(2,1)S(1)}, u32[]{:S(2)}, u32[]{:S(2)}) collective-permute-start(bf16[136,1024]{1,0:T(8,128)(2,1)S(1)} %collective-permute-done.1.refs_10_), channel_id=1, source_target_pairs={{0,4},{1,3},{4,8},{5,1},{8,12},{9,5},{12,14},{13,9},{14,10},{15,13... | collective-permute-start | bytes 835592 | tf_op jit(solution)/shard_map/o rows 2a/ppermute | solution.py:404
  15.9 7.2 %collective-permute-start.13 = (bf16[136,1024]{1,0:T(8,128)(2,1)S(1)}, bf16[136,1024]{1,0:T(8,128)(2,1)S(1)}, u32[]{:S(2)}, u32[]{:S(2)}) collective-permute-start(bf16[136,1024]{1,0:T(8,128)(2,1)S(1)} %collective-permute-done.7.refs_11_), channel_id=1, source_target_pairs={{0,4},{1,3},{4,8},{5,1},{8,12},{9,5},{12,14},{13,9},{14,10},{15,13... | collective-permute-start | bytes 835592 | tf_op jit(solution)/shard_map/o rows 2b/ppermute | solution.py:404
  19.4 6.5 %collective-permute-start.3 = (bf16[136,1024]{1,0:T(8,128)(2,1)S(1)}, bf16[136,1024]{1,0:T(8,128)(2,1)S(1)}, u32[]{:S(2)}, u32[]{:S(2)}) collective-permute-start(bf16[136,1024]{1,0:T(8,128)(2,1)S(1)} %collective-permute-done.2.refs_12_), channel_id=1, source_target_pairs={{0,4},{1,3},{4,8},{5,1},{8,12},{9,5},{12,14},{13,9},{14,10},{15,13... | collective-permute-start | bytes 835592 | tf_op jit(solution)/shard_map/o rows 3a/ppermute | solution.py:404
  21.0 23.4 %collective-permute-start.5 = (bf16[136,1024]{1,0:T(8,128)(2,1)S(1)}, bf16[136,1024]{1,0:T(8,128)(2,1)S(1)}, u32[]{:S(2)}, u32[]{:S(2)}) collective-permute-start(bf16[136,1024]{1,0:T(8,128)(2,1)S(1)} %collective-permute-done.1.refs_10_), channel_id=1, source_target_pairs={{0,16},{16,0},{1,17},{17,1},{2,18},{18,2},{3,19},{19,3},{4,20},{20... | collective-permute-start | bytes 835592 | tf_op jit(solution)/shard_map/o rows of partner/ppermute | solution.py:437
  21.5 27.6 %collective-permute-start.8 = (bf16[136,1024]{1,0:T(8,128)(2,1)S(1)}, bf16[136,1024]{1,0:T(8,128)(2,1)S(1)}, u32[]{:S(2)}, u32[]{:S(2)}) collective-permute-start(bf16[136,1024]{1,0:T(8,128)(2,1)S(1)} %collective-permute-done.7.refs_11_), channel_id=1, source_target_pairs={{0,16},{16,0},{1,17},{17,1},{2,18},{18,2},{3,19},{19,3},{4,20},{20... | collective-permute-start | bytes 835592 | tf_op jit(solution)/shard_map/o rows of partner/ppermute | solution.py:437
  23.0 10.0 %collective-permute-start.14 = (bf16[136,1024]{1,0:T(8,128)(2,1)S(1)}, bf16[136,1024]{1,0:T(8,128)(2,1)S(1)}, u32[]{:S(2)}, u32[]{:S(2)}) collective-permute-start(bf16[136,1024]{1,0:T(8,128)(2,1)S(1)} %collective-permute-done.13.refs_13_), channel_id=1, source_target_pairs={{0,4},{1,3},{4,8},{5,1},{8,12},{9,5},{12,14},{13,9},{14,10},{15,13... | collective-permute-start | bytes 835592 | tf_op jit(solution)/shard_map/o rows 3b/ppermute | solution.py:404
  26.0 9.3 %collective-permute-start.4 = (bf16[136,1024]{1,0:T(8,128)(2,1)S(1)}, bf16[136,1024]{1,0:T(8,128)(2,1)S(1)}, u32[]{:S(2)}, u32[]{:S(2)}) collective-permute-start(bf16[136,1024]{1,0:T(8,128)(2,1)S(1)} %collective-permute-done.3.refs_14_), channel_id=1, source_target_pairs={{0,4},{1,3},{4,8},{5,1},{8,12},{9,5},{12,14},{13,9},{14,10},{15,13... | collective-permute-start | bytes 835592 | tf_op jit(solution)/shard_map/o rows 4a/ppermute | solution.py:404
  33.0 18.9 %collective-permute-start.10 = (bf16[4,128,128]{2,1,0:T(8,128)(2,1)S(1)}, bf16[4,128,128]{2,1,0:T(8,128)(2,1)S(1)}, u32[]{:S(2)}, u32[]{:S(2)}) collective-permute-start(bf16[4,128,128]{2,1,0:T(8,128)(2,1)S(1)} %attend.5.refs_1_), channel_id=1, source_target_pairs={{0,1},{1,0},{2,3},{3,2},{4,5},{5,4},{6,7},{7,6},{8,9},{9,8},{10,11... | collective-permute-start | bytes 393224 | tf_op jit(solution)/shard_map/attended 1/ppermute | solution.py:408
  33.1 6.7 %collective-permute-start.15 = (bf16[136,1024]{1,0:T(8,128)(2,1)S(1)}, bf16[136,1024]{1,0:T(8,128)(2,1)S(1)}, u32[]{:S(2)}, u32[]{:S(2)}) collective-permute-start(bf16[136,1024]{1,0:T(8,128)(2,1)S(1)} %collective-permute-done.14.refs_15_), channel_id=1, source_target_pairs={{0,4},{1,3},{4,8},{5,1},{8,12},{9,5},{12,14},{13,9},{14,10},{15,13... | collective-permute-start | bytes 835592 | tf_op jit(solution)/shard_map/o rows 4b/ppermute | solution.py:404
  37.8 6.5 %copy-start = (bf16[136,1024]{1,0:T(8,128)(2,1)}, bf16[136,1024]{1,0:T(8,128)(2,1)S(1)}, u32[]{:S(2)}) copy-start(bf16[136,1024]{1,0:T(8,128)(2,1)S(1)} %get-tuple-element.36.refs_16_) | copy-start | bytes 835588
  37.8 6.7 %collective-permute-start.16 = (bf16[136,1024]{1,0:T(8,128)(2,1)S(1)}, bf16[136,1024]{1,0:T(8,128)(2,1)}, u32[]{:S(2)}, u32[]{:S(2)}) collective-permute-start(bf16[136,1024]{1,0:T(8,128)(2,1)S(1)} %get-tuple-element.36.refs_16_), channel_id=1, source_target_pairs={{0,4},{1,3},{4,8},{5,1},{8,12},{9,5},{12,14},{13,9},{14,10},{15,13... | collective-permute-start | bytes 835592 | tf_op jit(solution)/shard_map/o rows 5a/ppermute | solution.py:404
  39.7 7.8 %collective-permute-start.17 = (bf16[136,1024]{1,0:T(8,128)(2,1)S(1)}, bf16[136,1024]{1,0:T(8,128)(2,1)}, u32[]{:S(2)}, u32[]{:S(2)}) collective-permute-start(bf16[136,1024]{1,0:T(8,128)(2,1)S(1)} %collective-permute-done.15.refs_17_), channel_id=1, source_target_pairs={{0,4},{1,3},{4,8},{5,1},{8,12},{9,5},{12,14},{13,9},{14,10},{15,13... | collective-permute-start | bytes 835592 | tf_op jit(solution)/shard_map/o rows 5b/ppermute | solution.py:404
  44.4 7.4 %copy-start.2 = (bf16[136,1024]{1,0:T(8,128)(2,1)}, bf16[136,1024]{1,0:T(8,128)(2,1)S(1)}, u32[]{:S(2)}) copy-start(bf16[136,1024]{1,0:T(8,128)(2,1)S(1)} %collective-permute-done.5.refs_0_.refs_10_) | copy-start | bytes 835588
  44.4 9.3 %collective-permute-start.11 = (bf16[4,128,128]{2,1,0:T(8,128)(2,1)S(1)}, bf16[4,128,128]{2,1,0:T(8,128)(2,1)S(1)}, u32[]{:S(2)}, u32[]{:S(2)}) collective-permute-start(bf16[4,128,128]{2,1,0:T(8,128)(2,1)S(1)} %attend.6.refs_2_), channel_id=1, source_target_pairs={{0,1},{1,0},{2,3},{3,2},{4,5},{5,4},{6,7},{7,6},{8,9},{9,8},{10,11... | collective-permute-start | bytes 393224 | tf_op jit(solution)/shard_map/attended 2/ppermute | solution.py:408
  44.5 14.8 %collective-permute-start.18 = (bf16[136,1024]{1,0:T(8,128)(2,1)}, bf16[136,1024]{1,0:T(8,128)(2,1)}, u32[]{:S(2)}, u32[]{:S(2)}) collective-permute-start(bf16[136,1024]{1,0:T(8,128)(2,1)} %collective-permute-done.16.refs_18_), channel_id=1, source_target_pairs={{0,4},{1,3},{4,8},{5,1},{8,12},{9,5},{12,14},{13,9},{14,10},{15,13... | collective-permute-start | bytes 835592 | tf_op jit(solution)/shard_map/o rows 6a/ppermute | solution.py:404
  47.5 11.9 %collective-permute-start.19 = (bf16[136,1024]{1,0:T(8,128)(2,1)}, bf16[136,1024]{1,0:T(8,128)(2,1)}, u32[]{:S(2)}, u32[]{:S(2)}) collective-permute-start(bf16[136,1024]{1,0:T(8,128)(2,1)} %collective-permute-done.17.refs_19_), channel_id=1, source_target_pairs={{0,4},{1,3},{4,8},{5,1},{8,12},{9,5},{12,14},{13,9},{14,10},{15,13... | collective-permute-start | bytes 835592 | tf_op jit(solution)/shard_map/o rows 6b/ppermute | solution.py:404
  51.8 2.4 %collective-permute-start.12 = (bf16[4,128,128]{2,1,0:T(8,128)(2,1)S(1)}, bf16[4,128,128]{2,1,0:T(8,128)(2,1)S(1)}, u32[]{:S(2)}, u32[]{:S(2)}) collective-permute-start(bf16[4,128,128]{2,1,0:T(8,128)(2,1)S(1)} %attend.7.refs_3_), channel_id=1, source_target_pairs={{0,1},{1,0},{2,3},{3,2},{4,5},{5,4},{6,7},{7,6},{8,9},{9,8},{10,11... | collective-permute-start | bytes 393224 | tf_op jit(solution)/shard_map/attended 3/ppermute | solution.py:408
  51.9 2.3 %collective-permute-start.9 = (bf16[4,128,128]{2,1,0:T(8,128)(2,1)S(1)}, bf16[4,128,128]{2,1,0:T(8,128)(2,1)S(1)}, u32[]{:S(2)}, u32[]{:S(2)}) collective-permute-start(bf16[4,128,128]{2,1,0:T(8,128)(2,1)S(1)} %get-tuple-element.34.refs_0_), channel_id=1, source_target_pairs={{0,1},{1,0},{2,3},{3,2},{4,5},{5,4},{6,7},{7,6},{8,9},{9,8},{10,11... | collective-permute-start | bytes 393224 | tf_op jit(solution)/shard_map/attended 0/ppermute | solution.py:408
  53.7 5.7 %collective-permute-start.20 = (bf16[16,1024]{1,0:T(8,128)(2,1)S(1)}, bf16[16,1024]{1,0:T(8,128)(2,1)S(1)}, u32[]{:S(2)}, u32[]{:S(2)}) collective-permute-start(bf16[16,1024]{1,0:T(8,128)(2,1)S(1)} %pad_maximum_fusion), channel_id=1, source_target_pairs={{0,2},{1,5},{4,0},{5,9},{8,4},{9,13},{12,8},{13,15},{14,12},{15,11... | collective-permute-start | bytes 98312 | tf_op jit(solution)/shard_map/gate weights back/ppermute | solution.py:454
  61.4 2.5 %collective-permute-start.21 = (f32[128,1024]{1,0:T(8,128)S(1)}, f32[128,1024]{1,0:T(8,128)S(1)}, u32[]{:S(2)}, u32[]{:S(2)}) collective-permute-start(f32[128,1024]{1,0:T(8,128)S(1)} %get-tuple-element.40), channel_id=1, source_target_pairs={{0,1},{1,0},{2,3},{3,2},{4,5},{5,4},{6,7},{7,6},{8,9},{9,8},{10,11... | collective-permute-start | bytes 1572872 | tf_op jit(solution)/shard_map/projected/ppermute | solution.py:408
  64.0 11.5 %copy-start.7 = (bf16[1,2048,1024]{2,1,0:T(8,128)(2,1)S(1)}, bf16[1,2048,1024]{2,1,0:T(8,128)(2,1)}, u32[]{:S(2)}) copy-start(bf16[1,2048,1024]{2,1,0:T(8,128)(2,1)} %refs_4_.15) | copy-start | bytes 12582916
  64.0 11.5 %copy-start.9 = (bf16[1,512,2048]{2,1,0:T(8,128)(2,1)S(1)}, bf16[1,512,2048]{2,1,0:T(8,128)(2,1)}, u32[]{:S(2)}) copy-start(bf16[1,512,2048]{2,1,0:T(8,128)(2,1)} %refs_5_.15) | copy-start | bytes 6291460
  64.4 9.2 %collective-permute-start.23 = (bf16[128,2048]{1,0:T(8,128)(2,1)S(1)}, bf16[128,2048]{1,0:T(8,128)(2,1)S(1)}, u32[]{:S(2)}, u32[]{:S(2)}) collective-permute-start(bf16[128,2048]{1,0:T(8,128)(2,1)S(1)} %get-tuple-element.42.refs_0_), channel_id=1, source_target_pairs={{0,4},{1,3},{4,8},{5,1},{8,12},{9,5},{12,14},{13,9},{14,10},{15,13... | collective-permute-start | bytes 1572872 | tf_op jit(solution)/shard_map/rows out 1a/ppermute | solution.py:404
  73.6 1.9 %collective-permute-start.43 = (bf16[128,2048]{1,0:T(8,128)(2,1)S(1)}, bf16[128,2048]{1,0:T(8,128)(2,1)S(1)}, u32[]{:S(2)}, u32[]{:S(2)}) collective-permute-start(bf16[128,2048]{1,0:T(8,128)(2,1)S(1)} %collective-permute-done.23.refs_0_), channel_id=1, source_target_pairs={{0,1},{1,0},{2,3},{3,2},{4,5},{5,4},{6,7},{7,6},{8,9},{9,8},{10,11... | collective-permute-start | bytes 1572872 | tf_op jit(solution)/shard_map/rows across 1a/ppermute | solution.py:408
  73.6 9.2 %collective-permute-start.24 = (bf16[128,2048]{1,0:T(8,128)(2,1)S(1)}, bf16[128,2048]{1,0:T(8,128)(2,1)S(1)}, u32[]{:S(2)}, u32[]{:S(2)}) collective-permute-start(bf16[128,2048]{1,0:T(8,128)(2,1)S(1)} %collective-permute-done.23.refs_0_), channel_id=1, source_target_pairs={{0,4},{1,3},{4,8},{5,1},{8,12},{9,5},{12,14},{13,9},{14,10},{15,13... | collective-permute-start | bytes 1572872 | tf_op jit(solution)/shard_map/rows out 2a/ppermute | solution.py:404
  77.4 6.9 %collective-permute-start.44 = (bf16[128,2048]{1,0:T(8,128)(2,1)S(1)}, bf16[128,2048]{1,0:T(8,128)(2,1)S(1)}, u32[]{:S(2)}, u32[]{:S(2)}) collective-permute-start(bf16[128,2048]{1,0:T(8,128)(2,1)S(1)} %get-tuple-element.60), channel_id=1, source_target_pairs={{0,1},{1,0},{2,3},{3,2},{4,5},{5,4},{6,7},{7,6},{8,9},{9,8},{10,11... | collective-permute-start | bytes 1572872 | tf_op jit(solution)/shard_map/sums across 1a/ppermute | solution.py:408
  82.8 2.8 %collective-permute-start.41 = (bf16[128,2048]{1,0:T(8,128)(2,1)S(1)}, bf16[128,2048]{1,0:T(8,128)(2,1)S(1)}, u32[]{:S(2)}, u32[]{:S(2)}) collective-permute-start(bf16[128,2048]{1,0:T(8,128)(2,1)S(1)} %collective-permute-done.24.refs_0_), channel_id=1, source_target_pairs={{0,1},{1,0},{2,3},{3,2},{4,5},{5,4},{6,7},{7,6},{8,9},{9,8},{10,11... | collective-permute-start | bytes 1572872 | tf_op jit(solution)/shard_map/rows across 2a/ppermute | solution.py:408
  82.8 9.2 %collective-permute-start.25 = (bf16[128,2048]{1,0:T(8,128)(2,1)S(1)}, bf16[128,2048]{1,0:T(8,128)(2,1)S(1)}, u32[]{:S(2)}, u32[]{:S(2)}) collective-permute-start(bf16[128,2048]{1,0:T(8,128)(2,1)S(1)} %collective-permute-done.24.refs_0_), channel_id=1, source_target_pairs={{0,4},{1,3},{4,8},{5,1},{8,12},{9,5},{12,14},{13,9},{14,10},{15,13... | collective-permute-start | bytes 1572872 | tf_op jit(solution)/shard_map/rows out 3a/ppermute | solution.py:404
  84.4 13.1 %collective-permute-start.45 = (bf16[128,2048]{1,0:T(8,128)(2,1)S(1)}, bf16[128,2048]{1,0:T(8,128)(2,1)S(1)}, u32[]{:S(2)}, u32[]{:S(2)}) collective-permute-start(bf16[128,2048]{1,0:T(8,128)(2,1)S(1)} %add.24), channel_id=1, source_target_pairs={{0,4},{1,3},{4,8},{5,1},{8,12},{9,5},{12,14},{13,9},{14,10},{15,13... | collective-permute-start | bytes 1572872 | tf_op jit(solution)/shard_map/sums out 1a/ppermute | solution.py:404
  87.4 10.1 %collective-permute-start.42 = (bf16[128,2048]{1,0:T(8,128)(2,1)S(1)}, bf16[128,2048]{1,0:T(8,128)(2,1)S(1)}, u32[]{:S(2)}, u32[]{:S(2)}) collective-permute-start(bf16[128,2048]{1,0:T(8,128)(2,1)S(1)} %get-tuple-element.58), channel_id=1, source_target_pairs={{0,1},{1,0},{2,3},{3,2},{4,5},{5,4},{6,7},{7,6},{8,9},{9,8},{10,11... | collective-permute-start | bytes 1572872 | tf_op jit(solution)/shard_map/sums across 2a/ppermute | solution.py:408
  92.0 7.4 %collective-permute-start.39 = (bf16[128,2048]{1,0:T(8,128)(2,1)S(1)}, bf16[128,2048]{1,0:T(8,128)(2,1)S(1)}, u32[]{:S(2)}, u32[]{:S(2)}) collective-permute-start(bf16[128,2048]{1,0:T(8,128)(2,1)S(1)} %collective-permute-done.25.refs_6_.refs_0_), channel_id=1, source_target_pairs={{0,1},{1,0},{2,3},{3,2},{4,5},{5,4},{6,7},{7,6},{8,9},{9,8},{10,11... | collective-permute-start | bytes 1572872 | tf_op jit(solution)/shard_map/rows across 3a/ppermute | solution.py:408
  92.0 11.2 %collective-permute-start.27 = (bf16[128,2048]{1,0:T(8,128)(2,1)S(1)}, bf16[128,2048]{1,0:T(8,128)(2,1)S(1)}, u32[]{:S(2)}, u32[]{:S(2)}) collective-permute-start(bf16[128,2048]{1,0:T(8,128)(2,1)S(1)} %collective-permute-done.25.refs_6_.refs_0_), channel_id=1, source_target_pairs={{0,4},{1,3},{4,8},{5,1},{8,12},{9,5},{12,14},{13,9},{14,10},{15,13... | collective-permute-start | bytes 1572872 | tf_op jit(solution)/shard_map/rows out 4a/ppermute | solution.py:404
  97.8 11.0 %collective-permute-start.46 = (bf16[128,2048]{1,0:T(8,128)(2,1)S(1)}, bf16[128,2048]{1,0:T(8,128)(2,1)S(1)}, u32[]{:S(2)}, u32[]{:S(2)}) collective-permute-start(bf16[128,2048]{1,0:T(8,128)(2,1)S(1)} %add.25), channel_id=1, source_target_pairs={{0,4},{1,3},{4,8},{5,1},{8,12},{9,5},{12,14},{13,9},{14,10},{15,13... | collective-permute-start | bytes 1572872 | tf_op jit(solution)/shard_map/sums out 2a/ppermute | solution.py:404
  101.2 7.6 %collective-permute-start.40 = (bf16[128,2048]{1,0:T(8,128)(2,1)S(1)}, bf16[128,2048]{1,0:T(8,128)(2,1)S(1)}, u32[]{:S(2)}, u32[]{:S(2)}) collective-permute-start(bf16[128,2048]{1,0:T(8,128)(2,1)S(1)} %get-tuple-element.56), channel_id=1, source_target_pairs={{0,1},{1,0},{2,3},{3,2},{4,5},{5,4},{6,7},{7,6},{8,9},{9,8},{10,11... | collective-permute-start | bytes 1572872 | tf_op jit(solution)/shard_map/sums across 3a/ppermute | solution.py:408
  103.2 7.4 %collective-permute-start.37 = (bf16[128,2048]{1,0:T(8,128)(2,1)S(1)}, bf16[128,2048]{1,0:T(8,128)(2,1)S(1)}, u32[]{:S(2)}, u32[]{:S(2)}) collective-permute-start(bf16[128,2048]{1,0:T(8,128)(2,1)S(1)} %collective-permute-done.27.refs_0_), channel_id=1, source_target_pairs={{0,1},{1,0},{2,3},{3,2},{4,5},{5,4},{6,7},{7,6},{8,9},{9,8},{10,11... | collective-permute-start | bytes 1572872 | tf_op jit(solution)/shard_map/rows across 4a/ppermute | solution.py:408
  103.2 11.2 %collective-permute-start.28 = (bf16[128,2048]{1,0:T(8,128)(2,1)S(1)}, bf16[128,2048]{1,0:T(8,128)(2,1)S(1)}, u32[]{:S(2)}, u32[]{:S(2)}) collective-permute-start(bf16[128,2048]{1,0:T(8,128)(2,1)S(1)} %collective-permute-done.27.refs_0_), channel_id=1, source_target_pairs={{0,4},{1,3},{4,8},{5,1},{8,12},{9,5},{12,14},{13,9},{14,10},{15,13... | collective-permute-start | bytes 1572872 | tf_op jit(solution)/shard_map/rows out 5a/ppermute | solution.py:404
  109.0 11.0 %collective-permute-start.47 = (bf16[128,2048]{1,0:T(8,128)(2,1)S(1)}, bf16[128,2048]{1,0:T(8,128)(2,1)S(1)}, u32[]{:S(2)}, u32[]{:S(2)}) collective-permute-start(bf16[128,2048]{1,0:T(8,128)(2,1)S(1)} %add.26), channel_id=1, source_target_pairs={{0,4},{1,3},{4,8},{5,1},{8,12},{9,5},{12,14},{13,9},{14,10},{15,13... | collective-permute-start | bytes 1572872 | tf_op jit(solution)/shard_map/sums out 3a/ppermute | solution.py:404
  112.5 7.6 %collective-permute-start.38 = (bf16[128,2048]{1,0:T(8,128)(2,1)S(1)}, bf16[128,2048]{1,0:T(8,128)(2,1)S(1)}, u32[]{:S(2)}, u32[]{:S(2)}) collective-permute-start(bf16[128,2048]{1,0:T(8,128)(2,1)S(1)} %get-tuple-element.54), channel_id=1, source_target_pairs={{0,1},{1,0},{2,3},{3,2},{4,5},{5,4},{6,7},{7,6},{8,9},{9,8},{10,11... | collective-permute-start | bytes 1572872 | tf_op jit(solution)/shard_map/sums across 4a/ppermute | solution.py:408
  112.5 11.2 %collective-permute-start.22 = (bf16[128,2048]{1,0:T(8,128)(2,1)S(1)}, bf16[128,2048]{1,0:T(8,128)(2,1)S(1)}, u32[]{:S(2)}, u32[]{:S(2)}) collective-permute-start(bf16[128,2048]{1,0:T(8,128)(2,1)S(1)} %get-tuple-element.42.refs_0_), channel_id=1, source_target_pairs={{0,1},{1,0},{2,3},{3,2},{4,5},{5,4},{6,7},{7,6},{8,9},{9,8},{10,11... | collective-permute-start | bytes 1572872 | tf_op jit(solution)/shard_map/normed/ppermute | solution.py:408
  114.4 7.4 %collective-permute-start.35 = (bf16[128,2048]{1,0:T(8,128)(2,1)S(1)}, bf16[128,2048]{1,0:T(8,128)(2,1)S(1)}, u32[]{:S(2)}, u32[]{:S(2)}) collective-permute-start(bf16[128,2048]{1,0:T(8,128)(2,1)S(1)} %collective-permute-done.28.refs_0_), channel_id=1, source_target_pairs={{0,1},{1,0},{2,3},{3,2},{4,5},{5,4},{6,7},{7,6},{8,9},{9,8},{10,11... | collective-permute-start | bytes 1572872 | tf_op jit(solution)/shard_map/rows across 5a/ppermute | solution.py:408
  114.4 11.8 %collective-permute-start.29 = (bf16[128,2048]{1,0:T(8,128)(2,1)S(1)}, bf16[128,2048]{1,0:T(8,128)(2,1)S(1)}, u32[]{:S(2)}, u32[]{:S(2)}) collective-permute-start(bf16[128,2048]{1,0:T(8,128)(2,1)S(1)} %collective-permute-done.28.refs_0_), channel_id=1, source_target_pairs={{0,4},{1,3},{4,8},{5,1},{8,12},{9,5},{12,14},{13,9},{14,10},{15,13... | collective-permute-start | bytes 1572872 | tf_op jit(solution)/shard_map/rows out 6a/ppermute | solution.py:404
  120.2 11.0 %collective-permute-start.48 = (bf16[128,2048]{1,0:T(8,128)(2,1)S(1)}, bf16[128,2048]{1,0:T(8,128)(2,1)S(1)}, u32[]{:S(2)}, u32[]{:S(2)}) collective-permute-start(bf16[128,2048]{1,0:T(8,128)(2,1)S(1)} %add.27), channel_id=1, source_target_pairs={{0,4},{1,3},{4,8},{5,1},{8,12},{9,5},{12,14},{13,9},{14,10},{15,13... | collective-permute-start | bytes 1572872 | tf_op jit(solution)/shard_map/sums out 4a/ppermute | solution.py:404
  123.7 7.6 %collective-permute-start.36 = (bf16[128,2048]{1,0:T(8,128)(2,1)S(1)}, bf16[128,2048]{1,0:T(8,128)(2,1)S(1)}, u32[]{:S(2)}, u32[]{:S(2)}) collective-permute-start(bf16[128,2048]{1,0:T(8,128)(2,1)S(1)} %get-tuple-element.52), channel_id=1, source_target_pairs={{0,1},{1,0},{2,3},{3,2},{4,5},{5,4},{6,7},{7,6},{8,9},{9,8},{10,11... | collective-permute-start | bytes 1572872 | tf_op jit(solution)/shard_map/sums across 5a/ppermute | solution.py:408
  125.7 25.4 %collective-permute-start.26 = (bf16[128,2048]{1,0:T(8,128)(2,1)S(1)}, bf16[128,2048]{1,0:T(8,128)(2,1)S(1)}, u32[]{:S(2)}, u32[]{:S(2)}) collective-permute-start(bf16[128,2048]{1,0:T(8,128)(2,1)S(1)} %get-tuple-element.45), channel_id=1, source_target_pairs={{0,1},{1,0},{2,3},{3,2},{4,5},{5,4},{6,7},{7,6},{8,9},{9,8},{10,11... | collective-permute-start | bytes 1572872 | tf_op jit(solution)/shard_map/sums across 0a/ppermute | solution.py:408
  126.2 6.7 %collective-permute-start.33 = (bf16[128,2048]{1,0:T(8,128)(2,1)S(1)}, bf16[128,2048]{1,0:T(8,128)(2,1)S(1)}, u32[]{:S(2)}, u32[]{:S(2)}) collective-permute-start(bf16[128,2048]{1,0:T(8,128)(2,1)S(1)} %collective-permute-done.29.refs_0_), channel_id=1, source_target_pairs={{0,1},{1,0},{2,3},{3,2},{4,5},{5,4},{6,7},{7,6},{8,9},{9,8},{10,11... | collective-permute-start | bytes 1572872 | tf_op jit(solution)/shard_map/rows across 6a/ppermute | solution.py:408
  126.3 10.6 %collective-permute-start.30 = (bf16[128,2048]{1,0:T(8,128)(2,1)S(1)}, bf16[128,2048]{1,0:T(8,128)(2,1)S(1)}, u32[]{:S(2)}, u32[]{:S(2)}) collective-permute-start(bf16[128,2048]{1,0:T(8,128)(2,1)S(1)} %collective-permute-done.29.refs_0_), channel_id=1, source_target_pairs={{0,4},{1,3},{4,8},{5,1},{8,12},{9,5},{12,14},{13,9},{14,10},{15,13... | collective-permute-start | bytes 1572872 | tf_op jit(solution)/shard_map/rows out 7a/ppermute | solution.py:404
  131.4 8.3 %collective-permute-start.49 = (bf16[64,2048]{1,0:T(8,128)(2,1)S(1)}, bf16[64,2048]{1,0:T(8,128)(2,1)S(1)}, u32[]{:S(2)}, u32[]{:S(2)}) collective-permute-start(bf16[64,2048]{1,0:T(8,128)(2,1)S(1)} %add.28), channel_id=1, source_target_pairs={{0,4},{1,3},{4,8},{5,1},{8,12},{9,5},{12,14},{13,9},{14,10},{15,13... | collective-permute-start | bytes 786440 | tf_op jit(solution)/shard_map/sums out 5a/ppermute | solution.py:404
  134.8 4.9 %collective-permute-start.34 = (bf16[128,2048]{1,0:T(8,128)(2,1)S(1)}, bf16[128,2048]{1,0:T(8,128)(2,1)S(1)}, u32[]{:S(2)}, u32[]{:S(2)}) collective-permute-start(bf16[128,2048]{1,0:T(8,128)(2,1)S(1)} %get-tuple-element.50), channel_id=1, source_target_pairs={{0,1},{1,0},{2,3},{3,2},{4,5},{5,4},{6,7},{7,6},{8,9},{9,8},{10,11... | collective-permute-start | bytes 1572872 | tf_op jit(solution)/shard_map/sums across 6a/ppermute | solution.py:408
  135.0 8.3 %collective-permute-start.52 = (bf16[64,2048]{1,0:T(8,128)(2,1)S(1)}, bf16[64,2048]{1,0:T(8,128)(2,1)S(1)}, u32[]{:S(2)}, u32[]{:S(2)}) collective-permute-start(bf16[64,2048]{1,0:T(8,128)(2,1)S(1)} %add.31), channel_id=1, source_target_pairs={{0,4},{1,3},{4,8},{5,1},{8,12},{9,5},{12,14},{13,9},{14,10},{15,13... | collective-permute-start | bytes 786440 | tf_op jit(solution)/shard_map/sums out 5b/ppermute | solution.py:404
  136.9 4.5 %collective-permute-start.31 = (bf16[128,2048]{1,0:T(8,128)(2,1)S(1)}, bf16[128,2048]{1,0:T(8,128)(2,1)S(1)}, u32[]{:S(2)}, u32[]{:S(2)}) collective-permute-start(bf16[128,2048]{1,0:T(8,128)(2,1)S(1)} %collective-permute-done.30.refs_0_), channel_id=1, source_target_pairs={{0,1},{1,0},{2,3},{3,2},{4,5},{5,4},{6,7},{7,6},{8,9},{9,8},{10,11... | collective-permute-start | bytes 1572872 | tf_op jit(solution)/shard_map/rows across 7a/ppermute | solution.py:408
  139.8 6.4 %collective-permute-start.50 = (bf16[64,2048]{1,0:T(8,128)(2,1)S(1)}, bf16[64,2048]{1,0:T(8,128)(2,1)S(1)}, u32[]{:S(2)}, u32[]{:S(2)}) collective-permute-start(bf16[64,2048]{1,0:T(8,128)(2,1)S(1)} %add.29), channel_id=1, source_target_pairs={{0,4},{1,3},{4,8},{5,1},{8,12},{9,5},{12,14},{13,9},{14,10},{15,13... | collective-permute-start | bytes 786440 | tf_op jit(solution)/shard_map/sums out 6a/ppermute | solution.py:404
  143.3 3.0 %collective-permute-start.32 = (bf16[128,2048]{1,0:T(8,128)(2,1)S(1)}, bf16[128,2048]{1,0:T(8,128)(2,1)S(1)}, u32[]{:S(2)}, u32[]{:S(2)}) collective-permute-start(bf16[128,2048]{1,0:T(8,128)(2,1)S(1)} %get-tuple-element.48), channel_id=1, source_target_pairs={{0,1},{1,0},{2,3},{3,2},{4,5},{5,4},{6,7},{7,6},{8,9},{9,8},{10,11... | collective-permute-start | bytes 1572872 | tf_op jit(solution)/shard_map/sums across 7a/ppermute | solution.py:408
  143.5 6.4 %collective-permute-start.53 = (bf16[64,2048]{1,0:T(8,128)(2,1)S(1)}, bf16[64,2048]{1,0:T(8,128)(2,1)S(1)}, u32[]{:S(2)}, u32[]{:S(2)}) collective-permute-start(bf16[64,2048]{1,0:T(8,128)(2,1)S(1)} %add.32), channel_id=1, source_target_pairs={{0,4},{1,3},{4,8},{5,1},{8,12},{9,5},{12,14},{13,9},{14,10},{15,13... | collective-permute-start | bytes 786440 | tf_op jit(solution)/shard_map/sums out 6b/ppermute | solution.py:404
  146.3 6.4 %collective-permute-start.51 = (bf16[64,2048]{1,0:T(8,128)(2,1)S(1)}, bf16[64,2048]{1,0:T(8,128)(2,1)S(1)}, u32[]{:S(2)}, u32[]{:S(2)}) collective-permute-start(bf16[64,2048]{1,0:T(8,128)(2,1)S(1)} %add.30), channel_id=1, source_target_pairs={{0,4},{1,3},{4,8},{5,1},{8,12},{9,5},{12,14},{13,9},{14,10},{15,13... | collective-permute-start | bytes 786440 | tf_op jit(solution)/shard_map/sums out 7a/ppermute | solution.py:404
  150.0 6.4 %collective-permute-start.54 = (bf16[64,2048]{1,0:T(8,128)(2,1)S(1)}, bf16[64,2048]{1,0:T(8,128)(2,1)S(1)}, u32[]{:S(2)}, u32[]{:S(2)}) collective-permute-start(bf16[64,2048]{1,0:T(8,128)(2,1)S(1)} %add.33), channel_id=1, source_target_pairs={{0,4},{1,3},{4,8},{5,1},{8,12},{9,5},{12,14},{13,9},{14,10},{15,13... | collective-permute-start | bytes 786440 | tf_op jit(solution)/shard_map/sums out 7b/ppermute | solution.py:404
  (9 other events, 32.9 us)

commit v6 on v5

--- a/solution.py
+++ b/solution.py
@@ -45,24 +45,32 @@
     def way(self, g, k):
         return 1 if (g + k) % 2 == 0 else -1
 
-    def step(self, sign):
-        route = []
-        for g in range(self.groups):
-            for e, (i, k) in self.place.items():
-                target = self.at(i + sign * self.way(g, k), k)
-                route.append((g * self.count + e, g * self.count + target))
-        return route
+    def step(self):
+        return [
+            (g * self.count + e, g * self.count + self.at(i + self.way(g, k), k))
+            for g in range(self.groups)
+            for e, (i, k) in self.place.items()
+        ]
+
+    def back(self, flip_lane):
+        return [
+            (g * self.count + self.at(i + self.way(g, k), k ^ flip_lane), g * self.count + e)
+            for g in range(self.groups)
+            for e, (i, k) in self.place.items()
+        ]
 
     def sibling(self):
         return [(e, e ^ 1) for e in range(self.count)]
 
-    def source(self, s, flip_lane):
-        out = []
-        for g in (0, 1):
-            for e in range(self.count):
-                i, k = self.place[e]
-                out.append(self.at(i - s * self.way(g, k), k ^ flip_lane))
-        return out
+    def source(self, place, s, flip_lane):
+        me, odd = lax.rem(place, self.count), place // self.count
+        chip, lane = me // 2, lax.rem(me, 2)
+        evens = (self.pairs + 1) // 2
+        i = jnp.where(lax.rem(chip, 2) == 0, chip // 2, self.pairs - 1 - chip // 2)
+        way = 1 - 2 * lax.rem(odd + lane, 2)
+        i = lax.rem(i - s * way + 2 * self.pairs, self.pairs)
+        chip = jnp.where(i < evens, 2 * i, 2 * (self.pairs - 1 - i) + 1)
+        return 2 * chip + lax.rem(lane + flip_lane, 2)
 
 
 def swap_pairs(axis):
@@ -85,10 +93,11 @@
     scale = 1.0 / math.sqrt(HD)
     for h in range(count):
         cols = slice((first + h) * HD, (first + h + 1) * HD)
+        own = slice(h * HD, (h + 1) * HD)
         q = q_ref[:, cols]
         s0 = lax.dot_general(q, kv_ref[0, :, cols], dims, preferred_element_type=F32) * scale
         s1 = lax.dot_general(q, cache_ref[0, 0, 0, :, cols], dims, preferred_element_type=F32) * scale
-        s2 = lax.dot_general(q, far_ref[0, :, cols], dims, preferred_element_type=F32) * scale
+        s2 = lax.dot_general(q, far_ref[0, :, own], dims, preferred_element_type=F32) * scale
         s1 = jnp.where(near_ok, s1, -1e30)
         s2 = jnp.where(far_ok, s2, -1e30)
         m = jnp.max(jnp.maximum(jnp.maximum(s0, s1), s2), axis=1, keepdims=True)
@@ -98,7 +107,7 @@
         l = jnp.sum(w0 + w1 + w2, axis=1, keepdims=True)
         a = jnp.dot(w0.astype(BF16), kv_ref[1, :, cols], preferred_element_type=F32)
         a += jnp.dot(w1.astype(BF16), cache_ref[1, 0, 0, :, cols], preferred_element_type=F32)
-        a += jnp.dot(w2.astype(BF16), far_ref[1, :, cols], preferred_element_type=F32)
+        a += jnp.dot(w2.astype(BF16), far_ref[1, :, own], preferred_element_type=F32)
         out_ref[h] = (a / l).astype(BF16)
 
 
@@ -153,7 +162,11 @@
     return pl.pallas_call(
         functools.partial(attend_body, first, count, len(passed) + len(after)),
         out_shape=out,
-        in_specs=[scalars()] + [full()] * 4 + [anywhere()] * (len(passed) + len(after)),
+        grid=(1,),
+        in_specs=[scalars()]
+        + [full()] * 3
+        + [pl.BlockSpec((2, far.shape[1], count * HD), lambda i: (0, 0, first // count))]
+        + [anywhere()] * (len(passed) + len(after)),
         out_specs=[full()] + [anywhere()] * len(passed),
         input_output_aliases={5: 1} if passed else {},
         cost_estimate=cost(2.4),
@@ -162,7 +175,7 @@
     )(seg_len, queries, span_kv, cache_kv, far, *passed, *after)
 
 
-def pack_body(count, lane_ref, rows_ref, routes_ref, wts_ref, own_ref, other_ref):
+def pack_body(count, lane_ref, rows_ref, routes_ref, wts_ref, own_ref, other_ref, tail_ref):
     slab, half = rows_ref.shape[0], own_ref.shape[1]
     lane = lane_ref[0]
     own_ref[:slab] = rows_ref[:, pl.ds(pl.multiple_of(lane * half, HD), half)]
@@ -187,6 +200,10 @@
         out[slab:, : tail.shape[1]] = tail
         if tail.shape[1] < half:
             out[slab:, tail.shape[1] :] = jnp.zeros((8, half - tail.shape[1]), BF16)
+    tail_ref[:8, : tail.shape[1]] = tail
+    tail_ref[8:, : tail.shape[1]] = jnp.zeros_like(tail)
+    if tail.shape[1] < half:
+        tail_ref[:, tail.shape[1] :] = jnp.zeros((16, half - tail.shape[1]), BF16)
 
 
 def pack(count, lane, o_rows, routes, route_wts):
@@ -194,22 +211,22 @@
     out = jax.ShapeDtypeStruct((slab + 8, width // 2), BF16)
     return pl.pallas_call(
         functools.partial(pack_body, count),
-        out_shape=(out, out),
+        out_shape=(out, out, jax.ShapeDtypeStruct((16, width // 2), BF16)),
         in_specs=[scalars()] + [full()] * 3,
-        out_specs=(full(), full()),
+        out_specs=(full(), full(), full()),
         cost_estimate=cost(0.7),
         compiler_params=pltpu.CompilerParams(vmem_limit_bytes=8 * 2**20),
         name="pack",
     )(lane, o_rows, routes.T, route_wts.T)
 
 
-def project_body(first, blocks, pieces, carried, here, tail, table_ref, me_ref, *refs):
+def project_body(ring, steps, blocks, pieces, carried, here, tail, me_ref, *refs):
     refs = list(refs)
     mine = [refs.pop(0) for _ in range(pieces)]
     theirs = [refs.pop(0) for _ in range(pieces)]
     before = [refs.pop(0) for _ in range(2 if carried else 0)]
     source = [refs.pop(0) for _ in range(blocks)]
-    tail_refs = [refs.pop(0) for _ in range(tail // 2)]
+    tail_refs = [refs.pop(0) for _ in range(tail)]
     own_ref, give_ref, wts_ref, att = refs[:4]
     rows = own_ref.shape[0]
     slab = att.shape[2]
@@ -243,16 +260,16 @@
     for b in [*range(blocks - here, blocks), *range(blocks - here)]:
         if b < len(copies):
             copies[b].wait()
-        head = att[table_ref[place, first + b]]
+        head = att[ring.source(place, steps[b // 2], b % 2)]
         part = jnp.dot(head, source[b][:slab], preferred_element_type=F32)
         total = part if total is None else total + part
         if b >= tail:
             lines[b] = line(source[b], slab)
     for i, ref in enumerate(tail_refs):
-        lines[2 * i : 2 * i + 2] = [line(ref, 0), line(ref, 8)]
+        lines[i] = line(ref, 0)
     if carried:
         own_ref[...] = before[0][...] + total[:rows]
-        give_ref[...] = before[1][...] + total[rows:]
+        give_ref[...] = (before[1][...] + total[rows:]).astype(give_ref.dtype)
     else:
         own_ref[...] = total[:rows]
         give_ref[...] = total[rows:]
@@ -260,7 +277,7 @@
     wts_ref[...] = jnp.concatenate(lines, axis=0).T
 
 
-def project(table, place, first, mine, theirs, before, blocks, here, tails=()):
+def project(ring, place, steps, mine, theirs, before, blocks, here, tails=()):
     count = sum(part.shape[0] for part in mine)
     rows, slab = mine[0].shape[1:]
     half = blocks[0].shape[1]
@@ -272,10 +289,14 @@
         scratch += [pltpu.VMEM((away,) + blocks[0].shape, BF16), pltpu.SemaphoreType.DMA((away,))]
     return pl.pallas_call(
         functools.partial(
-            project_body, first, number, len(mine), bool(before), here, 2 * len(tails)
+            project_body, ring, steps, number, len(mine), bool(before), here, len(tails)
         ),
-        out_shape=(out, out, jax.ShapeDtypeStruct((rows, 128), F32)),
-        in_specs=[scalars(), scalars()]
+        out_shape=(
+            out,
+            jax.ShapeDtypeStruct((rows, half), BF16 if before else F32),
+            jax.ShapeDtypeStruct((rows, 128), F32),
+        ),
+        in_specs=[scalars()]
         + [full()] * (2 * len(mine) + len(before))
         + [in_hbm()] * away
         + [full()] * here
@@ -287,14 +308,14 @@
         ),
         compiler_params=pltpu.CompilerParams(vmem_limit_bytes=PRO_MIB * 2**20),
         name="project",
-    )(table, place, *mine, *theirs, *before, *blocks, *tails)
+    )(place, *mine, *theirs, *before, *blocks, *tails)
 
 
 def norm_body(lane_ref, resid_ref, own_ref, got_ref, gain_ref, sum_ref, out_ref):
     first = lane_ref[0] == 0
     half = own_ref.shape[1]
     own = own_ref[...]
-    got = got_ref[...]
+    got = got_ref[...].astype(F32)
     low = resid_ref[:, :half].astype(F32) + jnp.where(first, own, got)
     high = resid_ref[:, half:].astype(F32) + jnp.where(first, got, own)
     sum_ref[:, :half] = low
@@ -364,10 +385,10 @@
         term = jnp.concatenate([ref[c].astype(F32) for ref, c in zip(refs[at:], cut)], axis=0)
         at += len(cut)
         total = term if total is None else total + term
-    refs[-1][...] = total.astype(BF16)
-
-
-def add(cut, rows, terms):
+    refs[-1][...] = total.astype(refs[-1].dtype)
+
+
+def add(cut, rows, terms, kind):
     used, cuts = [], []
     for term in terms:
         size = rows // len(term)
@@ -380,7 +401,7 @@
         cuts.append(mine)
     return pl.pallas_call(
         functools.partial(add_body, cuts),
-        out_shape=jax.ShapeDtypeStruct((cut.stop - cut.start, used[0].shape[1]), BF16),
+        out_shape=jax.ShapeDtypeStruct((cut.stop - cut.start, used[0].shape[1]), kind),
         in_specs=[full()] * len(used),
         out_specs=full(),
         cost_estimate=cost(ADD_COST),
@@ -396,7 +417,7 @@
     rows, width = queries.shape
     me = lax.axis_index("expert")
     lane = me % 2
-    forward, backward, sibling = ring.step(1), ring.step(-1), ring.sibling()
+    forward, sibling = ring.step(), ring.sibling()
     place = lax.axis_index("group") % 2 * count + me
 
     def ahead(block, name="rows out"):
@@ -417,7 +438,7 @@
     with jax.named_scope("far segment"):
         far = lax.ppermute(far_segment(seg_len, cache_kv), "group", group_swap)
 
-    chain_a, other = pack(count, lane[None], o_rows, routes, route_wts)
+    chain_a, other, tail = pack(count, lane[None], o_rows, routes, route_wts)
     chain_b = across(other)
     blocks = [chain_a, chain_b]
     mine, theirs = [], []
@@ -449,15 +470,8 @@
     blocks += ends
     tails = []
     with jax.named_scope("gate weights back"):
-        tail = jnp.concatenate([blocks[0][slab:], blocks[1][slab:]], axis=0)
-        for _ in range(HOPS_X):
-            tail = lax.ppermute(tail, ("group", "expert"), backward)
-            tails.insert(0, tail)
-    sources = []
-    for s in order:
-        sources += [ring.source(s, 0), ring.source(s, 1)]
-    table = jnp.asarray([[line[e] for line in sources] for e in range(2 * count)], jnp.int32)
-
+        for route in (ring.back(0), ring.back(1)) if HOPS_X else ():
+            tails.append(lax.ppermute(tail, ("group", "expert"), route))
     if slab != HD:
         mine, theirs = (
             [jnp.concatenate(p).transpose(1, 0, 2).reshape(rows, count, slab).transpose(1, 0, 2)]
@@ -465,9 +479,9 @@
         )
     early = 2 * (pairs - 1 - HOPS_X)
     place = place[None]
-    first_own, first_give, wts_early = project(table, place, 0, mine, theirs, [], blocks[:early], 0)
+    first_own, first_give, wts_early = project(ring, place, order[: early // 2], mine, theirs, [], blocks[:early], 0)
     own, give, wts_late = project(
-        table, place, early, mine, theirs, [first_own, first_give], blocks[early:], 2, tails
+        ring, place, order[early // 2 :], mine, theirs, [first_own, first_give], blocks[early:], 2, tails
     )
     got = across(give, "projected")
     residual, normed = norm(lane[None], resid, own, got, norm_gain)
@@ -486,10 +500,10 @@
         keep, *give = expert((column_x, column_y), x[s], y[s], wx, wy, w_in, w_out, after, GIVE)
         return keep, [across(part, f"sums across {s}{'ab'[i]}") for i, part in enumerate(give)]
 
-    def combine(terms, parts):
+    def combine(terms, parts, kind=BF16):
         terms = [term if isinstance(term, list) else [term] for term in terms if len(term)]
         return [
-            add(slice(p * rows // parts, (p + 1) * rows // parts), rows, terms) for p in range(parts)
+            add(slice(p * rows // parts, (p + 1) * rows // parts), rows, terms, kind) for p in range(parts)
         ]
 
     travelling = []
@@ -499,8 +513,8 @@
         keep, back = sums(s)
         total = combine([keep, back, travelling], 2 if s >= TAIL else 1)
         travelling = [ahead(part, f"sums out {s}{'ab'[i]}") for i, part in enumerate(total)]
-    keep, back = sums(0, (x[min(LATE, pairs - 1)][0],))
-    return combine([residual, keep, back, travelling], 1)[0]
+    base = combine([residual, *sums(0, (x[min(LATE, pairs - 1)][0],))], 1, F32)
+    return combine([base, travelling], 1)[0]
 
 
 def solution(mesh):

time: 158 us -> 154 us (0.975)
  starting transfers between devices: 53.4 us -> 55.7 us
  waiting for transfers between devices: 63.9 us -> 61.7 us
  Pallas kernels: 36.5 us -> 34.6 us
  transfers between devices with their start and end apart: 55 -> 56, of which waited for: 25 -> 25; matrix products, arithmetic and copies ran while one was open for 1% -> 0% of each run, Pallas kernels for 19% -> 18%
where the time goes in v6:
time: 154 us
  waiting for transfers between devices  61.7 us (40%)
  starting transfers between devices  55.7 us (36%)
  Pallas kernels  34.6 us (22%)
  local copies, waits for them, and re-layouts  1.63 us (1%)
    ppermute x29, waiting for transfers between devices, ahead(): return lax.ppermute(block, ('group', 'expert'), forward)  57.7 us
    ppermute x29, starting transfers between devices, ahead(): return lax.ppermute(block, ('group', 'expert'), forward)  45.9 us
    pallas_call x8, Pallas kernels, expert(): pl.pallas_call(functools.partial(expert_body, cols, parts, len(after), gi...  15 us
    pallas_call x4, Pallas kernels, attend(): pl.pallas_call(functools.partial(attend_body, first, count, len(passed) +...  9.18 us
    pallas_call x2, Pallas kernels, project(): pl.pallas_call(functools.partial(project_body, ring, steps, number, len(m...  4.68 us
    ppermute x22, starting transfers between devices, across(): return lax.ppermute(block, 'expert', sibling)  3.11 us
    pallas_call x1, Pallas kernels, far_segment(): pl.pallas_call(far_body, out_shape=jax.ShapeDtypeStruct((2,) + cache_kv.s...  3.08 us
  transfers between devices with their start and end apart: 56, of which 25 were waited for; matrix products, arithmetic and copies ran while one was open for 0% of the time, Pallas kernels for 18%

profile of v6, /device:TPU:0, one launch (start us, length us, event | category | flops | bytes accessed | tf_op | source)
XLA Modules:
  0.0 154.1 jit_solution(12832411041260906346)
XLA Ops:
  0.0 3.1 %far_segment.1 = bf16[2,128,2048]{2,1,0:T(8,128)(2,1)} custom-call(s32[1,2]{1,0:T(1,128)} %len_ref.9, bf16[2,1,2,128,2048]{4,3,2,1,0:T(8,128)(2,1)} %cache_ref.9), custom_call_target="tpu_custom_call" | custom-call | flops 10200000512 | bytes 1000 | tf_op jit(solution)/shard_map/far segment/far_segment/pallas_call | solution.py:125
  3.1 3.0 %collective-permute-start = (bf16[2,128,2048]{2,1,0:T(8,128)(2,1)}, bf16[2,128,2048]{2,1,0:T(8,128)(2,1)}, u32[]{:S(2)}, u32[]{:S(2)}) collective-permute-start(bf16[2,128,2048]{2,1,0:T(8,128)(2,1)} %far_segment.1), channel_id=1, source_target_pairs={{0,16},{16,0},{1,17},{17,1},{2,18},{18,2},{3,19},{19,3},{4,20},{20... | collective-permute-start | bytes 3145736 | tf_op jit(solution)/shard_map/far segment/ppermute | solution.py:439
  6.8 1.6 %collective-permute-start.1 = (bf16[136,1024]{1,0:T(8,128)(2,1)S(1)}, bf16[136,1024]{1,0:T(8,128)(2,1)S(1)}, u32[]{:S(2)}, u32[]{:S(2)}) collective-permute-start(bf16[136,1024]{1,0:T(8,128)(2,1)S(1)} %get-tuple-element.34.refs_8_), channel_id=1, source_target_pairs={{0,4},{1,3},{4,8},{5,1},{8,12},{9,5},{12,14},{13,9},{14,10},{15,13... | collective-permute-start | bytes 835592 | tf_op jit(solution)/shard_map/o rows 1a/ppermute | solution.py:425
  8.4 1.6 %collective-permute-start.7 = (bf16[136,1024]{1,0:T(8,128)(2,1)S(1)}, bf16[136,1024]{1,0:T(8,128)(2,1)S(1)}, u32[]{:S(2)}, u32[]{:S(2)}) collective-permute-start(bf16[136,1024]{1,0:T(8,128)(2,1)S(1)} %collective-permute-done.6.refs_9_), channel_id=1, source_target_pairs={{0,4},{1,3},{4,8},{5,1},{8,12},{9,5},{12,14},{13,9},{14,10},{15,13... | collective-permute-start | bytes 835592 | tf_op jit(solution)/shard_map/o rows 1b/ppermute | solution.py:425
  10.0 3.4 %collective-permute-done.1.refs_10_ = bf16[136,1024]{1,0:T(8,128)(2,1)S(1)} collective-permute-done((bf16[136,1024]{1,0:T(8,128)(2,1)S(1)}, bf16[136,1024]{1,0:T(8,128)(2,1)S(1)}, u32[]{:S(2)}, u32[]{:S(2)}) %collective-permute-start.1) | collective-permute-done | bytes 278560 | tf_op jit(solution)/shard_map/o rows 1a/ppermute | solution.py:425
  13.4 1.6 %collective-permute-start.2 = (bf16[136,1024]{1,0:T(8,128)(2,1)S(1)}, bf16[136,1024]{1,0:T(8,128)(2,1)S(1)}, u32[]{:S(2)}, u32[]{:S(2)}) collective-permute-start(bf16[136,1024]{1,0:T(8,128)(2,1)S(1)} %collective-permute-done.1.refs_10_), channel_id=1, source_target_pairs={{0,4},{1,3},{4,8},{5,1},{8,12},{9,5},{12,14},{13,9},{14,10},{15,13... | collective-permute-start | bytes 835592 | tf_op jit(solution)/shard_map/o rows 2a/ppermute | solution.py:425
  14.9 1.4 collective-permute-done.7.refs_11_
  16.4 1.6 %collective-permute-start.13 = (bf16[136,1024]{1,0:T(8,128)(2,1)S(1)}, bf16[136,1024]{1,0:T(8,128)(2,1)S(1)}, u32[]{:S(2)}, u32[]{:S(2)}) collective-permute-start(bf16[136,1024]{1,0:T(8,128)(2,1)S(1)} %collective-permute-done.7.refs_11_), channel_id=1, source_target_pairs={{0,4},{1,3},{4,8},{5,1},{8,12},{9,5},{12,14},{13,9},{14,10},{15,13... | collective-permute-start | bytes 835592 | tf_op jit(solution)/shard_map/o rows 2b/ppermute | solution.py:425
  17.9 2.0 %collective-permute-done.2.refs_12_ = bf16[136,1024]{1,0:T(8,128)(2,1)S(1)} collective-permute-done((bf16[136,1024]{1,0:T(8,128)(2,1)S(1)}, bf16[136,1024]{1,0:T(8,128)(2,1)S(1)}, u32[]{:S(2)}, u32[]{:S(2)}) %collective-permute-start.2) | collective-permute-done | bytes 278560 | tf_op jit(solution)/shard_map/o rows 2a/ppermute | solution.py:425
  19.9 1.6 %collective-permute-start.3 = (bf16[136,1024]{1,0:T(8,128)(2,1)S(1)}, bf16[136,1024]{1,0:T(8,128)(2,1)S(1)}, u32[]{:S(2)}, u32[]{:S(2)}) collective-permute-start(bf16[136,1024]{1,0:T(8,128)(2,1)S(1)} %collective-permute-done.2.refs_12_), channel_id=1, source_target_pairs={{0,4},{1,3},{4,8},{5,1},{8,12},{9,5},{12,14},{13,9},{14,10},{15,13... | collective-permute-start | bytes 835592 | tf_op jit(solution)/shard_map/o rows 3a/ppermute | solution.py:425
  22.0 1.5 %collective-permute-start.8 = (bf16[136,1024]{1,0:T(8,128)(2,1)S(1)}, bf16[136,1024]{1,0:T(8,128)(2,1)S(1)}, u32[]{:S(2)}, u32[]{:S(2)}) collective-permute-start(bf16[136,1024]{1,0:T(8,128)(2,1)S(1)} %collective-permute-done.7.refs_11_), channel_id=1, source_target_pairs={{0,16},{16,0},{1,17},{17,1},{2,18},{18,2},{3,19},{19,3},{4,20},{20... | collective-permute-start | bytes 835592 | tf_op jit(solution)/shard_map/o rows of partner/ppermute | solution.py:458
  23.5 1.6 %collective-permute-start.14 = (bf16[136,1024]{1,0:T(8,128)(2,1)S(1)}, bf16[136,1024]{1,0:T(8,128)(2,1)S(1)}, u32[]{:S(2)}, u32[]{:S(2)}) collective-permute-start(bf16[136,1024]{1,0:T(8,128)(2,1)S(1)} %collective-permute-done.13.refs_13_), channel_id=1, source_target_pairs={{0,4},{1,3},{4,8},{5,1},{8,12},{9,5},{12,14},{13,9},{14,10},{15,13... | collective-permute-start | bytes 835592 | tf_op jit(solution)/shard_map/o rows 3b/ppermute | solution.py:425
  25.1 1.4 collective-permute-done.3.refs_14_
  26.5 1.6 %collective-permute-start.4 = (bf16[136,1024]{1,0:T(8,128)(2,1)S(1)}, bf16[136,1024]{1,0:T(8,128)(2,1)S(1)}, u32[]{:S(2)}, u32[]{:S(2)}) collective-permute-start(bf16[136,1024]{1,0:T(8,128)(2,1)S(1)} %collective-permute-done.3.refs_14_), channel_id=1, source_target_pairs={{0,4},{1,3},{4,8},{5,1},{8,12},{9,5},{12,14},{13,9},{14,10},{15,13... | collective-permute-start | bytes 835592 | tf_op jit(solution)/shard_map/o rows 4a/ppermute | solution.py:425
  28.0 2.4 %collective-permute-done.far_ref = bf16[2,128,2048]{2,1,0:T(8,128)(2,1)} collective-permute-done((bf16[2,128,2048]{2,1,0:T(8,128)(2,1)}, bf16[2,128,2048]{2,1,0:T(8,128)(2,1)}, u32[]{:S(2)}, u32[]{:S(2)}) %collective-permute-start) | collective-permute-done | bytes 1048608 | tf_op jit(solution)/shard_map/far segment/ppermute | solution.py:439
  30.4 2.3 %attend.5.refs_1_ = bf16[4,128,128]{2,1,0:T(8,128)(2,1)S(1)} custom-call(s32[1,2]{1,0:T(1,128)S(1)} %copy-done.17, bf16[128,2048]{1,0:T(8,128)(2,1)S(1)} %copy-done.11, bf16[2,128,2048]{2,1,0:T(8,128)(2,1)S(1)} %copy-done.9, bf16[2,1,2,128,2048]{4,3,2,1,0:T(8,128)(2,1)S(1)} %copy-done.7, bf16[2,128,2048]{2,1,0:T(8,128)(2,1)} %collective-permute-done.far_ref), custom_call_target="tpu_custom_call" | custom-call | flops 14400000000 | bytes 1000 | tf_op jit(solution)/shard_map/attend/pallas_call | solution.py:162
  32.8 2.2 %collective-permute-start.15 = (bf16[136,1024]{1,0:T(8,128)(2,1)S(1)}, bf16[136,1024]{1,0:T(8,128)(2,1)S(1)}, u32[]{:S(2)}, u32[]{:S(2)}) collective-permute-start(bf16[136,1024]{1,0:T(8,128)(2,1)S(1)} %collective-permute-done.14.refs_15_), channel_id=1, source_target_pairs={{0,4},{1,3},{4,8},{5,1},{8,12},{9,5},{12,14},{13,9},{14,10},{15,13... | collective-permute-start | bytes 835592 | tf_op jit(solution)/shard_map/o rows 4b/ppermute | solution.py:425
  35.0 2.3 %attend.4 = (bf16[4,128,128]{2,1,0:T(8,128)(2,1)S(1)}, bf16[136,1024]{1,0:T(8,128)(2,1)S(1)}) custom-call(s32[1,2]{1,0:T(1,128)S(1)} %copy-done.17, bf16[128,2048]{1,0:T(8,128)(2,1)S(1)} %copy-done.11, bf16[2,128,2048]{2,1,0:T(8,128)(2,1)S(1)} %copy-done.9, bf16[2,1,2,128,2048]{4,3,2,1,0:T(8,128)(2,1)S(1)} %copy-done.7, ...), custom_call_target="tpu_custom_call", output_to_operand_aliasing={{1}: (5, {})} | custom-call | flops 14400000000 | bytes 1000 | tf_op jit(solution)/shard_map/attend/pallas_call | solution.py:162
  37.3 1.6 %collective-permute-start.16 = (bf16[136,1024]{1,0:T(8,128)(2,1)S(1)}, bf16[136,1024]{1,0:T(8,128)(2,1)}, u32[]{:S(2)}, u32[]{:S(2)}) collective-permute-start(bf16[136,1024]{1,0:T(8,128)(2,1)S(1)} %get-tuple-element.37.refs_16_), channel_id=1, source_target_pairs={{0,4},{1,3},{4,8},{5,1},{8,12},{9,5},{12,14},{13,9},{14,10},{15,13... | collective-permute-start | bytes 835592 | tf_op jit(solution)/shard_map/o rows 5a/ppermute | solution.py:425
  39.5 2.1 %collective-permute-start.17 = (bf16[136,1024]{1,0:T(8,128)(2,1)S(1)}, bf16[136,1024]{1,0:T(8,128)(2,1)}, u32[]{:S(2)}, u32[]{:S(2)}) collective-permute-start(bf16[136,1024]{1,0:T(8,128)(2,1)S(1)} %collective-permute-done.15.refs_17_), channel_id=1, source_target_pairs={{0,4},{1,3},{4,8},{5,1},{8,12},{9,5},{12,14},{13,9},{14,10},{15,13... | collective-permute-start | bytes 835592 | tf_op jit(solution)/shard_map/o rows 5b/ppermute | solution.py:425
  41.5 2.3 %attend.6.refs_2_ = bf16[4,128,128]{2,1,0:T(8,128)(2,1)S(1)} custom-call(s32[1,2]{1,0:T(1,128)S(1)} %copy-done.17, bf16[128,2048]{1,0:T(8,128)(2,1)S(1)} %copy-done.11, bf16[2,128,2048]{2,1,0:T(8,128)(2,1)S(1)} %copy-done.9, bf16[2,1,2,128,2048]{4,3,2,1,0:T(8,128)(2,1)S(1)} %copy-done.7, bf16[2,128,2048]{2,1,0:T(8,128)(2,1)} %collective-permute-done.far_ref), custom_call_target="tpu_custom_call" | custom-call | flops 14400000000 | bytes 1000 | tf_op jit(solution)/shard_map/attend/pallas_call | solution.py:162
  44.0 1.6 %collective-permute-start.18 = (bf16[136,1024]{1,0:T(8,128)(2,1)}, bf16[136,1024]{1,0:T(8,128)(2,1)}, u32[]{:S(2)}, u32[]{:S(2)}) collective-permute-start(bf16[136,1024]{1,0:T(8,128)(2,1)} %collective-permute-done.16.refs_18_), channel_id=1, source_target_pairs={{0,4},{1,3},{4,8},{5,1},{8,12},{9,5},{12,14},{13,9},{14,10},{15,13... | collective-permute-start | bytes 835592 | tf_op jit(solution)/shard_map/o rows 6a/ppermute | solution.py:425
  45.6 1.4 collective-permute-done.17.refs_19_
  47.0 1.6 %collective-permute-start.19 = (bf16[136,1024]{1,0:T(8,128)(2,1)}, bf16[136,1024]{1,0:T(8,128)(2,1)}, u32[]{:S(2)}, u32[]{:S(2)}) collective-permute-start(bf16[136,1024]{1,0:T(8,128)(2,1)} %collective-permute-done.17.refs_19_), channel_id=1, source_target_pairs={{0,4},{1,3},{4,8},{5,1},{8,12},{9,5},{12,14},{13,9},{14,10},{15,13... | collective-permute-start | bytes 835592 | tf_op jit(solution)/shard_map/o rows 6b/ppermute | solution.py:425
  48.6 2.4 %attend.7.refs_3_ = bf16[4,128,128]{2,1,0:T(8,128)(2,1)S(1)} custom-call(s32[1,2]{1,0:T(1,128)S(1)} %copy-done.17, bf16[128,2048]{1,0:T(8,128)(2,1)S(1)} %copy-done.11, bf16[2,128,2048]{2,1,0:T(8,128)(2,1)S(1)} %copy-done.9, bf16[2,1,2,128,2048]{4,3,2,1,0:T(8,128)(2,1)S(1)} %copy-done.7, bf16[2,128,2048]{2,1,0:T(8,128)(2,1)} %collective-permute-done.far_ref, ...), custom_call_target="tpu_custom_call" | custom-call | flops 14400000000 | bytes 1000 | tf_op jit(solution)/shard_map/attend/pallas_call | solution.py:162
  54.2 2.7 %project.2 = (f32[128,1024]{1,0:T(8,128)S(1)}, f32[128,1024]{1,0:T(8,128)S(1)}, f32[128,128]{1,0:T(8,128)S(1)}) custom-call(s32[1]{0:T(128)} %bitcast.1.me_ref, bf16[4,128,128]{2,1,0:T(8,128)(2,1)S(1)} %get-tuple-element.35.refs_0_, bf16[4,128,128]{2,1,0:T(8,128)(2,1)S(1)} %attend.5.refs_1_, bf16[4,128,128]{2,1,0:T(8,128)(2,1)S(1)} %attend.6.refs_2_, ...), custom_call_target="tpu_custom_call" | custom-call | flops 805306368 | bytes 3145728 | tf_op jit(solution)/shard_map/project/pallas_call | solution.py:290
  57.0 2.0 %project.3 = (f32[128,1024]{1,0:T(8,128)S(1)}, bf16[128,1024]{1,0:T(8,128)(2,1)S(1)}, f32[128,128]{1,0:T(8,128)S(1)}) custom-call(s32[1]{0:T(128)} %bitcast.1.me_ref, bf16[4,128,128]{2,1,0:T(8,128)(2,1)S(1)} %get-tuple-element.35.refs_0_, bf16[4,128,128]{2,1,0:T(8,128)(2,1)S(1)} %attend.5.refs_1_, bf16[4,128,128]{2,1,0:T(8,128)(2,1)S(1)} %attend.6.refs_2_, ...), custom_call_target="tpu_custom_call" | custom-call | flops 268435456 | bytes 1048576 | tf_op jit(solution)/shard_map/project/pallas_call | solution.py:290
  61.2 1.6 %collective-permute-start.24 = (bf16[128,2048]{1,0:T(8,128)(2,1)S(1)}, bf16[128,2048]{1,0:T(8,128)(2,1)S(1)}, u32[]{:S(2)}, u32[]{:S(2)}) collective-permute-start(bf16[128,2048]{1,0:T(8,128)(2,1)S(1)} %get-tuple-element.44.refs_0_), channel_id=1, source_target_pairs={{0,4},{1,3},{4,8},{5,1},{8,12},{9,5},{12,14},{13,9},{14,10},{15,13... | collective-permute-start | bytes 1572872 | tf_op jit(solution)/shard_map/rows out 1a/ppermute | solution.py:425
  62.8 7.7 %collective-permute-done.24.refs_0_ = bf16[128,2048]{1,0:T(8,128)(2,1)S(1)} collective-permute-done((bf16[128,2048]{1,0:T(8,128)(2,1)S(1)}, bf16[128,2048]{1,0:T(8,128)(2,1)S(1)}, u32[]{:S(2)}, u32[]{:S(2)}) %collective-permute-start.24) | collective-permute-done | bytes 524320 | tf_op jit(solution)/shard_map/rows out 1a/ppermute | solution.py:425
  70.4 1.5 collective-permute-start.25
  72.4 1.9 %expert.15 = (bf16[128,2048]{1,0:T(8,128)(2,1)S(1)}, bf16[128,2048]{1,0:T(8,128)(2,1)S(1)}) custom-call(bf16[128,2048]{1,0:T(8,128)(2,1)S(1)} %collective-permute-done.24.refs_0_, bf16[128,2048]{1,0:T(8,128)(2,1)S(1)} %collective-permute-done.44.refs_1_, f32[128,128]{1,0:T(8,128)S(1)} %get-tuple-element.45.refs_2_.refs_3_, ...), custom_call_target="tpu_custom_call" | custom-call | flops 24000000000 | bytes 1000 | tf_op jit(solution)/shard_map/expert/pallas_call | solution.py:370
  74.4 5.2 %collective-permute-done.25.refs_0_ = bf16[128,2048]{1,0:T(8,128)(2,1)S(1)} collective-permute-done((bf16[128,2048]{1,0:T(8,128)(2,1)S(1)}, bf16[128,2048]{1,0:T(8,128)(2,1)S(1)}, u32[]{:S(2)}, u32[]{:S(2)}) %collective-permute-start.25) | collective-permute-done | bytes 524320 | tf_op jit(solution)/shard_map/rows out 2a/ppermute | solution.py:425
  79.6 1.5 collective-permute-start.26
  81.3 1.4 collective-permute-start.46
  82.7 1.9 %expert.14 = (bf16[128,2048]{1,0:T(8,128)(2,1)S(1)}, bf16[128,2048]{1,0:T(8,128)(2,1)S(1)}) custom-call(bf16[128,2048]{1,0:T(8,128)(2,1)S(1)} %collective-permute-done.25.refs_0_, bf16[128,2048]{1,0:T(8,128)(2,1)S(1)} %collective-permute-done.42.refs_1_, f32[128,128]{1,0:T(8,128)S(1)} %get-tuple-element.45.refs_2_.refs_3_, ...), custom_call_target="tpu_custom_call" | custom-call | flops 24000000000 | bytes 1000 | tf_op jit(solution)/shard_map/expert/pallas_call | solution.py:370
  84.7 4.1 %collective-permute-done.26.refs_6_.refs_0_ = bf16[128,2048]{1,0:T(8,128)(2,1)S(1)} collective-permute-done((bf16[128,2048]{1,0:T(8,128)(2,1)S(1)}, bf16[128,2048]{1,0:T(8,128)(2,1)S(1)}, u32[]{:S(2)}, u32[]{:S(2)}) %collective-permute-start.26) | collective-permute-done | bytes 524320 | tf_op jit(solution)/shard_map/rows out 3a/ppermute | solution.py:425
  88.8 1.5 collective-permute-start.28
  90.3 4.1 %collective-permute-done.46.refs_2_ = bf16[128,2048]{1,0:T(8,128)(2,1)S(1)} collective-permute-done((bf16[128,2048]{1,0:T(8,128)(2,1)S(1)}, bf16[128,2048]{1,0:T(8,128)(2,1)S(1)}, u32[]{:S(2)}, u32[]{:S(2)}) %collective-permute-start.46) | collective-permute-done | bytes 524320 | tf_op jit(solution)/shard_map/sums out 1a/ppermute | solution.py:425
  94.6 1.6 %collective-permute-start.47 = (bf16[128,2048]{1,0:T(8,128)(2,1)S(1)}, bf16[128,2048]{1,0:T(8,128)(2,1)S(1)}, u32[]{:S(2)}, u32[]{:S(2)}) collective-permute-start(bf16[128,2048]{1,0:T(8,128)(2,1)S(1)} %add.27), channel_id=1, source_target_pairs={{0,4},{1,3},{4,8},{5,1},{8,12},{9,5},{12,14},{13,9},{14,10},{15,13... | collective-permute-start | bytes 1572872 | tf_op jit(solution)/shard_map/sums out 2a/ppermute | solution.py:425
  96.2 1.9 %expert.13 = (bf16[128,2048]{1,0:T(8,128)(2,1)S(1)}, bf16[128,2048]{1,0:T(8,128)(2,1)S(1)}) custom-call(bf16[128,2048]{1,0:T(8,128)(2,1)S(1)} %collective-permute-done.26.refs_6_.refs_0_, bf16[128,2048]{1,0:T(8,128)(2,1)S(1)} %collective-permute-done.40.refs_1_, f32[128,128]{1,0:T(8,128)S(1)} %get-tuple-element.45.refs_2_.refs_3_, ...), custom_call_target="tpu_custom_call" | custom-call | flops 24000000000 | bytes 1000 | tf_op jit(solution)/shard_map/expert/pallas_call | solution.py:370
  98.2 1.9 %collective-permute-done.28.refs_0_ = bf16[128,2048]{1,0:T(8,128)(2,1)S(1)} collective-permute-done((bf16[128,2048]{1,0:T(8,128)(2,1)S(1)}, bf16[128,2048]{1,0:T(8,128)(2,1)S(1)}, u32[]{:S(2)}, u32[]{:S(2)}) %collective-permute-start.28) | collective-permute-done | bytes 524320 | tf_op jit(solution)/shard_map/rows out 4a/ppermute | solution.py:425
  100.1 1.5 collective-permute-start.29
  101.6 4.1 %collective-permute-done.47.refs_2_ = bf16[128,2048]{1,0:T(8,128)(2,1)S(1)} collective-permute-done((bf16[128,2048]{1,0:T(8,128)(2,1)S(1)}, bf16[128,2048]{1,0:T(8,128)(2,1)S(1)}, u32[]{:S(2)}, u32[]{:S(2)}) %collective-permute-start.47) | collective-permute-done | bytes 524320 | tf_op jit(solution)/shard_map/sums out 2a/ppermute | solution.py:425
  105.9 1.6 %collective-permute-start.48 = (bf16[128,2048]{1,0:T(8,128)(2,1)S(1)}, bf16[128,2048]{1,0:T(8,128)(2,1)S(1)}, u32[]{:S(2)}, u32[]{:S(2)}) collective-permute-start(bf16[128,2048]{1,0:T(8,128)(2,1)S(1)} %add.28), channel_id=1, source_target_pairs={{0,4},{1,3},{4,8},{5,1},{8,12},{9,5},{12,14},{13,9},{14,10},{15,13... | collective-permute-start | bytes 1572872 | tf_op jit(solution)/shard_map/sums out 3a/ppermute | solution.py:425
  107.4 1.9 %expert.12 = (bf16[128,2048]{1,0:T(8,128)(2,1)S(1)}, bf16[128,2048]{1,0:T(8,128)(2,1)S(1)}) custom-call(bf16[128,2048]{1,0:T(8,128)(2,1)S(1)} %collective-permute-done.28.refs_0_, bf16[128,2048]{1,0:T(8,128)(2,1)S(1)} %collective-permute-done.38.refs_1_, f32[128,128]{1,0:T(8,128)S(1)} %get-tuple-element.45.refs_2_.refs_3_, ...), custom_call_target="tpu_custom_call" | custom-call | flops 24000000000 | bytes 1000 | tf_op jit(solution)/shard_map/expert/pallas_call | solution.py:370
  109.9 1.4 collective-permute-done.29.refs_0_
  111.3 1.5 collective-permute-start.30
  112.8 4.1 %collective-permute-done.48.refs_2_ = bf16[128,2048]{1,0:T(8,128)(2,1)S(1)} collective-permute-done((bf16[128,2048]{1,0:T(8,128)(2,1)S(1)}, bf16[128,2048]{1,0:T(8,128)(2,1)S(1)}, u32[]{:S(2)}, u32[]{:S(2)}) %collective-permute-start.48) | collective-permute-done | bytes 524320 | tf_op jit(solution)/shard_map/sums out 3a/ppermute | solution.py:425
  117.1 1.6 %collective-permute-start.49 = (bf16[128,2048]{1,0:T(8,128)(2,1)S(1)}, bf16[128,2048]{1,0:T(8,128)(2,1)S(1)}, u32[]{:S(2)}, u32[]{:S(2)}) collective-permute-start(bf16[128,2048]{1,0:T(8,128)(2,1)S(1)} %add.29), channel_id=1, source_target_pairs={{0,4},{1,3},{4,8},{5,1},{8,12},{9,5},{12,14},{13,9},{14,10},{15,13... | collective-permute-start | bytes 1572872 | tf_op jit(solution)/shard_map/sums out 4a/ppermute | solution.py:425
  118.7 1.9 %expert.11 = (bf16[128,2048]{1,0:T(8,128)(2,1)S(1)}, bf16[128,2048]{1,0:T(8,128)(2,1)S(1)}) custom-call(bf16[128,2048]{1,0:T(8,128)(2,1)S(1)} %collective-permute-done.29.refs_0_, bf16[128,2048]{1,0:T(8,128)(2,1)S(1)} %collective-permute-done.36.refs_1_, f32[128,128]{1,0:T(8,128)S(1)} %get-tuple-element.45.refs_2_.refs_3_, ...), custom_call_target="tpu_custom_call" | custom-call | flops 24000000000 | bytes 1000 | tf_op jit(solution)/shard_map/expert/pallas_call | solution.py:370
  120.6 1.9 %expert.8 = (bf16[128,2048]{1,0:T(8,128)(2,1)S(1)}, bf16[128,2048]{1,0:T(8,128)(2,1)S(1)}) custom-call(bf16[128,2048]{1,0:T(8,128)(2,1)S(1)} %get-tuple-element.44.refs_0_, bf16[128,2048]{1,0:T(8,128)(2,1)S(1)} %collective-permute-done.23.refs_1_, f32[128,128]{1,0:T(8,128)S(1)} %get-tuple-element.45.refs_2_.refs_3_, ...), custom_call_target="tpu_custom_call" | custom-call | flops 24000000000 | bytes 1000 | tf_op jit(solution)/shard_map/expert/pallas_call | solution.py:370
  123.2 1.4 collective-permute-start.31
  124.6 3.6 %collective-permute-done.49.refs_2_ = bf16[128,2048]{1,0:T(8,128)(2,1)S(1)} collective-permute-done((bf16[128,2048]{1,0:T(8,128)(2,1)S(1)}, bf16[128,2048]{1,0:T(8,128)(2,1)S(1)}, u32[]{:S(2)}, u32[]{:S(2)}) %collective-permute-start.49) | collective-permute-done | bytes 524320 | tf_op jit(solution)/shard_map/sums out 4a/ppermute | solution.py:425
  128.2 1.6 %collective-permute-start.50 = (bf16[64,2048]{1,0:T(8,128)(2,1)S(1)}, bf16[64,2048]{1,0:T(8,128)(2,1)S(1)}, u32[]{:S(2)}, u32[]{:S(2)}) collective-permute-start(bf16[64,2048]{1,0:T(8,128)(2,1)S(1)} %add.30), channel_id=1, source_target_pairs={{0,4},{1,3},{4,8},{5,1},{8,12},{9,5},{12,14},{13,9},{14,10},{15,13... | collective-permute-start | bytes 786440 | tf_op jit(solution)/shard_map/sums out 5a/ppermute | solution.py:425
  129.8 1.9 %expert.10 = (bf16[128,2048]{1,0:T(8,128)(2,1)S(1)}, bf16[128,2048]{1,0:T(8,128)(2,1)S(1)}) custom-call(bf16[128,2048]{1,0:T(8,128)(2,1)S(1)} %collective-permute-done.30.refs_0_, bf16[128,2048]{1,0:T(8,128)(2,1)S(1)} %collective-permute-done.34.refs_1_, f32[128,128]{1,0:T(8,128)S(1)} %get-tuple-element.48.refs_2_.refs_3_, ...), custom_call_target="tpu_custom_call" | custom-call | flops 24000000000 | bytes 1000 | tf_op jit(solution)/shard_map/expert/pallas_call | solution.py:370
  131.9 1.4 collective-permute-start.53
  133.8 2.8 %collective-permute-done.50.refs_2_ = bf16[64,2048]{1,0:T(8,128)(2,1)S(1)} collective-permute-done((bf16[64,2048]{1,0:T(8,128)(2,1)S(1)}, bf16[64,2048]{1,0:T(8,128)(2,1)S(1)}, u32[]{:S(2)}, u32[]{:S(2)}) %collective-permute-start.50) | collective-permute-done | bytes 262176 | tf_op jit(solution)/shard_map/sums out 5a/ppermute | solution.py:425
  136.7 1.6 %collective-permute-start.51 = (bf16[64,2048]{1,0:T(8,128)(2,1)S(1)}, bf16[64,2048]{1,0:T(8,128)(2,1)S(1)}, u32[]{:S(2)}, u32[]{:S(2)}) collective-permute-start(bf16[64,2048]{1,0:T(8,128)(2,1)S(1)} %add.31), channel_id=1, source_target_pairs={{0,4},{1,3},{4,8},{5,1},{8,12},{9,5},{12,14},{13,9},{14,10},{15,13... | collective-permute-start | bytes 786440 | tf_op jit(solution)/shard_map/sums out 6a/ppermute | solution.py:425
  138.2 1.9 %expert.9 = (bf16[128,2048]{1,0:T(8,128)(2,1)S(1)}, bf16[128,2048]{1,0:T(8,128)(2,1)S(1)}) custom-call(bf16[128,2048]{1,0:T(8,128)(2,1)S(1)} %collective-permute-done.31.refs_0_, bf16[128,2048]{1,0:T(8,128)(2,1)S(1)} %collective-permute-done.32.refs_1_, f32[128,128]{1,0:T(8,128)S(1)} %get-tuple-element.48.refs_2_.refs_3_, ...), custom_call_target="tpu_custom_call" | custom-call | flops 24000000000 | bytes 1000 | tf_op jit(solution)/shard_map/expert/pallas_call | solution.py:370
  140.3 1.4 collective-permute-start.54
  143.2 1.6 %collective-permute-start.52 = (bf16[64,2048]{1,0:T(8,128)(2,1)S(1)}, bf16[64,2048]{1,0:T(8,128)(2,1)S(1)}, u32[]{:S(2)}, u32[]{:S(2)}) collective-permute-start(bf16[64,2048]{1,0:T(8,128)(2,1)S(1)} %add.32), channel_id=1, source_target_pairs={{0,4},{1,3},{4,8},{5,1},{8,12},{9,5},{12,14},{13,9},{14,10},{15,13... | collective-permute-start | bytes 786440 | tf_op jit(solution)/shard_map/sums out 7a/ppermute | solution.py:425
  144.8 2.0 %collective-permute-done.54.refs_2_ = bf16[64,2048]{1,0:T(8,128)(2,1)S(1)} collective-permute-done((bf16[64,2048]{1,0:T(8,128)(2,1)S(1)}, bf16[64,2048]{1,0:T(8,128)(2,1)S(1)}, u32[]{:S(2)}, u32[]{:S(2)}) %collective-permute-start.54) | collective-permute-done | bytes 262176 | tf_op jit(solution)/shard_map/sums out 6b/ppermute | solution.py:425
  146.8 1.4 collective-permute-start.55
  149.6 3.6 %collective-permute-done.55.refs_2_ = bf16[64,2048]{1,0:T(8,128)(2,1)S(1)} collective-permute-done((bf16[64,2048]{1,0:T(8,128)(2,1)S(1)}, bf16[64,2048]{1,0:T(8,128)(2,1)S(1)}, u32[]{:S(2)}, u32[]{:S(2)}) %collective-permute-start.55) | collective-permute-done | bytes 262176 | tf_op jit(solution)/shard_map/sums out 7b/ppermute | solution.py:425
  (113 shorter events, 14.9 us)
Async XLA Ops:
  3.1 27.3 %collective-permute-start = (bf16[2,128,2048]{2,1,0:T(8,128)(2,1)}, bf16[2,128,2048]{2,1,0:T(8,128)(2,1)}, u32[]{:S(2)}, u32[]{:S(2)}) collective-permute-start(bf16[2,128,2048]{2,1,0:T(8,128)(2,1)} %far_segment.1), channel_id=1, source_target_pairs={{0,16},{16,0},{1,17},{17,1},{2,18},{18,2},{3,19},{19,3},{4,20},{20... | collective-permute-start | bytes 3145736 | tf_op jit(solution)/shard_map/far segment/ppermute | solution.py:439
  6.1 24.3 %copy-start.7 = (bf16[2,1,2,128,2048]{4,3,2,1,0:T(8,128)(2,1)S(1)}, bf16[2,1,2,128,2048]{4,3,2,1,0:T(8,128)(2,1)}, u32[]{:S(2)}) copy-start(bf16[2,1,2,128,2048]{4,3,2,1,0:T(8,128)(2,1)} %cache_ref.9) | copy-start | bytes 6291460
  6.1 24.3 %copy-start.9 = (bf16[2,128,2048]{2,1,0:T(8,128)(2,1)S(1)}, bf16[2,128,2048]{2,1,0:T(8,128)(2,1)}, u32[]{:S(2)}) copy-start(bf16[2,128,2048]{2,1,0:T(8,128)(2,1)} %kv_ref.7) | copy-start | bytes 3145732
  6.1 24.3 %copy-start.11 = (bf16[128,2048]{1,0:T(8,128)(2,1)S(1)}, bf16[128,2048]{1,0:T(8,128)(2,1)}, u32[]{:S(2)}) copy-start(bf16[128,2048]{1,0:T(8,128)(2,1)} %q_ref.7) | copy-start | bytes 1572868
  6.1 24.3 %copy-start.17 = (s32[1,2]{1,0:T(1,128)S(1)}, s32[1,2]{1,0:T(1,128)}, u32[]{:S(2)}) copy-start(s32[1,2]{1,0:T(1,128)} %len_ref.9) | copy-start | bytes 28
  6.8 1.6 %collective-permute-start.6 = (bf16[136,1024]{1,0:T(8,128)(2,1)S(1)}, bf16[136,1024]{1,0:T(8,128)(2,1)S(1)}, u32[]{:S(2)}, u32[]{:S(2)}) collective-permute-start(bf16[136,1024]{1,0:T(8,128)(2,1)S(1)} %get-tuple-element.36), channel_id=1, source_target_pairs={{0,1},{1,0},{2,3},{3,2},{4,5},{5,4},{6,7},{7,6},{8,9},{9,8},{10,11... | collective-permute-start | bytes 835592 | tf_op jit(solution)/shard_map/to sibling/ppermute | solution.py:429
  6.8 6.5 %collective-permute-start.1 = (bf16[136,1024]{1,0:T(8,128)(2,1)S(1)}, bf16[136,1024]{1,0:T(8,128)(2,1)S(1)}, u32[]{:S(2)}, u32[]{:S(2)}) collective-permute-start(bf16[136,1024]{1,0:T(8,128)(2,1)S(1)} %get-tuple-element.34.refs_8_), channel_id=1, source_target_pairs={{0,4},{1,3},{4,8},{5,1},{8,12},{9,5},{12,14},{13,9},{14,10},{15,13... | collective-permute-start | bytes 835592 | tf_op jit(solution)/shard_map/o rows 1a/ppermute | solution.py:425
  8.4 8.0 %collective-permute-start.7 = (bf16[136,1024]{1,0:T(8,128)(2,1)S(1)}, bf16[136,1024]{1,0:T(8,128)(2,1)S(1)}, u32[]{:S(2)}, u32[]{:S(2)}) collective-permute-start(bf16[136,1024]{1,0:T(8,128)(2,1)S(1)} %collective-permute-done.6.refs_9_), channel_id=1, source_target_pairs={{0,4},{1,3},{4,8},{5,1},{8,12},{9,5},{12,14},{13,9},{14,10},{15,13... | collective-permute-start | bytes 835592 | tf_op jit(solution)/shard_map/o rows 1b/ppermute | solution.py:425
  13.4 6.5 %collective-permute-start.2 = (bf16[136,1024]{1,0:T(8,128)(2,1)S(1)}, bf16[136,1024]{1,0:T(8,128)(2,1)S(1)}, u32[]{:S(2)}, u32[]{:S(2)}) collective-permute-start(bf16[136,1024]{1,0:T(8,128)(2,1)S(1)} %collective-permute-done.1.refs_10_), channel_id=1, source_target_pairs={{0,4},{1,3},{4,8},{5,1},{8,12},{9,5},{12,14},{13,9},{14,10},{15,13... | collective-permute-start | bytes 835592 | tf_op jit(solution)/shard_map/o rows 2a/ppermute | solution.py:425
  16.4 7.2 %collective-permute-start.13 = (bf16[136,1024]{1,0:T(8,128)(2,1)S(1)}, bf16[136,1024]{1,0:T(8,128)(2,1)S(1)}, u32[]{:S(2)}, u32[]{:S(2)}) collective-permute-start(bf16[136,1024]{1,0:T(8,128)(2,1)S(1)} %collective-permute-done.7.refs_11_), channel_id=1, source_target_pairs={{0,4},{1,3},{4,8},{5,1},{8,12},{9,5},{12,14},{13,9},{14,10},{15,13... | collective-permute-start | bytes 835592 | tf_op jit(solution)/shard_map/o rows 2b/ppermute | solution.py:425
  19.9 6.5 %collective-permute-start.3 = (bf16[136,1024]{1,0:T(8,128)(2,1)S(1)}, bf16[136,1024]{1,0:T(8,128)(2,1)S(1)}, u32[]{:S(2)}, u32[]{:S(2)}) collective-permute-start(bf16[136,1024]{1,0:T(8,128)(2,1)S(1)} %collective-permute-done.2.refs_12_), channel_id=1, source_target_pairs={{0,4},{1,3},{4,8},{5,1},{8,12},{9,5},{12,14},{13,9},{14,10},{15,13... | collective-permute-start | bytes 835592 | tf_op jit(solution)/shard_map/o rows 3a/ppermute | solution.py:425
  21.5 22.3 %collective-permute-start.5 = (bf16[136,1024]{1,0:T(8,128)(2,1)S(1)}, bf16[136,1024]{1,0:T(8,128)(2,1)S(1)}, u32[]{:S(2)}, u32[]{:S(2)}) collective-permute-start(bf16[136,1024]{1,0:T(8,128)(2,1)S(1)} %collective-permute-done.1.refs_10_), channel_id=1, source_target_pairs={{0,16},{16,0},{1,17},{17,1},{2,18},{18,2},{3,19},{19,3},{4,20},{20... | collective-permute-start | bytes 835592 | tf_op jit(solution)/shard_map/o rows of partner/ppermute | solution.py:458
  22.0 26.6 %collective-permute-start.8 = (bf16[136,1024]{1,0:T(8,128)(2,1)S(1)}, bf16[136,1024]{1,0:T(8,128)(2,1)S(1)}, u32[]{:S(2)}, u32[]{:S(2)}) collective-permute-start(bf16[136,1024]{1,0:T(8,128)(2,1)S(1)} %collective-permute-done.7.refs_11_), channel_id=1, source_target_pairs={{0,16},{16,0},{1,17},{17,1},{2,18},{18,2},{3,19},{19,3},{4,20},{20... | collective-permute-start | bytes 835592 | tf_op jit(solution)/shard_map/o rows of partner/ppermute | solution.py:458
  23.5 9.3 %collective-permute-start.14 = (bf16[136,1024]{1,0:T(8,128)(2,1)S(1)}, bf16[136,1024]{1,0:T(8,128)(2,1)S(1)}, u32[]{:S(2)}, u32[]{:S(2)}) collective-permute-start(bf16[136,1024]{1,0:T(8,128)(2,1)S(1)} %collective-permute-done.13.refs_13_), channel_id=1, source_target_pairs={{0,4},{1,3},{4,8},{5,1},{8,12},{9,5},{12,14},{13,9},{14,10},{15,13... | collective-permute-start | bytes 835592 | tf_op jit(solution)/shard_map/o rows 3b/ppermute | solution.py:425
  26.5 8.5 %collective-permute-start.4 = (bf16[136,1024]{1,0:T(8,128)(2,1)S(1)}, bf16[136,1024]{1,0:T(8,128)(2,1)S(1)}, u32[]{:S(2)}, u32[]{:S(2)}) collective-permute-start(bf16[136,1024]{1,0:T(8,128)(2,1)S(1)} %collective-permute-done.3.refs_14_), channel_id=1, source_target_pairs={{0,4},{1,3},{4,8},{5,1},{8,12},{9,5},{12,14},{13,9},{14,10},{15,13... | collective-permute-start | bytes 835592 | tf_op jit(solution)/shard_map/o rows 4a/ppermute | solution.py:425
  32.7 18.3 %collective-permute-start.10 = (bf16[4,128,128]{2,1,0:T(8,128)(2,1)S(1)}, bf16[4,128,128]{2,1,0:T(8,128)(2,1)S(1)}, u32[]{:S(2)}, u32[]{:S(2)}) collective-permute-start(bf16[4,128,128]{2,1,0:T(8,128)(2,1)S(1)} %attend.5.refs_1_), channel_id=1, source_target_pairs={{0,1},{1,0},{2,3},{3,2},{4,5},{5,4},{6,7},{7,6},{8,9},{9,8},{10,11... | collective-permute-start | bytes 393224 | tf_op jit(solution)/shard_map/attended 1/ppermute | solution.py:429
  32.8 6.7 %collective-permute-start.15 = (bf16[136,1024]{1,0:T(8,128)(2,1)S(1)}, bf16[136,1024]{1,0:T(8,128)(2,1)S(1)}, u32[]{:S(2)}, u32[]{:S(2)}) collective-permute-start(bf16[136,1024]{1,0:T(8,128)(2,1)S(1)} %collective-permute-done.14.refs_15_), channel_id=1, source_target_pairs={{0,4},{1,3},{4,8},{5,1},{8,12},{9,5},{12,14},{13,9},{14,10},{15,13... | collective-permute-start | bytes 835592 | tf_op jit(solution)/shard_map/o rows 4b/ppermute | solution.py:425
  37.3 6.5 %copy-start = (bf16[136,1024]{1,0:T(8,128)(2,1)}, bf16[136,1024]{1,0:T(8,128)(2,1)S(1)}, u32[]{:S(2)}) copy-start(bf16[136,1024]{1,0:T(8,128)(2,1)S(1)} %get-tuple-element.37.refs_16_) | copy-start | bytes 835588
  37.3 6.7 %collective-permute-start.16 = (bf16[136,1024]{1,0:T(8,128)(2,1)S(1)}, bf16[136,1024]{1,0:T(8,128)(2,1)}, u32[]{:S(2)}, u32[]{:S(2)}) collective-permute-start(bf16[136,1024]{1,0:T(8,128)(2,1)S(1)} %get-tuple-element.37.refs_16_), channel_id=1, source_target_pairs={{0,4},{1,3},{4,8},{5,1},{8,12},{9,5},{12,14},{13,9},{14,10},{15,13... | collective-permute-start | bytes 835592 | tf_op jit(solution)/shard_map/o rows 5a/ppermute | solution.py:425
  39.5 7.5 %collective-permute-start.17 = (bf16[136,1024]{1,0:T(8,128)(2,1)S(1)}, bf16[136,1024]{1,0:T(8,128)(2,1)}, u32[]{:S(2)}, u32[]{:S(2)}) collective-permute-start(bf16[136,1024]{1,0:T(8,128)(2,1)S(1)} %collective-permute-done.15.refs_17_), channel_id=1, source_target_pairs={{0,4},{1,3},{4,8},{5,1},{8,12},{9,5},{12,14},{13,9},{14,10},{15,13... | collective-permute-start | bytes 835592 | tf_op jit(solution)/shard_map/o rows 5b/ppermute | solution.py:425
  43.8 7.1 %copy-start.2 = (bf16[136,1024]{1,0:T(8,128)(2,1)}, bf16[136,1024]{1,0:T(8,128)(2,1)S(1)}, u32[]{:S(2)}) copy-start(bf16[136,1024]{1,0:T(8,128)(2,1)S(1)} %collective-permute-done.5.refs_0_.refs_10_) | copy-start | bytes 835588
  43.9 7.7 %collective-permute-start.11 = (bf16[4,128,128]{2,1,0:T(8,128)(2,1)S(1)}, bf16[4,128,128]{2,1,0:T(8,128)(2,1)S(1)}, u32[]{:S(2)}, u32[]{:S(2)}) collective-permute-start(bf16[4,128,128]{2,1,0:T(8,128)(2,1)S(1)} %attend.6.refs_2_), channel_id=1, source_target_pairs={{0,1},{1,0},{2,3},{3,2},{4,5},{5,4},{6,7},{7,6},{8,9},{9,8},{10,11... | collective-permute-start | bytes 393224 | tf_op jit(solution)/shard_map/attended 2/ppermute | solution.py:429
  44.0 13.0 %collective-permute-start.18 = (bf16[136,1024]{1,0:T(8,128)(2,1)}, bf16[136,1024]{1,0:T(8,128)(2,1)}, u32[]{:S(2)}, u32[]{:S(2)}) collective-permute-start(bf16[136,1024]{1,0:T(8,128)(2,1)} %collective-permute-done.16.refs_18_), channel_id=1, source_target_pairs={{0,4},{1,3},{4,8},{5,1},{8,12},{9,5},{12,14},{13,9},{14,10},{15,13... | collective-permute-start | bytes 835592 | tf_op jit(solution)/shard_map/o rows 6a/ppermute | solution.py:425
  47.0 10.0 %collective-permute-start.19 = (bf16[136,1024]{1,0:T(8,128)(2,1)}, bf16[136,1024]{1,0:T(8,128)(2,1)}, u32[]{:S(2)}, u32[]{:S(2)}) collective-permute-start(bf16[136,1024]{1,0:T(8,128)(2,1)} %collective-permute-done.17.refs_19_), channel_id=1, source_target_pairs={{0,4},{1,3},{4,8},{5,1},{8,12},{9,5},{12,14},{13,9},{14,10},{15,13... | collective-permute-start | bytes 835592 | tf_op jit(solution)/shard_map/o rows 6b/ppermute | solution.py:425
  51.0 1.9 %collective-permute-start.12 = (bf16[4,128,128]{2,1,0:T(8,128)(2,1)S(1)}, bf16[4,128,128]{2,1,0:T(8,128)(2,1)S(1)}, u32[]{:S(2)}, u32[]{:S(2)}) collective-permute-start(bf16[4,128,128]{2,1,0:T(8,128)(2,1)S(1)} %attend.7.refs_3_), channel_id=1, source_target_pairs={{0,1},{1,0},{2,3},{3,2},{4,5},{5,4},{6,7},{7,6},{8,9},{9,8},{10,11... | collective-permute-start | bytes 393224 | tf_op jit(solution)/shard_map/attended 3/ppermute | solution.py:429
  51.1 2.2 %collective-permute-start.9 = (bf16[4,128,128]{2,1,0:T(8,128)(2,1)S(1)}, bf16[4,128,128]{2,1,0:T(8,128)(2,1)S(1)}, u32[]{:S(2)}, u32[]{:S(2)}) collective-permute-start(bf16[4,128,128]{2,1,0:T(8,128)(2,1)S(1)} %get-tuple-element.35.refs_0_), channel_id=1, source_target_pairs={{0,1},{1,0},{2,3},{3,2},{4,5},{5,4},{6,7},{7,6},{8,9},{9,8},{10,11... | collective-permute-start | bytes 393224 | tf_op jit(solution)/shard_map/attended 0/ppermute | solution.py:429
  51.5 5.4 %collective-permute-start.21 = (bf16[16,1024]{1,0:T(8,128)(2,1)}, bf16[16,1024]{1,0:T(8,128)(2,1)S(1)}, u32[]{:S(2)}, u32[]{:S(2)}) collective-permute-start(bf16[16,1024]{1,0:T(8,128)(2,1)} %copy-done.13), channel_id=1, source_target_pairs={{5,0},{2,1},{9,4},{0,5},{13,8},{4,9},{15,12},{8,13},{11,14},{12,15... | collective-permute-start | bytes 98312 | tf_op jit(solution)/shard_map/gate weights back/ppermute | solution.py:474
  52.8 4.2 %collective-permute-start.20 = (bf16[16,1024]{1,0:T(8,128)(2,1)}, bf16[16,1024]{1,0:T(8,128)(2,1)S(1)}, u32[]{:S(2)}, u32[]{:S(2)}) collective-permute-start(bf16[16,1024]{1,0:T(8,128)(2,1)} %copy-done.13), channel_id=1, source_target_pairs={{4,0},{3,1},{8,4},{1,5},{12,8},{5,9},{14,12},{9,13},{10,14},{13,15... | collective-permute-start | bytes 98312 | tf_op jit(solution)/shard_map/gate weights back/ppermute | solution.py:474
  59.0 1.8 %collective-permute-start.22 = (bf16[128,1024]{1,0:T(8,128)(2,1)S(1)}, bf16[128,1024]{1,0:T(8,128)(2,1)S(1)}, u32[]{:S(2)}, u32[]{:S(2)}) collective-permute-start(bf16[128,1024]{1,0:T(8,128)(2,1)S(1)} %get-tuple-element.42), channel_id=1, source_target_pairs={{0,1},{1,0},{2,3},{3,2},{4,5},{5,4},{6,7},{7,6},{8,9},{9,8},{10,11... | collective-permute-start | bytes 786440 | tf_op jit(solution)/shard_map/projected/ppermute | solution.py:429
  60.8 11.5 %copy-start.6 = (bf16[1,2048,1024]{2,1,0:T(8,128)(2,1)S(1)}, bf16[1,2048,1024]{2,1,0:T(8,128)(2,1)}, u32[]{:S(2)}) copy-start(bf16[1,2048,1024]{2,1,0:T(8,128)(2,1)} %refs_4_.15) | copy-start | bytes 12582916
  60.8 11.6 %copy-start.8 = (bf16[1,512,2048]{2,1,0:T(8,128)(2,1)S(1)}, bf16[1,512,2048]{2,1,0:T(8,128)(2,1)}, u32[]{:S(2)}) copy-start(bf16[1,512,2048]{2,1,0:T(8,128)(2,1)} %refs_5_.15) | copy-start | bytes 6291460
  61.2 9.2 %collective-permute-start.24 = (bf16[128,2048]{1,0:T(8,128)(2,1)S(1)}, bf16[128,2048]{1,0:T(8,128)(2,1)S(1)}, u32[]{:S(2)}, u32[]{:S(2)}) collective-permute-start(bf16[128,2048]{1,0:T(8,128)(2,1)S(1)} %get-tuple-element.44.refs_0_), channel_id=1, source_target_pairs={{0,4},{1,3},{4,8},{5,1},{8,12},{9,5},{12,14},{13,9},{14,10},{15,13... | collective-permute-start | bytes 1572872 | tf_op jit(solution)/shard_map/rows out 1a/ppermute | solution.py:425
  70.4 1.9 %collective-permute-start.44 = (bf16[128,2048]{1,0:T(8,128)(2,1)S(1)}, bf16[128,2048]{1,0:T(8,128)(2,1)S(1)}, u32[]{:S(2)}, u32[]{:S(2)}) collective-permute-start(bf16[128,2048]{1,0:T(8,128)(2,1)S(1)} %collective-permute-done.24.refs_0_), channel_id=1, source_target_pairs={{0,1},{1,0},{2,3},{3,2},{4,5},{5,4},{6,7},{7,6},{8,9},{9,8},{10,11... | collective-permute-start | bytes 1572872 | tf_op jit(solution)/shard_map/rows across 1a/ppermute | solution.py:429
  70.4 9.2 %collective-permute-start.25 = (bf16[128,2048]{1,0:T(8,128)(2,1)S(1)}, bf16[128,2048]{1,0:T(8,128)(2,1)S(1)}, u32[]{:S(2)}, u32[]{:S(2)}) collective-permute-start(bf16[128,2048]{1,0:T(8,128)(2,1)S(1)} %collective-permute-done.24.refs_0_), channel_id=1, source_target_pairs={{0,4},{1,3},{4,8},{5,1},{8,12},{9,5},{12,14},{13,9},{14,10},{15,13... | collective-permute-start | bytes 1572872 | tf_op jit(solution)/shard_map/rows out 2a/ppermute | solution.py:425
  74.2 6.9 %collective-permute-start.45 = (bf16[128,2048]{1,0:T(8,128)(2,1)S(1)}, bf16[128,2048]{1,0:T(8,128)(2,1)S(1)}, u32[]{:S(2)}, u32[]{:S(2)}) collective-permute-start(bf16[128,2048]{1,0:T(8,128)(2,1)S(1)} %get-tuple-element.62), channel_id=1, source_target_pairs={{0,1},{1,0},{2,3},{3,2},{4,5},{5,4},{6,7},{7,6},{8,9},{9,8},{10,11... | collective-permute-start | bytes 1572872 | tf_op jit(solution)/shard_map/sums across 1a/ppermute | solution.py:429
  79.6 3.1 %collective-permute-start.42 = (bf16[128,2048]{1,0:T(8,128)(2,1)S(1)}, bf16[128,2048]{1,0:T(8,128)(2,1)S(1)}, u32[]{:S(2)}, u32[]{:S(2)}) collective-permute-start(bf16[128,2048]{1,0:T(8,128)(2,1)S(1)} %collective-permute-done.25.refs_0_), channel_id=1, source_target_pairs={{0,1},{1,0},{2,3},{3,2},{4,5},{5,4},{6,7},{7,6},{8,9},{9,8},{10,11... | collective-permute-start | bytes 1572872 | tf_op jit(solution)/shard_map/rows across 2a/ppermute | solution.py:429
  79.6 9.2 %collective-permute-start.26 = (bf16[128,2048]{1,0:T(8,128)(2,1)S(1)}, bf16[128,2048]{1,0:T(8,128)(2,1)S(1)}, u32[]{:S(2)}, u32[]{:S(2)}) collective-permute-start(bf16[128,2048]{1,0:T(8,128)(2,1)S(1)} %collective-permute-done.25.refs_0_), channel_id=1, source_target_pairs={{0,4},{1,3},{4,8},{5,1},{8,12},{9,5},{12,14},{13,9},{14,10},{15,13... | collective-permute-start | bytes 1572872 | tf_op jit(solution)/shard_map/rows out 3a/ppermute | solution.py:425
  81.3 13.2 %collective-permute-start.46 = (bf16[128,2048]{1,0:T(8,128)(2,1)S(1)}, bf16[128,2048]{1,0:T(8,128)(2,1)S(1)}, u32[]{:S(2)}, u32[]{:S(2)}) collective-permute-start(bf16[128,2048]{1,0:T(8,128)(2,1)S(1)} %add.26), channel_id=1, source_target_pairs={{0,4},{1,3},{4,8},{5,1},{8,12},{9,5},{12,14},{13,9},{14,10},{15,13... | collective-permute-start | bytes 1572872 | tf_op jit(solution)/shard_map/sums out 1a/ppermute | solution.py:425
  84.6 9.8 %collective-permute-start.43 = (bf16[128,2048]{1,0:T(8,128)(2,1)S(1)}, bf16[128,2048]{1,0:T(8,128)(2,1)S(1)}, u32[]{:S(2)}, u32[]{:S(2)}) collective-permute-start(bf16[128,2048]{1,0:T(8,128)(2,1)S(1)} %get-tuple-element.60), channel_id=1, source_target_pairs={{0,1},{1,0},{2,3},{3,2},{4,5},{5,4},{6,7},{7,6},{8,9},{9,8},{10,11... | collective-permute-start | bytes 1572872 | tf_op jit(solution)/shard_map/sums across 2a/ppermute | solution.py:429
  88.8 7.4 %collective-permute-start.40 = (bf16[128,2048]{1,0:T(8,128)(2,1)S(1)}, bf16[128,2048]{1,0:T(8,128)(2,1)S(1)}, u32[]{:S(2)}, u32[]{:S(2)}) collective-permute-start(bf16[128,2048]{1,0:T(8,128)(2,1)S(1)} %collective-permute-done.26.refs_6_.refs_0_), channel_id=1, source_target_pairs={{0,1},{1,0},{2,3},{3,2},{4,5},{5,4},{6,7},{7,6},{8,9},{9,8},{10,11... | collective-permute-start | bytes 1572872 | tf_op jit(solution)/shard_map/rows across 3a/ppermute | solution.py:429
  88.8 11.2 %collective-permute-start.28 = (bf16[128,2048]{1,0:T(8,128)(2,1)S(1)}, bf16[128,2048]{1,0:T(8,128)(2,1)S(1)}, u32[]{:S(2)}, u32[]{:S(2)}) collective-permute-start(bf16[128,2048]{1,0:T(8,128)(2,1)S(1)} %collective-permute-done.26.refs_6_.refs_0_), channel_id=1, source_target_pairs={{0,4},{1,3},{4,8},{5,1},{8,12},{9,5},{12,14},{13,9},{14,10},{15,13... | collective-permute-start | bytes 1572872 | tf_op jit(solution)/shard_map/rows out 4a/ppermute | solution.py:425
  94.6 11.0 %collective-permute-start.47 = (bf16[128,2048]{1,0:T(8,128)(2,1)S(1)}, bf16[128,2048]{1,0:T(8,128)(2,1)S(1)}, u32[]{:S(2)}, u32[]{:S(2)}) collective-permute-start(bf16[128,2048]{1,0:T(8,128)(2,1)S(1)} %add.27), channel_id=1, source_target_pairs={{0,4},{1,3},{4,8},{5,1},{8,12},{9,5},{12,14},{13,9},{14,10},{15,13... | collective-permute-start | bytes 1572872 | tf_op jit(solution)/shard_map/sums out 2a/ppermute | solution.py:425
  98.1 7.6 %collective-permute-start.41 = (bf16[128,2048]{1,0:T(8,128)(2,1)S(1)}, bf16[128,2048]{1,0:T(8,128)(2,1)S(1)}, u32[]{:S(2)}, u32[]{:S(2)}) collective-permute-start(bf16[128,2048]{1,0:T(8,128)(2,1)S(1)} %get-tuple-element.58), channel_id=1, source_target_pairs={{0,1},{1,0},{2,3},{3,2},{4,5},{5,4},{6,7},{7,6},{8,9},{9,8},{10,11... | collective-permute-start | bytes 1572872 | tf_op jit(solution)/shard_map/sums across 3a/ppermute | solution.py:429
  100.0 7.4 %collective-permute-start.38 = (bf16[128,2048]{1,0:T(8,128)(2,1)S(1)}, bf16[128,2048]{1,0:T(8,128)(2,1)S(1)}, u32[]{:S(2)}, u32[]{:S(2)}) collective-permute-start(bf16[128,2048]{1,0:T(8,128)(2,1)S(1)} %collective-permute-done.28.refs_0_), channel_id=1, source_target_pairs={{0,1},{1,0},{2,3},{3,2},{4,5},{5,4},{6,7},{7,6},{8,9},{9,8},{10,11... | collective-permute-start | bytes 1572872 | tf_op jit(solution)/shard_map/rows across 4a/ppermute | solution.py:429
  100.1 11.2 %collective-permute-start.29 = (bf16[128,2048]{1,0:T(8,128)(2,1)S(1)}, bf16[128,2048]{1,0:T(8,128)(2,1)S(1)}, u32[]{:S(2)}, u32[]{:S(2)}) collective-permute-start(bf16[128,2048]{1,0:T(8,128)(2,1)S(1)} %collective-permute-done.28.refs_0_), channel_id=1, source_target_pairs={{0,4},{1,3},{4,8},{5,1},{8,12},{9,5},{12,14},{13,9},{14,10},{15,13... | collective-permute-start | bytes 1572872 | tf_op jit(solution)/shard_map/rows out 5a/ppermute | solution.py:425
  105.9 11.0 %collective-permute-start.48 = (bf16[128,2048]{1,0:T(8,128)(2,1)S(1)}, bf16[128,2048]{1,0:T(8,128)(2,1)S(1)}, u32[]{:S(2)}, u32[]{:S(2)}) collective-permute-start(bf16[128,2048]{1,0:T(8,128)(2,1)S(1)} %add.28), channel_id=1, source_target_pairs={{0,4},{1,3},{4,8},{5,1},{8,12},{9,5},{12,14},{13,9},{14,10},{15,13... | collective-permute-start | bytes 1572872 | tf_op jit(solution)/shard_map/sums out 3a/ppermute | solution.py:425
  109.3 7.6 %collective-permute-start.39 = (bf16[128,2048]{1,0:T(8,128)(2,1)S(1)}, bf16[128,2048]{1,0:T(8,128)(2,1)S(1)}, u32[]{:S(2)}, u32[]{:S(2)}) collective-permute-start(bf16[128,2048]{1,0:T(8,128)(2,1)S(1)} %get-tuple-element.56), channel_id=1, source_target_pairs={{0,1},{1,0},{2,3},{3,2},{4,5},{5,4},{6,7},{7,6},{8,9},{9,8},{10,11... | collective-permute-start | bytes 1572872 | tf_op jit(solution)/shard_map/sums across 4a/ppermute | solution.py:429
  109.4 11.2 %collective-permute-start.23 = (bf16[128,2048]{1,0:T(8,128)(2,1)S(1)}, bf16[128,2048]{1,0:T(8,128)(2,1)S(1)}, u32[]{:S(2)}, u32[]{:S(2)}) collective-permute-start(bf16[128,2048]{1,0:T(8,128)(2,1)S(1)} %get-tuple-element.44.refs_0_), channel_id=1, source_target_pairs={{0,1},{1,0},{2,3},{3,2},{4,5},{5,4},{6,7},{7,6},{8,9},{9,8},{10,11... | collective-permute-start | bytes 1572872 | tf_op jit(solution)/shard_map/normed/ppermute | solution.py:429
  111.3 7.4 %collective-permute-start.36 = (bf16[128,2048]{1,0:T(8,128)(2,1)S(1)}, bf16[128,2048]{1,0:T(8,128)(2,1)S(1)}, u32[]{:S(2)}, u32[]{:S(2)}) collective-permute-start(bf16[128,2048]{1,0:T(8,128)(2,1)S(1)} %collective-permute-done.29.refs_0_), channel_id=1, source_target_pairs={{0,1},{1,0},{2,3},{3,2},{4,5},{5,4},{6,7},{7,6},{8,9},{9,8},{10,11... | collective-permute-start | bytes 1572872 | tf_op jit(solution)/shard_map/rows across 5a/ppermute | solution.py:429
  111.3 11.8 %collective-permute-start.30 = (bf16[128,2048]{1,0:T(8,128)(2,1)S(1)}, bf16[128,2048]{1,0:T(8,128)(2,1)S(1)}, u32[]{:S(2)}, u32[]{:S(2)}) collective-permute-start(bf16[128,2048]{1,0:T(8,128)(2,1)S(1)} %collective-permute-done.29.refs_0_), channel_id=1, source_target_pairs={{0,4},{1,3},{4,8},{5,1},{8,12},{9,5},{12,14},{13,9},{14,10},{15,13... | collective-permute-start | bytes 1572872 | tf_op jit(solution)/shard_map/rows out 6a/ppermute | solution.py:425
  117.1 11.0 %collective-permute-start.49 = (bf16[128,2048]{1,0:T(8,128)(2,1)S(1)}, bf16[128,2048]{1,0:T(8,128)(2,1)S(1)}, u32[]{:S(2)}, u32[]{:S(2)}) collective-permute-start(bf16[128,2048]{1,0:T(8,128)(2,1)S(1)} %add.29), channel_id=1, source_target_pairs={{0,4},{1,3},{4,8},{5,1},{8,12},{9,5},{12,14},{13,9},{14,10},{15,13... | collective-permute-start | bytes 1572872 | tf_op jit(solution)/shard_map/sums out 4a/ppermute | solution.py:425
  120.5 7.6 %collective-permute-start.37 = (bf16[128,2048]{1,0:T(8,128)(2,1)S(1)}, bf16[128,2048]{1,0:T(8,128)(2,1)S(1)}, u32[]{:S(2)}, u32[]{:S(2)}) collective-permute-start(bf16[128,2048]{1,0:T(8,128)(2,1)S(1)} %get-tuple-element.54), channel_id=1, source_target_pairs={{0,1},{1,0},{2,3},{3,2},{4,5},{5,4},{6,7},{7,6},{8,9},{9,8},{10,11... | collective-permute-start | bytes 1572872 | tf_op jit(solution)/shard_map/sums across 5a/ppermute | solution.py:429
  122.5 25.8 %collective-permute-start.27 = (bf16[128,2048]{1,0:T(8,128)(2,1)S(1)}, bf16[128,2048]{1,0:T(8,128)(2,1)S(1)}, u32[]{:S(2)}, u32[]{:S(2)}) collective-permute-start(bf16[128,2048]{1,0:T(8,128)(2,1)S(1)} %get-tuple-element.47), channel_id=1, source_target_pairs={{0,1},{1,0},{2,3},{3,2},{4,5},{5,4},{6,7},{7,6},{8,9},{9,8},{10,11... | collective-permute-start | bytes 1572872 | tf_op jit(solution)/shard_map/sums across 0a/ppermute | solution.py:429
  123.1 6.7 %collective-permute-start.34 = (bf16[128,2048]{1,0:T(8,128)(2,1)S(1)}, bf16[128,2048]{1,0:T(8,128)(2,1)S(1)}, u32[]{:S(2)}, u32[]{:S(2)}) collective-permute-start(bf16[128,2048]{1,0:T(8,128)(2,1)S(1)} %collective-permute-done.30.refs_0_), channel_id=1, source_target_pairs={{0,1},{1,0},{2,3},{3,2},{4,5},{5,4},{6,7},{7,6},{8,9},{9,8},{10,11... | collective-permute-start | bytes 1572872 | tf_op jit(solution)/shard_map/rows across 6a/ppermute | solution.py:429
  123.2 10.6 %collective-permute-start.31 = (bf16[128,2048]{1,0:T(8,128)(2,1)S(1)}, bf16[128,2048]{1,0:T(8,128)(2,1)S(1)}, u32[]{:S(2)}, u32[]{:S(2)}) collective-permute-start(bf16[128,2048]{1,0:T(8,128)(2,1)S(1)} %collective-permute-done.30.refs_0_), channel_id=1, source_target_pairs={{0,4},{1,3},{4,8},{5,1},{8,12},{9,5},{12,14},{13,9},{14,10},{15,13... | collective-permute-start | bytes 1572872 | tf_op jit(solution)/shard_map/rows out 7a/ppermute | solution.py:425
  128.2 8.3 %collective-permute-start.50 = (bf16[64,2048]{1,0:T(8,128)(2,1)S(1)}, bf16[64,2048]{1,0:T(8,128)(2,1)S(1)}, u32[]{:S(2)}, u32[]{:S(2)}) collective-permute-start(bf16[64,2048]{1,0:T(8,128)(2,1)S(1)} %add.30), channel_id=1, source_target_pairs={{0,4},{1,3},{4,8},{5,1},{8,12},{9,5},{12,14},{13,9},{14,10},{15,13... | collective-permute-start | bytes 786440 | tf_op jit(solution)/shard_map/sums out 5a/ppermute | solution.py:425
  131.7 4.9 %collective-permute-start.35 = (bf16[128,2048]{1,0:T(8,128)(2,1)S(1)}, bf16[128,2048]{1,0:T(8,128)(2,1)S(1)}, u32[]{:S(2)}, u32[]{:S(2)}) collective-permute-start(bf16[128,2048]{1,0:T(8,128)(2,1)S(1)} %get-tuple-element.52), channel_id=1, source_target_pairs={{0,1},{1,0},{2,3},{3,2},{4,5},{5,4},{6,7},{7,6},{8,9},{9,8},{10,11... | collective-permute-start | bytes 1572872 | tf_op jit(solution)/shard_map/sums across 6a/ppermute | solution.py:429
  131.9 8.3 %collective-permute-start.53 = (bf16[64,2048]{1,0:T(8,128)(2,1)S(1)}, bf16[64,2048]{1,0:T(8,128)(2,1)S(1)}, u32[]{:S(2)}, u32[]{:S(2)}) collective-permute-start(bf16[64,2048]{1,0:T(8,128)(2,1)S(1)} %add.33), channel_id=1, source_target_pairs={{0,4},{1,3},{4,8},{5,1},{8,12},{9,5},{12,14},{13,9},{14,10},{15,13... | collective-permute-start | bytes 786440 | tf_op jit(solution)/shard_map/sums out 5b/ppermute | solution.py:425
  133.8 4.5 %collective-permute-start.32 = (bf16[128,2048]{1,0:T(8,128)(2,1)S(1)}, bf16[128,2048]{1,0:T(8,128)(2,1)S(1)}, u32[]{:S(2)}, u32[]{:S(2)}) collective-permute-start(bf16[128,2048]{1,0:T(8,128)(2,1)S(1)} %collective-permute-done.31.refs_0_), channel_id=1, source_target_pairs={{0,1},{1,0},{2,3},{3,2},{4,5},{5,4},{6,7},{7,6},{8,9},{9,8},{10,11... | collective-permute-start | bytes 1572872 | tf_op jit(solution)/shard_map/rows across 7a/ppermute | solution.py:429
  136.7 6.4 %collective-permute-start.51 = (bf16[64,2048]{1,0:T(8,128)(2,1)S(1)}, bf16[64,2048]{1,0:T(8,128)(2,1)S(1)}, u32[]{:S(2)}, u32[]{:S(2)}) collective-permute-start(bf16[64,2048]{1,0:T(8,128)(2,1)S(1)} %add.31), channel_id=1, source_target_pairs={{0,4},{1,3},{4,8},{5,1},{8,12},{9,5},{12,14},{13,9},{14,10},{15,13... | collective-permute-start | bytes 786440 | tf_op jit(solution)/shard_map/sums out 6a/ppermute | solution.py:425
  140.1 3.0 %collective-permute-start.33 = (bf16[128,2048]{1,0:T(8,128)(2,1)S(1)}, bf16[128,2048]{1,0:T(8,128)(2,1)S(1)}, u32[]{:S(2)}, u32[]{:S(2)}) collective-permute-start(bf16[128,2048]{1,0:T(8,128)(2,1)S(1)} %get-tuple-element.50), channel_id=1, source_target_pairs={{0,1},{1,0},{2,3},{3,2},{4,5},{5,4},{6,7},{7,6},{8,9},{9,8},{10,11... | collective-permute-start | bytes 1572872 | tf_op jit(solution)/shard_map/sums across 7a/ppermute | solution.py:429
  140.3 6.4 %collective-permute-start.54 = (bf16[64,2048]{1,0:T(8,128)(2,1)S(1)}, bf16[64,2048]{1,0:T(8,128)(2,1)S(1)}, u32[]{:S(2)}, u32[]{:S(2)}) collective-permute-start(bf16[64,2048]{1,0:T(8,128)(2,1)S(1)} %add.34), channel_id=1, source_target_pairs={{0,4},{1,3},{4,8},{5,1},{8,12},{9,5},{12,14},{13,9},{14,10},{15,13... | collective-permute-start | bytes 786440 | tf_op jit(solution)/shard_map/sums out 6b/ppermute | solution.py:425
  143.2 6.4 %collective-permute-start.52 = (bf16[64,2048]{1,0:T(8,128)(2,1)S(1)}, bf16[64,2048]{1,0:T(8,128)(2,1)S(1)}, u32[]{:S(2)}, u32[]{:S(2)}) collective-permute-start(bf16[64,2048]{1,0:T(8,128)(2,1)S(1)} %add.32), channel_id=1, source_target_pairs={{0,4},{1,3},{4,8},{5,1},{8,12},{9,5},{12,14},{13,9},{14,10},{15,13... | collective-permute-start | bytes 786440 | tf_op jit(solution)/shard_map/sums out 7a/ppermute | solution.py:425
  146.8 6.4 %collective-permute-start.55 = (bf16[64,2048]{1,0:T(8,128)(2,1)S(1)}, bf16[64,2048]{1,0:T(8,128)(2,1)S(1)}, u32[]{:S(2)}, u32[]{:S(2)}) collective-permute-start(bf16[64,2048]{1,0:T(8,128)(2,1)S(1)} %add.35), channel_id=1, source_target_pairs={{0,4},{1,3},{4,8},{5,1},{8,12},{9,5},{12,14},{13,9},{14,10},{15,13... | collective-permute-start | bytes 786440 | tf_op jit(solution)/shard_map/sums out 7b/ppermute | solution.py:425
  (10 other events, 35.6 us)

commit v7 on v6

--- a/solution.py
+++ b/solution.py
@@ -14,13 +14,13 @@
 HOPS_X = 1
 HELD = 4
 AFTER = {3: 0}
-TAIL = 5
+HALVED = (5, 6, 7)
 DEAD = 128.0
 ADD_COST = 2.0
 EXPERT_COST = 4.0
 AGP = 1
 GIVE = 1
-LATE = 3
+LATE = 2
 FAR_MIB = 60
 ATT_MIB = 8
 PRO_MIB = 14
@@ -511,7 +511,7 @@
         x.append([ahead(part, f"rows out {s}{'ab'[i]}") for i, part in enumerate(x[-1])])
         y.append([across(part, f"rows across {s}{'ab'[i]}") for i, part in enumerate(x[-1])])
         keep, back = sums(s)
-        total = combine([keep, back, travelling], 2 if s >= TAIL else 1)
+        total = combine([keep, back, travelling], 2 if s in HALVED else 1)
         travelling = [ahead(part, f"sums out {s}{'ab'[i]}") for i, part in enumerate(total)]
     base = combine([residual, *sums(0, (x[min(LATE, pairs - 1)][0],))], 1, F32)
     return combine([base, travelling], 1)[0]

time: 154 us -> 154 us (level)
  no operation moved by 1% of the time
where the time goes in v7:
time: 154 us
  waiting for transfers between devices  61.7 us (40%)
  starting transfers between devices  55.7 us (36%)
  Pallas kernels  34.6 us (22%)
  local copies, waits for them, and re-layouts  1.63 us (1%)
    ppermute x29, waiting for transfers between devices, ahead(): return lax.ppermute(block, ('group', 'expert'), forward)  57.7 us
    ppermute x29, starting transfers between devices, ahead(): return lax.ppermute(block, ('group', 'expert'), forward)  45.9 us
    pallas_call x8, Pallas kernels, expert(): pl.pallas_call(functools.partial(expert_body, cols, parts, len(after), gi...  15 us
    pallas_call x4, Pallas kernels, attend(): pl.pallas_call(functools.partial(attend_body, first, count, len(passed) +...  9.18 us
    pallas_call x2, Pallas kernels, project(): pl.pallas_call(functools.partial(project_body, ring, steps, number, len(m...  4.68 us
    ppermute x22, starting transfers between devices, across(): return lax.ppermute(block, 'expert', sibling)  3.11 us
    pallas_call x1, Pallas kernels, far_segment(): pl.pallas_call(far_body, out_shape=jax.ShapeDtypeStruct((2,) + cache_kv.s...  3.08 us
  transfers between devices with their start and end apart: 56, of which 25 were waited for; matrix products, arithmetic and copies ran while one was open for 0% of the time, Pallas kernels for 18%

profile of v7, /device:TPU:0, one launch (start us, length us, event | category | flops | bytes accessed | tf_op | source)
XLA Modules:
  0.0 154.1 jit_solution(13345206099621531452)
XLA Ops:
  0.0 3.1 %far_segment.1 = bf16[2,128,2048]{2,1,0:T(8,128)(2,1)} custom-call(s32[1,2]{1,0:T(1,128)} %len_ref.9, bf16[2,1,2,128,2048]{4,3,2,1,0:T(8,128)(2,1)} %cache_ref.9), custom_call_target="tpu_custom_call" | custom-call | flops 10200000512 | bytes 1000 | tf_op jit(solution)/shard_map/far segment/far_segment/pallas_call | solution.py:125
  3.1 3.0 %collective-permute-start = (bf16[2,128,2048]{2,1,0:T(8,128)(2,1)}, bf16[2,128,2048]{2,1,0:T(8,128)(2,1)}, u32[]{:S(2)}, u32[]{:S(2)}) collective-permute-start(bf16[2,128,2048]{2,1,0:T(8,128)(2,1)} %far_segment.1), channel_id=1, source_target_pairs={{0,16},{16,0},{1,17},{17,1},{2,18},{18,2},{3,19},{19,3},{4,20},{20... | collective-permute-start | bytes 3145736 | tf_op jit(solution)/shard_map/far segment/ppermute | solution.py:439
  6.8 1.6 %collective-permute-start.1 = (bf16[136,1024]{1,0:T(8,128)(2,1)S(1)}, bf16[136,1024]{1,0:T(8,128)(2,1)S(1)}, u32[]{:S(2)}, u32[]{:S(2)}) collective-permute-start(bf16[136,1024]{1,0:T(8,128)(2,1)S(1)} %get-tuple-element.34.refs_8_), channel_id=1, source_target_pairs={{0,4},{1,3},{4,8},{5,1},{8,12},{9,5},{12,14},{13,9},{14,10},{15,13... | collective-permute-start | bytes 835592 | tf_op jit(solution)/shard_map/o rows 1a/ppermute | solution.py:425
  8.4 1.6 %collective-permute-start.7 = (bf16[136,1024]{1,0:T(8,128)(2,1)S(1)}, bf16[136,1024]{1,0:T(8,128)(2,1)S(1)}, u32[]{:S(2)}, u32[]{:S(2)}) collective-permute-start(bf16[136,1024]{1,0:T(8,128)(2,1)S(1)} %collective-permute-done.6.refs_9_), channel_id=1, source_target_pairs={{0,4},{1,3},{4,8},{5,1},{8,12},{9,5},{12,14},{13,9},{14,10},{15,13... | collective-permute-start | bytes 835592 | tf_op jit(solution)/shard_map/o rows 1b/ppermute | solution.py:425
  10.0 3.4 %collective-permute-done.1.refs_10_ = bf16[136,1024]{1,0:T(8,128)(2,1)S(1)} collective-permute-done((bf16[136,1024]{1,0:T(8,128)(2,1)S(1)}, bf16[136,1024]{1,0:T(8,128)(2,1)S(1)}, u32[]{:S(2)}, u32[]{:S(2)}) %collective-permute-start.1) | collective-permute-done | bytes 278560 | tf_op jit(solution)/shard_map/o rows 1a/ppermute | solution.py:425
  13.4 1.6 %collective-permute-start.2 = (bf16[136,1024]{1,0:T(8,128)(2,1)S(1)}, bf16[136,1024]{1,0:T(8,128)(2,1)S(1)}, u32[]{:S(2)}, u32[]{:S(2)}) collective-permute-start(bf16[136,1024]{1,0:T(8,128)(2,1)S(1)} %collective-permute-done.1.refs_10_), channel_id=1, source_target_pairs={{0,4},{1,3},{4,8},{5,1},{8,12},{9,5},{12,14},{13,9},{14,10},{15,13... | collective-permute-start | bytes 835592 | tf_op jit(solution)/shard_map/o rows 2a/ppermute | solution.py:425
  14.9 1.4 collective-permute-done.7.refs_11_
  16.4 1.6 %collective-permute-start.13 = (bf16[136,1024]{1,0:T(8,128)(2,1)S(1)}, bf16[136,1024]{1,0:T(8,128)(2,1)S(1)}, u32[]{:S(2)}, u32[]{:S(2)}) collective-permute-start(bf16[136,1024]{1,0:T(8,128)(2,1)S(1)} %collective-permute-done.7.refs_11_), channel_id=1, source_target_pairs={{0,4},{1,3},{4,8},{5,1},{8,12},{9,5},{12,14},{13,9},{14,10},{15,13... | collective-permute-start | bytes 835592 | tf_op jit(solution)/shard_map/o rows 2b/ppermute | solution.py:425
  17.9 2.0 %collective-permute-done.2.refs_12_ = bf16[136,1024]{1,0:T(8,128)(2,1)S(1)} collective-permute-done((bf16[136,1024]{1,0:T(8,128)(2,1)S(1)}, bf16[136,1024]{1,0:T(8,128)(2,1)S(1)}, u32[]{:S(2)}, u32[]{:S(2)}) %collective-permute-start.2) | collective-permute-done | bytes 278560 | tf_op jit(solution)/shard_map/o rows 2a/ppermute | solution.py:425
  19.9 1.6 %collective-permute-start.3 = (bf16[136,1024]{1,0:T(8,128)(2,1)S(1)}, bf16[136,1024]{1,0:T(8,128)(2,1)S(1)}, u32[]{:S(2)}, u32[]{:S(2)}) collective-permute-start(bf16[136,1024]{1,0:T(8,128)(2,1)S(1)} %collective-permute-done.2.refs_12_), channel_id=1, source_target_pairs={{0,4},{1,3},{4,8},{5,1},{8,12},{9,5},{12,14},{13,9},{14,10},{15,13... | collective-permute-start | bytes 835592 | tf_op jit(solution)/shard_map/o rows 3a/ppermute | solution.py:425
  22.0 1.5 %collective-permute-start.8 = (bf16[136,1024]{1,0:T(8,128)(2,1)S(1)}, bf16[136,1024]{1,0:T(8,128)(2,1)S(1)}, u32[]{:S(2)}, u32[]{:S(2)}) collective-permute-start(bf16[136,1024]{1,0:T(8,128)(2,1)S(1)} %collective-permute-done.7.refs_11_), channel_id=1, source_target_pairs={{0,16},{16,0},{1,17},{17,1},{2,18},{18,2},{3,19},{19,3},{4,20},{20... | collective-permute-start | bytes 835592 | tf_op jit(solution)/shard_map/o rows of partner/ppermute | solution.py:458
  23.5 1.6 %collective-permute-start.14 = (bf16[136,1024]{1,0:T(8,128)(2,1)S(1)}, bf16[136,1024]{1,0:T(8,128)(2,1)S(1)}, u32[]{:S(2)}, u32[]{:S(2)}) collective-permute-start(bf16[136,1024]{1,0:T(8,128)(2,1)S(1)} %collective-permute-done.13.refs_13_), channel_id=1, source_target_pairs={{0,4},{1,3},{4,8},{5,1},{8,12},{9,5},{12,14},{13,9},{14,10},{15,13... | collective-permute-start | bytes 835592 | tf_op jit(solution)/shard_map/o rows 3b/ppermute | solution.py:425
  25.1 1.4 collective-permute-done.3.refs_14_
  26.5 1.6 %collective-permute-start.4 = (bf16[136,1024]{1,0:T(8,128)(2,1)S(1)}, bf16[136,1024]{1,0:T(8,128)(2,1)S(1)}, u32[]{:S(2)}, u32[]{:S(2)}) collective-permute-start(bf16[136,1024]{1,0:T(8,128)(2,1)S(1)} %collective-permute-done.3.refs_14_), channel_id=1, source_target_pairs={{0,4},{1,3},{4,8},{5,1},{8,12},{9,5},{12,14},{13,9},{14,10},{15,13... | collective-permute-start | bytes 835592 | tf_op jit(solution)/shard_map/o rows 4a/ppermute | solution.py:425
  28.0 2.4 %collective-permute-done.far_ref = bf16[2,128,2048]{2,1,0:T(8,128)(2,1)} collective-permute-done((bf16[2,128,2048]{2,1,0:T(8,128)(2,1)}, bf16[2,128,2048]{2,1,0:T(8,128)(2,1)}, u32[]{:S(2)}, u32[]{:S(2)}) %collective-permute-start) | collective-permute-done | bytes 1048608 | tf_op jit(solution)/shard_map/far segment/ppermute | solution.py:439
  30.4 2.3 %attend.5.refs_1_ = bf16[4,128,128]{2,1,0:T(8,128)(2,1)S(1)} custom-call(s32[1,2]{1,0:T(1,128)S(1)} %copy-done.17, bf16[128,2048]{1,0:T(8,128)(2,1)S(1)} %copy-done.11, bf16[2,128,2048]{2,1,0:T(8,128)(2,1)S(1)} %copy-done.9, bf16[2,1,2,128,2048]{4,3,2,1,0:T(8,128)(2,1)S(1)} %copy-done.7, bf16[2,128,2048]{2,1,0:T(8,128)(2,1)} %collective-permute-done.far_ref), custom_call_target="tpu_custom_call" | custom-call | flops 14400000000 | bytes 1000 | tf_op jit(solution)/shard_map/attend/pallas_call | solution.py:162
  32.8 2.2 %collective-permute-start.15 = (bf16[136,1024]{1,0:T(8,128)(2,1)S(1)}, bf16[136,1024]{1,0:T(8,128)(2,1)S(1)}, u32[]{:S(2)}, u32[]{:S(2)}) collective-permute-start(bf16[136,1024]{1,0:T(8,128)(2,1)S(1)} %collective-permute-done.14.refs_15_), channel_id=1, source_target_pairs={{0,4},{1,3},{4,8},{5,1},{8,12},{9,5},{12,14},{13,9},{14,10},{15,13... | collective-permute-start | bytes 835592 | tf_op jit(solution)/shard_map/o rows 4b/ppermute | solution.py:425
  35.0 2.3 %attend.4 = (bf16[4,128,128]{2,1,0:T(8,128)(2,1)S(1)}, bf16[136,1024]{1,0:T(8,128)(2,1)S(1)}) custom-call(s32[1,2]{1,0:T(1,128)S(1)} %copy-done.17, bf16[128,2048]{1,0:T(8,128)(2,1)S(1)} %copy-done.11, bf16[2,128,2048]{2,1,0:T(8,128)(2,1)S(1)} %copy-done.9, bf16[2,1,2,128,2048]{4,3,2,1,0:T(8,128)(2,1)S(1)} %copy-done.7, ...), custom_call_target="tpu_custom_call", output_to_operand_aliasing={{1}: (5, {})} | custom-call | flops 14400000000 | bytes 1000 | tf_op jit(solution)/shard_map/attend/pallas_call | solution.py:162
  37.3 1.6 %collective-permute-start.16 = (bf16[136,1024]{1,0:T(8,128)(2,1)S(1)}, bf16[136,1024]{1,0:T(8,128)(2,1)}, u32[]{:S(2)}, u32[]{:S(2)}) collective-permute-start(bf16[136,1024]{1,0:T(8,128)(2,1)S(1)} %get-tuple-element.37.refs_16_), channel_id=1, source_target_pairs={{0,4},{1,3},{4,8},{5,1},{8,12},{9,5},{12,14},{13,9},{14,10},{15,13... | collective-permute-start | bytes 835592 | tf_op jit(solution)/shard_map/o rows 5a/ppermute | solution.py:425
  39.5 2.1 %collective-permute-start.17 = (bf16[136,1024]{1,0:T(8,128)(2,1)S(1)}, bf16[136,1024]{1,0:T(8,128)(2,1)}, u32[]{:S(2)}, u32[]{:S(2)}) collective-permute-start(bf16[136,1024]{1,0:T(8,128)(2,1)S(1)} %collective-permute-done.15.refs_17_), channel_id=1, source_target_pairs={{0,4},{1,3},{4,8},{5,1},{8,12},{9,5},{12,14},{13,9},{14,10},{15,13... | collective-permute-start | bytes 835592 | tf_op jit(solution)/shard_map/o rows 5b/ppermute | solution.py:425
  41.5 2.3 %attend.6.refs_2_ = bf16[4,128,128]{2,1,0:T(8,128)(2,1)S(1)} custom-call(s32[1,2]{1,0:T(1,128)S(1)} %copy-done.17, bf16[128,2048]{1,0:T(8,128)(2,1)S(1)} %copy-done.11, bf16[2,128,2048]{2,1,0:T(8,128)(2,1)S(1)} %copy-done.9, bf16[2,1,2,128,2048]{4,3,2,1,0:T(8,128)(2,1)S(1)} %copy-done.7, bf16[2,128,2048]{2,1,0:T(8,128)(2,1)} %collective-permute-done.far_ref), custom_call_target="tpu_custom_call" | custom-call | flops 14400000000 | bytes 1000 | tf_op jit(solution)/shard_map/attend/pallas_call | solution.py:162
  44.0 1.6 %collective-permute-start.18 = (bf16[136,1024]{1,0:T(8,128)(2,1)}, bf16[136,1024]{1,0:T(8,128)(2,1)}, u32[]{:S(2)}, u32[]{:S(2)}) collective-permute-start(bf16[136,1024]{1,0:T(8,128)(2,1)} %collective-permute-done.16.refs_18_), channel_id=1, source_target_pairs={{0,4},{1,3},{4,8},{5,1},{8,12},{9,5},{12,14},{13,9},{14,10},{15,13... | collective-permute-start | bytes 835592 | tf_op jit(solution)/shard_map/o rows 6a/ppermute | solution.py:425
  45.6 1.4 collective-permute-done.17.refs_19_
  47.0 1.6 %collective-permute-start.19 = (bf16[136,1024]{1,0:T(8,128)(2,1)}, bf16[136,1024]{1,0:T(8,128)(2,1)}, u32[]{:S(2)}, u32[]{:S(2)}) collective-permute-start(bf16[136,1024]{1,0:T(8,128)(2,1)} %collective-permute-done.17.refs_19_), channel_id=1, source_target_pairs={{0,4},{1,3},{4,8},{5,1},{8,12},{9,5},{12,14},{13,9},{14,10},{15,13... | collective-permute-start | bytes 835592 | tf_op jit(solution)/shard_map/o rows 6b/ppermute | solution.py:425
  48.6 2.4 %attend.7.refs_3_ = bf16[4,128,128]{2,1,0:T(8,128)(2,1)S(1)} custom-call(s32[1,2]{1,0:T(1,128)S(1)} %copy-done.17, bf16[128,2048]{1,0:T(8,128)(2,1)S(1)} %copy-done.11, bf16[2,128,2048]{2,1,0:T(8,128)(2,1)S(1)} %copy-done.9, bf16[2,1,2,128,2048]{4,3,2,1,0:T(8,128)(2,1)S(1)} %copy-done.7, bf16[2,128,2048]{2,1,0:T(8,128)(2,1)} %collective-permute-done.far_ref, ...), custom_call_target="tpu_custom_call" | custom-call | flops 14400000000 | bytes 1000 | tf_op jit(solution)/shard_map/attend/pallas_call | solution.py:162
  54.2 2.7 %project.2 = (f32[128,1024]{1,0:T(8,128)S(1)}, f32[128,1024]{1,0:T(8,128)S(1)}, f32[128,128]{1,0:T(8,128)S(1)}) custom-call(s32[1]{0:T(128)} %bitcast.1.me_ref, bf16[4,128,128]{2,1,0:T(8,128)(2,1)S(1)} %get-tuple-element.35.refs_0_, bf16[4,128,128]{2,1,0:T(8,128)(2,1)S(1)} %attend.5.refs_1_, bf16[4,128,128]{2,1,0:T(8,128)(2,1)S(1)} %attend.6.refs_2_, ...), custom_call_target="tpu_custom_call" | custom-call | flops 805306368 | bytes 3145728 | tf_op jit(solution)/shard_map/project/pallas_call | solution.py:290
  57.0 2.0 %project.3 = (f32[128,1024]{1,0:T(8,128)S(1)}, bf16[128,1024]{1,0:T(8,128)(2,1)S(1)}, f32[128,128]{1,0:T(8,128)S(1)}) custom-call(s32[1]{0:T(128)} %bitcast.1.me_ref, bf16[4,128,128]{2,1,0:T(8,128)(2,1)S(1)} %get-tuple-element.35.refs_0_, bf16[4,128,128]{2,1,0:T(8,128)(2,1)S(1)} %attend.5.refs_1_, bf16[4,128,128]{2,1,0:T(8,128)(2,1)S(1)} %attend.6.refs_2_, ...), custom_call_target="tpu_custom_call" | custom-call | flops 268435456 | bytes 1048576 | tf_op jit(solution)/shard_map/project/pallas_call | solution.py:290
  61.2 1.6 %collective-permute-start.24 = (bf16[128,2048]{1,0:T(8,128)(2,1)S(1)}, bf16[128,2048]{1,0:T(8,128)(2,1)S(1)}, u32[]{:S(2)}, u32[]{:S(2)}) collective-permute-start(bf16[128,2048]{1,0:T(8,128)(2,1)S(1)} %get-tuple-element.44.refs_0_), channel_id=1, source_target_pairs={{0,4},{1,3},{4,8},{5,1},{8,12},{9,5},{12,14},{13,9},{14,10},{15,13... | collective-permute-start | bytes 1572872 | tf_op jit(solution)/shard_map/rows out 1a/ppermute | solution.py:425
  62.8 7.7 %collective-permute-done.24.refs_0_ = bf16[128,2048]{1,0:T(8,128)(2,1)S(1)} collective-permute-done((bf16[128,2048]{1,0:T(8,128)(2,1)S(1)}, bf16[128,2048]{1,0:T(8,128)(2,1)S(1)}, u32[]{:S(2)}, u32[]{:S(2)}) %collective-permute-start.24) | collective-permute-done | bytes 524320 | tf_op jit(solution)/shard_map/rows out 1a/ppermute | solution.py:425
  70.4 1.5 collective-permute-start.25
  72.4 1.9 %expert.15 = (bf16[128,2048]{1,0:T(8,128)(2,1)S(1)}, bf16[128,2048]{1,0:T(8,128)(2,1)S(1)}) custom-call(bf16[128,2048]{1,0:T(8,128)(2,1)S(1)} %collective-permute-done.24.refs_0_, bf16[128,2048]{1,0:T(8,128)(2,1)S(1)} %collective-permute-done.44.refs_1_, f32[128,128]{1,0:T(8,128)S(1)} %get-tuple-element.45.refs_2_.refs_3_, ...), custom_call_target="tpu_custom_call" | custom-call | flops 24000000000 | bytes 1000 | tf_op jit(solution)/shard_map/expert/pallas_call | solution.py:370
  74.4 5.2 %collective-permute-done.25.refs_6_.refs_0_ = bf16[128,2048]{1,0:T(8,128)(2,1)S(1)} collective-permute-done((bf16[128,2048]{1,0:T(8,128)(2,1)S(1)}, bf16[128,2048]{1,0:T(8,128)(2,1)S(1)}, u32[]{:S(2)}, u32[]{:S(2)}) %collective-permute-start.25) | collective-permute-done | bytes 524320 | tf_op jit(solution)/shard_map/rows out 2a/ppermute | solution.py:425
  79.6 1.5 collective-permute-start.27
  81.3 1.4 collective-permute-start.46
  82.7 1.9 %expert.14 = (bf16[128,2048]{1,0:T(8,128)(2,1)S(1)}, bf16[128,2048]{1,0:T(8,128)(2,1)S(1)}) custom-call(bf16[128,2048]{1,0:T(8,128)(2,1)S(1)} %collective-permute-done.25.refs_6_.refs_0_, bf16[128,2048]{1,0:T(8,128)(2,1)S(1)} %collective-permute-done.42.refs_1_, f32[128,128]{1,0:T(8,128)S(1)} %get-tuple-element.45.refs_2_.refs_3_, ...), custom_call_target="tpu_custom_call" | custom-call | flops 24000000000 | bytes 1000 | tf_op jit(solution)/shard_map/expert/pallas_call | solution.py:370
  84.7 4.1 %collective-permute-done.27.refs_0_ = bf16[128,2048]{1,0:T(8,128)(2,1)S(1)} collective-permute-done((bf16[128,2048]{1,0:T(8,128)(2,1)S(1)}, bf16[128,2048]{1,0:T(8,128)(2,1)S(1)}, u32[]{:S(2)}, u32[]{:S(2)}) %collective-permute-start.27) | collective-permute-done | bytes 524320 | tf_op jit(solution)/shard_map/rows out 3a/ppermute | solution.py:425
  88.8 1.5 collective-permute-start.28
  90.3 4.1 %collective-permute-done.46.refs_2_ = bf16[128,2048]{1,0:T(8,128)(2,1)S(1)} collective-permute-done((bf16[128,2048]{1,0:T(8,128)(2,1)S(1)}, bf16[128,2048]{1,0:T(8,128)(2,1)S(1)}, u32[]{:S(2)}, u32[]{:S(2)}) %collective-permute-start.46) | collective-permute-done | bytes 524320 | tf_op jit(solution)/shard_map/sums out 1a/ppermute | solution.py:425
  94.6 1.6 %collective-permute-start.47 = (bf16[128,2048]{1,0:T(8,128)(2,1)S(1)}, bf16[128,2048]{1,0:T(8,128)(2,1)S(1)}, u32[]{:S(2)}, u32[]{:S(2)}) collective-permute-start(bf16[128,2048]{1,0:T(8,128)(2,1)S(1)} %add.27), channel_id=1, source_target_pairs={{0,4},{1,3},{4,8},{5,1},{8,12},{9,5},{12,14},{13,9},{14,10},{15,13... | collective-permute-start | bytes 1572872 | tf_op jit(solution)/shard_map/sums out 2a/ppermute | solution.py:425
  96.2 1.9 %expert.13 = (bf16[128,2048]{1,0:T(8,128)(2,1)S(1)}, bf16[128,2048]{1,0:T(8,128)(2,1)S(1)}) custom-call(bf16[128,2048]{1,0:T(8,128)(2,1)S(1)} %collective-permute-done.27.refs_0_, bf16[128,2048]{1,0:T(8,128)(2,1)S(1)} %collective-permute-done.40.refs_1_, f32[128,128]{1,0:T(8,128)S(1)} %get-tuple-element.45.refs_2_.refs_3_, ...), custom_call_target="tpu_custom_call" | custom-call | flops 24000000000 | bytes 1000 | tf_op jit(solution)/shard_map/expert/pallas_call | solution.py:370
  98.2 1.9 %collective-permute-done.28.refs_0_ = bf16[128,2048]{1,0:T(8,128)(2,1)S(1)} collective-permute-done((bf16[128,2048]{1,0:T(8,128)(2,1)S(1)}, bf16[128,2048]{1,0:T(8,128)(2,1)S(1)}, u32[]{:S(2)}, u32[]{:S(2)}) %collective-permute-start.28) | collective-permute-done | bytes 524320 | tf_op jit(solution)/shard_map/rows out 4a/ppermute | solution.py:425
  100.1 1.5 collective-permute-start.29
  101.6 4.1 %collective-permute-done.47.refs_2_ = bf16[128,2048]{1,0:T(8,128)(2,1)S(1)} collective-permute-done((bf16[128,2048]{1,0:T(8,128)(2,1)S(1)}, bf16[128,2048]{1,0:T(8,128)(2,1)S(1)}, u32[]{:S(2)}, u32[]{:S(2)}) %collective-permute-start.47) | collective-permute-done | bytes 524320 | tf_op jit(solution)/shard_map/sums out 2a/ppermute | solution.py:425
  105.9 1.6 %collective-permute-start.48 = (bf16[128,2048]{1,0:T(8,128)(2,1)S(1)}, bf16[128,2048]{1,0:T(8,128)(2,1)S(1)}, u32[]{:S(2)}, u32[]{:S(2)}) collective-permute-start(bf16[128,2048]{1,0:T(8,128)(2,1)S(1)} %add.28), channel_id=1, source_target_pairs={{0,4},{1,3},{4,8},{5,1},{8,12},{9,5},{12,14},{13,9},{14,10},{15,13... | collective-permute-start | bytes 1572872 | tf_op jit(solution)/shard_map/sums out 3a/ppermute | solution.py:425
  107.4 1.9 %expert.12 = (bf16[128,2048]{1,0:T(8,128)(2,1)S(1)}, bf16[128,2048]{1,0:T(8,128)(2,1)S(1)}) custom-call(bf16[128,2048]{1,0:T(8,128)(2,1)S(1)} %collective-permute-done.28.refs_0_, bf16[128,2048]{1,0:T(8,128)(2,1)S(1)} %collective-permute-done.38.refs_1_, f32[128,128]{1,0:T(8,128)S(1)} %get-tuple-element.45.refs_2_.refs_3_, ...), custom_call_target="tpu_custom_call" | custom-call | flops 24000000000 | bytes 1000 | tf_op jit(solution)/shard_map/expert/pallas_call | solution.py:370
  109.9 1.4 collective-permute-done.29.refs_0_
  111.3 1.5 collective-permute-start.30
  112.8 4.1 %collective-permute-done.48.refs_2_ = bf16[128,2048]{1,0:T(8,128)(2,1)S(1)} collective-permute-done((bf16[128,2048]{1,0:T(8,128)(2,1)S(1)}, bf16[128,2048]{1,0:T(8,128)(2,1)S(1)}, u32[]{:S(2)}, u32[]{:S(2)}) %collective-permute-start.48) | collective-permute-done | bytes 524320 | tf_op jit(solution)/shard_map/sums out 3a/ppermute | solution.py:425
  117.1 1.6 %collective-permute-start.49 = (bf16[128,2048]{1,0:T(8,128)(2,1)S(1)}, bf16[128,2048]{1,0:T(8,128)(2,1)S(1)}, u32[]{:S(2)}, u32[]{:S(2)}) collective-permute-start(bf16[128,2048]{1,0:T(8,128)(2,1)S(1)} %add.29), channel_id=1, source_target_pairs={{0,4},{1,3},{4,8},{5,1},{8,12},{9,5},{12,14},{13,9},{14,10},{15,13... | collective-permute-start | bytes 1572872 | tf_op jit(solution)/shard_map/sums out 4a/ppermute | solution.py:425
  118.7 1.9 %expert.11 = (bf16[128,2048]{1,0:T(8,128)(2,1)S(1)}, bf16[128,2048]{1,0:T(8,128)(2,1)S(1)}) custom-call(bf16[128,2048]{1,0:T(8,128)(2,1)S(1)} %collective-permute-done.29.refs_0_, bf16[128,2048]{1,0:T(8,128)(2,1)S(1)} %collective-permute-done.36.refs_1_, f32[128,128]{1,0:T(8,128)S(1)} %get-tuple-element.45.refs_2_.refs_3_, ...), custom_call_target="tpu_custom_call" | custom-call | flops 24000000000 | bytes 1000 | tf_op jit(solution)/shard_map/expert/pallas_call | solution.py:370
  120.6 1.9 %expert.8 = (bf16[128,2048]{1,0:T(8,128)(2,1)S(1)}, bf16[128,2048]{1,0:T(8,128)(2,1)S(1)}) custom-call(bf16[128,2048]{1,0:T(8,128)(2,1)S(1)} %get-tuple-element.44.refs_0_, bf16[128,2048]{1,0:T(8,128)(2,1)S(1)} %collective-permute-done.23.refs_1_, f32[128,128]{1,0:T(8,128)S(1)} %get-tuple-element.45.refs_2_.refs_3_, ...), custom_call_target="tpu_custom_call" | custom-call | flops 24000000000 | bytes 1000 | tf_op jit(solution)/shard_map/expert/pallas_call | solution.py:370
  123.2 1.4 collective-permute-start.31
  124.6 3.6 %collective-permute-done.49.refs_2_ = bf16[128,2048]{1,0:T(8,128)(2,1)S(1)} collective-permute-done((bf16[128,2048]{1,0:T(8,128)(2,1)S(1)}, bf16[128,2048]{1,0:T(8,128)(2,1)S(1)}, u32[]{:S(2)}, u32[]{:S(2)}) %collective-permute-start.49) | collective-permute-done | bytes 524320 | tf_op jit(solution)/shard_map/sums out 4a/ppermute | solution.py:425
  128.2 1.6 %collective-permute-start.50 = (bf16[64,2048]{1,0:T(8,128)(2,1)S(1)}, bf16[64,2048]{1,0:T(8,128)(2,1)S(1)}, u32[]{:S(2)}, u32[]{:S(2)}) collective-permute-start(bf16[64,2048]{1,0:T(8,128)(2,1)S(1)} %add.30), channel_id=1, source_target_pairs={{0,4},{1,3},{4,8},{5,1},{8,12},{9,5},{12,14},{13,9},{14,10},{15,13... | collective-permute-start | bytes 786440 | tf_op jit(solution)/shard_map/sums out 5a/ppermute | solution.py:425
  129.8 1.9 %expert.10 = (bf16[128,2048]{1,0:T(8,128)(2,1)S(1)}, bf16[128,2048]{1,0:T(8,128)(2,1)S(1)}) custom-call(bf16[128,2048]{1,0:T(8,128)(2,1)S(1)} %collective-permute-done.30.refs_0_, bf16[128,2048]{1,0:T(8,128)(2,1)S(1)} %collective-permute-done.34.refs_1_, f32[128,128]{1,0:T(8,128)S(1)} %get-tuple-element.48.refs_2_.refs_3_, ...), custom_call_target="tpu_custom_call" | custom-call | flops 24000000000 | bytes 1000 | tf_op jit(solution)/shard_map/expert/pallas_call | solution.py:370
  131.9 1.4 collective-permute-start.53
  133.8 2.8 %collective-permute-done.50.refs_2_ = bf16[64,2048]{1,0:T(8,128)(2,1)S(1)} collective-permute-done((bf16[64,2048]{1,0:T(8,128)(2,1)S(1)}, bf16[64,2048]{1,0:T(8,128)(2,1)S(1)}, u32[]{:S(2)}, u32[]{:S(2)}) %collective-permute-start.50) | collective-permute-done | bytes 262176 | tf_op jit(solution)/shard_map/sums out 5a/ppermute | solution.py:425
  136.7 1.6 %collective-permute-start.51 = (bf16[64,2048]{1,0:T(8,128)(2,1)S(1)}, bf16[64,2048]{1,0:T(8,128)(2,1)S(1)}, u32[]{:S(2)}, u32[]{:S(2)}) collective-permute-start(bf16[64,2048]{1,0:T(8,128)(2,1)S(1)} %add.31), channel_id=1, source_target_pairs={{0,4},{1,3},{4,8},{5,1},{8,12},{9,5},{12,14},{13,9},{14,10},{15,13... | collective-permute-start | bytes 786440 | tf_op jit(solution)/shard_map/sums out 6a/ppermute | solution.py:425
  138.2 1.9 %expert.9 = (bf16[128,2048]{1,0:T(8,128)(2,1)S(1)}, bf16[128,2048]{1,0:T(8,128)(2,1)S(1)}) custom-call(bf16[128,2048]{1,0:T(8,128)(2,1)S(1)} %collective-permute-done.31.refs_0_, bf16[128,2048]{1,0:T(8,128)(2,1)S(1)} %collective-permute-done.32.refs_1_, f32[128,128]{1,0:T(8,128)S(1)} %get-tuple-element.48.refs_2_.refs_3_, ...), custom_call_target="tpu_custom_call" | custom-call | flops 24000000000 | bytes 1000 | tf_op jit(solution)/shard_map/expert/pallas_call | solution.py:370
  140.3 1.4 collective-permute-start.54
  143.2 1.6 %collective-permute-start.52 = (bf16[64,2048]{1,0:T(8,128)(2,1)S(1)}, bf16[64,2048]{1,0:T(8,128)(2,1)S(1)}, u32[]{:S(2)}, u32[]{:S(2)}) collective-permute-start(bf16[64,2048]{1,0:T(8,128)(2,1)S(1)} %add.32), channel_id=1, source_target_pairs={{0,4},{1,3},{4,8},{5,1},{8,12},{9,5},{12,14},{13,9},{14,10},{15,13... | collective-permute-start | bytes 786440 | tf_op jit(solution)/shard_map/sums out 7a/ppermute | solution.py:425
  144.8 2.0 %collective-permute-done.54.refs_2_ = bf16[64,2048]{1,0:T(8,128)(2,1)S(1)} collective-permute-done((bf16[64,2048]{1,0:T(8,128)(2,1)S(1)}, bf16[64,2048]{1,0:T(8,128)(2,1)S(1)}, u32[]{:S(2)}, u32[]{:S(2)}) %collective-permute-start.54) | collective-permute-done | bytes 262176 | tf_op jit(solution)/shard_map/sums out 6b/ppermute | solution.py:425
  146.8 1.4 collective-permute-start.55
  149.6 3.6 %collective-permute-done.55.refs_2_ = bf16[64,2048]{1,0:T(8,128)(2,1)S(1)} collective-permute-done((bf16[64,2048]{1,0:T(8,128)(2,1)S(1)}, bf16[64,2048]{1,0:T(8,128)(2,1)S(1)}, u32[]{:S(2)}, u32[]{:S(2)}) %collective-permute-start.55) | collective-permute-done | bytes 262176 | tf_op jit(solution)/shard_map/sums out 7b/ppermute | solution.py:425
  (113 shorter events, 14.9 us)
Async XLA Ops:
  3.1 27.3 %collective-permute-start = (bf16[2,128,2048]{2,1,0:T(8,128)(2,1)}, bf16[2,128,2048]{2,1,0:T(8,128)(2,1)}, u32[]{:S(2)}, u32[]{:S(2)}) collective-permute-start(bf16[2,128,2048]{2,1,0:T(8,128)(2,1)} %far_segment.1), channel_id=1, source_target_pairs={{0,16},{16,0},{1,17},{17,1},{2,18},{18,2},{3,19},{19,3},{4,20},{20... | collective-permute-start | bytes 3145736 | tf_op jit(solution)/shard_map/far segment/ppermute | solution.py:439
  6.1 24.3 %copy-start.7 = (bf16[2,1,2,128,2048]{4,3,2,1,0:T(8,128)(2,1)S(1)}, bf16[2,1,2,128,2048]{4,3,2,1,0:T(8,128)(2,1)}, u32[]{:S(2)}) copy-start(bf16[2,1,2,128,2048]{4,3,2,1,0:T(8,128)(2,1)} %cache_ref.9) | copy-start | bytes 6291460
  6.1 24.3 %copy-start.9 = (bf16[2,128,2048]{2,1,0:T(8,128)(2,1)S(1)}, bf16[2,128,2048]{2,1,0:T(8,128)(2,1)}, u32[]{:S(2)}) copy-start(bf16[2,128,2048]{2,1,0:T(8,128)(2,1)} %kv_ref.7) | copy-start | bytes 3145732
  6.1 24.3 %copy-start.11 = (bf16[128,2048]{1,0:T(8,128)(2,1)S(1)}, bf16[128,2048]{1,0:T(8,128)(2,1)}, u32[]{:S(2)}) copy-start(bf16[128,2048]{1,0:T(8,128)(2,1)} %q_ref.7) | copy-start | bytes 1572868
  6.1 24.3 %copy-start.17 = (s32[1,2]{1,0:T(1,128)S(1)}, s32[1,2]{1,0:T(1,128)}, u32[]{:S(2)}) copy-start(s32[1,2]{1,0:T(1,128)} %len_ref.9) | copy-start | bytes 28
  6.8 1.6 %collective-permute-start.6 = (bf16[136,1024]{1,0:T(8,128)(2,1)S(1)}, bf16[136,1024]{1,0:T(8,128)(2,1)S(1)}, u32[]{:S(2)}, u32[]{:S(2)}) collective-permute-start(bf16[136,1024]{1,0:T(8,128)(2,1)S(1)} %get-tuple-element.36), channel_id=1, source_target_pairs={{0,1},{1,0},{2,3},{3,2},{4,5},{5,4},{6,7},{7,6},{8,9},{9,8},{10,11... | collective-permute-start | bytes 835592 | tf_op jit(solution)/shard_map/to sibling/ppermute | solution.py:429
  6.8 6.5 %collective-permute-start.1 = (bf16[136,1024]{1,0:T(8,128)(2,1)S(1)}, bf16[136,1024]{1,0:T(8,128)(2,1)S(1)}, u32[]{:S(2)}, u32[]{:S(2)}) collective-permute-start(bf16[136,1024]{1,0:T(8,128)(2,1)S(1)} %get-tuple-element.34.refs_8_), channel_id=1, source_target_pairs={{0,4},{1,3},{4,8},{5,1},{8,12},{9,5},{12,14},{13,9},{14,10},{15,13... | collective-permute-start | bytes 835592 | tf_op jit(solution)/shard_map/o rows 1a/ppermute | solution.py:425
  8.4 8.0 %collective-permute-start.7 = (bf16[136,1024]{1,0:T(8,128)(2,1)S(1)}, bf16[136,1024]{1,0:T(8,128)(2,1)S(1)}, u32[]{:S(2)}, u32[]{:S(2)}) collective-permute-start(bf16[136,1024]{1,0:T(8,128)(2,1)S(1)} %collective-permute-done.6.refs_9_), channel_id=1, source_target_pairs={{0,4},{1,3},{4,8},{5,1},{8,12},{9,5},{12,14},{13,9},{14,10},{15,13... | collective-permute-start | bytes 835592 | tf_op jit(solution)/shard_map/o rows 1b/ppermute | solution.py:425
  13.4 6.5 %collective-permute-start.2 = (bf16[136,1024]{1,0:T(8,128)(2,1)S(1)}, bf16[136,1024]{1,0:T(8,128)(2,1)S(1)}, u32[]{:S(2)}, u32[]{:S(2)}) collective-permute-start(bf16[136,1024]{1,0:T(8,128)(2,1)S(1)} %collective-permute-done.1.refs_10_), channel_id=1, source_target_pairs={{0,4},{1,3},{4,8},{5,1},{8,12},{9,5},{12,14},{13,9},{14,10},{15,13... | collective-permute-start | bytes 835592 | tf_op jit(solution)/shard_map/o rows 2a/ppermute | solution.py:425
  16.4 7.2 %collective-permute-start.13 = (bf16[136,1024]{1,0:T(8,128)(2,1)S(1)}, bf16[136,1024]{1,0:T(8,128)(2,1)S(1)}, u32[]{:S(2)}, u32[]{:S(2)}) collective-permute-start(bf16[136,1024]{1,0:T(8,128)(2,1)S(1)} %collective-permute-done.7.refs_11_), channel_id=1, source_target_pairs={{0,4},{1,3},{4,8},{5,1},{8,12},{9,5},{12,14},{13,9},{14,10},{15,13... | collective-permute-start | bytes 835592 | tf_op jit(solution)/shard_map/o rows 2b/ppermute | solution.py:425
  19.9 6.5 %collective-permute-start.3 = (bf16[136,1024]{1,0:T(8,128)(2,1)S(1)}, bf16[136,1024]{1,0:T(8,128)(2,1)S(1)}, u32[]{:S(2)}, u32[]{:S(2)}) collective-permute-start(bf16[136,1024]{1,0:T(8,128)(2,1)S(1)} %collective-permute-done.2.refs_12_), channel_id=1, source_target_pairs={{0,4},{1,3},{4,8},{5,1},{8,12},{9,5},{12,14},{13,9},{14,10},{15,13... | collective-permute-start | bytes 835592 | tf_op jit(solution)/shard_map/o rows 3a/ppermute | solution.py:425
  21.5 22.3 %collective-permute-start.5 = (bf16[136,1024]{1,0:T(8,128)(2,1)S(1)}, bf16[136,1024]{1,0:T(8,128)(2,1)S(1)}, u32[]{:S(2)}, u32[]{:S(2)}) collective-permute-start(bf16[136,1024]{1,0:T(8,128)(2,1)S(1)} %collective-permute-done.1.refs_10_), channel_id=1, source_target_pairs={{0,16},{16,0},{1,17},{17,1},{2,18},{18,2},{3,19},{19,3},{4,20},{20... | collective-permute-start | bytes 835592 | tf_op jit(solution)/shard_map/o rows of partner/ppermute | solution.py:458
  22.0 26.6 %collective-permute-start.8 = (bf16[136,1024]{1,0:T(8,128)(2,1)S(1)}, bf16[136,1024]{1,0:T(8,128)(2,1)S(1)}, u32[]{:S(2)}, u32[]{:S(2)}) collective-permute-start(bf16[136,1024]{1,0:T(8,128)(2,1)S(1)} %collective-permute-done.7.refs_11_), channel_id=1, source_target_pairs={{0,16},{16,0},{1,17},{17,1},{2,18},{18,2},{3,19},{19,3},{4,20},{20... | collective-permute-start | bytes 835592 | tf_op jit(solution)/shard_map/o rows of partner/ppermute | solution.py:458
  23.5 9.3 %collective-permute-start.14 = (bf16[136,1024]{1,0:T(8,128)(2,1)S(1)}, bf16[136,1024]{1,0:T(8,128)(2,1)S(1)}, u32[]{:S(2)}, u32[]{:S(2)}) collective-permute-start(bf16[136,1024]{1,0:T(8,128)(2,1)S(1)} %collective-permute-done.13.refs_13_), channel_id=1, source_target_pairs={{0,4},{1,3},{4,8},{5,1},{8,12},{9,5},{12,14},{13,9},{14,10},{15,13... | collective-permute-start | bytes 835592 | tf_op jit(solution)/shard_map/o rows 3b/ppermute | solution.py:425
  26.5 8.5 %collective-permute-start.4 = (bf16[136,1024]{1,0:T(8,128)(2,1)S(1)}, bf16[136,1024]{1,0:T(8,128)(2,1)S(1)}, u32[]{:S(2)}, u32[]{:S(2)}) collective-permute-start(bf16[136,1024]{1,0:T(8,128)(2,1)S(1)} %collective-permute-done.3.refs_14_), channel_id=1, source_target_pairs={{0,4},{1,3},{4,8},{5,1},{8,12},{9,5},{12,14},{13,9},{14,10},{15,13... | collective-permute-start | bytes 835592 | tf_op jit(solution)/shard_map/o rows 4a/ppermute | solution.py:425
  32.7 18.3 %collective-permute-start.10 = (bf16[4,128,128]{2,1,0:T(8,128)(2,1)S(1)}, bf16[4,128,128]{2,1,0:T(8,128)(2,1)S(1)}, u32[]{:S(2)}, u32[]{:S(2)}) collective-permute-start(bf16[4,128,128]{2,1,0:T(8,128)(2,1)S(1)} %attend.5.refs_1_), channel_id=1, source_target_pairs={{0,1},{1,0},{2,3},{3,2},{4,5},{5,4},{6,7},{7,6},{8,9},{9,8},{10,11... | collective-permute-start | bytes 393224 | tf_op jit(solution)/shard_map/attended 1/ppermute | solution.py:429
  32.8 6.7 %collective-permute-start.15 = (bf16[136,1024]{1,0:T(8,128)(2,1)S(1)}, bf16[136,1024]{1,0:T(8,128)(2,1)S(1)}, u32[]{:S(2)}, u32[]{:S(2)}) collective-permute-start(bf16[136,1024]{1,0:T(8,128)(2,1)S(1)} %collective-permute-done.14.refs_15_), channel_id=1, source_target_pairs={{0,4},{1,3},{4,8},{5,1},{8,12},{9,5},{12,14},{13,9},{14,10},{15,13... | collective-permute-start | bytes 835592 | tf_op jit(solution)/shard_map/o rows 4b/ppermute | solution.py:425
  37.3 6.5 %copy-start = (bf16[136,1024]{1,0:T(8,128)(2,1)}, bf16[136,1024]{1,0:T(8,128)(2,1)S(1)}, u32[]{:S(2)}) copy-start(bf16[136,1024]{1,0:T(8,128)(2,1)S(1)} %get-tuple-element.37.refs_16_) | copy-start | bytes 835588
  37.3 6.7 %collective-permute-start.16 = (bf16[136,1024]{1,0:T(8,128)(2,1)S(1)}, bf16[136,1024]{1,0:T(8,128)(2,1)}, u32[]{:S(2)}, u32[]{:S(2)}) collective-permute-start(bf16[136,1024]{1,0:T(8,128)(2,1)S(1)} %get-tuple-element.37.refs_16_), channel_id=1, source_target_pairs={{0,4},{1,3},{4,8},{5,1},{8,12},{9,5},{12,14},{13,9},{14,10},{15,13... | collective-permute-start | bytes 835592 | tf_op jit(solution)/shard_map/o rows 5a/ppermute | solution.py:425
  39.5 7.5 %collective-permute-start.17 = (bf16[136,1024]{1,0:T(8,128)(2,1)S(1)}, bf16[136,1024]{1,0:T(8,128)(2,1)}, u32[]{:S(2)}, u32[]{:S(2)}) collective-permute-start(bf16[136,1024]{1,0:T(8,128)(2,1)S(1)} %collective-permute-done.15.refs_17_), channel_id=1, source_target_pairs={{0,4},{1,3},{4,8},{5,1},{8,12},{9,5},{12,14},{13,9},{14,10},{15,13... | collective-permute-start | bytes 835592 | tf_op jit(solution)/shard_map/o rows 5b/ppermute | solution.py:425
  43.8 7.1 %copy-start.2 = (bf16[136,1024]{1,0:T(8,128)(2,1)}, bf16[136,1024]{1,0:T(8,128)(2,1)S(1)}, u32[]{:S(2)}) copy-start(bf16[136,1024]{1,0:T(8,128)(2,1)S(1)} %collective-permute-done.5.refs_0_.refs_10_) | copy-start | bytes 835588
  43.9 7.7 %collective-permute-start.11 = (bf16[4,128,128]{2,1,0:T(8,128)(2,1)S(1)}, bf16[4,128,128]{2,1,0:T(8,128)(2,1)S(1)}, u32[]{:S(2)}, u32[]{:S(2)}) collective-permute-start(bf16[4,128,128]{2,1,0:T(8,128)(2,1)S(1)} %attend.6.refs_2_), channel_id=1, source_target_pairs={{0,1},{1,0},{2,3},{3,2},{4,5},{5,4},{6,7},{7,6},{8,9},{9,8},{10,11... | collective-permute-start | bytes 393224 | tf_op jit(solution)/shard_map/attended 2/ppermute | solution.py:429
  44.0 13.0 %collective-permute-start.18 = (bf16[136,1024]{1,0:T(8,128)(2,1)}, bf16[136,1024]{1,0:T(8,128)(2,1)}, u32[]{:S(2)}, u32[]{:S(2)}) collective-permute-start(bf16[136,1024]{1,0:T(8,128)(2,1)} %collective-permute-done.16.refs_18_), channel_id=1, source_target_pairs={{0,4},{1,3},{4,8},{5,1},{8,12},{9,5},{12,14},{13,9},{14,10},{15,13... | collective-permute-start | bytes 835592 | tf_op jit(solution)/shard_map/o rows 6a/ppermute | solution.py:425
  47.0 10.0 %collective-permute-start.19 = (bf16[136,1024]{1,0:T(8,128)(2,1)}, bf16[136,1024]{1,0:T(8,128)(2,1)}, u32[]{:S(2)}, u32[]{:S(2)}) collective-permute-start(bf16[136,1024]{1,0:T(8,128)(2,1)} %collective-permute-done.17.refs_19_), channel_id=1, source_target_pairs={{0,4},{1,3},{4,8},{5,1},{8,12},{9,5},{12,14},{13,9},{14,10},{15,13... | collective-permute-start | bytes 835592 | tf_op jit(solution)/shard_map/o rows 6b/ppermute | solution.py:425
  51.0 1.9 %collective-permute-start.12 = (bf16[4,128,128]{2,1,0:T(8,128)(2,1)S(1)}, bf16[4,128,128]{2,1,0:T(8,128)(2,1)S(1)}, u32[]{:S(2)}, u32[]{:S(2)}) collective-permute-start(bf16[4,128,128]{2,1,0:T(8,128)(2,1)S(1)} %attend.7.refs_3_), channel_id=1, source_target_pairs={{0,1},{1,0},{2,3},{3,2},{4,5},{5,4},{6,7},{7,6},{8,9},{9,8},{10,11... | collective-permute-start | bytes 393224 | tf_op jit(solution)/shard_map/attended 3/ppermute | solution.py:429
  51.1 2.2 %collective-permute-start.9 = (bf16[4,128,128]{2,1,0:T(8,128)(2,1)S(1)}, bf16[4,128,128]{2,1,0:T(8,128)(2,1)S(1)}, u32[]{:S(2)}, u32[]{:S(2)}) collective-permute-start(bf16[4,128,128]{2,1,0:T(8,128)(2,1)S(1)} %get-tuple-element.35.refs_0_), channel_id=1, source_target_pairs={{0,1},{1,0},{2,3},{3,2},{4,5},{5,4},{6,7},{7,6},{8,9},{9,8},{10,11... | collective-permute-start | bytes 393224 | tf_op jit(solution)/shard_map/attended 0/ppermute | solution.py:429
  51.5 5.4 %collective-permute-start.21 = (bf16[16,1024]{1,0:T(8,128)(2,1)}, bf16[16,1024]{1,0:T(8,128)(2,1)S(1)}, u32[]{:S(2)}, u32[]{:S(2)}) collective-permute-start(bf16[16,1024]{1,0:T(8,128)(2,1)} %copy-done.13), channel_id=1, source_target_pairs={{5,0},{2,1},{9,4},{0,5},{13,8},{4,9},{15,12},{8,13},{11,14},{12,15... | collective-permute-start | bytes 98312 | tf_op jit(solution)/shard_map/gate weights back/ppermute | solution.py:474
  52.8 4.2 %collective-permute-start.20 = (bf16[16,1024]{1,0:T(8,128)(2,1)}, bf16[16,1024]{1,0:T(8,128)(2,1)S(1)}, u32[]{:S(2)}, u32[]{:S(2)}) collective-permute-start(bf16[16,1024]{1,0:T(8,128)(2,1)} %copy-done.13), channel_id=1, source_target_pairs={{4,0},{3,1},{8,4},{1,5},{12,8},{5,9},{14,12},{9,13},{10,14},{13,15... | collective-permute-start | bytes 98312 | tf_op jit(solution)/shard_map/gate weights back/ppermute | solution.py:474
  59.0 1.8 %collective-permute-start.22 = (bf16[128,1024]{1,0:T(8,128)(2,1)S(1)}, bf16[128,1024]{1,0:T(8,128)(2,1)S(1)}, u32[]{:S(2)}, u32[]{:S(2)}) collective-permute-start(bf16[128,1024]{1,0:T(8,128)(2,1)S(1)} %get-tuple-element.42), channel_id=1, source_target_pairs={{0,1},{1,0},{2,3},{3,2},{4,5},{5,4},{6,7},{7,6},{8,9},{9,8},{10,11... | collective-permute-start | bytes 786440 | tf_op jit(solution)/shard_map/projected/ppermute | solution.py:429
  60.8 11.5 %copy-start.6 = (bf16[1,2048,1024]{2,1,0:T(8,128)(2,1)S(1)}, bf16[1,2048,1024]{2,1,0:T(8,128)(2,1)}, u32[]{:S(2)}) copy-start(bf16[1,2048,1024]{2,1,0:T(8,128)(2,1)} %refs_4_.15) | copy-start | bytes 12582916
  60.8 11.6 %copy-start.8 = (bf16[1,512,2048]{2,1,0:T(8,128)(2,1)S(1)}, bf16[1,512,2048]{2,1,0:T(8,128)(2,1)}, u32[]{:S(2)}) copy-start(bf16[1,512,2048]{2,1,0:T(8,128)(2,1)} %refs_5_.15) | copy-start | bytes 6291460
  61.2 9.2 %collective-permute-start.24 = (bf16[128,2048]{1,0:T(8,128)(2,1)S(1)}, bf16[128,2048]{1,0:T(8,128)(2,1)S(1)}, u32[]{:S(2)}, u32[]{:S(2)}) collective-permute-start(bf16[128,2048]{1,0:T(8,128)(2,1)S(1)} %get-tuple-element.44.refs_0_), channel_id=1, source_target_pairs={{0,4},{1,3},{4,8},{5,1},{8,12},{9,5},{12,14},{13,9},{14,10},{15,13... | collective-permute-start | bytes 1572872 | tf_op jit(solution)/shard_map/rows out 1a/ppermute | solution.py:425
  70.4 1.9 %collective-permute-start.44 = (bf16[128,2048]{1,0:T(8,128)(2,1)S(1)}, bf16[128,2048]{1,0:T(8,128)(2,1)S(1)}, u32[]{:S(2)}, u32[]{:S(2)}) collective-permute-start(bf16[128,2048]{1,0:T(8,128)(2,1)S(1)} %collective-permute-done.24.refs_0_), channel_id=1, source_target_pairs={{0,1},{1,0},{2,3},{3,2},{4,5},{5,4},{6,7},{7,6},{8,9},{9,8},{10,11... | collective-permute-start | bytes 1572872 | tf_op jit(solution)/shard_map/rows across 1a/ppermute | solution.py:429
  70.4 9.2 %collective-permute-start.25 = (bf16[128,2048]{1,0:T(8,128)(2,1)S(1)}, bf16[128,2048]{1,0:T(8,128)(2,1)S(1)}, u32[]{:S(2)}, u32[]{:S(2)}) collective-permute-start(bf16[128,2048]{1,0:T(8,128)(2,1)S(1)} %collective-permute-done.24.refs_0_), channel_id=1, source_target_pairs={{0,4},{1,3},{4,8},{5,1},{8,12},{9,5},{12,14},{13,9},{14,10},{15,13... | collective-permute-start | bytes 1572872 | tf_op jit(solution)/shard_map/rows out 2a/ppermute | solution.py:425
  74.2 6.9 %collective-permute-start.45 = (bf16[128,2048]{1,0:T(8,128)(2,1)S(1)}, bf16[128,2048]{1,0:T(8,128)(2,1)S(1)}, u32[]{:S(2)}, u32[]{:S(2)}) collective-permute-start(bf16[128,2048]{1,0:T(8,128)(2,1)S(1)} %get-tuple-element.62), channel_id=1, source_target_pairs={{0,1},{1,0},{2,3},{3,2},{4,5},{5,4},{6,7},{7,6},{8,9},{9,8},{10,11... | collective-permute-start | bytes 1572872 | tf_op jit(solution)/shard_map/sums across 1a/ppermute | solution.py:429
  79.6 3.1 %collective-permute-start.42 = (bf16[128,2048]{1,0:T(8,128)(2,1)S(1)}, bf16[128,2048]{1,0:T(8,128)(2,1)S(1)}, u32[]{:S(2)}, u32[]{:S(2)}) collective-permute-start(bf16[128,2048]{1,0:T(8,128)(2,1)S(1)} %collective-permute-done.25.refs_6_.refs_0_), channel_id=1, source_target_pairs={{0,1},{1,0},{2,3},{3,2},{4,5},{5,4},{6,7},{7,6},{8,9},{9,8},{10,11... | collective-permute-start | bytes 1572872 | tf_op jit(solution)/shard_map/rows across 2a/ppermute | solution.py:429
  79.6 9.2 %collective-permute-start.27 = (bf16[128,2048]{1,0:T(8,128)(2,1)S(1)}, bf16[128,2048]{1,0:T(8,128)(2,1)S(1)}, u32[]{:S(2)}, u32[]{:S(2)}) collective-permute-start(bf16[128,2048]{1,0:T(8,128)(2,1)S(1)} %collective-permute-done.25.refs_6_.refs_0_), channel_id=1, source_target_pairs={{0,4},{1,3},{4,8},{5,1},{8,12},{9,5},{12,14},{13,9},{14,10},{15,13... | collective-permute-start | bytes 1572872 | tf_op jit(solution)/shard_map/rows out 3a/ppermute | solution.py:425
  81.3 13.2 %collective-permute-start.46 = (bf16[128,2048]{1,0:T(8,128)(2,1)S(1)}, bf16[128,2048]{1,0:T(8,128)(2,1)S(1)}, u32[]{:S(2)}, u32[]{:S(2)}) collective-permute-start(bf16[128,2048]{1,0:T(8,128)(2,1)S(1)} %add.26), channel_id=1, source_target_pairs={{0,4},{1,3},{4,8},{5,1},{8,12},{9,5},{12,14},{13,9},{14,10},{15,13... | collective-permute-start | bytes 1572872 | tf_op jit(solution)/shard_map/sums out 1a/ppermute | solution.py:425
  84.6 9.8 %collective-permute-start.43 = (bf16[128,2048]{1,0:T(8,128)(2,1)S(1)}, bf16[128,2048]{1,0:T(8,128)(2,1)S(1)}, u32[]{:S(2)}, u32[]{:S(2)}) collective-permute-start(bf16[128,2048]{1,0:T(8,128)(2,1)S(1)} %get-tuple-element.60), channel_id=1, source_target_pairs={{0,1},{1,0},{2,3},{3,2},{4,5},{5,4},{6,7},{7,6},{8,9},{9,8},{10,11... | collective-permute-start | bytes 1572872 | tf_op jit(solution)/shard_map/sums across 2a/ppermute | solution.py:429
  88.8 7.4 %collective-permute-start.40 = (bf16[128,2048]{1,0:T(8,128)(2,1)S(1)}, bf16[128,2048]{1,0:T(8,128)(2,1)S(1)}, u32[]{:S(2)}, u32[]{:S(2)}) collective-permute-start(bf16[128,2048]{1,0:T(8,128)(2,1)S(1)} %collective-permute-done.27.refs_0_), channel_id=1, source_target_pairs={{0,1},{1,0},{2,3},{3,2},{4,5},{5,4},{6,7},{7,6},{8,9},{9,8},{10,11... | collective-permute-start | bytes 1572872 | tf_op jit(solution)/shard_map/rows across 3a/ppermute | solution.py:429
  88.8 11.2 %collective-permute-start.28 = (bf16[128,2048]{1,0:T(8,128)(2,1)S(1)}, bf16[128,2048]{1,0:T(8,128)(2,1)S(1)}, u32[]{:S(2)}, u32[]{:S(2)}) collective-permute-start(bf16[128,2048]{1,0:T(8,128)(2,1)S(1)} %collective-permute-done.27.refs_0_), channel_id=1, source_target_pairs={{0,4},{1,3},{4,8},{5,1},{8,12},{9,5},{12,14},{13,9},{14,10},{15,13... | collective-permute-start | bytes 1572872 | tf_op jit(solution)/shard_map/rows out 4a/ppermute | solution.py:425
  94.6 11.0 %collective-permute-start.47 = (bf16[128,2048]{1,0:T(8,128)(2,1)S(1)}, bf16[128,2048]{1,0:T(8,128)(2,1)S(1)}, u32[]{:S(2)}, u32[]{:S(2)}) collective-permute-start(bf16[128,2048]{1,0:T(8,128)(2,1)S(1)} %add.27), channel_id=1, source_target_pairs={{0,4},{1,3},{4,8},{5,1},{8,12},{9,5},{12,14},{13,9},{14,10},{15,13... | collective-permute-start | bytes 1572872 | tf_op jit(solution)/shard_map/sums out 2a/ppermute | solution.py:425
  98.1 7.6 %collective-permute-start.41 = (bf16[128,2048]{1,0:T(8,128)(2,1)S(1)}, bf16[128,2048]{1,0:T(8,128)(2,1)S(1)}, u32[]{:S(2)}, u32[]{:S(2)}) collective-permute-start(bf16[128,2048]{1,0:T(8,128)(2,1)S(1)} %get-tuple-element.58), channel_id=1, source_target_pairs={{0,1},{1,0},{2,3},{3,2},{4,5},{5,4},{6,7},{7,6},{8,9},{9,8},{10,11... | collective-permute-start | bytes 1572872 | tf_op jit(solution)/shard_map/sums across 3a/ppermute | solution.py:429
  100.0 7.4 %collective-permute-start.38 = (bf16[128,2048]{1,0:T(8,128)(2,1)S(1)}, bf16[128,2048]{1,0:T(8,128)(2,1)S(1)}, u32[]{:S(2)}, u32[]{:S(2)}) collective-permute-start(bf16[128,2048]{1,0:T(8,128)(2,1)S(1)} %collective-permute-done.28.refs_0_), channel_id=1, source_target_pairs={{0,1},{1,0},{2,3},{3,2},{4,5},{5,4},{6,7},{7,6},{8,9},{9,8},{10,11... | collective-permute-start | bytes 1572872 | tf_op jit(solution)/shard_map/rows across 4a/ppermute | solution.py:429
  100.1 11.2 %collective-permute-start.29 = (bf16[128,2048]{1,0:T(8,128)(2,1)S(1)}, bf16[128,2048]{1,0:T(8,128)(2,1)S(1)}, u32[]{:S(2)}, u32[]{:S(2)}) collective-permute-start(bf16[128,2048]{1,0:T(8,128)(2,1)S(1)} %collective-permute-done.28.refs_0_), channel_id=1, source_target_pairs={{0,4},{1,3},{4,8},{5,1},{8,12},{9,5},{12,14},{13,9},{14,10},{15,13... | collective-permute-start | bytes 1572872 | tf_op jit(solution)/shard_map/rows out 5a/ppermute | solution.py:425
  105.9 11.0 %collective-permute-start.48 = (bf16[128,2048]{1,0:T(8,128)(2,1)S(1)}, bf16[128,2048]{1,0:T(8,128)(2,1)S(1)}, u32[]{:S(2)}, u32[]{:S(2)}) collective-permute-start(bf16[128,2048]{1,0:T(8,128)(2,1)S(1)} %add.28), channel_id=1, source_target_pairs={{0,4},{1,3},{4,8},{5,1},{8,12},{9,5},{12,14},{13,9},{14,10},{15,13... | collective-permute-start | bytes 1572872 | tf_op jit(solution)/shard_map/sums out 3a/ppermute | solution.py:425
  109.3 7.6 %collective-permute-start.39 = (bf16[128,2048]{1,0:T(8,128)(2,1)S(1)}, bf16[128,2048]{1,0:T(8,128)(2,1)S(1)}, u32[]{:S(2)}, u32[]{:S(2)}) collective-permute-start(bf16[128,2048]{1,0:T(8,128)(2,1)S(1)} %get-tuple-element.56), channel_id=1, source_target_pairs={{0,1},{1,0},{2,3},{3,2},{4,5},{5,4},{6,7},{7,6},{8,9},{9,8},{10,11... | collective-permute-start | bytes 1572872 | tf_op jit(solution)/shard_map/sums across 4a/ppermute | solution.py:429
  109.4 11.2 %collective-permute-start.23 = (bf16[128,2048]{1,0:T(8,128)(2,1)S(1)}, bf16[128,2048]{1,0:T(8,128)(2,1)S(1)}, u32[]{:S(2)}, u32[]{:S(2)}) collective-permute-start(bf16[128,2048]{1,0:T(8,128)(2,1)S(1)} %get-tuple-element.44.refs_0_), channel_id=1, source_target_pairs={{0,1},{1,0},{2,3},{3,2},{4,5},{5,4},{6,7},{7,6},{8,9},{9,8},{10,11... | collective-permute-start | bytes 1572872 | tf_op jit(solution)/shard_map/normed/ppermute | solution.py:429
  111.3 7.4 %collective-permute-start.36 = (bf16[128,2048]{1,0:T(8,128)(2,1)S(1)}, bf16[128,2048]{1,0:T(8,128)(2,1)S(1)}, u32[]{:S(2)}, u32[]{:S(2)}) collective-permute-start(bf16[128,2048]{1,0:T(8,128)(2,1)S(1)} %collective-permute-done.29.refs_0_), channel_id=1, source_target_pairs={{0,1},{1,0},{2,3},{3,2},{4,5},{5,4},{6,7},{7,6},{8,9},{9,8},{10,11... | collective-permute-start | bytes 1572872 | tf_op jit(solution)/shard_map/rows across 5a/ppermute | solution.py:429
  111.3 11.8 %collective-permute-start.30 = (bf16[128,2048]{1,0:T(8,128)(2,1)S(1)}, bf16[128,2048]{1,0:T(8,128)(2,1)S(1)}, u32[]{:S(2)}, u32[]{:S(2)}) collective-permute-start(bf16[128,2048]{1,0:T(8,128)(2,1)S(1)} %collective-permute-done.29.refs_0_), channel_id=1, source_target_pairs={{0,4},{1,3},{4,8},{5,1},{8,12},{9,5},{12,14},{13,9},{14,10},{15,13... | collective-permute-start | bytes 1572872 | tf_op jit(solution)/shard_map/rows out 6a/ppermute | solution.py:425
  117.1 11.0 %collective-permute-start.49 = (bf16[128,2048]{1,0:T(8,128)(2,1)S(1)}, bf16[128,2048]{1,0:T(8,128)(2,1)S(1)}, u32[]{:S(2)}, u32[]{:S(2)}) collective-permute-start(bf16[128,2048]{1,0:T(8,128)(2,1)S(1)} %add.29), channel_id=1, source_target_pairs={{0,4},{1,3},{4,8},{5,1},{8,12},{9,5},{12,14},{13,9},{14,10},{15,13... | collective-permute-start | bytes 1572872 | tf_op jit(solution)/shard_map/sums out 4a/ppermute | solution.py:425
  120.5 7.6 %collective-permute-start.37 = (bf16[128,2048]{1,0:T(8,128)(2,1)S(1)}, bf16[128,2048]{1,0:T(8,128)(2,1)S(1)}, u32[]{:S(2)}, u32[]{:S(2)}) collective-permute-start(bf16[128,2048]{1,0:T(8,128)(2,1)S(1)} %get-tuple-element.54), channel_id=1, source_target_pairs={{0,1},{1,0},{2,3},{3,2},{4,5},{5,4},{6,7},{7,6},{8,9},{9,8},{10,11... | collective-permute-start | bytes 1572872 | tf_op jit(solution)/shard_map/sums across 5a/ppermute | solution.py:429
  122.5 25.8 %collective-permute-start.26 = (bf16[128,2048]{1,0:T(8,128)(2,1)S(1)}, bf16[128,2048]{1,0:T(8,128)(2,1)S(1)}, u32[]{:S(2)}, u32[]{:S(2)}) collective-permute-start(bf16[128,2048]{1,0:T(8,128)(2,1)S(1)} %get-tuple-element.47), channel_id=1, source_target_pairs={{0,1},{1,0},{2,3},{3,2},{4,5},{5,4},{6,7},{7,6},{8,9},{9,8},{10,11... | collective-permute-start | bytes 1572872 | tf_op jit(solution)/shard_map/sums across 0a/ppermute | solution.py:429
  123.1 6.7 %collective-permute-start.34 = (bf16[128,2048]{1,0:T(8,128)(2,1)S(1)}, bf16[128,2048]{1,0:T(8,128)(2,1)S(1)}, u32[]{:S(2)}, u32[]{:S(2)}) collective-permute-start(bf16[128,2048]{1,0:T(8,128)(2,1)S(1)} %collective-permute-done.30.refs_0_), channel_id=1, source_target_pairs={{0,1},{1,0},{2,3},{3,2},{4,5},{5,4},{6,7},{7,6},{8,9},{9,8},{10,11... | collective-permute-start | bytes 1572872 | tf_op jit(solution)/shard_map/rows across 6a/ppermute | solution.py:429
  123.2 10.6 %collective-permute-start.31 = (bf16[128,2048]{1,0:T(8,128)(2,1)S(1)}, bf16[128,2048]{1,0:T(8,128)(2,1)S(1)}, u32[]{:S(2)}, u32[]{:S(2)}) collective-permute-start(bf16[128,2048]{1,0:T(8,128)(2,1)S(1)} %collective-permute-done.30.refs_0_), channel_id=1, source_target_pairs={{0,4},{1,3},{4,8},{5,1},{8,12},{9,5},{12,14},{13,9},{14,10},{15,13... | collective-permute-start | bytes 1572872 | tf_op jit(solution)/shard_map/rows out 7a/ppermute | solution.py:425
  128.2 8.3 %collective-permute-start.50 = (bf16[64,2048]{1,0:T(8,128)(2,1)S(1)}, bf16[64,2048]{1,0:T(8,128)(2,1)S(1)}, u32[]{:S(2)}, u32[]{:S(2)}) collective-permute-start(bf16[64,2048]{1,0:T(8,128)(2,1)S(1)} %add.30), channel_id=1, source_target_pairs={{0,4},{1,3},{4,8},{5,1},{8,12},{9,5},{12,14},{13,9},{14,10},{15,13... | collective-permute-start | bytes 786440 | tf_op jit(solution)/shard_map/sums out 5a/ppermute | solution.py:425
  131.7 4.9 %collective-permute-start.35 = (bf16[128,2048]{1,0:T(8,128)(2,1)S(1)}, bf16[128,2048]{1,0:T(8,128)(2,1)S(1)}, u32[]{:S(2)}, u32[]{:S(2)}) collective-permute-start(bf16[128,2048]{1,0:T(8,128)(2,1)S(1)} %get-tuple-element.52), channel_id=1, source_target_pairs={{0,1},{1,0},{2,3},{3,2},{4,5},{5,4},{6,7},{7,6},{8,9},{9,8},{10,11... | collective-permute-start | bytes 1572872 | tf_op jit(solution)/shard_map/sums across 6a/ppermute | solution.py:429
  131.9 8.3 %collective-permute-start.53 = (bf16[64,2048]{1,0:T(8,128)(2,1)S(1)}, bf16[64,2048]{1,0:T(8,128)(2,1)S(1)}, u32[]{:S(2)}, u32[]{:S(2)}) collective-permute-start(bf16[64,2048]{1,0:T(8,128)(2,1)S(1)} %add.33), channel_id=1, source_target_pairs={{0,4},{1,3},{4,8},{5,1},{8,12},{9,5},{12,14},{13,9},{14,10},{15,13... | collective-permute-start | bytes 786440 | tf_op jit(solution)/shard_map/sums out 5b/ppermute | solution.py:425
  133.8 4.5 %collective-permute-start.32 = (bf16[128,2048]{1,0:T(8,128)(2,1)S(1)}, bf16[128,2048]{1,0:T(8,128)(2,1)S(1)}, u32[]{:S(2)}, u32[]{:S(2)}) collective-permute-start(bf16[128,2048]{1,0:T(8,128)(2,1)S(1)} %collective-permute-done.31.refs_0_), channel_id=1, source_target_pairs={{0,1},{1,0},{2,3},{3,2},{4,5},{5,4},{6,7},{7,6},{8,9},{9,8},{10,11... | collective-permute-start | bytes 1572872 | tf_op jit(solution)/shard_map/rows across 7a/ppermute | solution.py:429
  136.7 6.4 %collective-permute-start.51 = (bf16[64,2048]{1,0:T(8,128)(2,1)S(1)}, bf16[64,2048]{1,0:T(8,128)(2,1)S(1)}, u32[]{:S(2)}, u32[]{:S(2)}) collective-permute-start(bf16[64,2048]{1,0:T(8,128)(2,1)S(1)} %add.31), channel_id=1, source_target_pairs={{0,4},{1,3},{4,8},{5,1},{8,12},{9,5},{12,14},{13,9},{14,10},{15,13... | collective-permute-start | bytes 786440 | tf_op jit(solution)/shard_map/sums out 6a/ppermute | solution.py:425
  140.1 3.0 %collective-permute-start.33 = (bf16[128,2048]{1,0:T(8,128)(2,1)S(1)}, bf16[128,2048]{1,0:T(8,128)(2,1)S(1)}, u32[]{:S(2)}, u32[]{:S(2)}) collective-permute-start(bf16[128,2048]{1,0:T(8,128)(2,1)S(1)} %get-tuple-element.50), channel_id=1, source_target_pairs={{0,1},{1,0},{2,3},{3,2},{4,5},{5,4},{6,7},{7,6},{8,9},{9,8},{10,11... | collective-permute-start | bytes 1572872 | tf_op jit(solution)/shard_map/sums across 7a/ppermute | solution.py:429
  140.3 6.4 %collective-permute-start.54 = (bf16[64,2048]{1,0:T(8,128)(2,1)S(1)}, bf16[64,2048]{1,0:T(8,128)(2,1)S(1)}, u32[]{:S(2)}, u32[]{:S(2)}) collective-permute-start(bf16[64,2048]{1,0:T(8,128)(2,1)S(1)} %add.34), channel_id=1, source_target_pairs={{0,4},{1,3},{4,8},{5,1},{8,12},{9,5},{12,14},{13,9},{14,10},{15,13... | collective-permute-start | bytes 786440 | tf_op jit(solution)/shard_map/sums out 6b/ppermute | solution.py:425
  143.2 6.4 %collective-permute-start.52 = (bf16[64,2048]{1,0:T(8,128)(2,1)S(1)}, bf16[64,2048]{1,0:T(8,128)(2,1)S(1)}, u32[]{:S(2)}, u32[]{:S(2)}) collective-permute-start(bf16[64,2048]{1,0:T(8,128)(2,1)S(1)} %add.32), channel_id=1, source_target_pairs={{0,4},{1,3},{4,8},{5,1},{8,12},{9,5},{12,14},{13,9},{14,10},{15,13... | collective-permute-start | bytes 786440 | tf_op jit(solution)/shard_map/sums out 7a/ppermute | solution.py:425
  146.8 6.4 %collective-permute-start.55 = (bf16[64,2048]{1,0:T(8,128)(2,1)S(1)}, bf16[64,2048]{1,0:T(8,128)(2,1)S(1)}, u32[]{:S(2)}, u32[]{:S(2)}) collective-permute-start(bf16[64,2048]{1,0:T(8,128)(2,1)S(1)} %add.35), channel_id=1, source_target_pairs={{0,4},{1,3},{4,8},{5,1},{8,12},{9,5},{12,14},{13,9},{14,10},{15,13... | collective-permute-start | bytes 786440 | tf_op jit(solution)/shard_map/sums out 7b/ppermute | solution.py:425
  (10 other events, 35.6 us)
